TPU v7x, 32 devices: a whole 2x2x4 slice. The times are simulated.
32 devices in a mesh: fsdp: 4 (over y, x), dp: 8 (over z, core).
Axes of the slice: x: 2, y: 2, z: 4, core: 2. Of those that a mesh axis runs over, the one named last changes fastest.
Arguments:
- tokens: bfloat16 [32768, 768], P(('fsdp', 'dp')), may hold values from -7.5 to 7.5
- cotangent: bfloat16 [64, 204, 768], P(('fsdp', 'dp')), may hold values from -6 to 6
- positions: int32 [64, 204], P(('fsdp', 'dp')), may hold values from 0 to 511, as said below
- counts: int32 [64], P(('fsdp', 'dp')), may hold values from 10 to 204, as said below
- qkv_weight: float32 [768, 2304], P('dp', 'fsdp'), may hold values from -0.21875 to 0.21875
- qkv_moment: float32 [768, 2304], P('dp', 'fsdp'), may hold values from -0.00024414062 to 0.00024414062
- qkv_second: float32 [768, 2304], P('dp', 'fsdp'), may hold values from 1.3852441e-10 to 5.5409766e-10
- out_weight: float32 [768, 768], P('dp', 'fsdp'), may hold values from -2.5 to 2.5
- out_moment: float32 [768, 768], P('dp', 'fsdp'), may hold values from -0.00024414062 to 0.00024414062
- out_second: float32 [768, 768], P('dp', 'fsdp'), may hold values from 1.3852442e-11 to 5.5409767e-11
- up_weight: float32 [768, 3072], P('dp', 'fsdp'), may hold values from -0.21875 to 0.21875
- up_moment: float32 [768, 3072], P('dp', 'fsdp'), may hold values from -0.00024414062 to 0.00024414062
- up_second: float32 [768, 3072], P('dp', 'fsdp'), may hold values from 1.3852441e-10 to 5.5409766e-10
- down_projection_weight: float32 [3072, 768], P('dp', 'fsdp'), may hold values from -0.15625 to 0.15625
- down_moment: float32 [3072, 768], P('dp', 'fsdp'), may hold values from -0.00024414062 to 0.00024414062
- down_second: float32 [3072, 768], P('dp', 'fsdp'), may hold values from 1.3852441e-10 to 5.5409766e-10
- proj_weight: float32 [256, 512], P('fsdp', 'dp'), may hold values from -0.25 to 0.25
- proj_moment: float32 [256, 512], P('fsdp', 'dp'), may hold values from -0.00024414062 to 0.00024414062
- proj_second: float32 [256, 512], P('fsdp', 'dp'), may hold values from 1.3852441e-10 to 5.5409766e-10
- vec_weight: float32 [9984], P(('fsdp', 'dp')), may hold values from -0.8 to 4
- vec_moment: float32 [9984], P(('fsdp', 'dp')), may hold values from -0.0007324219 to 0.0007324219
- vec_second: float32 [9984], P(('fsdp', 'dp')), may hold values from 1.2467197e-09 to 4.986879e-09
Outputs:
- output: bfloat16 [32768, 768], P(('fsdp', 'dp'))
- grad_input: bfloat16 [32768, 768], P(('fsdp', 'dp'))
- grad_norm: float32 [], replicated
- qkv_next: float32 [768, 2304], P('dp', 'fsdp')
- qkv_moment_next: float32 [768, 2304], P('dp', 'fsdp')
- qkv_second_next: float32 [768, 2304], P('dp', 'fsdp')
- qkv_copy: bfloat16 [768, 2304], P('dp', 'fsdp')
- out_next: float32 [768, 768], P('dp', 'fsdp')
- out_moment_next: float32 [768, 768], P('dp', 'fsdp')
- out_second_next: float32 [768, 768], P('dp', 'fsdp')
- out_copy: bfloat16 [768, 768], P('dp', 'fsdp')
- up_next: float32 [768, 3072], P('dp', 'fsdp')
- up_moment_next: float32 [768, 3072], P('dp', 'fsdp')
- up_second_next: float32 [768, 3072], P('dp', 'fsdp')
- up_copy: bfloat16 [768, 3072], P('dp', 'fsdp')
- down_next: float32 [3072, 768], P('dp', 'fsdp')
- down_moment_next: float32 [3072, 768], P('dp', 'fsdp')
- down_second_next: float32 [3072, 768], P('dp', 'fsdp')
- down_copy: bfloat16 [3072, 768], P('dp', 'fsdp')
- proj_next: float32 [256, 512], P('fsdp', 'dp')
- proj_moment_next: float32 [256, 512], P('fsdp', 'dp')
- proj_second_next: float32 [256, 512], P('fsdp', 'dp')
- proj_copy: bfloat16 [256, 512], P('fsdp', 'dp')
- vec_next: float32 [9984], P(('fsdp', 'dp'))
- vec_moment_next: float32 [9984], P(('fsdp', 'dp'))
- vec_second_next: float32 [9984], P(('fsdp', 'dp'))
- vec_copy: bfloat16 [9984], P(('fsdp', 'dp'))
Inputs may be any that keep to these rules, and one draw needn't show every extreme that they name: `positions`: positions of one sequence are all different. `counts`: slot j of a sequence is masked exactly when j < its count; some sequence has exactly 204 in every draw.
All inputs are finite; a program needn't handle non-finite values.
Results may differ from a plain program's by a relative error of at most 0.018.
Values may be sent and summed in bfloat16 or wider, within the bound.
No kernel may reach another device: no remote copies, remote signals or barrier semaphores. Data moves between devices by JAX's collectives and lax.ppermute only.
A program may use at most 192 MiB of HBM per device.

v0:
```python
import jax
import jax.numpy as jnp
from jax import lax
from jax.sharding import PartitionSpec as P

HEADS = 12
STEP = 10


NORM_EPS = 1e-05
CLIP_NORM = 1.0
BETA_ONE = 0.9
BETA_TWO = 0.999
ADAM_EPS = 1e-08
DECAY_RATE = 0.01
RATE_QKV = 0.05
RATE_OUT = 0.4
RATE_UP = 0.05
RATE_DOWN = 0.05
RATE_PROJ = 0.05
RATE_VEC = 1.0


def split_up(value, dim, peers):
    dims = value.shape
    blocks = value.reshape(*dims[:dim], peers, dims[dim] // peers, *dims[dim + 1 :])
    return jnp.moveaxis(blocks, dim, 0)


def sum_at_owner(value, axis, dim):
    blocks = split_up(value, dim, lax.axis_size(axis))
    arrived = lax.all_to_all(blocks, axis, split_axis=0, concat_axis=0, tiled=True)
    return arrived.astype(jnp.float32).sum(axis=0)


def side_by_side(arrays, axis, dim, along):
    ends, at = ([], 0)
    for a in arrays[:-1]:
        at += a.shape[along]
        ends.append(at)
    both = jnp.concatenate(arrays, axis=along)
    return tuple(jnp.split(sum_at_owner(both, axis, dim), ends, axis=along))


def layer_norm(summed, gains, shifts):
    average = jnp.mean(summed, axis=-1, keepdims=True)
    centered = summed - average
    variance = jnp.mean(centered * centered, axis=-1, keepdims=True)
    return centered * lax.rsqrt(variance + NORM_EPS) * gains + shifts


def norm_back(summed, gains, shifts, grad_out):
    result, pullback = jax.vjp(layer_norm, summed, gains, shifts)
    return pullback(grad_out)


def gelu_exact(values):
    return jax.nn.gelu(values, approximate=False)


def split_vector(vec_full, model_width, hidden_width):
    mark_one = 3 * model_width
    mark_two = mark_one + model_width
    mark_three = mark_two + hidden_width
    mark_four = mark_three + model_width
    return (
        vec_full[:mark_one],
        vec_full[mark_one:mark_two],
        vec_full[mark_two:mark_three],
        vec_full[mark_three:mark_four],
        vec_full[mark_four : mark_four + model_width],
        vec_full[mark_four + model_width : mark_four + 2 * model_width],
        vec_full[mark_four + 2 * model_width : mark_four + 3 * model_width],
        vec_full[mark_four + 3 * model_width : mark_four + 4 * model_width],
    )


def adam_update(weight, moment, second, grad, scale_clip, rate, decay):
    clipped = grad * scale_clip
    new_moment = BETA_ONE * moment + (1.0 - BETA_ONE) * clipped
    new_second = BETA_TWO * second + (1.0 - BETA_TWO) * clipped * clipped
    moment_hat = new_moment / (1.0 - BETA_ONE**STEP)
    second_hat = new_second / (1.0 - BETA_TWO**STEP)
    new_weight = weight - rate * (moment_hat / (jnp.sqrt(second_hat) + ADAM_EPS) + decay * weight)
    return (new_weight, new_moment, new_second, new_weight.astype(jnp.bfloat16))


def fetch_whole(low_qkv, low_out, low_up, low_down, low_proj, low_vec):
    rows = (
        lax.all_gather(low_qkv, "dp", axis=0, tiled=True),
        lax.all_gather(low_out, "dp", axis=0, tiled=True),
        lax.all_gather(low_up, "dp", axis=0, tiled=True),
        lax.all_gather(low_down, "dp", axis=0, tiled=True),
        lax.all_gather(low_proj, "dp", axis=1, tiled=True),
        lax.all_gather(low_vec, "dp", axis=0, tiled=True),
    )
    return (
        lax.all_gather(rows[0], "fsdp", axis=1, tiled=True),
        lax.all_gather(rows[1], "fsdp", axis=1, tiled=True),
        lax.all_gather(rows[2], "fsdp", axis=1, tiled=True),
        lax.all_gather(rows[3], "fsdp", axis=1, tiled=True),
        lax.all_gather(rows[4], "fsdp", axis=0, tiled=True),
        lax.all_gather(rows[5], "fsdp", axis=0, tiled=True),
    )


def on_device(
    tokens,
    cotangent,
    positions,
    counts,
    qkv_weight,
    qkv_moment,
    qkv_second,
    out_weight,
    out_moment,
    out_second,
    up_weight,
    up_moment,
    up_second,
    down_projection_weight,
    down_moment,
    down_second,
    proj_weight,
    proj_moment,
    proj_second,
    vec_weight,
    vec_moment,
    vec_second,
):
    low_qkv = qkv_weight.astype(jnp.bfloat16)
    low_out = out_weight.astype(jnp.bfloat16)
    low_up = up_weight.astype(jnp.bfloat16)
    low_down = down_projection_weight.astype(jnp.bfloat16)
    low_proj = proj_weight.astype(jnp.bfloat16)
    low_vec = vec_weight.astype(jnp.bfloat16)
    qkv_full, out_full, up_full, down_full, projection_gathered, vec_full = fetch_whole(
        low_qkv, low_out, low_up, low_down, low_proj, low_vec
    )
    seq_count = counts.shape[0]
    row_count = tokens.shape[0]
    seq_length = row_count // seq_count
    model_width = tokens.shape[1]
    head_width = model_width // HEADS
    hidden_width = vec_full.shape[0] - 9 * model_width
    proj_rows = projection_gathered.shape[0]
    score_scale = head_width ** (-0.5)
    bias_qkv, bias_out, bias_up, bias_down, gain_one, shift_one, gain_two, shift_two = split_vector(
        vec_full.astype(jnp.float32), model_width, hidden_width
    )
    pre_qkv = jnp.dot(tokens, qkv_full, preferred_element_type=jnp.float32)
    qkv_low = (pre_qkv + bias_qkv).astype(jnp.bfloat16)
    queries = qkv_low[:, :model_width].reshape(seq_count, seq_length, HEADS, head_width)
    key_value_pair = qkv_low[:, model_width:].reshape(seq_count, seq_length, 2 * model_width)
    projected = jnp.einsum(
        "bu,vur->vbr", projection_gathered, key_value_pair, preferred_element_type=jnp.float32
    ).astype(jnp.bfloat16)
    key_heads = projected[:, :, :model_width].reshape(seq_count, proj_rows, HEADS, head_width)
    value_heads = projected[:, :, model_width:].reshape(seq_count, proj_rows, HEADS, head_width)
    scores = (
        jnp.einsum("slhe,sjhe->shlj", queries, key_heads, preferred_element_type=jnp.float32)
        * score_scale
    )
    peak = jnp.max(scores, axis=-1, keepdims=True)
    log_total = peak + jnp.log(jnp.sum(jnp.exp(scores - peak), axis=-1, keepdims=True))
    soft_low = jnp.exp(scores - log_total).astype(jnp.bfloat16)
    context = jnp.einsum(
        "shlj,sjhe->slhe", soft_low, value_heads, preferred_element_type=jnp.float32
    )
    attended = context.reshape(row_count, model_width).astype(jnp.bfloat16)
    first_sum = (
        tokens.astype(jnp.float32)
        + jnp.dot(attended, out_full, preferred_element_type=jnp.float32)
        + bias_out
    )
    normed_one = layer_norm(first_sum, gain_one, shift_one)
    normed_low = normed_one.astype(jnp.bfloat16)
    hidden_pre = jnp.dot(normed_low, up_full, preferred_element_type=jnp.float32) + bias_up
    active = gelu_exact(hidden_pre).astype(jnp.bfloat16)
    second_sum = (
        normed_one + jnp.dot(active, down_full, preferred_element_type=jnp.float32) + bias_down
    )
    output = layer_norm(second_sum, gain_two, shift_two).astype(jnp.bfloat16)
    slot_live = jnp.arange(positions.shape[1], dtype=jnp.int32)[None, :] < counts[:, None]
    one_hot_rows = (
        (positions[:, :, None] == jnp.arange(seq_length, dtype=jnp.int32)[None, None, :])
        & slot_live[:, :, None]
    ).astype(jnp.bfloat16)
    dense = jnp.einsum(
        "bej,bef->bjf", one_hot_rows, cotangent, preferred_element_type=jnp.float32
    ).reshape(row_count, model_width)
    qkv_full, out_full, up_full, down_full, projection_gathered, vec_full = fetch_whole(
        low_qkv, low_out, low_up, low_down, low_proj, low_vec
    )
    d_second, d_gain_two, d_shift_two = norm_back(second_sum, gain_two, shift_two, dense)
    d_bias_down = jnp.sum(d_second, axis=0)
    d_second_low = d_second.astype(jnp.bfloat16)
    grad_down = jnp.einsum("rf,rd->fd", active, d_second_low, preferred_element_type=jnp.float32)
    d_active = jnp.einsum("rd,fd->rf", d_second_low, down_full, preferred_element_type=jnp.float32)
    gelu_value, gelu_pull = jax.vjp(gelu_exact, hidden_pre)
    d_hidden = gelu_pull(d_active)[0]
    d_bias_up = jnp.sum(d_hidden, axis=0)
    d_hidden_low = d_hidden.astype(jnp.bfloat16)
    grad_up = jnp.einsum("rd,rf->df", normed_low, d_hidden_low, preferred_element_type=jnp.float32)
    d_normed = d_second + jnp.einsum(
        "rf,df->rd", d_hidden_low, up_full, preferred_element_type=jnp.float32
    )
    d_first, d_gain_one, d_shift_one = norm_back(first_sum, gain_one, shift_one, d_normed)
    d_bias_out = jnp.sum(d_first, axis=0)
    d_first_low = d_first.astype(jnp.bfloat16)
    grad_out = jnp.einsum("rd,re->de", attended, d_first_low, preferred_element_type=jnp.float32)
    d_attended = jnp.einsum("re,de->rd", d_first_low, out_full, preferred_element_type=jnp.float32)
    d_attended = d_attended.astype(jnp.bfloat16).reshape(seq_count, seq_length, HEADS, head_width)
    scores_again = (
        jnp.einsum("slhe,sjhe->shlj", queries, key_heads, preferred_element_type=jnp.float32)
        * score_scale
    )
    probs_again = jnp.exp(scores_again - log_total)
    probs_low = probs_again.astype(jnp.bfloat16)
    d_value_heads = jnp.einsum(
        "shlj,slhe->sjhe", probs_low, d_attended, preferred_element_type=jnp.float32
    )
    d_probs = jnp.einsum(
        "slhe,sjhe->shlj", d_attended, value_heads, preferred_element_type=jnp.float32
    )
    d_scores = probs_again * (d_probs - jnp.sum(probs_again * d_probs, axis=-1, keepdims=True))
    d_raw_low = (d_scores * score_scale).astype(jnp.bfloat16)
    d_queries = jnp.einsum(
        "shlj,sjhe->slhe", d_raw_low, key_heads, preferred_element_type=jnp.float32
    ).reshape(row_count, model_width)
    d_key_heads = jnp.einsum(
        "shlj,slhe->sjhe", d_raw_low, queries, preferred_element_type=jnp.float32
    )
    projected_gradient = jnp.concatenate(
        [
            d_key_heads.reshape(seq_count, proj_rows, model_width),
            d_value_heads.reshape(seq_count, proj_rows, model_width),
        ],
        axis=-1,
    ).astype(jnp.bfloat16)
    d_kv = jnp.einsum(
        "cq,uct->uqt", projection_gathered, projected_gradient, preferred_element_type=jnp.float32
    ).reshape(row_count, 2 * model_width)
    projection_gradient = jnp.einsum(
        "nhy,nxy->hx", projected_gradient, key_value_pair, preferred_element_type=jnp.float32
    )
    d_qkv = jnp.concatenate([d_queries, d_kv], axis=-1)
    d_bias_qkv = jnp.sum(d_qkv, axis=0)
    d_qkv_low = d_qkv.astype(jnp.bfloat16)
    grad_qkv = jnp.einsum("rd,re->de", tokens, d_qkv_low, preferred_element_type=jnp.float32)
    grad_input = (
        d_first + jnp.einsum("re,de->rd", d_qkv_low, qkv_full, preferred_element_type=jnp.float32)
    ).astype(jnp.bfloat16)
    grad_vec = jnp.concatenate(
        [
            d_bias_qkv,
            d_bias_out,
            d_bias_up,
            d_bias_down,
            d_gain_one,
            d_shift_one,
            d_gain_two,
            d_shift_two,
        ]
    )
    col_part = (
        lax.psum_scatter(
            grad_qkv.astype(jnp.bfloat16), "fsdp", scatter_dimension=1, tiled=True
        ).astype(jnp.float32),
        lax.psum_scatter(
            grad_out.astype(jnp.bfloat16), "fsdp", scatter_dimension=1, tiled=True
        ).astype(jnp.float32),
        lax.psum_scatter(
            grad_up.astype(jnp.bfloat16), "fsdp", scatter_dimension=1, tiled=True
        ).astype(jnp.float32),
        lax.psum_scatter(
            grad_down.astype(jnp.bfloat16), "fsdp", scatter_dimension=1, tiled=True
        ).astype(jnp.float32),
        lax.psum_scatter(
            projection_gradient.astype(jnp.bfloat16), "fsdp", scatter_dimension=0, tiled=True
        ).astype(jnp.float32),
        lax.psum_scatter(
            grad_vec.astype(jnp.bfloat16), "fsdp", scatter_dimension=0, tiled=True
        ).astype(jnp.float32),
    )
    owned = (
        *side_by_side(
            (
                col_part[0].astype(jnp.bfloat16),
                col_part[1].astype(jnp.bfloat16),
                col_part[2].astype(jnp.bfloat16),
            ),
            "dp",
            0,
            1,
        ),
        sum_at_owner(col_part[3].astype(jnp.bfloat16), "dp", 0),
        sum_at_owner(col_part[4].astype(jnp.bfloat16), "dp", 1),
        sum_at_owner(col_part[5].astype(jnp.bfloat16), "dp", 0),
    )
    owned_qkv, owned_out, owned_up, owned_down, owned_proj, owned_vec = owned
    local_squares = (
        jnp.sum(owned_qkv * owned_qkv)
        + jnp.sum(owned_out * owned_out)
        + jnp.sum(owned_up * owned_up)
        + jnp.sum(owned_down * owned_down)
        + jnp.sum(owned_proj * owned_proj)
        + jnp.sum(owned_vec * owned_vec)
    )
    all_squares = lax.psum(local_squares, ("fsdp", "dp"))
    grad_norm = jnp.sqrt(all_squares)
    scale_clip = jnp.minimum(1.0, CLIP_NORM / grad_norm)
    qkv_parts = adam_update(
        qkv_weight, qkv_moment, qkv_second, owned_qkv, scale_clip, RATE_QKV, DECAY_RATE
    )
    out_parts = adam_update(
        out_weight, out_moment, out_second, owned_out, scale_clip, RATE_OUT, DECAY_RATE
    )
    up_parts = adam_update(
        up_weight, up_moment, up_second, owned_up, scale_clip, RATE_UP, DECAY_RATE
    )
    down_parts = adam_update(
        down_projection_weight,
        down_moment,
        down_second,
        owned_down,
        scale_clip,
        RATE_DOWN,
        DECAY_RATE,
    )
    proj_parts = adam_update(
        proj_weight, proj_moment, proj_second, owned_proj, scale_clip, RATE_PROJ, DECAY_RATE
    )
    vec_parts = adam_update(
        vec_weight, vec_moment, vec_second, owned_vec, scale_clip, RATE_VEC, 0.0
    )
    return (
        output,
        grad_input,
        grad_norm,
        qkv_parts[0],
        qkv_parts[1],
        qkv_parts[2],
        qkv_parts[3],
        out_parts[0],
        out_parts[1],
        out_parts[2],
        out_parts[3],
        up_parts[0],
        up_parts[1],
        up_parts[2],
        up_parts[3],
        down_parts[0],
        down_parts[1],
        down_parts[2],
        down_parts[3],
        proj_parts[0],
        proj_parts[1],
        proj_parts[2],
        proj_parts[3],
        vec_parts[0],
        vec_parts[1],
        vec_parts[2],
        vec_parts[3],
    )


def solution(mesh):
    placed = (
        P(("fsdp", "dp"), None),
        P(("fsdp", "dp"), None, None),
        P(("fsdp", "dp"), None),
        P(("fsdp", "dp")),
        P("dp", "fsdp"),
        P("dp", "fsdp"),
        P("dp", "fsdp"),
        P("dp", "fsdp"),
        P("dp", "fsdp"),
        P("dp", "fsdp"),
        P("dp", "fsdp"),
        P("dp", "fsdp"),
        P("dp", "fsdp"),
        P("dp", "fsdp"),
        P("dp", "fsdp"),
        P("dp", "fsdp"),
        P("fsdp", "dp"),
        P("fsdp", "dp"),
        P("fsdp", "dp"),
        P(("fsdp", "dp")),
        P(("fsdp", "dp")),
        P(("fsdp", "dp")),
    )
    return jax.shard_map(
        on_device,
        mesh=mesh,
        in_specs=placed,
        out_specs=(
            P(("fsdp", "dp"), None),
            P(("fsdp", "dp"), None),
            P(),
            P("dp", "fsdp"),
            P("dp", "fsdp"),
            P("dp", "fsdp"),
            P("dp", "fsdp"),
            P("dp", "fsdp"),
            P("dp", "fsdp"),
            P("dp", "fsdp"),
            P("dp", "fsdp"),
            P("dp", "fsdp"),
            P("dp", "fsdp"),
            P("dp", "fsdp"),
            P("dp", "fsdp"),
            P("dp", "fsdp"),
            P("dp", "fsdp"),
            P("dp", "fsdp"),
            P("dp", "fsdp"),
            P("fsdp", "dp"),
            P("fsdp", "dp"),
            P("fsdp", "dp"),
            P("fsdp", "dp"),
            P(("fsdp", "dp")),
            P(("fsdp", "dp")),
            P(("fsdp", "dp")),
            P(("fsdp", "dp")),
        ),
        check_vma=False,
    )
```

profile of v0, /device:TPU:0, one launch (start us, length us, event | category | flops | bytes accessed | tf_op | source)
XLA Modules:
  0.0 708.1 jit_solution(14608186016115926447)
XLA Ops:
  11.8 22.7 %all_gather.46 = bf16[768,576]{1,0:T(8,128)(2,1)S(1)} all-gather(bf16[96,576]{1,0:T(8,128)(2,1)S(1)} %convert_element_type.141), channel_id=1, replica_groups=mesh['fsdp'=4,'dp'=8] {'dp'}, dimensions={0}, use_global_device_ids=true | all-gather | bytes 995328 | tf_op jit(solution)/shard_map/all_gather | solution.py:90
  35.9 14.4 %all_gather.52 = bf16[768,192]{1,0:T(8,128)(2,1)S(1)} all-gather(bf16[96,192]{1,0:T(8,128)(2,1)S(1)} %convert_element_type.152), channel_id=1, replica_groups=mesh['fsdp'=4,'dp'=8] {'dp'}, dimensions={0}, use_global_device_ids=true | all-gather | bytes 331776 | tf_op jit(solution)/shard_map/all_gather | solution.py:91
  54.7 15.6 %all-reduce = bf16[2496]{0:T(1024)(128)(2,1)S(1)} all-reduce(bf16[2496]{0:T(1024)(128)(2,1)S(1)} %dynamic-update-slice), channel_id=1, replica_groups=mesh['fsdp'=4,'dp'=8] {'dp'}, use_global_device_ids=true, to_apply=%add | all-reduce | flops 2496 | bytes 9984
  70.6 16.8 %all-reduce.1 = bf16[9984]{0:T(1024)(128)(2,1)S(1)} all-reduce(bf16[9984]{0:T(1024)(128)(2,1)S(1)} %dynamic-update-slice.1), channel_id=1, replica_groups=mesh['fsdp'=4,'dp'=8] {'fsdp'}, use_global_device_ids=true, to_apply=%add.1 | all-reduce | flops 9984 | bytes 39936
  87.5 3.0 fusion.106
  90.5 3.7 copy.165
  94.3 14.0 %all_gather.50 = bf16[64,512]{0,1:T(8,128)(2,1)S(1)} all-gather(bf16[64,64]{0,1:T(8,128)(2,1)S(1)} %copy.128), channel_id=1, replica_groups=mesh['fsdp'=4,'dp'=8] {'dp'}, dimensions={1}, use_global_device_ids=true | all-gather | bytes 73728 | tf_op jit(solution)/shard_map/all_gather | solution.py:94
  110.0 8.2 %all_gather.51 = bf16[256,512]{1,0:T(8,128)(2,1)S(1)} all-gather(bf16[64,512]{1,0:T(8,128)(2,1)S(1)} %copy.129), channel_id=1, replica_groups=mesh['fsdp'=4,'dp'=8] {'fsdp'}, dimensions={0}, use_global_device_ids=true | all-gather | bytes 327680 | tf_op jit(solution)/shard_map/all_gather | solution.py:102
  118.6 6.2 add_convert_fusion
  130.6 2.9 reshape.204
  133.5 3.6 multiply_reduce_fusion.1
  141.6 3.0 fusion.38
  146.7 3.8 fusion.103
  152.5 51.4 %all-gather.13.cloned.1.call-done = bf16[768,3072]{1,0:T(8,128)(2,1)} async-done(((bf16[768,768]{1,0:T(8,128)(2,1)}), bf16[768,3072]{1,0:T(8,128)(2,1)}) %all-gather.13.cloned.1.call-update) | async-done | bytes 4718608 | tf_op jit(solution)/shard_map/all_gather | solution.py:100
  203.9 37.6 %multiply_convert_fusion.1 = (bf16[1024,3072]{1,0:T(8,128)(2,1)}, f32[1024,3072]{1,0:T(8,128)}, f32[1024,3072]{1,0:T(8,128)}) fusion(f32[3072]{0:T(1024)S(1)} %slice.56, bf16[768,3072]{1,0:T(8,128)(2,1)} %all-gather.13.cloned.1.call-done, f32[1024,768]{0,1:T(8,128)} %copy-done.7, f32[768]{0:T(1024)S(1)} %get-tuple-element.177, ...), kind=kOutput, calls=%fused_computation.7 | convolution fusion | flops 5043388416 | bytes 39348224 | tf_op jit(solution)/shard_map/dot_general | solution.py:178
  241.5 21.2 %all-gather.17.cloned.1.call-done = bf16[3072,768]{0,1:T(8,128)(2,1)} async-done(((bf16[3072,192]{0,1:T(8,128)(2,1)}), bf16[3072,768]{0,1:T(8,128)(2,1)}) %all-gather.17.cloned.1.call-update) | async-done | bytes 4718608 | tf_op jit(solution)/shard_map/all_gather | solution.py:101
  262.7 9.4 %fusion.104 = (f32[1024]{0:T(1024)S(1)}, f32[1024,768]{0,1:T(8,128)S(1)}) fusion(f32[768]{0:T(1024)S(1)} %get-tuple-element.175, bf16[1024,3072]{1,0:T(8,128)(2,1)} %get-tuple-element.168, bf16[3072,768]{0,1:T(8,128)(2,1)} %all-gather.17.cloned.1.call-done, f32[768]{0:T(1024)S(1)} %get-tuple-element.177, f32[768]{0:T(1024)S(1)} %get-tuple-element.176, ...), kind=kOutput, calls=%fused_computation.164 | convolution fusion | flops 4837342208 | bytes 17323008 | tf_op jit(solution)/shard_map/dot_general | solution.py:181
  277.7 19.2 %fusion.105 = (bf16[3072]{0:T(1024)(128)(2,1)S(1)}, bf16[1024,3072]{1,0:T(8,128)(2,1)}) fusion(f32[1024,3072]{1,0:T(8,128)} %get-tuple-element.169, bf16[3072,768]{0,1:T(8,128)(2,1)} %all-gather.17.cloned.1.call-done, f32[1024,768]{0,1:T(8,128)S(1)} %get-tuple-element.167, f32[1024]{0:T(1024)S(1)} %negate_multiply_fusion.2, ...), kind=kOutput, calls=%fused_computation.165 | convolution fusion | flops 4883739648 | bytes 39344128 | tf_op jit(solution)/shard_map/rd,fd->rf/dot_general | solution.py:199
  296.9 10.0 %multiply_reduce_fusion.3 = (bf16[768]{0:T(1024)(128)(2,1)S(1)}, f32[1024]{0:T(1024)S(1)}, bf16[768]{0:T(1024)(128)(2,1)S(1)}, f32[1024,768]{0,1:T(8,128)S(1)}) fusion(f32[1024,768]{0,1:T(8,128)S(1)} %copy-done.8, f32[1024]{0:T(1024)S(1)} %fusion.67, f32[1024]{0:T(1024)S(1)} %broadcast_multiply_fusion.1, f32[768]{0:T(1024)S(1)} %get-tuple-element.176, ...), kind=kOutput, calls=%fused_computation.43 | convolution fusion | flops 4839699456 | bytes 20469760 | tf_op jit(solution)/shard_map/rf,df->rd/dot_general | solution.py:205
  312.5 2.9 reshape.207
  315.4 7.0 convolution_convert_fusion.7
  322.4 6.3 fusion.43
  329.0 19.6 %fusion.39 = bf16[2,12,64,256]{3,2,1,0:T(8,128)(2,1)S(1)} fusion(f32[2,12,512,256]{2,3,1,0:T(8,128)} %fusion.43, f32[2,12,512,256]{2,3,1,0:T(8,128)} %copy-done.2, f32[2,12,512]{2,1,0:T(8,128)S(1)} %copy-done.28, bf16[2,512,12,64]{1,0,3,2:T(2,128)(2,1)} %copy-done.13), kind=kOutput, calls=%fused_computation.71 | convolution fusion | flops 431370496 | bytes 27574272 | tf_op jit(solution)/shard_map/shlj,slhe->sjhe/dot_general | solution.py:231
  348.9 3.6 fusion.48
  352.6 9.5 %convolution_convert_fusion = bf16[3072,768]{0,1:T(8,128)(2,1)} fusion(bf16[1024,3072]{1,0:T(8,128)(2,1)} %get-tuple-element.168, f32[1024,768]{0,1:T(8,128)} %copy-done.10, f32[1024]{0:T(1024)S(1)} %negate_multiply_fusion.2), kind=kOutput, calls=%fused_computation.35 | convolution fusion | flops 4835770368 | bytes 14159872 | tf_op jit(solution)/shard_map/rf,rd->fd/dot_general | solution.py:198
  362.2 4.9 convolution_convert_fusion.6
  367.2 20.3 %fusion.33 = f32[2,512,12,64]{1,3,2,0:T(8,128)} fusion(bf16[2,256,12,64]{1,3,2,0:T(8,128)(2,1)S(1)} %bitcast.90, f32[2,12,512,256]{2,3,1,0:T(8,128)} %fusion.43, f32[2,12,512,256]{2,3,1,0:T(8,128)} %copy-done.2, f32[2,12,512]{2,1,0:T(8,128)S(1)} %copy-done.28), kind=kOutput, calls=%fused_computation.65 | convolution fusion | flops 430977280 | bytes 29147136 | tf_op jit(solution)/shard_map/shlj,sjhe->slhe/dot_general | solution.py:228
  387.6 4.3 copy.142
  394.4 3.6 copy.149
  399.0 2.7 copy-done.4
  401.6 6.0 fusion.27
  407.7 10.1 %convolution_convert_fusion.1 = bf16[768,3072]{1,0:T(8,128)(2,1)} fusion(bf16[1024,3072]{1,0:T(8,128)(2,1)} %get-tuple-element.190, f32[1024,768]{0,1:T(8,128)} %copy-done.7, f32[768]{0:T(1024)S(1)} %get-tuple-element.177, f32[768]{0:T(1024)S(1)} %get-tuple-element.176, f32[1024]{0:T(1024)S(1)} %fusion.67, f32[1024]{0:T(1024)S(1)} %broadcast_multiply_fusion.1), kind=kOutput, calls=%fused_computation.36 | convolution fusion | flops 4838129664 | bytes 14170112 | tf_op jit(solution)/shard_map/rd,rf->df/dot_general | solution.py:204
  418.5 5.0 fusion.17
  429.3 15.7 %all-reduce.2 = bf16[9984]{0:T(1024)(128)(2,1)S(1)} all-reduce(bf16[9984]{0:T(1024)(128)(2,1)S(1)} %constant_dynamic-update-slice_fusion), channel_id=7, replica_groups=mesh['fsdp'=4,'dp'=8] {'fsdp'}, use_global_device_ids=true, to_apply=%region_32.0.clone | all-reduce | flops 9984 | bytes 39936
  447.0 4.6 all-to-all-start.3
  453.5 3.8 all-to-all-done.3
  457.3 3.4 all-to-all-start.2
  463.1 3.4 all-to-all-done.2
  466.5 3.6 all-to-all-start.1
  471.2 49.0 %reduce-scatter.6.cloned.1.call-done = bf16[768,576]{0,1:T(8,128)(2,1)} async-done(((bf16[768,2304]{0,1:T(8,128)(2,1)}), bf16[768,576]{0,1:T(8,128)(2,1)}) %reduce-scatter.6.cloned.1.call-update) | async-done | bytes 884752 | tf_op jit(solution)/shard_map/reduce_scatter | solution.py:267
  521.7 58.8 %reduce-scatter.10.cloned.1.call-done = bf16[768,768]{1,0:T(8,128)(2,1)} async-done(((bf16[768,3072]{1,0:T(8,128)(2,1)}), bf16[768,768]{1,0:T(8,128)(2,1)}) %reduce-scatter.10.cloned.1.call-update) | async-done | bytes 1179664 | tf_op jit(solution)/shard_map/reduce_scatter | solution.py:273
  580.6 4.6 concatenate.16
  586.2 4.9 all-to-all-start
  591.1 2.6 copy.156
  593.7 10.7 %add_convert_fusion.1 = bf16[1024,768]{0,1:T(8,128)(2,1)} fusion(f32[1024,768]{0,1:T(8,128)} %copy-done.9, bf16[768,2304]{0,1:T(8,128)(2,1)} %all-gather.7.cloned.1.call-done, f32[1024]{0:T(1024)S(1)} %negate_multiply_fusion.1, f32[1024,1536]{1,0:T(8,128)} %bitcast.79, f32[1024,768]{1,0:T(8,128)} %copy.149), kind=kOutput, calls=%fused_computation.44 | convolution fusion | flops 3635675136 | bytes 17698816 | tf_op jit(solution)/shard_map/re,de->rd/dot_general | solution.py:252
  608.1 37.7 %all-to-all-done = bf16[8,96,1536]{2,1,0:T(8,128)(2,1)S(1)} async-done(((bf16[8,96,1536]{2,1,0:T(8,128)(2,1)}), bf16[8,96,1536]{2,1,0:T(8,128)(2,1)S(1)}, u32[]{:S(2)}, u32[]{:S(2)}) %all-to-all-start) | async-done | bytes 2359328 | tf_op jit(solution)/shard_map/all_to_all | solution.py:32
  652.2 2.6 copy.157
  654.9 36.9 %psum.7 = f32[]{:T(128)} all-reduce(f32[]{:T(128)S(6)} %add.232), channel_id=1, replica_groups=mesh['fsdp'=4,'dp'=8] {'fsdp','dp'}, use_global_device_ids=true, to_apply=%region_35.0 | all-reduce | flops 1 | bytes 8 | tf_op jit(solution)/shard_map/psum | solution.py:310
  (222 shorter events, 70.6 us)
Async XLA Ops:
  7.2 80.3 %copy-start = (bf16[2,204,768]{2,0,1:T(2,128)(2,1)S(1)}, bf16[2,204,768]{2,0,1:T(2,128)(2,1)}, u32[]{:S(2)}) copy-start(bf16[2,204,768]{2,0,1:T(2,128)(2,1)} %param.23) | copy-start | bytes 1880068
  7.2 28.6 %copy-start.29 = (f32[96,192]{1,0:T(8,128)S(1)}, f32[96,192]{1,0:T(8,128)}, u32[]{:S(2)}) copy-start(f32[96,192]{1,0:T(8,128)} %param.29) | copy-start | bytes 221188
  7.2 44.0 %all-gather.11.cloned.1.call-start = ((), (), s32[]{:S(2)}) async-start(), calls=%async_computation.11 | async-start | bytes 1327104 | tf_op jit(solution)/shard_map/all_gather | solution.py:92
  9.0 109.2 %all-gather.15.cloned.1.call-start = ((), (), s32[]{:S(2)}) async-start(), calls=%async_computation.13 | async-start | bytes 1327104 | tf_op jit(solution)/shard_map/all_gather | solution.py:93
  10.7 41.2 %copy-start.43 = (f32[312]{0:T(512)S(1)}, f32[312]{0:T(512)}, u32[]{:S(2)}) copy-start(f32[312]{0:T(512)} %param.41) | copy-start | bytes 3748
  10.7 41.2 %copy-start.51 = (u32[32]{0:T(128)S(1)}, u32[32]{0:T(128)}, u32[]{:S(2)}) copy-start(u32[32]{0:T(128)} %constant.29) | copy-start | bytes 388
  10.7 42.4 %copy-start.46 = (u32[32]{0:T(128)S(1)}, u32[32]{0:T(128)}, u32[]{:S(2)}) copy-start(u32[32]{0:T(128)} %constant.34) | copy-start | bytes 388
  10.7 76.6 %copy-start.50 = (s32[2]{0:T(128)S(1)}, s32[2]{0:T(128)}, u32[]{:S(2)}) copy-start(s32[2]{0:T(128)} %param.25) | copy-start | bytes 28
  10.8 76.7 %copy-start.45 = (s32[2,204]{1,0:T(2,128)S(1)}, s32[2,204]{1,0:T(2,128)}, u32[]{:S(2)}) copy-start(s32[2,204]{1,0:T(2,128)} %param.24) | copy-start | bytes 4900
  10.8 107.8 %all-gather.7.cloned.1.call-start = ((), (), s32[]{:S(2)}) async-start(), calls=%async_computation.9 | async-start | bytes 4423680 | tf_op jit(solution)/shard_map/all_gather | solution.py:98
  35.8 110.9 %all-gather.9.cloned.1.call-start = ((), (), s32[]{:S(2)}) async-start(), calls=%async_computation.10 | async-start | bytes 1474560 | tf_op jit(solution)/shard_map/all_gather | solution.py:99
  51.2 152.7 %all-gather.13.cloned.1.call-start = ((), (), s32[]{:S(2)}) async-start(), calls=%async_computation.12 | async-start | bytes 5898240 | tf_op jit(solution)/shard_map/all_gather | solution.py:100
  51.8 210.9 %all-gather.17.cloned.1.call-start = ((), (), s32[]{:S(2)}) async-start(), calls=%async_computation.14 | async-start | bytes 5898240 | tf_op jit(solution)/shard_map/all_gather | solution.py:101
  90.5 17.8 %copy-start.21 = (bf16[1024,768]{1,0:T(8,128)(2,1)S(1)}, bf16[1024,768]{1,0:T(8,128)(2,1)}, u32[]{:S(2)}) copy-start(bf16[1024,768]{1,0:T(8,128)(2,1)} %param.22) | copy-start | bytes 4718596
  118.2 8.8 %copy-start.19 = (bf16[256,512]{1,0:T(8,128)(2,1)}, bf16[256,512]{1,0:T(8,128)(2,1)S(1)}, u32[]{:S(2)}) copy-start(bf16[256,512]{1,0:T(8,128)(2,1)S(1)} %all_gather.51) | copy-start | bytes 786436
  118.2 333.4 %reduce-scatter.14.cloned.1.call-start = ((), (), s32[]{:S(2)}) async-start(), calls=%async_computation.19 | async-start | bytes 327680 | tf_op jit(solution)/shard_map/reduce_scatter | solution.py:279
  129.0 10.3 %copy-start.11 = (bf16[2,256,768]{1,2,0:T(8,128)(2,1)}, bf16[2,256,768]{1,2,0:T(8,128)(2,1)S(1)}, u32[]{:S(2)}) copy-start(bf16[2,256,768]{1,2,0:T(8,128)(2,1)S(1)} %get-tuple-element.172) | copy-start | bytes 2359300
  139.3 5.3 copy-start.27
  277.6 19.2 %copy-start.10 = (f32[1024,768]{0,1:T(8,128)}, f32[1024,768]{0,1:T(8,128)S(1)}, u32[]{:S(2)}) copy-start(f32[1024,768]{0,1:T(8,128)S(1)} %get-tuple-element.167) | copy-start | bytes 9437188
  277.6 19.2 %copy-start.8 = (f32[1024,768]{0,1:T(8,128)S(1)}, f32[1024,768]{0,1:T(8,128)}, u32[]{:S(2)}) copy-start(f32[1024,768]{0,1:T(8,128)} %copy-done.7) | copy-start | bytes 9437188
  315.4 7.0 copy-start.12
  352.5 108.1 %reduce-scatter.12.cloned.1.call-start = ((), (), s32[]{:S(2)}) async-start(), calls=%async_computation.18 | async-start | bytes 5898240 | tf_op jit(solution)/shard_map/reduce_scatter | solution.py:276
  362.2 107.9 %reduce-scatter.8.cloned.1.call-start = ((), (), s32[]{:S(2)}) async-start(), calls=%async_computation.16 | async-start | bytes 1474560 | tf_op jit(solution)/shard_map/reduce_scatter | solution.py:270
  367.2 153.0 %reduce-scatter.6.cloned.1.call-start = ((), (), s32[]{:S(2)}) async-start(), calls=%async_computation.15 | async-start | bytes 4423680 | tf_op jit(solution)/shard_map/reduce_scatter | solution.py:267
  407.6 172.9 %reduce-scatter.10.cloned.1.call-start = ((), (), s32[]{:S(2)}) async-start(), calls=%async_computation.17 | async-start | bytes 5898240 | tf_op jit(solution)/shard_map/reduce_scatter | solution.py:273
  423.4 5.8 copy-start.42
  447.0 10.2 %all-to-all-start.3 = ((bf16[8,2,156]{2,1,0:T(2,128)(2,1)}), bf16[8,2,156]{2,1,0:T(2,128)(2,1)S(1)}, u32[]{:S(2)}, u32[]{:S(2)}) async-start(bf16[8,2,156]{2,1,0:T(2,128)(2,1)} %reshape.230), calls=%async_computation.8 | async-start | bytes 16384 | tf_op jit(solution)/shard_map/all_to_all | solution.py:32
  457.3 9.2 %all-to-all-start.2 = ((bf16[8,2,2048]{2,1,0:T(2,128)(2,1)}), bf16[8,2,2048]{2,1,0:T(2,128)(2,1)S(1)}, u32[]{:S(2)}, u32[]{:S(2)}) async-start(bf16[8,2,2048]{2,1,0:T(2,128)(2,1)} %reshape.228), calls=%async_computation.7 | async-start | bytes 131072 | tf_op jit(solution)/shard_map/all_to_all | solution.py:32
  466.5 118.8 %all-to-all-start.1 = ((bf16[8,384,192]{1,2,0:T(8,128)(2,1)}), bf16[8,384,192]{1,2,0:T(8,128)(2,1)S(1)}, u32[]{:S(2)}, u32[]{:S(2)}) async-start(bf16[8,384,192]{1,2,0:T(8,128)(2,1)} %bitcast.75), calls=%async_computation.5 | async-start | bytes 2359296 | tf_op jit(solution)/shard_map/all_to_all | solution.py:32
  586.2 59.5 %all-to-all-start = ((bf16[8,96,1536]{2,1,0:T(8,128)(2,1)}), bf16[8,96,1536]{2,1,0:T(8,128)(2,1)S(1)}, u32[]{:S(2)}, u32[]{:S(2)}) async-start(bf16[8,96,1536]{2,1,0:T(8,128)(2,1)} %bitcast.17), calls=%async_computation.3 | async-start | bytes 4718592 | tf_op jit(solution)/shard_map/all_to_all | solution.py:32
  607.4 85.1 %copy-start.26 = (f32[96,576]{1,0:T(8,128)S(1)}, f32[96,576]{1,0:T(8,128)}, u32[]{:S(2)}) copy-start(f32[96,576]{1,0:T(8,128)} %param.26) | copy-start | bytes 663556
  646.2 48.7 %copy-start.30 = (f32[96,192]{1,0:T(8,128)S(1)}, f32[96,192]{1,0:T(8,128)}, u32[]{:S(2)}) copy-start(f32[96,192]{1,0:T(8,128)} %param.29) | copy-start | bytes 221188
  646.2 48.7 %copy-start.39 = (f32[96,192]{1,0:T(8,128)S(1)}, f32[96,192]{1,0:T(8,128)}, u32[]{:S(2)}) copy-start(f32[96,192]{1,0:T(8,128)} %param.30) | copy-start | bytes 221188
  646.2 50.4 %copy-start.24 = (f32[96,768]{1,0:T(8,128)S(1)}, f32[96,768]{1,0:T(8,128)}, u32[]{:S(2)}) copy-start(f32[96,768]{1,0:T(8,128)} %param.32) | copy-start | bytes 884740
  646.2 50.4 %copy-start.31 = (f32[96,768]{1,0:T(8,128)S(1)}, f32[96,768]{1,0:T(8,128)}, u32[]{:S(2)}) copy-start(f32[96,768]{1,0:T(8,128)} %param.33) | copy-start | bytes 884740
  646.2 50.4 %copy-start.32 = (f32[96,768]{1,0:T(8,128)S(1)}, f32[96,768]{1,0:T(8,128)}, u32[]{:S(2)}) copy-start(f32[96,768]{1,0:T(8,128)} %param.34) | copy-start | bytes 884740
  648.2 46.6 %copy-start.16 = (f32[96,1536]{1,0:T(8,128)S(1)}, f32[96,1536]{1,0:T(8,128)}, u32[]{:S(2)}) copy-start(f32[96,1536]{1,0:T(8,128)} %copy-done.15) | copy-start | bytes 1769476
  652.2 45.5 %copy-start.25 = (f32[384,192]{0,1:T(8,128)S(1)}, f32[384,192]{0,1:T(8,128)}, u32[]{:S(2)}) copy-start(f32[384,192]{0,1:T(8,128)} %param.35) | copy-start | bytes 884740
  652.2 45.5 %copy-start.33 = (f32[384,192]{0,1:T(8,128)S(1)}, f32[384,192]{0,1:T(8,128)}, u32[]{:S(2)}) copy-start(f32[384,192]{0,1:T(8,128)} %param.36) | copy-start | bytes 884740
  654.9 44.0 %copy-start.36 = (f32[64,64]{1,0:T(8,128)S(1)}, f32[64,64]{1,0:T(8,128)}, u32[]{:S(2)}) copy-start(f32[64,64]{1,0:T(8,128)} %copy-done.35) | copy-start | bytes 49156
  654.9 44.0 %copy-start.38 = (f32[64,64]{1,0:T(8,128)S(1)}, f32[64,64]{1,0:T(8,128)}, u32[]{:S(2)}) copy-start(f32[64,64]{1,0:T(8,128)} %param.38) | copy-start | bytes 49156
  654.9 44.0 %copy-start.40 = (f32[64,64]{1,0:T(8,128)S(1)}, f32[64,64]{1,0:T(8,128)}, u32[]{:S(2)}) copy-start(f32[64,64]{1,0:T(8,128)} %param.39) | copy-start | bytes 49156
  692.5 7.7 %copy-start.1 = (bf16[2,204,768]{2,0,1:T(2,128)(2,1)S(1)}, bf16[2,204,768]{2,0,1:T(2,128)(2,1)}, u32[]{:S(2)}) copy-start(bf16[2,204,768]{2,0,1:T(2,128)(2,1)} %param.23) | copy-start | bytes 1880068
  692.5 5.2 copy-start.34
  692.5 6.3 copy-start.41
  692.5 7.0 copy-start.44
  692.5 7.0 copy-start.47
  692.6 7.0 copy-start.48
  (20 other events, 59.0 us)
Sparse Core Ops, SparseCore 0:
  10.3 29.3 all-gather.10
  41.9 22.5 all-gather.14
  66.9 47.0 all-gather.6
  116.2 28.8 all-gather.8
  146.8 57.0 all-gather.12
  205.6 57.0 all-gather.16
  352.6 24.0 reduce-scatter.13
  380.0 57.3 reduce-scatter.11
  441.2 28.5 reduce-scatter.7
  473.0 47.2 reduce-scatter.5
  523.5 57.0 reduce-scatter.9
where the time goes:
time: 715 us; the launch traced here: 708 us
  waiting for transfers between devices  226 us (32%)
  matrix products  197 us (28%)
  blocking collectives  144 us (20%)
  local copies, waits for them, and re-layouts  65.2 us (9%)
  other arithmetic  35.1 us (5%)
  between operations  22.9 us (3%)
  starting transfers between devices  17.2 us (2%)
    reduce_scatter x1, waiting for transfers between devices, on_device(): lax.psum_scatter(grad_up.astype(jnp.bfloat16), 'fsdp', scatter_dimension=...  58.8 us
    all_gather x1, waiting for transfers between devices, fetch_whole(): lax.all_gather(rows[2], 'fsdp', axis=1, tiled=True)  51.4 us
    reduce_scatter x1, waiting for transfers between devices, on_device(): lax.psum_scatter(grad_qkv.astype(jnp.bfloat16), 'fsdp', scatter_dimension...  49 us
    unnamed x3, blocking collectives  48.1 us
    all_to_all x4, waiting for transfers between devices, sum_at_owner(): lax.all_to_all(blocks, axis, split_axis=0, concat_axis=0, tiled=True)  44.8 us
    dot_general x1, matrix products, on_device(): jnp.dot(normed_low, up_full, preferred_element_type=jnp.float32) + bias_up  37.6 us
    psum x1, blocking collectives, on_device(): all_squares = lax.psum(local_squares, ('fsdp', 'dp'))  36.9 us
    unnamed x128, local copies, waits for them, and re-layouts  27.6 us
  transfers between devices with their start and end apart: 15, of which 7 were waited for; matrix products, arithmetic and copies ran while one was open for 26% of the time, Pallas kernels for 0%

commit v1 on v0

--- a/solution.py
+++ b/solution.py
@@ -1,12 +1,15 @@
+import functools
+import math
+
 import jax
 import jax.numpy as jnp
 from jax import lax
+from jax.experimental import pallas as pl
+from jax.experimental.pallas import tpu as pltpu
 from jax.sharding import PartitionSpec as P
 
 HEADS = 12
 STEP = 10
-
-
 NORM_EPS = 1e-05
 CLIP_NORM = 1.0
 BETA_ONE = 0.9
@@ -19,6 +22,1259 @@
 RATE_DOWN = 0.05
 RATE_PROJ = 0.05
 RATE_VEC = 1.0
+
+BF = jnp.bfloat16
+F32 = jnp.float32
+LOG2E = math.log2(math.e)
+MIB = 1 << 20
+
+
+def nn(a, b):
+    return jnp.dot(a, b, preferred_element_type=F32)
+
+
+def nt(a, b):
+    return lax.dot_general(a, b, (((1,), (1,)), ((), ())), preferred_element_type=F32)
+
+
+def sds(shape, dtype):
+    return jax.ShapeDtypeStruct(tuple(shape), dtype)
+
+
+def whole(shape):
+    n = len(shape)
+    return pl.BlockSpec(tuple(shape), lambda *_: (0,) * n)
+
+
+def nbytes(x):
+    return math.prod(x.shape) * jnp.dtype(x.dtype).itemsize
+
+
+def call(
+    kernel,
+    name,
+    out_shape,
+    args,
+    grid=(1,),
+    in_specs=None,
+    out_specs=None,
+    scratch=(),
+    place=None,
+    flops=0,
+    exps=0,
+    vmem=48,
+):
+    many = isinstance(out_shape, (list, tuple))
+    outs = list(out_shape) if many else [out_shape]
+    if in_specs is None:
+        in_specs = [whole(a.shape) for a in args]
+    if out_specs is None:
+        out_specs = [whole(o.shape) for o in outs]
+    moved = sum(nbytes(a) for a in args) + sum(nbytes(o) for o in outs)
+    result = pl.pallas_call(
+        kernel,
+        name=name,
+        out_shape=outs,
+        grid_spec=pltpu.PrefetchScalarGridSpec(
+            num_scalar_prefetch=0 if place is None else 1,
+            grid=grid,
+            in_specs=in_specs,
+            out_specs=out_specs,
+            scratch_shapes=list(scratch),
+        ),
+        cost_estimate=pl.CostEstimate(
+            flops=int(flops), bytes_accessed=int(moved), transcendentals=int(exps)
+        ),
+        compiler_params=pltpu.CompilerParams(
+            vmem_limit_bytes=vmem * MIB,
+            dimension_semantics=("arbitrary",) * len(grid),
+        ),
+    )(*(() if place is None else (place,)), *args)
+    return result if many else result[0]
+
+
+def norm_stats(summed):
+    average = jnp.mean(summed, axis=-1, keepdims=True)
+    centered = summed - average
+    variance = jnp.mean(centered * centered, axis=-1, keepdims=True)
+    inverse = lax.rsqrt(variance + NORM_EPS)
+    return centered * inverse, inverse
+
+
+def norm_grad(shaped, inverse, gains, grad):
+    inner = grad * gains
+    first = jnp.mean(inner, axis=-1, keepdims=True)
+    second = jnp.mean(inner * shaped, axis=-1, keepdims=True)
+    return inverse * (inner - first - shaped * second)
+
+
+def normal_parts(values):
+    size = jnp.abs(values)
+    base = 1.0 + (0.3275911 * math.sqrt(0.5)) * size
+    t = pl.reciprocal(base, approx=True)
+    t = t * (2.0 - base * t)
+    bell = jnp.exp2(values * values * (-0.5 * LOG2E))
+    poly = 0.5 * 1.061405429
+    for c in (-1.453152027, 1.421413741, -0.284496736, 0.254829592):
+        poly = poly * t + 0.5 * c
+    tail = poly * t * bell
+    return bell, jnp.where(values >= 0.0, 1.0 - tail, tail)
+
+
+def pack_kernel(qkv, out, up, down, proj, vec, a_ref, b_ref, c_ref, small):
+    rows, wide = qkv.shape
+    a_ref[:rows, :wide] = qkv[...].astype(BF)
+    a_ref[:rows, wide:] = out[...].astype(BF)
+    small[...] = jnp.zeros_like(small)
+    height, width = proj.shape
+    for g in range(height // 8):
+        small[0:8, g * width : (g + 1) * width] = proj[8 * g : 8 * g + 8, :]
+    start = (height // 8) * width
+    room = small.shape[1] - start
+    small[0:1, start:] = vec[:, :room]
+    left = vec.shape[1] - room
+    small[1:2, start : start + left] = vec[:, room:]
+    a_ref[rows:, :] = small[...].astype(BF)
+    b_ref[...] = up[...].astype(BF)
+    thin = down.shape[1]
+    for g in range(down.shape[0] // rows):
+        c_ref[:, g * thin : (g + 1) * thin] = down[rows * g : rows * (g + 1), :].astype(BF)
+
+
+def pack(qkv, out, up, down, proj, vec):
+    rows, wide = qkv.shape[0], qkv.shape[1] + out.shape[1]
+    return call(
+        pack_kernel,
+        "pack_weights",
+        [sds((rows + 16, wide), BF), sds((rows, wide), BF), sds((rows, wide), BF)],
+        (qkv, out, up, down, proj, vec),
+        scratch=[pltpu.VMEM((16, wide), F32)],
+    )
+
+
+def order_kernel(marked, pos, x, front, rest, frontt, xt, back):
+    length = x.shape[1]
+    half = front.shape[1]
+    col = lax.broadcasted_iota(jnp.int32, (half, length), 1)
+    row = lax.broadcasted_iota(jnp.int32, (half, length), 0)
+    hot = (pos[0] == col) & (row < marked)
+    listed = jnp.sum(hot.astype(F32), axis=0, keepdims=True)
+    free = 1.0 - listed
+    before = (
+        lax.broadcasted_iota(jnp.int32, (length, length), 0)
+        < lax.broadcasted_iota(jnp.int32, (length, length), 1)
+    ).astype(BF)
+    rank = nn(jnp.broadcast_to(free, (16, length)).astype(BF), before)[0:1, :]
+    target = jnp.where(free > 0.5, rank.astype(jnp.int32) + marked, -1)
+    one = hot | (target == row)
+    two = target == (row + half)
+    one = jnp.where(one, 1.0, 0.0)
+    two = jnp.where(two, 1.0, 0.0)
+    values = x[0]
+    head = nn(one.astype(BF), values)
+    front[0] = head.astype(BF)
+    rest[0] = nn(two.astype(BF), values).astype(BF)
+    frontt[...] = head.T.astype(BF)
+    xt[...] = values.T
+    back[0, :, :half] = one.T.astype(BF)
+    back[0, :, half:] = two.T.astype(BF)
+
+
+def order_rows(tokens, positions):
+    seqs, length, width = tokens.shape
+    marked = positions.shape[1]
+    half = length // 2
+    pos = jnp.pad(positions, ((0, 0), (0, half - marked)), constant_values=-1)[:, :, None]
+    rows = sds((seqs, half, width), BF)
+    spec = pl.BlockSpec((1, half, width), lambda s: (s, 0, 0))
+    return call(
+        functools.partial(order_kernel, marked),
+        "order_rows",
+        [
+            rows,
+            rows,
+            sds((width, seqs * half), BF),
+            sds((width, seqs * length), BF),
+            sds((seqs, length, length), BF),
+        ],
+        (pos, tokens),
+        grid=(seqs,),
+        in_specs=[
+            pl.BlockSpec((1, half, 1), lambda s: (s, 0, 0)),
+            pl.BlockSpec((1, length, width), lambda s: (s, 0, 0)),
+        ],
+        out_specs=[
+            spec,
+            spec,
+            pl.BlockSpec((width, half), lambda s: (0, s)),
+            pl.BlockSpec((width, length), lambda s: (0, s)),
+            pl.BlockSpec((1, length, length), lambda s: (s, 0, 0)),
+        ],
+        flops=2 * seqs * length * length * width,
+    )
+
+
+def qkv_kernel(front, rest, x, weight, vec, proj, q_front, q_rest, kv, kvp):
+    width = front.shape[2]
+    piece = width // 2
+    for j in range(2):
+        cols = slice(j * piece, (j + 1) * piece)
+        w = weight[:, cols]
+        bias = vec[:, cols]
+        q_front[0, :, cols] = (nn(front[0], w) + bias).astype(BF)
+        q_rest[0, :, cols] = (nn(rest[0], w) + bias).astype(BF)
+    for j in range(4):
+        cols = slice(j * piece, (j + 1) * piece)
+        at = slice(width + j * piece, width + (j + 1) * piece)
+        part = (nn(x[0], weight[:, at]) + vec[:, at]).astype(BF)
+        kv[0, :, cols] = part
+        kvp[0, :, cols] = nn(proj[...], part).astype(BF)
+
+
+def make_qkv(front, rest, x, weight, vec, proj):
+    seqs, half, width = front.shape
+    length = x.shape[1]
+    rows = proj.shape[0]
+
+    def per(*shape):
+        return pl.BlockSpec((1, *shape), lambda s: (s, 0, 0))
+
+    return call(
+        qkv_kernel,
+        "make_qkv",
+        [
+            sds(front.shape, BF),
+            sds(front.shape, BF),
+            sds((seqs, length, 2 * width), BF),
+            sds((seqs, rows, 2 * width), BF),
+        ],
+        (front, rest, x, weight, vec, proj),
+        grid=(seqs,),
+        in_specs=[
+            per(half, width),
+            per(half, width),
+            per(length, width),
+            whole(weight.shape),
+            whole(vec.shape),
+            whole(proj.shape),
+        ],
+        out_specs=[per(half, width), per(half, width), per(length, 2 * width), per(rows, 2 * width)],
+        flops=2 * seqs * length * width * width * 3 + 2 * seqs * rows * length * 2 * width,
+    )
+
+
+def attend_kernel(head, q_front, q_rest, keys, values, o_front, o_rest):
+    lane = lax.broadcasted_iota(jnp.int32, (1, 2 * head), 1)
+    k, v = keys[0], values[0]
+    zero = jnp.zeros_like(k)
+    factor = LOG2E / math.sqrt(head)
+    pairs = [
+        (jnp.where(own, k, zero), jnp.where(own, v, zero)) for own in (lane < head, lane >= head)
+    ]
+    for q_ref, o_ref in ((q_front, o_front), (q_rest, o_rest)):
+        total = None
+        for kh, vh in pairs:
+            s = nt(q_ref[0], kh)
+            e = jnp.exp2((s - jnp.max(s, axis=-1, keepdims=True)) * factor)
+            scale = 1.0 / jnp.sum(e, axis=-1, keepdims=True)
+            part = nn(e.astype(BF), vh) * scale
+            total = part if total is None else total + part
+        o_ref[0] = total.astype(BF)
+
+
+def attend(q_front, q_rest, kvp):
+    seqs, half, width = q_front.shape
+    rows = kvp.shape[1]
+    head = width // HEADS
+    pairs = HEADS // 2
+    spec = pl.BlockSpec((1, half, 2 * head), lambda s, p: (s, 0, p))
+    return call(
+        functools.partial(attend_kernel, head),
+        "attend",
+        [sds(q_front.shape, BF)] * 2,
+        (q_front, q_rest, kvp, kvp),
+        grid=(seqs, pairs),
+        in_specs=[
+            spec,
+            spec,
+            pl.BlockSpec((1, rows, 2 * head), lambda s, p: (s, 0, p)),
+            pl.BlockSpec((1, rows, 2 * head), lambda s, p: (s, 0, p + pairs)),
+        ],
+        out_specs=[spec, spec],
+        flops=2 * seqs * HEADS * 2 * half * rows * 2 * head * 2,
+        exps=seqs * HEADS * 2 * half * rows,
+    )
+
+
+def join_kernel(marks, keep, attended, x, weight, vec, normed, low, *more):
+    bias, gain, shift = (vec[:, a:b] for a, b in marks)
+    summed = x[...].astype(F32) + nn(attended[...], weight[...]) + bias
+    shaped, _ = norm_stats(summed)
+    result = shaped * gain + shift
+    normed[...] = result
+    low[...] = result.astype(BF)
+    if keep:
+        kept, lowt, attendedt = more
+        kept[...] = summed
+        lowt[...] = result.T.astype(BF)
+        attendedt[...] = attended[...].T
+
+
+def join(attended, x, weight, vec, marks, keep):
+    rows, width = x.shape
+    block = min(256, rows)
+    spec = pl.BlockSpec((block, width), lambda i: (i, 0))
+    across = pl.BlockSpec((width, block), lambda i: (0, i))
+    outs = [sds((rows, width), F32), sds((rows, width), BF)]
+    specs = [spec, spec]
+    if keep:
+        outs += [sds((rows, width), F32), sds((width, rows), BF), sds((width, rows), BF)]
+        specs += [spec, across, across]
+    return call(
+        functools.partial(join_kernel, marks, keep),
+        "join_front" if keep else "join_rest",
+        outs,
+        (attended, x, weight, vec),
+        grid=(rows // block,),
+        in_specs=[spec, spec, whole(weight.shape), whole(vec.shape)],
+        out_specs=specs,
+        flops=2 * rows * width * width,
+    )
+
+
+def lift_kernel(keep, low, weight, bias, active, *more):
+    rows = low.shape[0]
+    step = 128
+    w = weight[0]
+    for r in range(0, rows, step):
+        u = nn(low[r : r + step, :], w) + bias[...]
+        bell, share = normal_parts(u)
+        a = u * share
+        active[r : r + step, :] = a.astype(BF)
+        if keep:
+            slope, activet = more
+            slope[r : r + step, :] = (share + u * bell * (1.0 / math.sqrt(2.0 * math.pi))).astype(BF)
+            activet[:, r : r + step] = a.T.astype(BF)
+
+
+def lift(low, weight, vec, mark, keep):
+    rows, width = low.shape
+    parts, _, piece = weight.shape
+    first = mark // piece
+    spec = pl.BlockSpec((rows, piece), lambda f: (0, f))
+    outs, specs = [sds((rows, parts * piece), BF)], [spec]
+    if keep:
+        outs += [sds((rows, parts * piece), BF), sds((parts * piece, rows), BF)]
+        specs += [spec, pl.BlockSpec((piece, rows), lambda f: (f, 0))]
+    return call(
+        functools.partial(lift_kernel, keep),
+        "lift_front" if keep else "lift_rest",
+        outs,
+        (low, weight, vec),
+        grid=(parts,),
+        in_specs=[
+            whole(low.shape),
+            pl.BlockSpec((1, width, piece), lambda f: (f, 0, 0)),
+            pl.BlockSpec((1, piece), lambda f: (0, first + f)),
+        ],
+        out_specs=specs,
+        flops=2 * rows * width * parts * piece,
+        exps=2 * rows * parts * piece,
+    )
+
+
+def lower_rest_kernel(marks, active, normed, weight, vec, output):
+    bias, gain, shift = (vec[:, a:b] for a, b in marks)
+    summed = normed[...] + nn(active[...], weight[...]) + bias
+    shaped, _ = norm_stats(summed)
+    output[...] = (shaped * gain + shift).astype(BF)
+
+
+def lower_front_kernel(marks, active, normed, weight, vec, dy, output, d_sum, d_low, sums):
+    bias, gain, shift = (vec[:, a:b] for a, b in marks)
+    summed = normed[...] + nn(active[...], weight[...]) + bias
+    shaped, inverse = norm_stats(summed)
+    output[...] = (shaped * gain + shift).astype(BF)
+    grad = dy[...].astype(F32)
+    back = norm_grad(shaped, inverse, gain, grad)
+    d_sum[...] = back
+    d_low[...] = back.astype(BF)
+
+    @pl.when(pl.program_id(0) == 0)
+    def _():
+        sums[...] = jnp.zeros_like(sums)
+
+    sums[0:1, :] += jnp.sum(grad * shaped, axis=0, keepdims=True)
+    sums[1:2, :] += jnp.sum(grad, axis=0, keepdims=True)
+    sums[2:3, :] += jnp.sum(back, axis=0, keepdims=True)
+
+
+def lower(active, normed, weight, vec, marks, dy=None):
+    rows, width = normed.shape
+    hidden = active.shape[1]
+    block = min(256, rows)
+    spec = pl.BlockSpec((block, width), lambda i: (i, 0))
+    wide = pl.BlockSpec((block, hidden), lambda i: (i, 0))
+    flops = 2 * rows * width * hidden
+    if dy is None:
+        return call(
+            functools.partial(lower_rest_kernel, marks),
+            "lower_rest",
+            sds((rows, width), BF),
+            (active, normed, weight, vec),
+            grid=(rows // block,),
+            in_specs=[wide, spec, whole(weight.shape), whole(vec.shape)],
+            out_specs=[spec],
+            flops=flops,
+        )
+    return call(
+        functools.partial(lower_front_kernel, marks),
+        "lower_front",
+        [
+            sds((rows, width), BF),
+            sds((rows, width), F32),
+            sds((rows, width), BF),
+            sds((8, width), F32),
+        ],
+        (active, normed, weight, vec, dy),
+        grid=(rows // block,),
+        in_specs=[wide, spec, whole(weight.shape), whole(vec.shape), spec],
+        out_specs=[spec, spec, spec, whole((8, width))],
+        flops=flops,
+    )
+
+
+def hidden_back_kernel(d_low, weight, slope, d_hidden, sums):
+    step = 256
+    for r in range(0, d_low.shape[0], step):
+        du = nt(d_low[r : r + step, :], weight[...]) * slope[r : r + step, :].astype(F32)
+        d_hidden[r : r + step, :] = du.astype(BF)
+        part = jnp.sum(du, axis=0, keepdims=True)
+        if r == 0:
+            sums[...] = part
+        else:
+            sums[...] += part
+
+
+def hidden_back(d_low, weight, slope):
+    rows, width = d_low.shape
+    hidden = weight.shape[0]
+    piece = width
+    spec = pl.BlockSpec((rows, piece), lambda f: (0, f))
+    return call(
+        hidden_back_kernel,
+        "hidden_back",
+        [sds((rows, hidden), BF), sds((1, hidden), F32)],
+        (d_low, weight, slope),
+        grid=(hidden // piece,),
+        in_specs=[whole(d_low.shape), pl.BlockSpec((piece, width), lambda f: (f, 0)), spec],
+        out_specs=[spec, pl.BlockSpec((1, piece), lambda f: (0, f))],
+        flops=2 * rows * width * hidden,
+    )
+
+
+def first_back_kernel(
+    marks, d_hidden, up, d_sum, kept, vec, weight, d_first, d_low, d_attended, sums, total
+):
+    part = nt(d_hidden[...], up[0])
+
+    @pl.when(pl.program_id(0) == 0)
+    def _():
+        total[...] = d_sum[...] + part
+
+    @pl.when(pl.program_id(0) > 0)
+    def _():
+        total[...] += part
+
+    @pl.when(pl.program_id(0) == pl.num_programs(0) - 1)
+    def _():
+        gain = vec[:, marks[0] : marks[1]]
+        grad = total[...]
+        shaped, inverse = norm_stats(kept[...])
+        back = norm_grad(shaped, inverse, gain, grad)
+        low = back.astype(BF)
+        d_first[...] = back
+        d_low[...] = low
+        sums[...] = jnp.zeros_like(sums)
+        sums[0:1, :] = jnp.sum(grad * shaped, axis=0, keepdims=True)
+        sums[1:2, :] = jnp.sum(grad, axis=0, keepdims=True)
+        sums[2:3, :] = jnp.sum(back, axis=0, keepdims=True)
+        d_attended[...] = nt(low, weight[...]).astype(BF)
+
+
+def first_back(d_hidden, up, d_sum, kept, vec, weight, marks):
+    rows, width = d_sum.shape
+    parts, _, piece = up.shape
+    full = (rows, width)
+    return call(
+        functools.partial(first_back_kernel, marks),
+        "first_back",
+        [sds(full, F32), sds(full, BF), sds(full, BF), sds((8, width), F32)],
+        (d_hidden, up, d_sum, kept, vec, weight),
+        grid=(parts,),
+        in_specs=[
+            pl.BlockSpec((rows, piece), lambda f: (0, f)),
+            pl.BlockSpec((1, width, piece), lambda f: (f, 0, 0)),
+            whole(full),
+            whole(full),
+            whole(vec.shape),
+            whole(weight.shape),
+        ],
+        out_specs=[whole(full), whole(full), whole(full), whole((8, width))],
+        scratch=[pltpu.VMEM(full, F32)],
+        flops=2 * rows * width * (parts * piece + width),
+    )
+
+
+def attend_back_kernel(head, queries, keys, values, grads, d_q, d_k, d_v, sums):
+    lane = lax.broadcasted_iota(jnp.int32, (1, 2 * head), 1)
+    line = lax.broadcasted_iota(jnp.int32, (2 * head, 1), 0)
+    q, k, v, g = queries[0], keys[0], values[0], grads[0]
+    zero = jnp.zeros_like(k)
+    kt = k.T
+    scale = 1.0 / math.sqrt(head)
+    dq = dk = dv = None
+    for own, ownt in ((lane < head, line < head), (lane >= head, line >= head)):
+        s = nt(jnp.where(own, k, zero), q)
+        e = jnp.exp2((s - jnp.max(s, axis=0, keepdims=True)) * (LOG2E * scale))
+        p = e * (1.0 / jnp.sum(e, axis=0, keepdims=True))
+        dv_part = nn(p.astype(BF), jnp.where(own, g, jnp.zeros_like(g)))
+        dp = nt(jnp.where(own, v, zero), g)
+        both = p * dp
+        ds = ((both - p * jnp.sum(both, axis=0, keepdims=True)) * scale).astype(BF)
+        dk_part = nn(ds, jnp.where(own, q, jnp.zeros_like(q)))
+        dq_part = nn(jnp.where(ownt, kt, jnp.zeros_like(kt)), ds)
+        dv = dv_part if dv is None else dv + dv_part
+        dk = dk_part if dk is None else dk + dk_part
+        dq = dq_part if dq is None else dq + dq_part
+    dq = dq.T
+    d_q[0] = dq.astype(BF)
+    d_k[0] = dk.astype(BF)
+    d_v[0] = dv.astype(BF)
+    sums[0] = jnp.sum(dq, axis=0, keepdims=True)
+
+
+def attend_back(queries, kvp, grads):
+    seqs, half, width = queries.shape
+    rows = kvp.shape[1]
+    head = width // HEADS
+    pairs = HEADS // 2
+    spec = pl.BlockSpec((1, half, 2 * head), lambda s, p: (s, 0, p))
+    proj = pl.BlockSpec((1, rows, 2 * head), lambda s, p: (s, 0, p))
+    return call(
+        functools.partial(attend_back_kernel, head),
+        "attend_back",
+        [
+            sds(queries.shape, BF),
+            sds((seqs, rows, width), BF),
+            sds((seqs, rows, width), BF),
+            sds((seqs, 1, width), F32),
+        ],
+        (queries, kvp, kvp, grads),
+        grid=(seqs, pairs),
+        in_specs=[
+            spec,
+            proj,
+            pl.BlockSpec((1, rows, 2 * head), lambda s, p: (s, 0, p + pairs)),
+            spec,
+        ],
+        out_specs=[spec, proj, proj, pl.BlockSpec((1, 1, 2 * head), lambda s, p: (s, 0, p))],
+        flops=2 * seqs * HEADS * half * rows * 2 * head * 5,
+        exps=seqs * HEADS * half * rows,
+    )
+
+
+def spread_kernel(d_k, d_v, kv, projt, d_kv, d_proj, sums):
+    width = d_k.shape[2]
+    grad = None
+    for j, ref in enumerate((d_k, d_v)):
+        cols = slice(j * width, (j + 1) * width)
+        part = nn(projt[...], ref[0])
+        d_kv[0, :, cols] = part.astype(BF)
+        sums[0, :, cols] = jnp.sum(part, axis=0, keepdims=True)
+        more = nt(ref[0], kv[0, :, cols])
+        grad = more if grad is None else grad + more
+
+    @pl.when(pl.program_id(0) == 0)
+    def _():
+        d_proj[...] = grad
+
+    @pl.when(pl.program_id(0) > 0)
+    def _():
+        d_proj[...] += grad
+
+
+def spread(d_k, d_v, kv, projt):
+    seqs, rows, width = d_k.shape
+    length = kv.shape[1]
+
+    def per(*shape):
+        return pl.BlockSpec((1, *shape), lambda s: (s, 0, 0))
+
+    return call(
+        spread_kernel,
+        "spread_kv",
+        [
+            sds((seqs, length, 2 * width), BF),
+            sds((rows, length), F32),
+            sds((seqs, 1, 2 * width), F32),
+        ],
+        (d_k, d_v, kv, projt),
+        grid=(seqs,),
+        in_specs=[
+            per(rows, width),
+            per(rows, width),
+            per(length, 2 * width),
+            whole(projt.shape),
+        ],
+        out_specs=[per(length, 2 * width), whole((rows, length)), per(1, 2 * width)],
+        flops=2 * seqs * rows * length * 2 * width * 2,
+    )
+
+
+def input_back_kernel(d_kv, d_q, d_first, weight, back, result):
+    width = d_q.shape[2]
+    half = d_q.shape[1]
+    front = d_first[0] + nt(d_q[0], weight[:, :width])
+    high = front.astype(BF)
+    low = (front - high.astype(F32)).astype(BF)
+    place = back[0, :, :half]
+    total = nt(d_kv[0], weight[:, width:]) + nn(place, high) + nn(place, low)
+    result[0] = total.astype(BF)
+
+
+def input_back(d_kv, d_q, d_first, weight, back):
+    seqs, length, wide = d_kv.shape
+    half, width = d_q.shape[1:]
+
+    def per(*shape):
+        return pl.BlockSpec((1, *shape), lambda s: (s, 0, 0))
+
+    return call(
+        input_back_kernel,
+        "input_back",
+        sds((seqs, length, width), BF),
+        (d_kv, d_q, d_first, weight, back),
+        grid=(seqs,),
+        in_specs=[
+            per(length, wide),
+            per(half, width),
+            per(half, width),
+            whole(weight.shape),
+            per(length, length),
+        ],
+        out_specs=[per(length, width)],
+        flops=2 * seqs * length * width * (wide + width // 2 + length),
+    )
+
+
+def restore_kernel(front, rest, back, result):
+    half = front.shape[1]
+    total = nn(back[0, :, :half], front[0]) + nn(back[0, :, half:], rest[0])
+    result[0] = total.astype(BF)
+
+
+def restore(front, rest, back):
+    seqs, half, width = front.shape
+    length = back.shape[1]
+
+    def per(*shape):
+        return pl.BlockSpec((1, *shape), lambda s: (s, 0, 0))
+
+    return call(
+        restore_kernel,
+        "restore_order",
+        sds((seqs, length, width), BF),
+        (front, rest, back),
+        grid=(seqs,),
+        in_specs=[per(half, width), per(half, width), per(length, length)],
+        out_specs=[per(length, width)],
+        flops=2 * seqs * length * length * width,
+    )
+
+
+def grad_up_kernel(place, lowt, d_hidden, result):
+    slots, _, rows, count = lowt.shape
+    part = nn(lowt[...].reshape(slots * rows, count), d_hidden[...]).astype(BF)
+    for z in range(slots):
+        result[0, (z - place[1] + slots) % slots] = part[z * rows : (z + 1) * rows]
+
+
+def grad_up(place, lowt, d_hidden, other, fsdp, slots):
+    width, count = lowt.shape
+    rows = width // (2 * slots)
+    piece = d_hidden.shape[1] // fsdp
+    lowt = lowt.reshape(slots, 2, rows, count)
+    return call(
+        grad_up_kernel,
+        "grad_up",
+        sds((fsdp, slots, rows, piece), BF),
+        (lowt, d_hidden),
+        grid=(fsdp,),
+        in_specs=[
+            pl.BlockSpec((slots, 1, rows, count), lambda f, p: (0, p[2] ^ other, 0, 0)),
+            pl.BlockSpec((count, piece), lambda f, p: (0, f)),
+        ],
+        out_specs=[pl.BlockSpec((1, slots, rows, piece), lambda f, p: (f ^ p[0], 0, 0, 0))],
+        place=place,
+        flops=2 * width // 2 * count * piece * fsdp,
+    )
+
+
+def grad_down_kernel(place, activet, d_low, result, work):
+    fsdp, _, rows, wide = result.shape
+    thin = d_low.shape[1] // fsdp
+    work[...] = nn(activet[0, 0], d_low[...]).astype(BF)
+    for f in range(fsdp):
+        for g in range(wide // thin):
+            result[f ^ place[0], 0, :, g * thin : (g + 1) * thin] = work[
+                g * rows : (g + 1) * rows, f * thin : (f + 1) * thin
+            ]
+
+
+def grad_down(place, activet, d_low, other, fsdp, slots):
+    hidden, count = activet.shape
+    width = d_low.shape[1]
+    tall = hidden // (2 * slots)
+    thin = width // fsdp
+    rows = tall * thin // width
+    activet = activet.reshape(slots, 2, tall, count)
+    return call(
+        grad_down_kernel,
+        "grad_down",
+        sds((fsdp, slots, rows, width), BF),
+        (activet, d_low),
+        grid=(slots,),
+        in_specs=[
+            pl.BlockSpec((1, 1, tall, count), lambda z, p: (z, p[2] ^ other, 0, 0)),
+            whole(d_low.shape),
+        ],
+        out_specs=[
+            pl.BlockSpec(
+                (fsdp, 1, rows, width), lambda z, p: (0, (z - p[1] + slots) % slots, 0, 0)
+            )
+        ],
+        scratch=[pltpu.VMEM((tall, width), BF)],
+        place=place,
+        flops=2 * hidden // 2 * count * width,
+    )
+
+
+def grad_rest_kernel(
+    other,
+    place,
+    xt,
+    frontt,
+    attendedt,
+    d_q,
+    d_kv,
+    d_low,
+    d_proj,
+    q_sums,
+    kv_sums,
+    one_sums,
+    up_sums,
+    two_sums,
+    result,
+    work_qkv,
+    work_out,
+    vector,
+    small,
+):
+    fsdp, slots, tall, wide = result.shape
+    rows = tall - 16
+    width = d_q.shape[1]
+    count = d_q.shape[0]
+    work_qkv[:, :width] = nn(frontt[...].reshape(slots * rows, count), d_q[...]).astype(BF)
+    left = xt[...].reshape(slots * rows, d_kv.shape[0])
+    for j in range(2):
+        cols = slice(j * width, (j + 1) * width)
+        work_qkv[:, (j + 1) * width : (j + 2) * width] = nn(left, d_kv[:, cols]).astype(BF)
+    work_out[...] = nn(attendedt[...].reshape(slots * rows, count), d_low[...]).astype(BF)
+    hidden = up_sums.shape[1]
+    at = 0
+    for value in (
+        jnp.sum(q_sums[...], axis=0),
+        jnp.sum(kv_sums[...], axis=0),
+        one_sums[2:3, :],
+        up_sums[...],
+        two_sums[2:3, :],
+        one_sums[0:1, :],
+        one_sums[1:2, :],
+        two_sums[0:1, :],
+        two_sums[1:2, :],
+    ):
+        size = value.shape[1]
+        vector[:, at : at + size] = value
+        at += size
+    piece = 3 * width // fsdp
+    thin = width // fsdp
+    entries = vector.shape[1] // (2 * fsdp * slots)
+    height = d_proj.shape[0] // fsdp
+    across = d_proj.shape[1] // (2 * slots)
+    start = (height // 8) * across
+    room = wide - start
+    first = (place[2] ^ other) == 0
+    small[...] = jnp.zeros_like(small)
+    for f in range(fsdp):
+        for z in range(slots):
+            at = (f ^ place[0], (z - place[1] + slots) % slots)
+            lines = slice(z * rows, (z + 1) * rows)
+            result[at[0], at[1], :rows, :piece] = work_qkv[lines, f * piece : (f + 1) * piece]
+            result[at[0], at[1], :rows, piece:] = work_out[lines, f * thin : (f + 1) * thin]
+            for g in range(height // 8):
+                both = d_proj[
+                    f * height + 8 * g : f * height + 8 * g + 8,
+                    2 * z * across : 2 * (z + 1) * across,
+                ]
+                small[0:8, g * across : (g + 1) * across] = jnp.where(
+                    first, both[:, :across], both[:, across:]
+                )
+            base = (f * 2 * slots + 2 * z) * entries
+            own = jnp.where(
+                first,
+                vector[:, base : base + entries],
+                vector[:, base + entries : base + 2 * entries],
+            )
+            small[0:1, start:] = own[:, :room]
+            small[1:2, start : start + entries - room] = own[:, room:]
+            result[at[0], at[1], rows:, :] = small[...].astype(BF)
+
+
+def grad_rest(place, xt, frontt, attendedt, d_q, d_kv, d_low, d_proj, sums, other, fsdp, slots):
+    width, tokens = xt.shape
+    count = frontt.shape[1]
+    rows = width // (2 * slots)
+    wide = 4 * width // fsdp
+
+    def lines(n):
+        return pl.BlockSpec((slots, 1, rows, n), lambda i, p: (0, p[2] ^ other, 0, 0))
+
+    def split(value):
+        return value.reshape(slots, 2, rows, value.shape[1])
+
+    plain = (d_q, d_kv, d_low, d_proj, *sums)
+    entries = sum(math.prod(s.shape[1:]) for s in sums[:2]) + 6 * width + sums[3].shape[1]
+    return call(
+        functools.partial(grad_rest_kernel, other),
+        "grad_rest",
+        sds((fsdp, slots, rows + 16, wide), BF),
+        (split(xt), split(frontt), split(attendedt), *plain),
+        in_specs=[lines(tokens), lines(count), lines(count), *(whole(a.shape) for a in plain)],
+        scratch=[
+            pltpu.VMEM((slots * rows, 3 * width), BF),
+            pltpu.VMEM((slots * rows, width), BF),
+            pltpu.VMEM((1, entries), F32),
+            pltpu.VMEM((16, wide), F32),
+        ],
+        place=place,
+        flops=width * width * (2 * count + 2 * tokens),
+    )
+
+
+def swap_core(value):
+    n = lax.axis_size("dp")
+    return lax.ppermute(value, "dp", [(i, i ^ 1) for i in range(n)])
+
+
+def shift_slot(value, by):
+    n = lax.axis_size("dp")
+    return lax.ppermute(value, "dp", [(i, (i + 2 * by) % n) for i in range(n)])
+
+
+def swap_fsdp(value, bits):
+    n = lax.axis_size("fsdp")
+    return lax.ppermute(value, "fsdp", [(i, i ^ bits) for i in range(n)])
+
+
+SOURCES = [
+    (bits, steps, other)
+    for other in (0, 1)
+    for bits in (0, 1, 2, 3)
+    for steps in ((0, 1), (2, 3))
+]
+
+
+def gather_piece(own):
+    back = [own] + [shift_slot(own, k) for k in (1, 2, 3)]
+    near = jnp.stack(back[:2])
+    far = jnp.stack(back[2:])
+    x_near, y_near = swap_fsdp(near, 1), swap_fsdp(near, 2)
+    x_far, y_far = swap_fsdp(far, 1), swap_fsdp(far, 2)
+    d_near = swap_fsdp(x_near, 2)
+    d_far = swap_fsdp(y_far, 1)
+    ours = [near, far, x_near, x_far, y_near, y_far, d_near, d_far]
+    return ours + [swap_core(a) for a in ours]
+
+
+def source_places(place, slots):
+    for n, (bits, steps, other) in enumerate(SOURCES):
+        for i, back in enumerate(steps):
+            f = place[0] ^ bits
+            z = (place[1] - back + slots) % slots
+            yield n, i, f, z, place[2] ^ other
+
+
+def fetch_blocks(place, refs, work, sems, slots, at):
+    copies = []
+    for number, (n, i, f, z, c) in enumerate(source_places(place, slots)):
+        copies.append(
+            pltpu.make_async_copy(refs[n].at[i], work.at[at(f, z, c)], sems.at[number])
+        )
+    for copy in copies:
+        copy.start()
+    for copy in copies:
+        copy.wait()
+
+
+def first_whole_kernel(slots, fsdp, height, across, place, *refs):
+    blocks = refs[:16]
+    qkv, out, vec, proj, projt, work, matrix, sems = refs[16:]
+    fetch_blocks(place, blocks, work, sems, slots, lambda f, z, c: (c, z, f))
+    wide = work.shape[4]
+    rows = work.shape[3] - 16
+    piece = qkv.shape[1] // fsdp
+    thin = out.shape[1] // fsdp
+    entries = vec.shape[1] // (2 * slots * fsdp)
+    start = (height // 8) * across
+    room = wide - start
+    for f in range(fsdp):
+        for z in range(slots):
+            for c in range(2):
+                d = 2 * z + c
+                lines = slice(d * rows, (d + 1) * rows)
+                qkv[lines, f * piece : (f + 1) * piece] = work[c, z, f, :rows, :piece]
+                out[lines, f * thin : (f + 1) * thin] = work[c, z, f, :rows, piece:]
+                small = work[c, z, f, rows:, :].astype(F32)
+                for g in range(height // 8):
+                    matrix[
+                        f * height + 8 * g : f * height + 8 * g + 8, d * across : (d + 1) * across
+                    ] = small[0:8, g * across : (g + 1) * across]
+                base = (f * 2 * slots + d) * entries
+                vec[:, base : base + room] = small[0:1, start:]
+                vec[:, base + room : base + entries] = small[1:2, start : start + entries - room]
+    proj[...] = matrix[...].astype(BF)
+    projt[...] = matrix[...].T.astype(BF)
+
+
+def first_whole(place, blocks, fsdp, slots, width, proj_shape, entries):
+    tall, wide = blocks[0].shape[1:]
+    height, across = proj_shape[0] // fsdp, proj_shape[1] // (2 * slots)
+    return call(
+        functools.partial(first_whole_kernel, slots, fsdp, height, across),
+        "whole_first",
+        [
+            sds((width, 3 * width), BF),
+            sds((width, width), BF),
+            sds((1, entries), F32),
+            sds(proj_shape, BF),
+            sds(proj_shape[::-1], BF),
+        ],
+        blocks,
+        in_specs=[pl.BlockSpec(memory_space=pl.ANY)] * 16,
+        scratch=[
+            pltpu.VMEM((2, slots, fsdp, tall, wide), BF),
+            pltpu.VMEM(proj_shape, F32),
+            pltpu.SemaphoreType.DMA((32,)),
+        ],
+        place=place,
+    )
+
+
+def up_whole_kernel(slots, place, *refs):
+    blocks, result, sems = refs[:16], refs[16], refs[17]
+    fetch_blocks(place, blocks, result, sems, slots, lambda f, z, c: (f, 2 * z + c))
+
+
+def up_whole(place, blocks, fsdp, slots):
+    rows, wide = blocks[0].shape[1:]
+    result = call(
+        functools.partial(up_whole_kernel, slots),
+        "whole_up",
+        sds((fsdp, 2 * slots, rows, wide), BF),
+        blocks,
+        in_specs=[pl.BlockSpec(memory_space=pl.ANY)] * 16,
+        scratch=[pltpu.SemaphoreType.DMA((32,))],
+        place=place,
+    )
+    return result.reshape(fsdp, 2 * slots * rows, wide)
+
+
+def down_whole_kernel(slots, fsdp, place, *refs):
+    blocks, result, work, sems = refs[:16], refs[16], refs[17], refs[18]
+    fetch_blocks(place, blocks, work, sems, slots, lambda f, z, c: (c, z, f))
+    rows, wide = work.shape[3:]
+    thin = result.shape[1] // fsdp
+    count = wide // thin
+    for z in range(slots):
+        for c in range(2):
+            for g in range(count):
+                top = (2 * z + c) * count * rows + g * rows
+                for f in range(fsdp):
+                    result[top : top + rows, f * thin : (f + 1) * thin] = work[
+                        c, z, f, :, g * thin : (g + 1) * thin
+                    ]
+
+
+def down_whole(place, blocks, fsdp, slots, hidden, width):
+    rows, wide = blocks[0].shape[1:]
+    return call(
+        functools.partial(down_whole_kernel, slots, fsdp),
+        "whole_down",
+        sds((hidden, width), BF),
+        blocks,
+        in_specs=[pl.BlockSpec(memory_space=pl.ANY)] * 16,
+        scratch=[
+            pltpu.VMEM((2, slots, fsdp, rows, wide), BF),
+            pltpu.SemaphoreType.DMA((32,)),
+        ],
+        place=place,
+    )
+
+
+def added(*parts):
+    total = parts[0].astype(F32)
+    for p in parts[1:]:
+        total = total + p.astype(F32)
+    return total
+
+
+def reduce_piece(mine, theirs):
+    came = swap_core(theirs)
+
+    def chip(rel, lo, hi):
+        return added(mine[rel, lo:hi], came[rel, lo:hi])
+
+    def pair(a, b, lo, hi):
+        return jnp.stack([chip(a, lo, hi), chip(b, lo, hi)]).astype(BF)
+
+    from_x = swap_fsdp(pair(1, 3, 0, 2), 1)
+    from_y = swap_fsdp(pair(2, 3, 2, 4), 2)
+    over_y = swap_fsdp((chip(2, 0, 2) + from_x[1].astype(F32)).astype(BF), 2)
+    over_x = swap_fsdp((chip(1, 2, 4) + from_y[1].astype(F32)).astype(BF), 1)
+    near = chip(0, 0, 2) + from_x[0].astype(F32) + over_y.astype(F32)
+    far = chip(0, 2, 4) + from_y[0].astype(F32) + over_x.astype(F32)
+    one = shift_slot(near[1].astype(BF), 1)
+    two = shift_slot(far[0].astype(BF), 2)
+    three = shift_slot(far[1].astype(BF), 3)
+    return (near[0] + two.astype(F32)) + (one.astype(F32) + three.astype(F32))
+
+
+def sum_everywhere(value):
+    a, b, c = (swap_fsdp(value, k) for k in (1, 2, 3))
+    value = (value + a) + (b + c)
+    a, b, c = (shift_slot(value, k) for k in (1, 2, 3))
+    value = (value + b) + (a + c)
+    return value + swap_core(value)
+
+
+def adam(weight, moment, second, grad, scale_clip, rate, decay):
+    clipped = grad * scale_clip
+    new_moment = BETA_ONE * moment + (1.0 - BETA_ONE) * clipped
+    new_second = BETA_TWO * second + (1.0 - BETA_TWO) * clipped * clipped
+    moment_hat = new_moment / (1.0 - BETA_ONE**STEP)
+    second_hat = new_second / (1.0 - BETA_TWO**STEP)
+    new_weight = weight - rate * (moment_hat / (jnp.sqrt(second_hat) + ADAM_EPS) + decay * weight)
+    return new_weight, new_moment, new_second, new_weight.astype(BF)
+
+
+def update_kernel(rates, squares, g_first, g_up, g_down, *refs):
+    ins, outs = refs[:18], refs[18:-1]
+    norm_ref, outs = outs[0], outs[1:]
+    vector = refs[-1]
+    norm = jnp.sqrt(squares[0:1, 0:1])
+    norm_ref[...] = norm
+    clip = jnp.minimum(1.0, CLIP_NORM / norm)
+
+    def put(n, place, grad):
+        new = adam(*(ins[3 * n + i][place] for i in range(3)), grad, clip, *rates[n])
+        for i in range(4):
+            outs[4 * n + i][place] = new[i]
+
+    rows, wide = g_up.shape
+    piece = ins[0].shape[1]
+    every = (slice(None), slice(None))
+    put(0, every, g_first[:rows, :piece])
+    put(1, every, g_first[:rows, piece:])
+    put(2, every, g_up[...])
+    thin = ins[9].shape[1]
+    for g in range(wide // thin):
+        put(3, (slice(g * rows, (g + 1) * rows), slice(None)), g_down[:, g * thin : (g + 1) * thin])
+    height, across = ins[12].shape
+    for g in range(height // 8):
+        put(
+            4,
+            (slice(8 * g, 8 * g + 8), slice(None)),
+            g_first[rows : rows + 8, g * across : (g + 1) * across],
+        )
+    start = (height // 8) * across
+    room = wide - start
+    entries = ins[15].shape[1]
+    vector[:, :room] = g_first[rows : rows + 1, start:]
+    vector[:, room:] = g_first[rows + 1 : rows + 2, start : start + entries - room]
+    put(5, every, vector[...])
+
+
+def update(squares, g_first, g_up, g_down, states, rates):
+    outs = [sds((1, 1), F32)]
+    for n in range(6):
+        shape = states[3 * n].shape
+        outs += [sds(shape, F32)] * 3 + [sds(shape, BF)]
+    return call(
+        functools.partial(update_kernel, rates),
+        "update",
+        outs,
+        (squares, g_first, g_up, g_down, *states),
+        scratch=[pltpu.VMEM(states[15].shape, F32)],
+    )
+
+
+def on_device(
+    tokens,
+    cotangent,
+    positions,
+    counts,
+    qkv_weight,
+    qkv_moment,
+    qkv_second,
+    out_weight,
+    out_moment,
+    out_second,
+    up_weight,
+    up_moment,
+    up_second,
+    down_projection_weight,
+    down_moment,
+    down_second,
+    proj_weight,
+    proj_moment,
+    proj_second,
+    vec_weight,
+    vec_moment,
+    vec_second,
+):
+    fsdp, slots = lax.axis_size("fsdp"), lax.axis_size("dp") // 2
+    place = jnp.stack(
+        [lax.axis_index("fsdp"), lax.axis_index("dp") // 2, lax.axis_index("dp") % 2]
+    ).astype(jnp.int32)
+    seqs = counts.shape[0]
+    rows, width = tokens.shape
+    length = rows // seqs
+    half = length // 2
+    marked = positions.shape[1]
+    hidden = down_projection_weight.shape[0] * slots * 2
+    proj_shape = (proj_weight.shape[0] * fsdp, proj_weight.shape[1] * 2 * slots)
+    entries = vec_weight.shape[0] * fsdp * 2 * slots
+    rates = (
+        (RATE_QKV, DECAY_RATE),
+        (RATE_OUT, DECAY_RATE),
+        (RATE_UP, DECAY_RATE),
+        (RATE_DOWN, DECAY_RATE),
+        (RATE_PROJ, DECAY_RATE),
+        (RATE_VEC, 0.0),
+    )
+
+    row = tuple(v[None, :] for v in (vec_weight, vec_moment, vec_second))
+    own_first, own_up, own_down = pack(
+        qkv_weight, out_weight, up_weight, down_projection_weight, proj_weight, row[0]
+    )
+    blocks_first = gather_piece(own_first)
+    blocks_up = gather_piece(own_up)
+    blocks_down = gather_piece(own_down)
+
+    x = tokens.reshape(seqs, length, width)
+    front, rest, frontt, xt, back = order_rows(x, positions)
+    live = jnp.arange(marked, dtype=jnp.int32)[None, :] < counts[:, None]
+    dy = jnp.pad(
+        jnp.where(live[:, :, None], cotangent, jnp.zeros_like(cotangent)),
+        ((0, 0), (0, half - marked), (0, 0)),
+    ).reshape(seqs * half, width)
+
+    qkv_full, out_full, vec, proj, projt = first_whole(
+        place, blocks_first, fsdp, slots, width, proj_shape, entries
+    )
+    q_front, q_rest, kv, kvp = make_qkv(front, rest, x, qkv_full, vec, proj)
+    a_front, a_rest = attend(q_front, q_rest, kvp)
+
+    m1 = 3 * width
+    m2 = m1 + width
+    m3 = m2 + hidden
+    m4 = m3 + width
+    ends = [m4 + i * width for i in range(5)]
+    marks_one = ((m1, m2), (ends[0], ends[1]), (ends[1], ends[2]))
+    marks_two = ((m3, m4), (ends[2], ends[3]), (ends[3], ends[4]))
+
+    def flat(v):
+        return v.reshape(seqs * half, width)
+
+    h_front, low_front, kept, lowt, attendedt = join(
+        flat(a_front), flat(front), out_full, vec, marks_one, True
+    )
+    h_rest, low_rest = join(flat(a_rest), flat(rest), out_full, vec, marks_one, False)
+    up_full = up_whole(place, blocks_up, fsdp, slots)
+    act_front, slope, activet = lift(low_front, up_full, vec, m2, True)
+    act_rest = lift(low_rest, up_full, vec, m2, False)[0]
+    down_full = down_whole(place, blocks_down, fsdp, slots, hidden, width)
+    out_front, d_sum, d_low, two_sums = lower(act_front, h_front, down_full, vec, marks_two, dy)
+
+    theirs = grad_down(place, activet, d_low, 1, fsdp, slots)
+    mine = grad_down(place, activet, d_low, 0, fsdp, slots)
+    g_down = reduce_piece(mine, theirs)
+    d_hidden, up_sums = hidden_back(d_low, down_full, slope)
+    theirs = grad_up(place, lowt, d_hidden, 1, fsdp, slots)
+    mine = grad_up(place, lowt, d_hidden, 0, fsdp, slots)
+    g_up = reduce_piece(mine, theirs)
+    d_first, d_first_low, d_attended, one_sums = first_back(
+        d_hidden, up_full, d_sum, kept, vec, out_full, (ends[0], ends[1])
+    )
+    d_q, d_k, d_v, q_sums = attend_back(q_front, kvp, d_attended.reshape(seqs, half, width))
+    d_kv, d_proj, kv_sums = spread(d_k, d_v, kv, projt)
+    sums = (q_sums, kv_sums, one_sums, up_sums, two_sums)
+    give = (
+        xt,
+        frontt,
+        attendedt,
+        flat(d_q),
+        d_kv.reshape(rows, 2 * width),
+        d_first_low,
+        d_proj,
+        sums,
+    )
+    theirs = grad_rest(place, *give, 1, fsdp, slots)
+    mine = grad_rest(place, *give, 0, fsdp, slots)
+    g_first = reduce_piece(mine, theirs)
+
+    out_rest = lower(act_rest, h_rest, down_full, vec, marks_two)
+    output = restore(
+        out_front.reshape(seqs, half, width), out_rest.reshape(seqs, half, width), back
+    ).reshape(rows, width)
+    grad_input = input_back(
+        d_kv, d_q, d_first.reshape(seqs, half, width), qkv_full, back
+    ).reshape(rows, width)
+
+    squares = jnp.sum(g_first * g_first) + jnp.sum(g_up * g_up) + jnp.sum(g_down * g_down)
+    squares = sum_everywhere(jnp.broadcast_to(squares, (8, 128)))
+    states = (
+        qkv_weight,
+        qkv_moment,
+        qkv_second,
+        out_weight,
+        out_moment,
+        out_second,
+        up_weight,
+        up_moment,
+        up_second,
+        down_projection_weight,
+        down_moment,
+        down_second,
+        proj_weight,
+        proj_moment,
+        proj_second,
+        *row,
+    )
+    new = update(squares, g_first, g_up, g_down, states, rates)
+    norm, new = new[0].reshape(()), new[1:]
+    return (output, grad_input, norm, *new[:20], *(v[0] for v in new[20:]))
 
 
 def split_up(value, dim, peers):
@@ -104,7 +1360,7 @@
     )
 
 
-def on_device(
+def on_any_mesh(
     tokens,
     cotangent,
     positions,
@@ -366,62 +1622,14 @@
 
 
 def solution(mesh):
-    placed = (
-        P(("fsdp", "dp"), None),
-        P(("fsdp", "dp"), None, None),
-        P(("fsdp", "dp"), None),
-        P(("fsdp", "dp")),
-        P("dp", "fsdp"),
-        P("dp", "fsdp"),
-        P("dp", "fsdp"),
-        P("dp", "fsdp"),
-        P("dp", "fsdp"),
-        P("dp", "fsdp"),
-        P("dp", "fsdp"),
-        P("dp", "fsdp"),
-        P("dp", "fsdp"),
-        P("dp", "fsdp"),
-        P("dp", "fsdp"),
-        P("dp", "fsdp"),
-        P("fsdp", "dp"),
-        P("fsdp", "dp"),
-        P("fsdp", "dp"),
-        P(("fsdp", "dp")),
-        P(("fsdp", "dp")),
-        P(("fsdp", "dp")),
-    )
+    matrix = P("dp", "fsdp")
+    tall = P("fsdp", "dp")
+    every = P(("fsdp", "dp"))
+    small = mesh.shape["fsdp"] == 4 and mesh.shape["dp"] == 8
     return jax.shard_map(
-        on_device,
+        on_device if small else on_any_mesh,
         mesh=mesh,
-        in_specs=placed,
-        out_specs=(
-            P(("fsdp", "dp"), None),
-            P(("fsdp", "dp"), None),
-            P(),
-            P("dp", "fsdp"),
-            P("dp", "fsdp"),
-            P("dp", "fsdp"),
-            P("dp", "fsdp"),
-            P("dp", "fsdp"),
-            P("dp", "fsdp"),
-            P("dp", "fsdp"),
-            P("dp", "fsdp"),
-            P("dp", "fsdp"),
-            P("dp", "fsdp"),
-            P("dp", "fsdp"),
-            P("dp", "fsdp"),
-            P("dp", "fsdp"),
-            P("dp", "fsdp"),
-            P("dp", "fsdp"),
-            P("dp", "fsdp"),
-            P("fsdp", "dp"),
-            P("fsdp", "dp"),
-            P("fsdp", "dp"),
-            P("fsdp", "dp"),
-            P(("fsdp", "dp")),
-            P(("fsdp", "dp")),
-            P(("fsdp", "dp")),
-            P(("fsdp", "dp")),
-        ),
+        in_specs=(every,) * 4 + (matrix,) * 12 + (tall,) * 3 + (every,) * 3,
+        out_specs=(every, every, P()) + (matrix,) * 16 + (tall,) * 4 + (every,) * 4,
         check_vma=False,
     )

time: 715 us -> 433 us (0.61)
  matrix products: 197 us -> 0 us
  Pallas kernels: 0 us -> 167 us
  blocking collectives: 144 us -> 0 us
  waiting for transfers between devices: 226 us -> 101 us
  starting transfers between devices: 17.2 us -> 92.6 us
  local copies, waits for them, and re-layouts: 65.2 us -> 40.9 us
  between operations: 22.9 us -> 4.55 us
  other arithmetic: 35.1 us -> 19.5 us
    dot_general x22 -> x0, matrix products: 197 us -> none  [the longest x1 37.6 us: on_device(): jnp.dot(normed_low, up_full, preferred_element_type=jnp.float32) + bias_up]
    pallas_call x0 -> x26, Pallas kernels: none -> 167 us  [call(): pl.pallas_call(kernel, name=name, out_shape=outs, grid_spec=pltpu.Prefetc...]
    reduce_scatter x5 -> x0, waiting for transfers between devices: 108 us -> none  [the longest x1 58.8 us: on_device(): lax.psum_scatter(grad_up.astype(jnp.bfloat16), 'fsdp', scatter_dimension=...]
    ppermute x0 -> x82, waiting for transfers between devices: none -> 101 us  [the longest x33 73.5 us: swap_fsdp(): return lax.ppermute(value, 'fsdp', [(i, i ^ bits) for i in range(n)])]
    ppermute x0 -> x82, starting transfers between devices: none -> 92.6 us  [the longest x21 49.3 us: shift_slot(): return lax.ppermute(value, 'dp', [(i, (i + 2 * by) % n) for i in range(n)])]
    all_gather x6 -> x0, waiting for transfers between devices: 72.7 us -> none  [the longest x1 51.4 us: fetch_whole(): lax.all_gather(rows[2], 'fsdp', axis=1, tiled=True)]
    all_gather x4 -> x0, blocking collectives: 59.3 us -> none  [the longest x1 22.7 us: fetch_whole(): lax.all_gather(low_qkv, 'dp', axis=0, tiled=True)]
    unnamed x3 -> x0, blocking collectives: 48.1 us -> none
  transfers between devices with their start and end apart: 15 -> 82, of which waited for: 7 -> 26; matrix products, arithmetic and copies ran while one was open for 26% -> 6% of each run, Pallas kernels for 0% -> 24%
where the time goes in v1:
time: 433 us; the launch traced here: 425 us
  Pallas kernels  167 us (39%)
  waiting for transfers between devices  101 us (23%)
  starting transfers between devices  92.6 us (21%)
  local copies, waits for them, and re-layouts  40.9 us (9%)
  other arithmetic  19.5 us (5%)
  between operations  4.55 us (1%)
    pallas_call x26, Pallas kernels, call(): pl.pallas_call(kernel, name=name, out_shape=outs, grid_spec=pltpu.Prefetc...  167 us
    ppermute x33, waiting for transfers between devices, swap_fsdp(): return lax.ppermute(value, 'fsdp', [(i, i ^ bits) for i in range(n)])  73.5 us
    ppermute x21, starting transfers between devices, shift_slot(): return lax.ppermute(value, 'dp', [(i, (i + 2 * by) % n) for i in range(n)])  49.3 us
    ppermute x33, starting transfers between devices, swap_fsdp(): return lax.ppermute(value, 'fsdp', [(i, i ^ bits) for i in range(n)])  39.4 us
    unnamed x260, local copies, waits for them, and re-layouts  36.8 us
    ppermute x21, waiting for transfers between devices, shift_slot(): return lax.ppermute(value, 'dp', [(i, (i + 2 * by) % n) for i in range(n)])  27 us
  transfers between devices with their start and end apart: 82, of which 26 were waited for; matrix products, arithmetic and copies ran while one was open for 6% of the time, Pallas kernels for 24%

profile of v1, /device:TPU:0, one launch (start us, length us, event | category | flops | bytes accessed | tf_op | source)
XLA Modules:
  0.0 425.4 jit_solution(11321359406829114911)
XLA Ops:
  6.2 3.1 collective-permute-start.34
  16.1 6.9 %collective-permute-start.35 = (bf16[96,768]{1,0:T(8,128)(2,1)S(1)}, bf16[96,768]{1,0:T(8,128)(2,1)S(1)}, u32[]{:S(2)}, u32[]{:S(2)}) collective-permute-start(bf16[96,768]{1,0:T(8,128)(2,1)S(1)} %get-tuple-element.113), channel_id=1, source_target_pairs={{0,4},{1,5},{2,6},{3,7},{4,0},{5,1},{6,2},{7,3},{8,12},{9,13},{10,... | collective-permute-start | bytes 442376 | tf_op jit(solution)/shard_map/ppermute | solution.py:882
  23.1 5.6 %collective-permute-done.18 = bf16[96,768]{1,0:T(8,128)(2,1)S(1)} collective-permute-done((bf16[96,768]{1,0:T(8,128)(2,1)S(1)}, bf16[96,768]{1,0:T(8,128)(2,1)S(1)}, u32[]{:S(2)}, u32[]{:S(2)}) %collective-permute-start.18) | collective-permute-done | bytes 147488 | tf_op jit(solution)/shard_map/ppermute | solution.py:882
  30.5 6.4 %collective-permute-start.2 = (bf16[112,768]{1,0:T(8,128)(2,1)S(1)}, bf16[112,768]{1,0:T(8,128)(2,1)S(1)}, u32[]{:S(2)}, u32[]{:S(2)}) collective-permute-start(bf16[112,768]{1,0:T(8,128)(2,1)S(1)} %get-tuple-element.100), channel_id=1, source_target_pairs={{0,6},{1,7},{2,0},{3,1},{4,2},{5,3},{6,4},{7,5},{8,14},{9,15},{10,... | collective-permute-start | bytes 516104 | tf_op jit(solution)/shard_map/ppermute | solution.py:882
  37.6 2.5 collective-permute-start
  43.6 8.4 %collective-permute-done.1 = bf16[112,768]{1,0:T(8,128)(2,1)S(1)} collective-permute-done((bf16[112,768]{1,0:T(8,128)(2,1)S(1)}, bf16[112,768]{1,0:T(8,128)(2,1)S(1)}, u32[]{:S(2)}, u32[]{:S(2)}) %collective-permute-start.1) | collective-permute-done | bytes 172064 | tf_op jit(solution)/shard_map/ppermute | solution.py:882
  57.8 4.1 collective-permute-done.40.refs_5_
  61.9 2.4 collective-permute-done.38.refs_3_
  68.2 2.3 collective-permute-done.20.refs_2_
  74.6 2.4 collective-permute-done.21.refs_3_
  79.0 2.9 collective-permute-done.5.refs_4_
  81.9 2.5 collective-permute-done.3.refs_2_
  84.9 4.4 %collective-permute-done.6.refs_5_ = bf16[2,112,768]{2,1,0:T(8,128)(2,1)} collective-permute-done((bf16[2,112,768]{2,1,0:T(8,128)(2,1)S(1)}, bf16[2,112,768]{2,1,0:T(8,128)(2,1)}, u32[]{:S(2)}, u32[]{:S(2)}) %collective-permute-start.6) | collective-permute-done | bytes 344096 | tf_op jit(solution)/shard_map/ppermute | solution.py:887
  108.7 4.3 %collective-permute-done.25.refs_7_ = bf16[2,96,768]{2,1,0:T(8,128)(2,1)} collective-permute-done((bf16[2,96,768]{2,1,0:T(8,128)(2,1)}, bf16[2,96,768]{2,1,0:T(8,128)(2,1)}, u32[]{:S(2)}, u32[]{:S(2)}) %collective-permute-start.25) | collective-permute-done | bytes 294944 | tf_op jit(solution)/shard_map/ppermute | solution.py:887
  114.9 4.9 %collective-permute-done.8.refs_7_ = bf16[2,112,768]{2,1,0:T(8,128)(2,1)} collective-permute-done((bf16[2,112,768]{2,1,0:T(8,128)(2,1)}, bf16[2,112,768]{2,1,0:T(8,128)(2,1)}, u32[]{:S(2)}, u32[]{:S(2)}) %collective-permute-start.8) | collective-permute-done | bytes 344096 | tf_op jit(solution)/shard_map/ppermute | solution.py:887
  125.9 3.4 order_rows.1
  130.6 10.9 %whole_down.1.weight = bf16[3072,768]{1,0:T(8,128)(2,1)} custom-call(s32[3]{0:T(128)S(1)} %pad_add_fusion.place, bf16[2,96,768]{2,1,0:T(8,128)(2,1)S(1)} %pad_maximum_fusion.10.refs_0_, bf16[2,96,768]{2,1,0:T(8,128)(2,1)S(1)} %pad_maximum_fusion.11.refs_1_, bf16[2,96,768]{2,1,0:T(8,128)(2,1)S(1)} %copy-done.59, bf16[2,96,768]{2,1,0:T(8,128)(2,1)S(1)} %copy-done.67, ...), custom_call_target="tpu_custom_call" | custom-call | bytes 9437184 | tf_op jit(solution)/shard_map/whole_down/pallas_call | solution.py:74
  141.6 8.4 %whole_up.1 = bf16[4,8,96,768]{3,2,1,0:T(8,128)(2,1)} custom-call(s32[3]{0:T(128)S(1)} %pad_add_fusion.place, bf16[2,96,768]{2,1,0:T(8,128)(2,1)S(1)} %copy-done.25, bf16[2,96,768]{2,1,0:T(8,128)(2,1)S(1)} %copy-done.27, bf16[2,96,768]{2,1,0:T(8,128)(2,1)S(1)} %copy-done.71, bf16[2,96,768]{2,1,0:T(8,128)(2,1)} %collective-permute-done.21.refs_3_, ...), custom_call_target="tpu_custom_call" | custom-call | bytes 9437184 | tf_op jit(solution)/shard_map/whole_up/pallas_call | solution.py:74
  150.1 8.5 %whole_first.1 = (bf16[768,2304]{1,0:T(8,128)(2,1)}, bf16[768,768]{1,0:T(8,128)(2,1)}, f32[1,9984]{1,0:T(1,128)S(1)}, bf16[256,512]{1,0:T(8,128)(2,1)S(1)}, bf16[512,256]{1,0:T(8,128)(2,1)S(1)}) custom-call(s32[3]{0:T(128)S(1)} %pad_add_fusion.place, bf16[2,112,768]{2,1,0:T(8,128)(2,1)S(1)} %pad_maximum_fusion.6.refs_0_, ...), custom_call_target="tpu_custom_call" | custom-call | bytes 10787840 | tf_op jit(solution)/shard_map/whole_first/pallas_call | solution.py:74
  158.7 10.1 %make_qkv.1 = (bf16[2,256,768]{2,1,0:T(8,128)(2,1)S(1)}, bf16[2,256,768]{2,1,0:T(8,128)(2,1)S(1)}, bf16[2,512,1536]{2,1,0:T(8,128)(2,1)}, bf16[2,256,1536]{2,1,0:T(8,128)(2,1)S(1)}) custom-call(bf16[2,256,768]{2,1,0:T(8,128)(2,1)S(1)} %get-tuple-element.98.front, bf16[2,256,768]{2,1,0:T(8,128)(2,1)S(1)} %get-tuple-element.99.rest, ...), custom_call_target="tpu_custom_call" | custom-call | flops 4429185024 | bytes 13278208 | tf_op jit(solution)/shard_map/make_qkv/pallas_call | solution.py:74
  168.8 11.1 %attend.1 = (bf16[2,256,768]{2,1,0:T(8,128)(2,1)S(1)}, bf16[2,256,768]{2,1,0:T(8,128)(2,1)S(1)}) custom-call(bf16[2,256,768]{2,1,0:T(8,128)(2,1)S(1)} %get-tuple-element.104.q_front.queries, bf16[2,256,768]{2,1,0:T(8,128)(2,1)S(1)} %get-tuple-element.105.q_rest, bf16[2,256,1536]{2,1,0:T(8,128)(2,1)S(1)} %get-tuple-element.106.keys.values, ...), custom_call_target="tpu_custom_call" | custom-call | flops 1610612736 | bytes 6291456 | tf_op jit(solution)/shard_map/attend/pallas_call | solution.py:74
  180.8 2.8 join_front.1
  183.5 11.6 %lift_front.1 = (bf16[512,3072]{1,0:T(8,128)(2,1)S(1)}, bf16[512,3072]{1,0:T(8,128)(2,1)}, bf16[3072,512]{1,0:T(8,128)(2,1)}) custom-call(bf16[512,768]{1,0:T(8,128)(2,1)S(1)} %get-tuple-element.109.low, bf16[4,768,768]{2,1,0:T(8,128)(2,1)} %bitcast.131, f32[1,9984]{1,0:T(1,128)S(1)} %get-tuple-element.102.vec.bias), custom_call_target="tpu_custom_call" | custom-call | flops 2415919104 | bytes 14982144 | tf_op jit(solution)/shard_map/lift_front/pallas_call | solution.py:74
  196.8 7.3 %lower_front.1 = (bf16[512,768]{1,0:T(8,128)(2,1)S(1)}, f32[512,768]{1,0:T(8,128)S(1)}, bf16[512,768]{1,0:T(8,128)(2,1)S(1)}, f32[8,768]{1,0:T(8,128)S(1)}) custom-call(bf16[512,3072]{1,0:T(8,128)(2,1)} %copy-done.15, f32[512,768]{1,0:T(8,128)S(1)} %copy-done.21, bf16[3072,768]{1,0:T(8,128)(2,1)} %whole_down.1.weight, ...), custom_call_target="tpu_custom_call" | custom-call | flops 2415919104 | bytes 13433856 | tf_op jit(solution)/shard_map/lower_front/pallas_call | solution.py:74
  204.1 6.4 %hidden_back.1 = (bf16[512,3072]{1,0:T(8,128)(2,1)S(1)}, f32[1,3072]{1,0:T(1,128)S(1)}) custom-call(bf16[512,768]{1,0:T(8,128)(2,1)S(1)} %get-tuple-element.119.d_low, bf16[3072,768]{1,0:T(8,128)(2,1)} %whole_down.1.weight, bf16[512,3072]{1,0:T(8,128)(2,1)} %get-tuple-element.120.slope), custom_call_target="tpu_custom_call" | custom-call | flops 2415919104 | bytes 11808768 | tf_op jit(solution)/shard_map/hidden_back/pallas_call | solution.py:74
  212.2 5.5 %grad_down.3 = bf16[4,4,96,768]{3,2,1,0:T(8,128)(2,1)} custom-call(s32[3]{0:T(128)S(1)} %pad_add_fusion.place, bf16[4,2,384,512]{3,2,1,0:T(8,128)(2,1)} %bitcast.134, bf16[512,768]{1,0:T(8,128)(2,1)S(1)} %get-tuple-element.119.d_low), custom_call_target="tpu_custom_call" | custom-call | flops 1207959552 | bytes 6291456 | tf_op jit(solution)/shard_map/grad_down/pallas_call | solution.py:74
  218.1 5.5 %grad_up.3 = bf16[4,4,96,768]{3,2,1,0:T(8,128)(2,1)} custom-call(s32[3]{0:T(128)S(1)} %pad_add_fusion.place, bf16[4,2,96,512]{3,2,1,0:T(8,128)(2,1)S(1)} %bitcast.115, bf16[512,3072]{1,0:T(8,128)(2,1)} %copy-done), custom_call_target="tpu_custom_call" | custom-call | flops 1207959552 | bytes 6291456 | tf_op jit(solution)/shard_map/grad_up/pallas_call | solution.py:74
  223.7 8.4 %first_back.1 = (f32[512,768]{1,0:T(8,128)S(1)}, bf16[512,768]{1,0:T(8,128)(2,1)S(1)}, bf16[512,768]{1,0:T(8,128)(2,1)S(1)}, f32[8,768]{1,0:T(8,128)S(1)}) custom-call(bf16[512,3072]{1,0:T(8,128)(2,1)} %copy-done, bf16[4,768,768]{2,1,0:T(8,128)(2,1)} %bitcast.132, f32[512,768]{1,0:T(8,128)S(1)} %get-tuple-element.122.d_sum, ...), custom_call_target="tpu_custom_call" | custom-call | flops 3019898880 | bytes 15399936 | tf_op jit(solution)/shard_map/first_back/pallas_call | solution.py:74
  233.3 11.5 %attend_back.1 = (bf16[2,256,768]{2,1,0:T(8,128)(2,1)S(1)}, bf16[2,256,768]{2,1,0:T(8,128)(2,1)S(1)}, bf16[2,256,768]{2,1,0:T(8,128)(2,1)S(1)}, f32[2,1,768]{2,1,0:T(1,128)S(1)}) custom-call(bf16[2,256,768]{2,1,0:T(8,128)(2,1)S(1)} %copy-done.120, bf16[2,256,1536]{2,1,0:T(8,128)(2,1)S(1)} %get-tuple-element.106.keys.values, ...), custom_call_target="tpu_custom_call" | custom-call | flops 2013265920 | bytes 7084032 | tf_op jit(solution)/shard_map/attend_back/pallas_call | solution.py:74
  244.8 3.8 spread_kv.1
  250.4 7.5 %grad_rest.3 = bf16[4,4,112,768]{3,2,1,0:T(8,128)(2,1)} custom-call(s32[3]{0:T(128)S(1)} %pad_add_fusion.place, bf16[4,2,96,1024]{3,2,1,0:T(8,128)(2,1)S(1)} %bitcast.109, bf16[4,2,96,512]{3,2,1,0:T(8,128)(2,1)S(1)} %bitcast.111, bf16[4,2,96,512]{3,2,1,0:T(8,128)(2,1)S(1)} %bitcast.113, bf16[512,768]{1,0:T(8,128)(2,1)S(1)} %bitcast.117, ...), custom_call_target="tpu_custom_call" | custom-call | flops 1811939328 | bytes 11220992 | tf_op jit(solution)/shard_map/grad_rest/pallas_call | solution.py:74
  269.2 4.4 %grad_up.2 = bf16[4,4,96,768]{3,2,1,0:T(8,128)(2,1)S(1)} custom-call(s32[3]{0:T(128)S(1)} %pad_add_fusion.place, bf16[4,2,96,512]{3,2,1,0:T(8,128)(2,1)S(1)} %bitcast.116, bf16[512,3072]{1,0:T(8,128)(2,1)} %copy-done), custom_call_target="tpu_custom_call" | custom-call | flops 1207959552 | bytes 6291456 | tf_op jit(solution)/shard_map/grad_up/pallas_call | solution.py:74
  273.6 5.1 %grad_down.2 = bf16[4,4,96,768]{3,2,1,0:T(8,128)(2,1)S(1)} custom-call(s32[3]{0:T(128)S(1)} %pad_add_fusion.place, bf16[4,2,384,512]{3,2,1,0:T(8,128)(2,1)} %bitcast.135, bf16[512,768]{1,0:T(8,128)(2,1)S(1)} %copy-done.10), custom_call_target="tpu_custom_call" | custom-call | flops 1207959552 | bytes 6291456 | tf_op jit(solution)/shard_map/grad_down/pallas_call | solution.py:74
  278.9 7.6 %grad_rest.2 = bf16[4,4,112,768]{3,2,1,0:T(8,128)(2,1)} custom-call(s32[3]{0:T(128)S(1)} %pad_add_fusion.place, bf16[4,2,96,1024]{3,2,1,0:T(8,128)(2,1)S(1)} %bitcast.110, bf16[4,2,96,512]{3,2,1,0:T(8,128)(2,1)S(1)} %bitcast.112, bf16[4,2,96,512]{3,2,1,0:T(8,128)(2,1)S(1)} %bitcast.114, bf16[512,768]{1,0:T(8,128)(2,1)S(1)} %bitcast.118, ...), custom_call_target="tpu_custom_call" | custom-call | flops 1811939328 | bytes 11220992 | tf_op jit(solution)/shard_map/grad_rest/pallas_call | solution.py:74
  286.4 7.7 %input_back.1 = bf16[2,512,768]{2,1,0:T(8,128)(2,1)} custom-call(bf16[2,512,1536]{2,1,0:T(8,128)(2,1)} %copy-done.1, bf16[2,256,768]{2,1,0:T(8,128)(2,1)S(1)} %copy-done.14, f32[2,256,768]{2,1,0:T(8,128)S(1)} %bitcast.129, bf16[768,2304]{1,0:T(8,128)(2,1)} %get-tuple-element.101.weight, bf16[2,512,512]{2,1,0:T(8,128)(2,1)S(1)} %copy-done.29), custom_call_target="tpu_custom_call" | custom-call | flops 3825205248 | bytes 11665408 | tf_op jit(solution)/shard_map/input_back/pallas_call | solution.py:74
  304.7 7.2 %collective-permute-done.70 = bf16[2,2,96,768]{3,2,1,0:T(8,128)(2,1)S(1)} collective-permute-done((bf16[2,2,96,768]{3,2,1,0:T(8,128)(2,1)S(1)}, bf16[2,2,96,768]{3,2,1,0:T(8,128)(2,1)S(1)}, u32[]{:S(2)}, u32[]{:S(2)}) %collective-permute-start.70) | collective-permute-done | bytes 589856 | tf_op jit(solution)/shard_map/ppermute | solution.py:887
  317.0 7.6 %collective-permute-done.62 = bf16[2,2,96,768]{3,2,1,0:T(8,128)(2,1)S(1)} collective-permute-done((bf16[2,2,96,768]{3,2,1,0:T(8,128)(2,1)S(1)}, bf16[2,2,96,768]{3,2,1,0:T(8,128)(2,1)S(1)}, u32[]{:S(2)}, u32[]{:S(2)}) %collective-permute-start.62) | collective-permute-done | bytes 589856 | tf_op jit(solution)/shard_map/ppermute | solution.py:887
  328.4 17.2 %collective-permute-done.69 = bf16[2,96,768]{2,1,0:T(8,128)(2,1)S(1)} collective-permute-done((bf16[2,96,768]{2,1,0:T(8,128)(2,1)S(1)}, bf16[2,96,768]{2,1,0:T(8,128)(2,1)S(1)}, u32[]{:S(2)}, u32[]{:S(2)}) %collective-permute-start.69) | collective-permute-done | bytes 294944 | tf_op jit(solution)/shard_map/ppermute | solution.py:887
  348.6 2.5 collective-permute-done.61
  362.0 3.2 collective-permute-start.66
  367.4 6.6 %collective-permute-start.57 = (bf16[112,768]{1,0:T(8,128)(2,1)S(1)}, bf16[112,768]{1,0:T(8,128)(2,1)S(1)}, u32[]{:S(2)}, u32[]{:S(2)}) collective-permute-start(bf16[112,768]{1,0:T(8,128)(2,1)S(1)} %fusion.15), channel_id=1, source_target_pairs={{0,2},{1,3},{2,4},{3,5},{4,6},{5,7},{6,0},{7,1},{8,10},{9,11},{10,... | collective-permute-start | bytes 516104 | tf_op jit(solution)/shard_map/ppermute | solution.py:882
  375.6 2.9 collective-permute-start.58
  378.5 2.7 collective-permute-done.66
  381.9 7.2 %collective-permute-done.56 = bf16[112,768]{1,0:T(8,128)(2,1)S(1)} collective-permute-done((bf16[112,768]{1,0:T(8,128)(2,1)S(1)}, bf16[112,768]{1,0:T(8,128)(2,1)S(1)}, u32[]{:S(2)}, u32[]{:S(2)}) %collective-permute-start.56) | collective-permute-done | bytes 172064 | tf_op jit(solution)/shard_map/ppermute | solution.py:882
  395.3 8.2 %lift_rest.1.active = bf16[512,3072]{1,0:T(8,128)(2,1)S(1)} custom-call(bf16[512,768]{1,0:T(8,128)(2,1)S(1)} %copy-done.118, bf16[4,768,768]{2,1,0:T(8,128)(2,1)} %bitcast.133, f32[1,9984]{1,0:T(1,128)S(1)} %copy-done.33), custom_call_target="tpu_custom_call" | custom-call | flops 2415919104 | bytes 8690688 | tf_op jit(solution)/shard_map/lift_rest/pallas_call | solution.py:74
  403.6 4.3 %collective-permute-start.80 = (f32[8,128]{1,0:T(8,128)S(1)}, f32[8,128]{1,0:T(8,128)S(1)}, u32[]{:S(2)}, u32[]{:S(2)}) collective-permute-start(f32[8,128]{1,0:T(8,128)S(1)} %add_add_fusion.1), channel_id=1, source_target_pairs={{0,6},{1,7},{2,0},{3,1},{4,2},{5,3},{6,4},{7,5},{8,14},{9,15},{10,... | collective-permute-start | bytes 12296 | tf_op jit(solution)/shard_map/ppermute | solution.py:882
  408.8 5.7 %lower_rest.1 = bf16[512,768]{1,0:T(8,128)(2,1)S(1)} custom-call(bf16[512,3072]{1,0:T(8,128)(2,1)S(1)} %lift_rest.1.active, f32[512,768]{1,0:T(8,128)S(1)} %copy-done.20, bf16[3072,768]{1,0:T(8,128)(2,1)} %whole_down.1.weight, f32[1,9984]{1,0:T(1,128)S(1)} %copy-done.33), custom_call_target="tpu_custom_call" | custom-call | flops 2415919104 | bytes 10263552 | tf_op jit(solution)/shard_map/lower_rest/pallas_call | solution.py:74
  417.1 2.3 update.1
  (449 shorter events, 132.8 us)
Async XLA Ops:
  9.3 13.8 %collective-permute-start.19 = (bf16[96,768]{1,0:T(8,128)(2,1)S(1)}, bf16[96,768]{1,0:T(8,128)(2,1)S(1)}, u32[]{:S(2)}, u32[]{:S(2)}) collective-permute-start(bf16[96,768]{1,0:T(8,128)(2,1)S(1)} %get-tuple-element.110), channel_id=1, source_target_pairs={{0,6},{1,7},{2,0},{3,1},{4,2},{5,3},{6,4},{7,5},{8,14},{9,15},{10,... | collective-permute-start | bytes 442376 | tf_op jit(solution)/shard_map/ppermute | solution.py:882
  11.3 17.4 %collective-permute-start.18 = (bf16[96,768]{1,0:T(8,128)(2,1)S(1)}, bf16[96,768]{1,0:T(8,128)(2,1)S(1)}, u32[]{:S(2)}, u32[]{:S(2)}) collective-permute-start(bf16[96,768]{1,0:T(8,128)(2,1)S(1)} %get-tuple-element.110), channel_id=1, source_target_pairs={{0,4},{1,5},{2,6},{3,7},{4,0},{5,1},{6,2},{7,3},{8,12},{9,13},{10,... | collective-permute-start | bytes 442376 | tf_op jit(solution)/shard_map/ppermute | solution.py:882
  12.3 18.2 %collective-permute-start.17 = (bf16[96,768]{1,0:T(8,128)(2,1)S(1)}, bf16[96,768]{1,0:T(8,128)(2,1)S(1)}, u32[]{:S(2)}, u32[]{:S(2)}) collective-permute-start(bf16[96,768]{1,0:T(8,128)(2,1)S(1)} %get-tuple-element.110), channel_id=1, source_target_pairs={{0,2},{1,3},{2,4},{3,5},{4,6},{5,7},{6,0},{7,1},{8,10},{9,11},{10,... | collective-permute-start | bytes 442376 | tf_op jit(solution)/shard_map/ppermute | solution.py:882
  13.9 23.0 %collective-permute-start.36 = (bf16[96,768]{1,0:T(8,128)(2,1)S(1)}, bf16[96,768]{1,0:T(8,128)(2,1)S(1)}, u32[]{:S(2)}, u32[]{:S(2)}) collective-permute-start(bf16[96,768]{1,0:T(8,128)(2,1)S(1)} %get-tuple-element.113), channel_id=1, source_target_pairs={{0,6},{1,7},{2,0},{3,1},{4,2},{5,3},{6,4},{7,5},{8,14},{9,15},{10,... | collective-permute-start | bytes 442376 | tf_op jit(solution)/shard_map/ppermute | solution.py:882
  16.1 21.5 %collective-permute-start.35 = (bf16[96,768]{1,0:T(8,128)(2,1)S(1)}, bf16[96,768]{1,0:T(8,128)(2,1)S(1)}, u32[]{:S(2)}, u32[]{:S(2)}) collective-permute-start(bf16[96,768]{1,0:T(8,128)(2,1)S(1)} %get-tuple-element.113), channel_id=1, source_target_pairs={{0,4},{1,5},{2,6},{3,7},{4,0},{5,1},{6,2},{7,3},{8,12},{9,13},{10,... | collective-permute-start | bytes 442376 | tf_op jit(solution)/shard_map/ppermute | solution.py:882
  23.0 30.6 %collective-permute-start.43 = (bf16[2,96,768]{2,1,0:T(8,128)(2,1)S(1)}, bf16[2,96,768]{2,1,0:T(8,128)(2,1)S(1)}, u32[]{:S(2)}, u32[]{:S(2)}) collective-permute-start(bf16[2,96,768]{2,1,0:T(8,128)(2,1)S(1)} %pad_maximum_fusion.10.refs_0_), channel_id=1, source_target_pairs={{0,1},{1,0},{2,3},{3,2},{4,5},{5,4},{6,7},{7,6},{8,9},{9,8},{10,11... | collective-permute-start | bytes 884744 | tf_op jit(solution)/shard_map/ppermute | solution.py:877
  28.7 27.2 %collective-permute-start.39 = (bf16[2,96,768]{2,1,0:T(8,128)(2,1)S(1)}, bf16[2,96,768]{2,1,0:T(8,128)(2,1)S(1)}, u32[]{:S(2)}, u32[]{:S(2)}) collective-permute-start(bf16[2,96,768]{2,1,0:T(8,128)(2,1)S(1)} %pad_maximum_fusion.10.refs_0_), channel_id=1, source_target_pairs={{0,16},{8,24},{16,0},{24,8},{1,17},{9,25},{17,1},{25,9},{2,18},{10... | collective-permute-start | bytes 884744 | tf_op jit(solution)/shard_map/ppermute | solution.py:887
  30.5 11.2 %collective-permute-start.2 = (bf16[112,768]{1,0:T(8,128)(2,1)S(1)}, bf16[112,768]{1,0:T(8,128)(2,1)S(1)}, u32[]{:S(2)}, u32[]{:S(2)}) collective-permute-start(bf16[112,768]{1,0:T(8,128)(2,1)S(1)} %get-tuple-element.100), channel_id=1, source_target_pairs={{0,6},{1,7},{2,0},{3,1},{4,2},{5,3},{6,4},{7,5},{8,14},{9,15},{10,... | collective-permute-start | bytes 516104 | tf_op jit(solution)/shard_map/ppermute | solution.py:882
  36.9 15.2 %collective-permute-start.1 = (bf16[112,768]{1,0:T(8,128)(2,1)S(1)}, bf16[112,768]{1,0:T(8,128)(2,1)S(1)}, u32[]{:S(2)}, u32[]{:S(2)}) collective-permute-start(bf16[112,768]{1,0:T(8,128)(2,1)S(1)} %get-tuple-element.100), channel_id=1, source_target_pairs={{0,4},{1,5},{2,6},{3,7},{4,0},{5,1},{6,2},{7,3},{8,12},{9,13},{10,... | collective-permute-start | bytes 516104 | tf_op jit(solution)/shard_map/ppermute | solution.py:882
  37.6 14.4 %collective-permute-start = (bf16[112,768]{1,0:T(8,128)(2,1)S(1)}, bf16[112,768]{1,0:T(8,128)(2,1)S(1)}, u32[]{:S(2)}, u32[]{:S(2)}) collective-permute-start(bf16[112,768]{1,0:T(8,128)(2,1)S(1)} %get-tuple-element.100), channel_id=1, source_target_pairs={{0,2},{1,3},{2,4},{3,5},{4,6},{5,7},{6,0},{7,1},{8,10},{9,11},{10,... | collective-permute-start | bytes 516104 | tf_op jit(solution)/shard_map/ppermute | solution.py:882
  41.6 14.3 %collective-permute-start.37 = (bf16[2,96,768]{2,1,0:T(8,128)(2,1)S(1)}, bf16[2,96,768]{2,1,0:T(8,128)(2,1)S(1)}, u32[]{:S(2)}, u32[]{:S(2)}) collective-permute-start(bf16[2,96,768]{2,1,0:T(8,128)(2,1)S(1)} %pad_maximum_fusion.10.refs_0_), channel_id=1, source_target_pairs={{0,8},{8,0},{16,24},{24,16},{1,9},{9,1},{17,25},{25,17},{2,10},{10... | collective-permute-start | bytes 884744 | tf_op jit(solution)/shard_map/ppermute | solution.py:887
  55.9 12.2 %collective-permute-start.22 = (bf16[2,96,768]{2,1,0:T(8,128)(2,1)S(1)}, bf16[2,96,768]{2,1,0:T(8,128)(2,1)S(1)}, u32[]{:S(2)}, u32[]{:S(2)}) collective-permute-start(bf16[2,96,768]{2,1,0:T(8,128)(2,1)S(1)} %pad_maximum_fusion.8.refs_0_), channel_id=1, source_target_pairs={{0,16},{8,24},{16,0},{24,8},{1,17},{9,25},{17,1},{25,9},{2,18},{10... | collective-permute-start | bytes 884744 | tf_op jit(solution)/shard_map/ppermute | solution.py:887
  57.2 13.3 %collective-permute-start.20 = (bf16[2,96,768]{2,1,0:T(8,128)(2,1)S(1)}, bf16[2,96,768]{2,1,0:T(8,128)(2,1)S(1)}, u32[]{:S(2)}, u32[]{:S(2)}) collective-permute-start(bf16[2,96,768]{2,1,0:T(8,128)(2,1)S(1)} %pad_maximum_fusion.8.refs_0_), channel_id=1, source_target_pairs={{0,8},{8,0},{16,24},{24,16},{1,9},{9,1},{17,25},{25,17},{2,10},{10... | collective-permute-start | bytes 884744 | tf_op jit(solution)/shard_map/ppermute | solution.py:887
  65.4 11.5 %collective-permute-start.21 = (bf16[2,96,768]{2,1,0:T(8,128)(2,1)S(1)}, bf16[2,96,768]{2,1,0:T(8,128)(2,1)}, u32[]{:S(2)}, u32[]{:S(2)}) collective-permute-start(bf16[2,96,768]{2,1,0:T(8,128)(2,1)S(1)} %pad_maximum_fusion.9.refs_1_), channel_id=1, source_target_pairs={{0,8},{8,0},{16,24},{24,16},{1,9},{9,1},{17,25},{25,17},{2,10},{10... | collective-permute-start | bytes 884744 | tf_op jit(solution)/shard_map/ppermute | solution.py:887
  70.5 11.3 %collective-permute-start.5 = (bf16[2,112,768]{2,1,0:T(8,128)(2,1)S(1)}, bf16[2,112,768]{2,1,0:T(8,128)(2,1)S(1)}, u32[]{:S(2)}, u32[]{:S(2)}) collective-permute-start(bf16[2,112,768]{2,1,0:T(8,128)(2,1)S(1)} %pad_maximum_fusion.6.refs_0_), channel_id=1, source_target_pairs={{0,16},{8,24},{16,0},{24,8},{1,17},{9,25},{17,1},{25,9},{2,18},{10... | collective-permute-start | bytes 1032200 | tf_op jit(solution)/shard_map/ppermute | solution.py:887
  71.8 12.6 %collective-permute-start.3 = (bf16[2,112,768]{2,1,0:T(8,128)(2,1)S(1)}, bf16[2,112,768]{2,1,0:T(8,128)(2,1)}, u32[]{:S(2)}, u32[]{:S(2)}) collective-permute-start(bf16[2,112,768]{2,1,0:T(8,128)(2,1)S(1)} %pad_maximum_fusion.6.refs_0_), channel_id=1, source_target_pairs={{0,8},{8,0},{16,24},{24,16},{1,9},{9,1},{17,25},{25,17},{2,10},{10... | collective-permute-start | bytes 1032200 | tf_op jit(solution)/shard_map/ppermute | solution.py:887
  77.0 12.4 %collective-permute-start.6 = (bf16[2,112,768]{2,1,0:T(8,128)(2,1)S(1)}, bf16[2,112,768]{2,1,0:T(8,128)(2,1)}, u32[]{:S(2)}, u32[]{:S(2)}) collective-permute-start(bf16[2,112,768]{2,1,0:T(8,128)(2,1)S(1)} %pad_maximum_fusion.7.refs_1_), channel_id=1, source_target_pairs={{0,16},{8,24},{16,0},{24,8},{1,17},{9,25},{17,1},{25,9},{2,18},{10... | collective-permute-start | bytes 1032200 | tf_op jit(solution)/shard_map/ppermute | solution.py:887
  77.5 13.5 %collective-permute-start.4 = (bf16[2,112,768]{2,1,0:T(8,128)(2,1)S(1)}, bf16[2,112,768]{2,1,0:T(8,128)(2,1)}, u32[]{:S(2)}, u32[]{:S(2)}) collective-permute-start(bf16[2,112,768]{2,1,0:T(8,128)(2,1)S(1)} %pad_maximum_fusion.7.refs_1_), channel_id=1, source_target_pairs={{0,8},{8,0},{16,24},{24,16},{1,9},{9,1},{17,25},{25,17},{2,10},{10... | collective-permute-start | bytes 1032200 | tf_op jit(solution)/shard_map/ppermute | solution.py:887
  99.3 14.2 %collective-permute-start.13 = (bf16[2,112,768]{2,1,0:T(8,128)(2,1)S(1)}, bf16[2,112,768]{2,1,0:T(8,128)(2,1)S(1)}, u32[]{:S(2)}, u32[]{:S(2)}) collective-permute-start(bf16[2,112,768]{2,1,0:T(8,128)(2,1)S(1)} %collective-permute-done.5.refs_4_), channel_id=1, source_target_pairs={{0,1},{1,0},{2,3},{3,2},{4,5},{5,4},{6,7},{7,6},{8,9},{9,8},{10,11... | collective-permute-start | bytes 1032200 | tf_op jit(solution)/shard_map/ppermute | solution.py:877
  100.1 13.4 %collective-permute-start.7 = (bf16[2,112,768]{2,1,0:T(8,128)(2,1)}, bf16[2,112,768]{2,1,0:T(8,128)(2,1)}, u32[]{:S(2)}, u32[]{:S(2)}) collective-permute-start(bf16[2,112,768]{2,1,0:T(8,128)(2,1)} %collective-permute-done.3.refs_2_), channel_id=1, source_target_pairs={{0,16},{8,24},{16,0},{24,8},{1,17},{9,25},{17,1},{25,9},{2,18},{10... | collective-permute-start | bytes 1032200 | tf_op jit(solution)/shard_map/ppermute | solution.py:887
  107.3 12.5 %collective-permute-start.8 = (bf16[2,112,768]{2,1,0:T(8,128)(2,1)}, bf16[2,112,768]{2,1,0:T(8,128)(2,1)}, u32[]{:S(2)}, u32[]{:S(2)}) collective-permute-start(bf16[2,112,768]{2,1,0:T(8,128)(2,1)} %collective-permute-done.6.refs_5_), channel_id=1, source_target_pairs={{0,8},{8,0},{16,24},{24,16},{1,9},{9,1},{17,25},{25,17},{2,10},{10... | collective-permute-start | bytes 1032200 | tf_op jit(solution)/shard_map/ppermute | solution.py:887
  119.8 30.3 %collective-permute-start.11 = (bf16[2,112,768]{2,1,0:T(8,128)(2,1)}, bf16[2,112,768]{2,1,0:T(8,128)(2,1)}, u32[]{:S(2)}, u32[]{:S(2)}) collective-permute-start(bf16[2,112,768]{2,1,0:T(8,128)(2,1)} %collective-permute-done.3.refs_2_), channel_id=1, source_target_pairs={{0,1},{1,0},{2,3},{3,2},{4,5},{5,4},{6,7},{7,6},{8,9},{9,8},{10,11... | collective-permute-start | bytes 1032200 | tf_op jit(solution)/shard_map/ppermute | solution.py:877
  119.8 30.3 %collective-permute-start.14 = (bf16[2,112,768]{2,1,0:T(8,128)(2,1)}, bf16[2,112,768]{2,1,0:T(8,128)(2,1)}, u32[]{:S(2)}, u32[]{:S(2)}) collective-permute-start(bf16[2,112,768]{2,1,0:T(8,128)(2,1)} %collective-permute-done.6.refs_5_), channel_id=1, source_target_pairs={{0,1},{1,0},{2,3},{3,2},{4,5},{5,4},{6,7},{7,6},{8,9},{9,8},{10,11... | collective-permute-start | bytes 1032200 | tf_op jit(solution)/shard_map/ppermute | solution.py:877
  120.3 29.8 %collective-permute-start.12 = (bf16[2,112,768]{2,1,0:T(8,128)(2,1)}, bf16[2,112,768]{2,1,0:T(8,128)(2,1)}, u32[]{:S(2)}, u32[]{:S(2)}) collective-permute-start(bf16[2,112,768]{2,1,0:T(8,128)(2,1)} %collective-permute-done.4.refs_3_), channel_id=1, source_target_pairs={{0,1},{1,0},{2,3},{3,2},{4,5},{5,4},{6,7},{7,6},{8,9},{9,8},{10,11... | collective-permute-start | bytes 1032200 | tf_op jit(solution)/shard_map/ppermute | solution.py:877
  120.4 29.7 %collective-permute-start.15 = (bf16[2,112,768]{2,1,0:T(8,128)(2,1)}, bf16[2,112,768]{2,1,0:T(8,128)(2,1)}, u32[]{:S(2)}, u32[]{:S(2)}) collective-permute-start(bf16[2,112,768]{2,1,0:T(8,128)(2,1)} %collective-permute-done.7.refs_6_), channel_id=1, source_target_pairs={{0,1},{1,0},{2,3},{3,2},{4,5},{5,4},{6,7},{7,6},{8,9},{9,8},{10,11... | collective-permute-start | bytes 1032200 | tf_op jit(solution)/shard_map/ppermute | solution.py:877
  120.8 29.3 %collective-permute-start.16 = (bf16[2,112,768]{2,1,0:T(8,128)(2,1)}, bf16[2,112,768]{2,1,0:T(8,128)(2,1)}, u32[]{:S(2)}, u32[]{:S(2)}) collective-permute-start(bf16[2,112,768]{2,1,0:T(8,128)(2,1)} %collective-permute-done.8.refs_7_), channel_id=1, source_target_pairs={{0,1},{1,0},{2,3},{3,2},{4,5},{5,4},{6,7},{7,6},{8,9},{9,8},{10,11... | collective-permute-start | bytes 1032200 | tf_op jit(solution)/shard_map/ppermute | solution.py:877
  217.7 76.4 %collective-permute-start.67 = (bf16[4,4,96,768]{3,2,1,0:T(8,128)(2,1)}, bf16[4,4,96,768]{3,2,1,0:T(8,128)(2,1)}, u32[]{:S(2)}, u32[]{:S(2)}) collective-permute-start(bf16[4,4,96,768]{3,2,1,0:T(8,128)(2,1)} %grad_down.3), channel_id=1, source_target_pairs={{0,1},{1,0},{2,3},{3,2},{4,5},{5,4},{6,7},{7,6},{8,9},{9,8},{10,11... | collective-permute-start | bytes 7077896 | tf_op jit(solution)/shard_map/ppermute | solution.py:877
  223.7 74.8 %collective-permute-start.59 = (bf16[4,4,96,768]{3,2,1,0:T(8,128)(2,1)}, bf16[4,4,96,768]{3,2,1,0:T(8,128)(2,1)}, u32[]{:S(2)}, u32[]{:S(2)}) collective-permute-start(bf16[4,4,96,768]{3,2,1,0:T(8,128)(2,1)} %grad_up.3), channel_id=1, source_target_pairs={{0,1},{1,0},{2,3},{3,2},{4,5},{5,4},{6,7},{7,6},{8,9},{9,8},{10,11... | collective-permute-start | bytes 7077896 | tf_op jit(solution)/shard_map/ppermute | solution.py:877
  257.9 43.9 %collective-permute-start.51 = (bf16[4,4,112,768]{3,2,1,0:T(8,128)(2,1)}, bf16[4,4,112,768]{3,2,1,0:T(8,128)(2,1)}, u32[]{:S(2)}, u32[]{:S(2)}) collective-permute-start(bf16[4,4,112,768]{3,2,1,0:T(8,128)(2,1)} %grad_rest.3), channel_id=1, source_target_pairs={{0,1},{1,0},{2,3},{3,2},{4,5},{5,4},{6,7},{7,6},{8,9},{9,8},{10,11... | collective-permute-start | bytes 8257544 | tf_op jit(solution)/shard_map/ppermute | solution.py:877
  295.7 16.3 %collective-permute-start.70 = (bf16[2,2,96,768]{3,2,1,0:T(8,128)(2,1)S(1)}, bf16[2,2,96,768]{3,2,1,0:T(8,128)(2,1)S(1)}, u32[]{:S(2)}, u32[]{:S(2)}) collective-permute-start(bf16[2,2,96,768]{3,2,1,0:T(8,128)(2,1)S(1)} %pad_maximum_fusion.5), channel_id=1, source_target_pairs={{0,16},{8,24},{16,0},{24,8},{1,17},{9,25},{17,1},{25,9},{2,18},{10... | collective-permute-start | bytes 1769480 | tf_op jit(solution)/shard_map/ppermute | solution.py:887
  296.8 16.3 %collective-permute-start.68 = (bf16[2,2,96,768]{3,2,1,0:T(8,128)(2,1)S(1)}, bf16[2,2,96,768]{3,2,1,0:T(8,128)(2,1)S(1)}, u32[]{:S(2)}, u32[]{:S(2)}) collective-permute-start(bf16[2,2,96,768]{3,2,1,0:T(8,128)(2,1)S(1)} %pad_maximum_fusion.4), channel_id=1, source_target_pairs={{0,8},{8,0},{16,24},{24,16},{1,9},{9,1},{17,25},{25,17},{2,10},{10... | collective-permute-start | bytes 1769480 | tf_op jit(solution)/shard_map/ppermute | solution.py:887
  300.0 24.6 %collective-permute-start.62 = (bf16[2,2,96,768]{3,2,1,0:T(8,128)(2,1)S(1)}, bf16[2,2,96,768]{3,2,1,0:T(8,128)(2,1)S(1)}, u32[]{:S(2)}, u32[]{:S(2)}) collective-permute-start(bf16[2,2,96,768]{3,2,1,0:T(8,128)(2,1)S(1)} %pad_maximum_fusion.3), channel_id=1, source_target_pairs={{0,16},{8,24},{16,0},{24,8},{1,17},{9,25},{17,1},{25,9},{2,18},{10... | collective-permute-start | bytes 1769480 | tf_op jit(solution)/shard_map/ppermute | solution.py:887
  301.1 24.9 %collective-permute-start.60 = (bf16[2,2,96,768]{3,2,1,0:T(8,128)(2,1)S(1)}, bf16[2,2,96,768]{3,2,1,0:T(8,128)(2,1)S(1)}, u32[]{:S(2)}, u32[]{:S(2)}) collective-permute-start(bf16[2,2,96,768]{3,2,1,0:T(8,128)(2,1)S(1)} %pad_maximum_fusion.2), channel_id=1, source_target_pairs={{0,8},{8,0},{16,24},{24,16},{1,9},{9,1},{17,25},{25,17},{2,10},{10... | collective-permute-start | bytes 1769480 | tf_op jit(solution)/shard_map/ppermute | solution.py:887
  303.6 51.7 %collective-permute-start.54 = (bf16[2,2,112,768]{3,2,1,0:T(8,128)(2,1)S(1)}, bf16[2,2,112,768]{3,2,1,0:T(8,128)(2,1)S(1)}, u32[]{:S(2)}, u32[]{:S(2)}) collective-permute-start(bf16[2,2,112,768]{3,2,1,0:T(8,128)(2,1)S(1)} %pad_maximum_fusion.1), channel_id=1, source_target_pairs={{0,16},{8,24},{16,0},{24,8},{1,17},{9,25},{17,1},{25,9},{2,18},{10... | collective-permute-start | bytes 2064392 | tf_op jit(solution)/shard_map/ppermute | solution.py:887
  314.4 31.2 %collective-permute-start.69 = (bf16[2,96,768]{2,1,0:T(8,128)(2,1)S(1)}, bf16[2,96,768]{2,1,0:T(8,128)(2,1)S(1)}, u32[]{:S(2)}, u32[]{:S(2)}) collective-permute-start(bf16[2,96,768]{2,1,0:T(8,128)(2,1)S(1)} %get-tuple-element.239), channel_id=1, source_target_pairs={{0,16},{8,24},{16,0},{24,8},{1,17},{9,25},{17,1},{25,9},{2,18},{10... | collective-permute-start | bytes 884744 | tf_op jit(solution)/shard_map/ppermute | solution.py:887
  315.5 31.6 %collective-permute-start.71 = (bf16[2,96,768]{2,1,0:T(8,128)(2,1)S(1)}, bf16[2,96,768]{2,1,0:T(8,128)(2,1)S(1)}, u32[]{:S(2)}, u32[]{:S(2)}) collective-permute-start(bf16[2,96,768]{2,1,0:T(8,128)(2,1)S(1)} %get-tuple-element.240), channel_id=1, source_target_pairs={{0,8},{8,0},{16,24},{24,16},{1,9},{9,1},{17,25},{25,17},{2,10},{10... | collective-permute-start | bytes 884744 | tf_op jit(solution)/shard_map/ppermute | solution.py:887
  324.6 30.8 %collective-permute-start.52 = (bf16[2,2,112,768]{3,2,1,0:T(8,128)(2,1)S(1)}, bf16[2,2,112,768]{3,2,1,0:T(8,128)(2,1)S(1)}, u32[]{:S(2)}, u32[]{:S(2)}) collective-permute-start(bf16[2,2,112,768]{3,2,1,0:T(8,128)(2,1)S(1)} %pad_maximum_fusion), channel_id=1, source_target_pairs={{0,8},{8,0},{16,24},{24,16},{1,9},{9,1},{17,25},{25,17},{2,10},{10... | collective-permute-start | bytes 2064392 | tf_op jit(solution)/shard_map/ppermute | solution.py:887
  327.3 23.8 %collective-permute-start.61 = (bf16[2,96,768]{2,1,0:T(8,128)(2,1)S(1)}, bf16[2,96,768]{2,1,0:T(8,128)(2,1)S(1)}, u32[]{:S(2)}, u32[]{:S(2)}) collective-permute-start(bf16[2,96,768]{2,1,0:T(8,128)(2,1)S(1)} %get-tuple-element.247), channel_id=1, source_target_pairs={{0,16},{8,24},{16,0},{24,8},{1,17},{9,25},{17,1},{25,9},{2,18},{10... | collective-permute-start | bytes 884744 | tf_op jit(solution)/shard_map/ppermute | solution.py:887
  351.1 10.9 %collective-permute-start.72 = (bf16[96,768]{1,0:T(8,128)(2,1)S(1)}, bf16[96,768]{1,0:T(8,128)(2,1)S(1)}, u32[]{:S(2)}, u32[]{:S(2)}) collective-permute-start(bf16[96,768]{1,0:T(8,128)(2,1)S(1)} %get-tuple-element.255), channel_id=1, source_target_pairs={{0,4},{1,5},{2,6},{3,7},{4,0},{5,1},{6,2},{7,3},{8,12},{9,13},{10,... | collective-permute-start | bytes 442376 | tf_op jit(solution)/shard_map/ppermute | solution.py:882
  359.0 16.5 %collective-permute-start.65 = (bf16[96,768]{1,0:T(8,128)(2,1)S(1)}, bf16[96,768]{1,0:T(8,128)(2,1)S(1)}, u32[]{:S(2)}, u32[]{:S(2)}) collective-permute-start(bf16[96,768]{1,0:T(8,128)(2,1)S(1)} %fusion.16), channel_id=1, source_target_pairs={{0,2},{1,3},{2,4},{3,5},{4,6},{5,7},{6,0},{7,1},{8,10},{9,11},{10,... | collective-permute-start | bytes 442376 | tf_op jit(solution)/shard_map/ppermute | solution.py:882
  361.9 16.5 %collective-permute-start.64 = (bf16[96,768]{1,0:T(8,128)(2,1)S(1)}, bf16[96,768]{1,0:T(8,128)(2,1)S(1)}, u32[]{:S(2)}, u32[]{:S(2)}) collective-permute-start(bf16[96,768]{1,0:T(8,128)(2,1)S(1)} %get-tuple-element.257), channel_id=1, source_target_pairs={{0,4},{1,5},{2,6},{3,7},{4,0},{5,1},{6,2},{7,3},{8,12},{9,13},{10,... | collective-permute-start | bytes 442376 | tf_op jit(solution)/shard_map/ppermute | solution.py:882
  362.0 19.2 %collective-permute-start.66 = (bf16[96,768]{1,0:T(8,128)(2,1)S(1)}, bf16[96,768]{1,0:T(8,128)(2,1)S(1)}, u32[]{:S(2)}, u32[]{:S(2)}) collective-permute-start(bf16[96,768]{1,0:T(8,128)(2,1)S(1)} %get-tuple-element.258), channel_id=1, source_target_pairs={{0,6},{1,7},{2,0},{3,1},{4,2},{5,3},{6,4},{7,5},{8,14},{9,15},{10,... | collective-permute-start | bytes 442376 | tf_op jit(solution)/shard_map/ppermute | solution.py:882
  367.4 14.5 %collective-permute-start.57 = (bf16[112,768]{1,0:T(8,128)(2,1)S(1)}, bf16[112,768]{1,0:T(8,128)(2,1)S(1)}, u32[]{:S(2)}, u32[]{:S(2)}) collective-permute-start(bf16[112,768]{1,0:T(8,128)(2,1)S(1)} %fusion.15), channel_id=1, source_target_pairs={{0,2},{1,3},{2,4},{3,5},{4,6},{5,7},{6,0},{7,1},{8,10},{9,11},{10,... | collective-permute-start | bytes 516104 | tf_op jit(solution)/shard_map/ppermute | solution.py:882
  374.0 15.0 %collective-permute-start.56 = (bf16[112,768]{1,0:T(8,128)(2,1)S(1)}, bf16[112,768]{1,0:T(8,128)(2,1)S(1)}, u32[]{:S(2)}, u32[]{:S(2)}) collective-permute-start(bf16[112,768]{1,0:T(8,128)(2,1)S(1)} %get-tuple-element.253), channel_id=1, source_target_pairs={{0,4},{1,5},{2,6},{3,7},{4,0},{5,1},{6,2},{7,3},{8,12},{9,13},{10,... | collective-permute-start | bytes 516104 | tf_op jit(solution)/shard_map/ppermute | solution.py:882
  375.6 13.5 %collective-permute-start.58 = (bf16[112,768]{1,0:T(8,128)(2,1)S(1)}, bf16[112,768]{1,0:T(8,128)(2,1)S(1)}, u32[]{:S(2)}, u32[]{:S(2)}) collective-permute-start(bf16[112,768]{1,0:T(8,128)(2,1)S(1)} %get-tuple-element.254), channel_id=1, source_target_pairs={{0,6},{1,7},{2,0},{3,1},{4,2},{5,3},{6,4},{7,5},{8,14},{9,15},{10,... | collective-permute-start | bytes 516104 | tf_op jit(solution)/shard_map/ppermute | solution.py:882
  391.7 11.8 %collective-permute-start.76 = (f32[8,128]{1,0:T(8,128)S(1)}, f32[8,128]{1,0:T(8,128)S(1)}, u32[]{:S(2)}, u32[]{:S(2)}) collective-permute-start(f32[8,128]{1,0:T(8,128)S(1)} %broadcast_in_dim.33), channel_id=1, source_target_pairs={{0,16},{8,24},{16,0},{24,8},{1,17},{9,25},{17,1},{25,9},{2,18},{10... | collective-permute-start | bytes 12296 | tf_op jit(solution)/shard_map/ppermute | solution.py:887
  392.2 11.3 %collective-permute-start.77 = (f32[8,128]{1,0:T(8,128)S(1)}, f32[8,128]{1,0:T(8,128)S(1)}, u32[]{:S(2)}, u32[]{:S(2)}) collective-permute-start(f32[8,128]{1,0:T(8,128)S(1)} %broadcast_in_dim.33), channel_id=1, source_target_pairs={{0,24},{8,16},{16,8},{24,0},{1,25},{9,17},{17,9},{25,1},{2,26},{10... | collective-permute-start | bytes 12296 | tf_op jit(solution)/shard_map/ppermute | solution.py:887
  403.6 11.1 %collective-permute-start.80 = (f32[8,128]{1,0:T(8,128)S(1)}, f32[8,128]{1,0:T(8,128)S(1)}, u32[]{:S(2)}, u32[]{:S(2)}) collective-permute-start(f32[8,128]{1,0:T(8,128)S(1)} %add_add_fusion.1), channel_id=1, source_target_pairs={{0,6},{1,7},{2,0},{3,1},{4,2},{5,3},{6,4},{7,5},{8,14},{9,15},{10,... | collective-permute-start | bytes 12296 | tf_op jit(solution)/shard_map/ppermute | solution.py:882
  (160 other events, 1866.9 us)

commit v2 on v0

--- a/solution.py
+++ b/solution.py
@@ -1,12 +1,15 @@
+import functools
+import math
+
 import jax
 import jax.numpy as jnp
 from jax import lax
+from jax.experimental import pallas as pl
+from jax.experimental.pallas import tpu as pltpu
 from jax.sharding import PartitionSpec as P
 
 HEADS = 12
 STEP = 10
-
-
 NORM_EPS = 1e-05
 CLIP_NORM = 1.0
 BETA_ONE = 0.9
@@ -19,6 +22,1414 @@
 RATE_DOWN = 0.05
 RATE_PROJ = 0.05
 RATE_VEC = 1.0
+
+BF = jnp.bfloat16
+F32 = jnp.float32
+LOG2E = math.log2(math.e)
+MIB = 1 << 20
+
+
+def nn(a, b):
+    return jnp.dot(a, b, preferred_element_type=F32)
+
+
+def nt(a, b):
+    return lax.dot_general(a, b, (((1,), (1,)), ((), ())), preferred_element_type=F32)
+
+
+def sds(shape, dtype):
+    return jax.ShapeDtypeStruct(tuple(shape), dtype)
+
+
+def call(
+    kernel, name, out_shape, args, scratch=(), place=None, flops=0, vmem=16, space=pltpu.VMEM, alias=()
+):
+    many = isinstance(out_shape, (list, tuple))
+    outs = list(out_shape) if many else [out_shape]
+    specs = [pl.BlockSpec(memory_space=space)] * len(args)
+    if place is not None:
+        args = (place, *args)
+        specs = [pl.BlockSpec(memory_space=pltpu.SMEM), *specs]
+    moved = sum(math.prod(a.shape) * jnp.dtype(a.dtype).itemsize for a in (*args, *outs))
+    result = pl.pallas_call(
+        kernel,
+        name=name,
+        out_shape=outs,
+        in_specs=specs,
+        out_specs=[pl.BlockSpec(memory_space=pltpu.VMEM)] * len(outs),
+        scratch_shapes=list(scratch),
+        input_output_aliases=dict(alias),
+        cost_estimate=pl.CostEstimate(
+            flops=int(flops) // 1000, bytes_accessed=int(moved) // 1000, transcendentals=0
+        ),
+        compiler_params=pltpu.CompilerParams(vmem_limit_bytes=vmem * MIB),
+    )(*args)
+    return result if many else result[0]
+
+
+def lanes(start, size):
+    return pl.ds(pl.multiple_of(start, 128), size)
+
+
+def lines(start, size):
+    return pl.ds(pl.multiple_of(start, 16), size)
+
+
+def norm_stats(summed):
+    average = jnp.mean(summed, axis=-1, keepdims=True)
+    centered = summed - average
+    variance = jnp.mean(centered * centered, axis=-1, keepdims=True)
+    inverse = lax.rsqrt(variance + NORM_EPS)
+    return centered * inverse, inverse
+
+
+def norm_grad(shaped, inverse, gains, grad):
+    inner = grad * gains
+    first = jnp.mean(inner, axis=-1, keepdims=True)
+    second = jnp.mean(inner * shaped, axis=-1, keepdims=True)
+    return inverse * (inner - first - shaped * second)
+
+
+def normal_parts(values):
+    size = jnp.abs(values)
+    base = 1.0 + (0.3275911 * math.sqrt(0.5)) * size
+    t = pl.reciprocal(base, approx=True)
+    t = t * (2.0 - base * t)
+    bell = jnp.exp2(values * values * (-0.5 * LOG2E))
+    poly = 0.5 * 1.061405429
+    for c in (-1.453152027, 1.421413741, -0.284496736, 0.254829592):
+        poly = poly * t + 0.5 * c
+    tail = poly * t * bell
+    return bell, jnp.where(values >= 0.0, 1.0 - tail, tail)
+
+
+def lanes_below(width):
+    return lax.broadcasted_iota(jnp.int32, (1, 2 * width), 1) < width
+
+
+def swap_halves(value):
+    width = value.shape[1] // 2
+    return jnp.concatenate([value[:, width:], value[:, :width]], axis=1)
+
+
+def pack_kernel(place, *refs):
+    given, (own, a_ref, bc_ref), (small, sems), held = refs[:6], refs[6:9], refs[9:11], refs[11:]
+    copies = [pltpu.make_async_copy(a, b, sems.at[i]) for i, (a, b) in enumerate(zip(given, held))]
+    for copy in copies:
+        copy.start()
+    for copy in copies:
+        copy.wait()
+    qkv, out, up, down, proj, vec = held
+    vec = vec[...].reshape(1, vec.shape[0])
+    odd = (place[0] & 1) == 1
+    rows, wide = up.shape
+    tile = 128
+    half = tile // 2
+    full = qkv.shape[1] - half
+    after = full + tile
+    q, o = qkv[...], out[...]
+
+    def pick(one, two):
+        return jnp.where(odd, one, two).astype(BF)
+
+    a_ref[:rows, :full] = pick(q[:, half:], q[:, :full])
+    a_ref[:rows, full : full + half] = pick(o[:, :half], q[:, full:])
+    a_ref[:rows, full + half : after] = pick(q[:, :half], o[:, tile:])
+    a_ref[:rows, after:] = pick(o[:, half:], o[:, :tile])
+    small[...] = jnp.zeros_like(small)
+    height, width = proj.shape
+    for g in range(height // 8):
+        small[0:8, g * width : (g + 1) * width] = proj[8 * g : 8 * g + 8, :]
+    start = (height // 8) * width
+    room = wide - start
+    small[0:1, start:] = vec[:, :room]
+    left = vec.shape[1] - room
+    small[1:2, start : start + left] = vec[:, room:]
+    a_ref[rows:, :] = small[...].astype(BF)
+    bc_ref[:rows, :] = up[...].astype(BF)
+    across = down.shape[1]
+    for h in range(down.shape[0] // rows):
+        bc_ref[rows:, h * across : (h + 1) * across] = down[rows * h : rows * (h + 1), :].astype(BF)
+    tall = a_ref.shape[0]
+    own[:tall, :] = a_ref[...]
+    own[tall:, :] = bc_ref[...]
+
+
+def pack(place, *given):
+    rows, wide = given[2].shape
+    tall = rows + 16
+    return call(
+        pack_kernel,
+        "pack_weights",
+        [sds((tall + 2 * rows, wide), BF), sds((tall, wide), BF), sds((2 * rows, wide), BF)],
+        given,
+        scratch=[
+            pltpu.VMEM((16, wide), F32),
+            pltpu.SemaphoreType.DMA((len(given),)),
+            *(pltpu.VMEM(a.shape, F32) for a in given),
+        ],
+        place=place,
+        space=pltpu.HBM,
+    )
+
+
+def split_cores(place, value, rows, mine, theirs, cols):
+    first = place[2] == 0
+    for z in range(value.shape[0] // (2 * rows)):
+        one = value[2 * z * rows : (2 * z + 1) * rows]
+        two = value[(2 * z + 1) * rows : (2 * z + 2) * rows]
+        mine[z * rows : (z + 1) * rows, cols] = jnp.where(first, one, two)
+        theirs[z * rows : (z + 1) * rows, cols] = jnp.where(first, two, one)
+
+
+def order_kernel(
+    marked, rows, place, pos, x, front, rest, frontt, frontt_other, xt, xt_other, back
+):
+    seqs, length, _ = x.shape
+    half = front.shape[1]
+    col = lax.broadcasted_iota(jnp.int32, (half, length), 1)
+    row = lax.broadcasted_iota(jnp.int32, (half, length), 0)
+    before = (
+        lax.broadcasted_iota(jnp.int32, (length, length), 0)
+        < lax.broadcasted_iota(jnp.int32, (length, length), 1)
+    ).astype(BF)
+    for s in range(seqs):
+        hot = (pos[s] == col) & (row < marked)
+        free = 1.0 - jnp.sum(hot.astype(F32), axis=0, keepdims=True)
+        rank = nn(jnp.broadcast_to(free, (16, length)).astype(BF), before)[0:1, :]
+        target = jnp.where(free > 0.5, rank.astype(jnp.int32) + marked, -1)
+        one = jnp.where(hot | (target == row), 1.0, 0.0)
+        two = jnp.where(target == (row + half), 1.0, 0.0)
+        values = x[s]
+        head = nn(one.astype(BF), values)
+        front[s] = head.astype(BF)
+        rest[s] = nn(two.astype(BF), values).astype(BF)
+        at = slice(s * half, (s + 1) * half)
+        split_cores(place, head.T.astype(BF), rows, frontt, frontt_other, at)
+        at = slice(s * length, (s + 1) * length)
+        split_cores(place, values.T, rows, xt, xt_other, at)
+        back[s, :, :half] = one.T.astype(BF)
+        back[s, :, half:] = two.T.astype(BF)
+
+
+def order_rows(place, tokens, positions, slots):
+    seqs, length, width = tokens.shape
+    marked = positions.shape[1]
+    half = length // 2
+    pos = jnp.pad(positions, ((0, 0), (0, half - marked)), constant_values=-1)[:, :, None]
+    rows = sds((seqs, half, width), BF)
+    front = sds((width // 2, seqs * half), BF)
+    every = sds((width // 2, seqs * length), BF)
+    return call(
+        functools.partial(order_kernel, marked, width // (2 * slots)),
+        "order_rows",
+        [rows, rows, front, front, every, every, sds((seqs, length, length), BF)],
+        (pos, tokens),
+        place=place,
+        flops=2 * seqs * length * length * width,
+    )
+
+
+def qkv_kernel(front, rest, x, weight, vec, proj, q_front, q_rest, kv, kvp):
+    seqs, _, width = front.shape
+    piece = width // 2
+    for s in range(seqs):
+        for j in range(2):
+            cols = slice(j * piece, (j + 1) * piece)
+            w = weight[:, cols]
+            bias = vec[:, cols]
+            q_front[s, :, cols] = (nn(front[s], w) + bias).astype(BF)
+            q_rest[s, :, cols] = (nn(rest[s], w) + bias).astype(BF)
+        for j in range(4):
+            cols = slice(j * piece, (j + 1) * piece)
+            at = slice(width + j * piece, width + (j + 1) * piece)
+            part = (nn(x[s], weight[:, at]) + vec[:, at]).astype(BF)
+            kv[s, :, cols] = part
+            kvp[s, :, cols] = nn(proj[...], part).astype(BF)
+
+
+def make_qkv(front, rest, x, weight, vec, proj):
+    seqs, half, width = front.shape
+    length = x.shape[1]
+    rows = proj.shape[0]
+    return call(
+        qkv_kernel,
+        "make_qkv",
+        [
+            sds(front.shape, BF),
+            sds(front.shape, BF),
+            sds((seqs, length, 2 * width), BF),
+            sds((seqs, rows, 2 * width), BF),
+        ],
+        (front, rest, x, weight, vec, proj),
+        flops=2 * seqs * length * width * width * 3 + 2 * seqs * rows * length * 2 * width,
+    )
+
+
+def attend_kernel(head, q_front, q_rest, kvp, o_front, o_rest):
+    seqs, _, width = q_front.shape
+    below = lanes_below(head)
+    factor = LOG2E / math.sqrt(head)
+
+    def pair(p, carry):
+        at = lanes(p * 2 * head, 2 * head)
+        for s in range(seqs):
+            k, v = kvp[s, :, at], kvp[s, :, lanes(width + p * 2 * head, 2 * head)]
+            zero = jnp.zeros_like(k)
+            heads = [(jnp.where(own, k, zero), jnp.where(own, v, zero)) for own in (below, ~below)]
+            for q_ref, o_ref in ((q_front, o_front), (q_rest, o_rest)):
+                q = q_ref[s, :, at]
+                total = None
+                for kh, vh in heads:
+                    scores = nt(q, kh)
+                    e = jnp.exp2((scores - jnp.max(scores, axis=-1, keepdims=True)) * factor)
+                    scale = 1.0 / jnp.sum(e, axis=-1, keepdims=True)
+                    part = nn(e.astype(BF), vh) * scale
+                    total = part if total is None else total + part
+                o_ref[s, :, at] = total.astype(BF)
+        return carry
+
+    lax.fori_loop(0, HEADS // 2, pair, 0)
+
+
+def attend(q_front, q_rest, kvp):
+    seqs, half, width = q_front.shape
+    rows = kvp.shape[1]
+    head = width // HEADS
+    return call(
+        functools.partial(attend_kernel, head),
+        "attend",
+        [sds(q_front.shape, BF)] * 2,
+        (q_front, q_rest, kvp),
+        flops=2 * seqs * HEADS * 2 * half * rows * 2 * head * 2,
+    )
+
+
+def join_kernel(marks, keep, rows, place, attended, x, weight, vec, normed, low, *more):
+    bias, gain, shift = (vec[:, a:b] for a, b in marks)
+    step = 256
+    for r in range(0, x.shape[0], step):
+        at = slice(r, r + step)
+        part = attended[at, :]
+        summed = x[at, :].astype(F32) + nn(part, weight[...]) + bias
+        shaped, _ = norm_stats(summed)
+        result = shaped * gain + shift
+        normed[at, :] = result
+        low[at, :] = result.astype(BF)
+        if keep:
+            kept, lowt, lowt_other, attendedt, attendedt_other = more
+            kept[at, :] = summed
+            split_cores(place, result.T.astype(BF), rows, lowt, lowt_other, at)
+            split_cores(place, part.T, rows, attendedt, attendedt_other, at)
+
+
+def join(place, attended, x, weight, vec, marks, keep, slots):
+    rows, width = x.shape
+    outs = [sds((rows, width), F32), sds((rows, width), BF)]
+    if keep:
+        outs += [sds((rows, width), F32)] + [sds((width // 2, rows), BF)] * 4
+    return call(
+        functools.partial(join_kernel, marks, keep, width // (2 * slots)),
+        "join_front" if keep else "join_rest",
+        outs,
+        (attended, x, weight, vec),
+        place=place,
+        flops=2 * rows * width * width,
+    )
+
+
+def lift_kernel(mark, keep, place, low, weight, vec, active, *more):
+    rows = low.shape[0]
+    parts, _, piece = weight.shape
+    step = 128
+    for f in range(parts):
+        cols = slice(f * piece, (f + 1) * piece)
+        bias = vec[:, mark + f * piece : mark + (f + 1) * piece]
+        for r in range(0, rows, step):
+            at = slice(r, r + step)
+            u = nn(low[at, :], weight[f]) + bias
+            bell, share = normal_parts(u)
+            a = (u * share).astype(BF)
+            active[at, cols] = a
+            if keep:
+                slope, give = more
+                factor = 1.0 / math.sqrt(2.0 * math.pi)
+                slope[at, cols] = (share + u * bell * factor).astype(BF)
+                half = piece // 2
+                give[at, f * half : (f + 1) * half] = jnp.where(
+                    place[2] == 0, a[:, half:], a[:, :half]
+                )
+
+
+def lift(place, low, weight, vec, mark, keep):
+    rows, width = low.shape
+    parts, _, piece = weight.shape
+    outs = [sds((rows, parts * piece), BF)]
+    if keep:
+        outs += [sds((rows, parts * piece), BF), sds((rows, parts * piece // 2), BF)]
+    return call(
+        functools.partial(lift_kernel, mark, keep),
+        "lift_front" if keep else "lift_rest",
+        outs,
+        (low, weight, vec),
+        place=place,
+        flops=2 * rows * width * parts * piece,
+    )
+
+
+def lower_kernel(marks, active, normed, weight, vec, *refs):
+    bias, gain, shift = (vec[:, a:b] for a, b in marks)
+    step = 256
+    for r in range(0, normed.shape[0], step):
+        at = slice(r, r + step)
+        summed = normed[at, :] + nt(active[at, :], weight[...]) + bias
+        shaped, inverse = norm_stats(summed)
+        if len(refs) == 1:
+            refs[0][at, :] = (shaped * gain + shift).astype(BF)
+            continue
+        dy, output, d_sum, d_low, d_lowt, sums = refs
+        output[at, :] = (shaped * gain + shift).astype(BF)
+        grad = dy[at, :].astype(F32)
+        back = norm_grad(shaped, inverse, gain, grad)
+        d_sum[at, :] = back
+        d_low[at, :] = back.astype(BF)
+        d_lowt[:, at] = back.T.astype(BF)
+        new = [jnp.sum(v, axis=0, keepdims=True) for v in (grad * shaped, grad, back)]
+        for i, v in enumerate(new):
+            sums[i : i + 1, :] = v if r == 0 else sums[i : i + 1, :] + v
+
+
+def lower(active, normed, weight, vec, marks, dy=None):
+    rows, width = normed.shape
+    hidden = active.shape[1]
+    full = (rows, width)
+    if dy is None:
+        outs, more = [sds(full, BF)], ()
+    else:
+        outs = [
+            sds(full, BF),
+            sds(full, F32),
+            sds(full, BF),
+            sds((width, rows), BF),
+            sds((8, width), F32),
+        ]
+        more = (dy,)
+    return call(
+        functools.partial(lower_kernel, marks),
+        "lower_rest" if dy is None else "lower_front",
+        outs,
+        (active, normed, weight, vec, *more),
+        flops=2 * rows * width * hidden,
+    )
+
+
+def hidden_back_kernel(d_low, weight, slope, d_hidden, sums):
+    rows, piece = d_low.shape
+    step = 256
+    for f in range(weight.shape[1] // piece):
+        cols = slice(f * piece, (f + 1) * piece)
+        for r in range(0, rows, step):
+            at = slice(r, r + step)
+            du = nn(d_low[at, :], weight[:, cols]) * slope[at, cols].astype(F32)
+            d_hidden[at, cols] = du.astype(BF)
+            part = jnp.sum(du, axis=0, keepdims=True)
+            sums[:, cols] = part if r == 0 else sums[:, cols] + part
+
+
+def hidden_back(d_low, weight, slope):
+    rows, width = d_low.shape
+    hidden = weight.shape[1]
+    return call(
+        hidden_back_kernel,
+        "hidden_back",
+        [sds((rows, hidden), BF), sds((1, hidden), F32)],
+        (d_low, weight, slope),
+        flops=2 * rows * width * hidden,
+    )
+
+
+def first_back_kernel(
+    marks, d_hidden, up, d_sum, kept, vec, weight, d_first, d_low, d_attended, sums
+):
+    gain = vec[:, marks[0] : marks[1]]
+    parts, _, piece = up.shape
+    step = 256
+    for r in range(0, d_sum.shape[0], step):
+        at = slice(r, r + step)
+        grad = d_sum[at, :]
+        for f in range(parts):
+            grad = grad + nt(d_hidden[at, f * piece : (f + 1) * piece], up[f])
+        shaped, inverse = norm_stats(kept[at, :])
+        back = norm_grad(shaped, inverse, gain, grad)
+        low = back.astype(BF)
+        d_first[at, :] = back
+        d_low[at, :] = low
+        d_attended[at, :] = nt(low, weight[...]).astype(BF)
+        new = [jnp.sum(v, axis=0, keepdims=True) for v in (grad * shaped, grad, back)]
+        for i, v in enumerate(new):
+            sums[i : i + 1, :] = v if r == 0 else sums[i : i + 1, :] + v
+
+
+def first_back(d_hidden, up, d_sum, kept, vec, weight, marks):
+    rows, width = d_sum.shape
+    parts, _, piece = up.shape
+    full = (rows, width)
+    return call(
+        functools.partial(first_back_kernel, marks),
+        "first_back",
+        [sds(full, F32), sds(full, BF), sds(full, BF), sds((8, width), F32)],
+        (d_hidden, up, d_sum, kept, vec, weight),
+        flops=2 * rows * width * (parts * piece + width),
+    )
+
+
+def attend_back_kernel(head, s, queries, kvp, grads, *refs):
+    d_q, d_k, d_v, sums = refs[-4:]
+    width = queries.shape[2]
+    below = lanes_below(head)
+    line = lax.broadcasted_iota(jnp.int32, (2 * head, 1), 0) < head
+    scale = 1.0 / math.sqrt(head)
+
+    def pair(n, carry):
+        at = lanes(n * 2 * head, 2 * head)
+        q, k, g = queries[s, :, at], kvp[s, :, at], grads[s, :, at]
+        v = kvp[s, :, lanes(width + n * 2 * head, 2 * head)]
+        zero = jnp.zeros_like(k)
+        none = jnp.zeros_like(q)
+        kt = k.T
+        dq = dk = dv = None
+        for own, ownt in ((below, line), (~below, ~line)):
+            scores = nt(jnp.where(own, k, zero), q)
+            top = jnp.max(scores, axis=0, keepdims=True)
+            e = jnp.exp2((scores - top) * (LOG2E * scale))
+            p = e * (1.0 / jnp.sum(e, axis=0, keepdims=True))
+            dv_part = nn(p.astype(BF), jnp.where(own, g, none))
+            dp = nt(jnp.where(own, v, zero), g)
+            both = p * dp
+            ds = ((both - p * jnp.sum(both, axis=0, keepdims=True)) * scale).astype(BF)
+            dk_part = nn(ds, jnp.where(own, q, none))
+            dq_part = nn(jnp.where(ownt, kt, jnp.zeros_like(kt)), ds)
+            dv = dv_part if dv is None else dv + dv_part
+            dk = dk_part if dk is None else dk + dk_part
+            dq = dq_part if dq is None else dq + dq_part
+        dq = dq.T
+        d_q[s, :, at] = dq.astype(BF)
+        d_k[s, :, at] = dk.astype(BF)
+        d_v[s, :, at] = dv.astype(BF)
+        sums[s, :, at] = jnp.sum(dq, axis=0, keepdims=True)
+        return carry
+
+    lax.fori_loop(0, HEADS // 2, pair, 0)
+
+
+def attend_back(s, queries, kvp, grads, before=()):
+    seqs, half, width = queries.shape
+    rows = kvp.shape[1]
+    head = width // HEADS
+    return call(
+        functools.partial(attend_back_kernel, head, s),
+        "attend_back",
+        [
+            sds(queries.shape, BF),
+            sds((seqs, rows, width), BF),
+            sds((seqs, rows, width), BF),
+            sds((seqs, 1, width), F32),
+        ],
+        (queries, kvp, grads, *before),
+        flops=2 * HEADS * half * rows * 2 * head * 5,
+        alias=[(3 + i, i) for i in range(len(before))],
+    )
+
+
+def spread_kernel(d_k, d_v, kv, projt, q_sums, one_sums, up_sums, two_sums, d_kv, small, vector):
+    width = d_k.shape[2]
+    grad, k_sums = None, [None, None]
+    for s in range(d_k.shape[0]):
+        for j, ref in enumerate((d_k, d_v)):
+            cols = slice(j * width, (j + 1) * width)
+            part = nn(projt[...], ref[s])
+            d_kv[s, :, cols] = part.astype(BF)
+            new = jnp.sum(part, axis=0, keepdims=True)
+            k_sums[j] = new if s == 0 else k_sums[j] + new
+            more = nt(ref[s], kv[s, :, cols])
+            grad = more if grad is None else grad + more
+    rows, across = grad.shape
+    small[:rows, :] = grad
+    at = 0
+    for value in (
+        jnp.sum(q_sums[...], axis=0),
+        *k_sums,
+        one_sums[2:3, :],
+        up_sums[...],
+        two_sums[2:3, :],
+        one_sums[0:1, :],
+        one_sums[1:2, :],
+        two_sums[0:1, :],
+        two_sums[1:2, :],
+    ):
+        size = value.shape[1]
+        vector[:, at : at + size] = value
+        at += size
+    vector[:, at:] = jnp.zeros((1, vector.shape[1] - at), F32)
+    small[rows:, :] = jnp.zeros((small.shape[0] - rows, across), F32)
+    for r in range(vector.shape[1] // across):
+        small[rows + r : rows + r + 1, :] = vector[:, r * across : (r + 1) * across]
+
+
+def spread(d_k, d_v, kv, projt, q_sums, one_sums, up_sums, two_sums, entries):
+    seqs, rows, width = d_k.shape
+    length = kv.shape[1]
+    extra = -(-entries // length)
+    return call(
+        spread_kernel,
+        "spread_kv",
+        [sds((seqs, length, 2 * width), BF), sds((rows + -(-extra // 8) * 8, length), F32)],
+        (d_k, d_v, kv, projt, q_sums, one_sums, up_sums, two_sums),
+        scratch=[pltpu.VMEM((1, extra * length), F32)],
+        flops=2 * seqs * rows * length * 2 * width * 2,
+    )
+
+
+def input_back_kernel(d_kv, d_q, d_first, weight, back, result):
+    seqs, half, width = d_q.shape
+    for s in range(seqs):
+        front = d_first[s] + nt(d_q[s], weight[:, :width])
+        high = front.astype(BF)
+        low = (front - high.astype(F32)).astype(BF)
+        place = back[s, :, :half]
+        total = nt(d_kv[s], weight[:, width:]) + nn(place, high) + nn(place, low)
+        result[s] = total.astype(BF)
+
+
+def input_back(d_kv, d_q, d_first, weight, back):
+    seqs, length, wide = d_kv.shape
+    half, width = d_q.shape[1:]
+    return call(
+        input_back_kernel,
+        "input_back",
+        sds((seqs, length, width), BF),
+        (d_kv, d_q, d_first, weight, back),
+        flops=2 * seqs * length * width * (wide + width // 2 + length),
+    )
+
+
+def restore_kernel(front, rest, back, result):
+    seqs, half, _ = front.shape
+    for s in range(seqs):
+        total = nn(back[s, :, :half], front[s]) + nn(back[s, :, half:], rest[s])
+        result[s] = total.astype(BF)
+
+
+def restore(front, rest, back):
+    seqs, half, width = front.shape
+    length = back.shape[1]
+    return call(
+        restore_kernel,
+        "restore_order",
+        sds((seqs, length, width), BF),
+        (front, rest, back),
+        flops=2 * seqs * length * length * width,
+    )
+
+
+def route(rel, slot, send_x, stay_x, send_y, stay_y):
+    if slot < 2:
+        return (send_x if rel & 1 else stay_x), rel >> 1, slot
+    return (send_y if rel & 2 else stay_y), rel & 1, slot - 2
+
+
+def grad_up_kernel(place, lowt, lowt_other, d_hidden, d_hidden_other, *refs):
+    outs, work = refs[:4], refs[4]
+    slots, rows, piece = work.shape
+    for rel in range(4):
+        cols = lanes((rel ^ place[0]) * piece, piece)
+        part = nn(lowt[...], d_hidden[:, cols]) + nn(lowt_other[...], d_hidden_other[:, cols])
+        work[...] = part.astype(BF).reshape(work.shape)
+        for slot in range(slots):
+            ref, i, j = route(rel, slot, *outs)
+            ref[i, j] = work[(place[1] + slot) % slots]
+
+
+def grad_up(place, lowt, lowt_other, d_hidden, d_hidden_other, fsdp, slots):
+    width, count = lowt.shape
+    rows = width // slots
+    piece = d_hidden.shape[1] // fsdp
+    return call(
+        grad_up_kernel,
+        "grad_up",
+        [sds((2, 2, rows, piece), BF)] * 4,
+        (lowt, lowt_other, d_hidden, d_hidden_other),
+        scratch=[pltpu.VMEM((slots, rows, piece), BF)],
+        place=place,
+        flops=2 * width * 2 * count * piece * fsdp,
+    )
+
+
+def grad_down_kernel(place, d_lowt, d_lowt_other, active, active_other, *refs):
+    outs, work = refs[:4], refs[4]
+    _, _, rows, wide = outs[0].shape
+    piece = work.shape[1]
+    for slot in range(4):
+        z = (place[1] + slot) % 4
+        work[...] = (
+            nn(d_lowt[...], active[:, lanes((2 * z + place[2]) * piece, piece)])
+            + nn(d_lowt_other[...], active_other[:, lanes(z * piece, piece)])
+        ).astype(BF)
+        for rel in range(4):
+            ref, i, j = route(rel, slot, *outs)
+            for h in range(wide // piece):
+                top = (rel ^ place[0]) * rows * (wide // piece) + h * rows
+                ref[i, j, :, h * piece : (h + 1) * piece] = work[lines(top, rows), :]
+
+
+def grad_down(place, d_lowt, d_lowt_other, active, active_other, rows, slots):
+    width, count = d_lowt.shape
+    hidden = active.shape[1]
+    piece = hidden // (2 * slots)
+    return call(
+        grad_down_kernel,
+        "grad_down",
+        [sds((2, 2, rows, width), BF)] * 4,
+        (d_lowt, d_lowt_other, active, active_other),
+        scratch=[pltpu.VMEM((width, piece), BF)],
+        place=place,
+        flops=2 * hidden * 2 * count * width,
+    )
+
+
+def grad_rest_kernel(place, *refs):
+    pairs, sums, refs = refs[:12], refs[12:14], refs[14:]
+    outs, (work_qkv, work_out, vector, smalls, small, d_proj) = refs[:4], refs[4:]
+    slots, rows, _ = work_qkv.shape
+    _, _, tall, wide = outs[0].shape
+    fsdp = smalls.shape[0]
+    xt, xt_o, frontt, frontt_o, attendedt, attendedt_o = pairs[:6]
+    d_q, d_q_o, d_kv, d_kv_o, d_low, d_low_o = pairs[6:]
+    width = d_q.shape[1]
+
+    def both(a, a_o, b, b_o):
+        total = nn(a[...], b) + nn(a_o[...], b_o)
+        return total.astype(BF).reshape(slots, rows, total.shape[1])
+
+    work_qkv[:, :, :width] = both(frontt, frontt_o, d_q[...], d_q_o[...])
+    for j in range(2):
+        cols = slice(j * width, (j + 1) * width)
+        work_qkv[:, :, (j + 1) * width : (j + 2) * width] = both(
+            xt, xt_o, d_kv[:, cols], d_kv_o[:, cols]
+        )
+    work_out[...] = both(attendedt, attendedt_o, d_low[...], d_low_o[...])
+    d_proj[...] = sums[0][...] + sums[1][...]
+    across = d_proj.shape[1]
+    height = sums[0].shape[0] - (-(-vector.shape[1] // (8 * across))) * 8
+    for at in range(0, vector.shape[1], across):
+        size = min(across, vector.shape[1] - at)
+        line = height + at // across
+        vector[:, at : at + size] = d_proj[line : line + 1, :size]
+    entries = vector.shape[1] // (2 * fsdp * slots)
+    height = height // fsdp
+    across = across // (2 * slots)
+    start = (height // 8) * across
+    room = wide - start
+    first = place[2] == 0
+    small[...] = jnp.zeros_like(small)
+    for f in range(fsdp):
+        for z in range(slots):
+            for g in range(height // 8):
+                at = (
+                    slice(f * height + 8 * g, f * height + 8 * g + 8),
+                    slice(2 * z * across, 2 * (z + 1) * across),
+                )
+                part = d_proj[at]
+                small[0:8, g * across : (g + 1) * across] = jnp.where(
+                    first, part[:, :across], part[:, across:]
+                )
+            base = (f * 2 * slots + 2 * z) * entries
+            own = jnp.where(
+                first,
+                vector[:, base : base + entries],
+                vector[:, base + entries : base + 2 * entries],
+            )
+            small[0:1, start:] = own[:, :room]
+            small[1:2, start : start + entries - room] = own[:, room:]
+            smalls[f, z] = small[...].astype(BF)
+    below = lanes_below(64)
+    for rel in range(fsdp):
+        f = rel ^ place[0]
+        even = (f & 1) == 0
+        for slot in range(slots):
+            z = (place[1] + slot) % slots
+            ref, i, j = route(rel, slot, *outs)
+            put = ref.at[i, j]
+            q_first = 9 * (f // 2) + 5 * (f & 1)
+            o_pair = 3 * (f // 2)
+            put[:rows, :512] = work_qkv[z, :, lanes(q_first * 128, 512)]
+            shared = work_qkv[z, :, lanes((9 * (f // 2) + 4) * 128, 128)]
+            out_shared = work_out[z, :, lanes((o_pair + 1) * 128, 128)]
+            put[:rows, 512:640] = jnp.where(below == even, shared, swap_halves(out_shared))
+            put[:rows, 640:] = work_out[z, :, lanes((o_pair + 2 * (f & 1)) * 128, 128)]
+            put[rows:, :] = smalls[f, z]
+
+
+def grad_rest(place, pairs, small, small_other, entries, fsdp, slots):
+    width, tokens = 2 * pairs[0].shape[0], pairs[0].shape[1]
+    count = pairs[2].shape[1]
+    rows = width // (2 * slots)
+    wide = 4 * width // fsdp
+    return call(
+        grad_rest_kernel,
+        "grad_rest",
+        [sds((2, 2, rows + 16, wide), BF)] * 4,
+        (*pairs, small, small_other),
+        scratch=[
+            pltpu.VMEM((slots, rows, 3 * width), BF),
+            pltpu.VMEM((slots, rows, width), BF),
+            pltpu.VMEM((1, entries), F32),
+            pltpu.VMEM((fsdp, slots, 16, wide), BF),
+            pltpu.VMEM((16, wide), F32),
+            pltpu.VMEM(small.shape, F32),
+        ],
+        place=place,
+        flops=width * width * (4 * count + 4 * tokens),
+    )
+
+
+def swap_core(value, name="core"):
+    n = lax.axis_size("dp")
+    with jax.named_scope(name):
+        return lax.ppermute(value, "dp", [(i, i ^ 1) for i in range(n)])
+
+
+def shift_slot(value, by, name="slot"):
+    n = lax.axis_size("dp")
+    with jax.named_scope(f"{name}_z{by}"):
+        return lax.ppermute(value, "dp", [(i, (i + 2 * by) % n) for i in range(n)])
+
+
+def swap_fsdp(value, bits, name="fsdp"):
+    n = lax.axis_size("fsdp")
+    with jax.named_scope(f"{name}_{' xyd'[bits]}"):
+        return lax.ppermute(value, "fsdp", [(i, i ^ bits) for i in range(n)])
+
+
+def tie(*values):
+    return lax.optimization_barrier(values)
+
+
+def segments_of(array, tall, blocks, cut, diagonal, low_at, high_at):
+    found = []
+    for first, back, rows in blocks:
+        found += [(array, n * tall + first, n, back, 0, rows) for n in range(3)]
+        low = min(max(cut - first, 0), rows)
+        if low:
+            found.append((diagonal, low_at + first, 3, back, 0, low))
+        if low < rows:
+            found.append((diagonal, high_at + first + low - cut, 3, back, low, rows - low))
+    return found
+
+
+def block_parts(segments, place, refs, slots):
+    arrays = len(refs) // 2
+    for other in (0, 1):
+        for n, top, bits, back, line, rows in segments:
+            z = (place[1] - back + slots) % slots
+            ref = refs[other * arrays + n]
+            yield ref, top, place[0] ^ bits, 2 * z + (place[2] ^ other), line, rows
+
+
+def first_whole_kernel(segments, slots, fsdp, height, across, place, *refs):
+    count = len(refs) - 8
+    blocks = refs[:count]
+    qkv, out, vec, proj, projt, halves, smalls, matrix = refs[count:]
+    rows = qkv.shape[0] // (2 * slots)
+    wide = smalls.shape[3]
+    for ref, top, f, d, line, size in block_parts(segments, place, blocks, slots):
+        body = min(line + size, rows) - line
+        if body > 0:
+            src = slice(top, top + body)
+            dst = lines(d * rows + line, body)
+            qkv[dst, lanes(128 * (9 * (f // 2) + 5 * (f & 1)), 512)] = ref[src, :512]
+            halves[f, dst, :] = ref[src, 512:640]
+            out[dst, lanes(128 * (3 * (f // 2) + 2 * (f & 1)), 128)] = ref[src, 640:]
+        else:
+            body = 0
+        if body < size:
+            smalls[f, d] = ref[top + body : top + size, :]
+    entries = vec.shape[1] // (2 * slots * fsdp)
+    start = (height // 8) * across
+    room = wide - start
+    below = lanes_below(64)
+    for f in range(fsdp):
+        for d in range(2 * slots):
+            small = smalls[f, d].astype(F32)
+            for g in range(height // 8):
+                matrix[
+                    f * height + 8 * g : f * height + 8 * g + 8, d * across : (d + 1) * across
+                ] = small[0:8, g * across : (g + 1) * across]
+            base = (f * 2 * slots + d) * entries
+            vec[:, base : base + room] = small[0:1, start:]
+            vec[:, base + room : base + entries] = small[1:2, start : start + entries - room]
+    for f in range(0, fsdp, 2):
+        one, two = halves[f], halves[f + 1]
+        at = 128 * (9 * (f // 2) + 4)
+        qkv[:, at : at + 128] = jnp.where(below, one, two)
+        at = 128 * (3 * (f // 2) + 1)
+        out[:, at : at + 128] = swap_halves(jnp.where(below, two, one))
+    proj[...] = matrix[...].astype(BF)
+    projt[...] = matrix[...].T.astype(BF)
+
+
+def first_whole(place, blocks, segments, fsdp, slots, width, proj_shape, entries):
+    wide = blocks[0].shape[1]
+    height, across = proj_shape[0] // fsdp, proj_shape[1] // (2 * slots)
+    return call(
+        functools.partial(first_whole_kernel, segments, slots, fsdp, height, across),
+        "whole_first",
+        [
+            sds((width, 3 * width), BF),
+            sds((width, width), BF),
+            sds((1, entries), F32),
+            sds(proj_shape, BF),
+            sds(proj_shape[::-1], BF),
+        ],
+        blocks,
+        scratch=[
+            pltpu.VMEM((fsdp, width, 128), BF),
+            pltpu.VMEM((fsdp, 2 * slots, 16, wide), BF),
+            pltpu.VMEM(proj_shape, F32),
+        ],
+        place=place,
+    )
+
+
+def up_whole_kernel(segments, rows, slots, place, *refs):
+    blocks, result = refs[:-1], refs[-1]
+    for ref, top, f, d, line, size in block_parts(segments, place, blocks, slots):
+        result[f, lines(d * rows + line, size), :] = ref[top : top + size, :]
+
+
+def up_whole(place, blocks, segments, rows, fsdp, slots):
+    wide = blocks[0].shape[1]
+    return call(
+        functools.partial(up_whole_kernel, segments, rows, slots),
+        "whole_up",
+        sds((fsdp, 2 * slots * rows, wide), BF),
+        blocks,
+        place=place,
+    )
+
+
+def down_whole_kernel(segments, rows, slots, place, *refs):
+    blocks, result = refs[:-1], refs[-1]
+    piece = result.shape[1] // (2 * slots)
+    parts = blocks[0].shape[1] // piece
+    for ref, top, f, d, line, size in block_parts(segments, place, blocks, slots):
+        for h in range(parts):
+            dst = lines((f * parts + h) * rows + line, size)
+            result[dst, lanes(d * piece, piece)] = ref[
+                top : top + size, h * piece : (h + 1) * piece
+            ]
+
+
+def down_whole(place, blocks, segments, rows, slots, hidden, width):
+    return call(
+        functools.partial(down_whole_kernel, segments, rows, slots),
+        "whole_down",
+        sds((width, hidden), BF),
+        blocks,
+        place=place,
+    )
+
+
+def stack_kernel(ranges, *refs):
+    at = 0
+    for (first, last), ref in zip(ranges, refs[:-1]):
+        refs[-1][at : at + last - first, :] = ref[first:last, :]
+        at += last - first
+
+
+def stack(*parts):
+    arrays, ranges = [p[0] for p in parts], [p[1:] for p in parts]
+    rows = sum(b - a for a, b in ranges)
+    return call(
+        functools.partial(stack_kernel, ranges),
+        "stack",
+        sds((rows, arrays[0].shape[1]), BF),
+        arrays,
+    )
+
+
+def second_stage_kernel(stay_x, from_x, stay_y, from_y, over_y, over_x, kept):
+    for stay, came, over, at in ((stay_x, from_x, over_y, 0), (stay_y, from_y, over_x, 1)):
+        over[...] = (stay[1].astype(F32) + came[1].astype(F32)).astype(BF)
+        kept[at] = (stay[0].astype(F32) + came[0].astype(F32)).astype(BF)
+
+
+def second_stage(stay_x, from_x, stay_y, from_y):
+    shape = stay_x.shape
+    return call(
+        second_stage_kernel,
+        "second_stage",
+        [sds(shape[1:], BF), sds(shape[1:], BF), sds(shape, BF)],
+        (stay_x, from_x, stay_y, from_y),
+    )
+
+
+def third_stage_kernel(count, *refs):
+    ins, owns, sends = refs[: 3 * count], refs[3 * count : 4 * count], refs[4 * count :]
+    at = 0
+    for n in range(count):
+        kept, over_y, over_x = ins[3 * n : 3 * n + 3]
+        rows = kept.shape[2]
+        put = slice(at, at + rows)
+        at += rows
+        owns[n][...] = kept[0, 0].astype(F32) + over_y[0].astype(F32)
+        sends[0][put, :] = (kept[0, 1].astype(F32) + over_y[1].astype(F32)).astype(BF)
+        sends[1][put, :] = (kept[1, 0].astype(F32) + over_x[0].astype(F32)).astype(BF)
+        sends[2][put, :] = (kept[1, 1].astype(F32) + over_x[1].astype(F32)).astype(BF)
+
+
+def third_stage(*pieces):
+    shapes = [p[0].shape[2:] for p in pieces]
+    rows = sum(a for a, _ in shapes)
+    count = len(pieces)
+    got = call(
+        functools.partial(third_stage_kernel, count),
+        "third_stage",
+        [sds(a, F32) for a in shapes] + [sds((rows, shapes[0][1]), BF)] * 3,
+        [a for p in pieces for a in p],
+    )
+    return got[:count], got[count:]
+
+
+def last_stage_kernel(count, *refs):
+    owns, (one, two, three) = refs[:count], refs[count : count + 3]
+    results, squares = refs[count + 3 : -1], refs[-1]
+    at = 0
+    sums = None
+    for own, result in zip(owns, results):
+        put = slice(at, at + own.shape[0])
+        at += own.shape[0]
+        total = (own[...] + two[put, :].astype(F32)) + (
+            one[put, :].astype(F32) + three[put, :].astype(F32)
+        )
+        result[...] = total
+        part = jnp.sum(total * total, axis=0, keepdims=True)
+        sums = part if sums is None else sums + part
+    squares[...] = jnp.broadcast_to(jnp.sum(sums), squares.shape)
+
+
+def last_stage(owns, came):
+    return call(
+        functools.partial(last_stage_kernel, len(owns)),
+        "last_stage",
+        [sds(a.shape, F32) for a in owns] + [sds((8, 128), F32)],
+        (*owns, *came),
+    )
+
+
+def sum_everywhere(value):
+    a, b, c = (swap_fsdp(value, k, "norm") for k in (1, 2, 3))
+    value = (value + a) + (b + c)
+    a, b, c = (shift_slot(value, k, "norm") for k in (1, 2, 3))
+    value = (value + b) + (a + c)
+    return value + swap_core(value)
+
+
+def adam(weight, moment, second, grad, scale_clip, rate, decay):
+    clipped = grad * scale_clip
+    new_moment = BETA_ONE * moment + (1.0 - BETA_ONE) * clipped
+    new_second = BETA_TWO * second + (1.0 - BETA_TWO) * clipped * clipped
+    moment_hat = new_moment / (1.0 - BETA_ONE**STEP)
+    second_hat = new_second / (1.0 - BETA_TWO**STEP)
+    new_weight = weight - rate * (moment_hat / (jnp.sqrt(second_hat) + ADAM_EPS) + decay * weight)
+    return new_weight, new_moment, new_second, new_weight.astype(BF)
+
+
+def update_kernel(rates, place, squares, g_first, g_up, g_down, *refs):
+    ins, outs = refs[:18], refs[18:-3]
+    norm_ref, outs = outs[0], outs[1:]
+    vector, wide_work, thin_work = refs[-3:]
+    odd = (place[0] & 1) == 1
+    norm = jnp.sqrt(squares[0:1, 0:1])
+    norm_ref[...] = norm
+    clip = jnp.minimum(1.0, CLIP_NORM / norm)
+
+    def put(n, place, grad):
+        new = adam(*(ins[3 * n + i][place] for i in range(3)), grad, clip, *rates[n])
+        for i in range(4):
+            outs[4 * n + i][place] = new[i]
+
+    rows, wide = g_up.shape
+    piece = ins[0].shape[1]
+    every = (slice(None), slice(None))
+    wide_work[:, :64] = g_first[:rows, 576:640]
+    wide_work[:, 64:] = g_first[:rows, :512]
+    put(0, every, jnp.where(odd, wide_work[...], g_first[:rows, :piece]))
+
+    def thin(full, first, second):
+        thin_work[0, :, :128] = full
+        thin_work[0, :, 128:] = second
+        thin_work[1, :, :64] = first
+        thin_work[1, :, 64:] = full
+        return jnp.where(odd, thin_work[1], thin_work[0])
+
+    put(1, every, thin(g_first[:rows, 640:], g_first[:rows, 512:576], g_first[:rows, 576:640]))
+    put(2, every, g_up[...])
+    across = ins[9].shape[1]
+    for h in range(wide // across):
+        put(
+            3,
+            (slice(h * rows, (h + 1) * rows), slice(None)),
+            g_down[:, h * across : (h + 1) * across],
+        )
+    height, across = ins[12].shape
+    for g in range(height // 8):
+        put(
+            4,
+            (slice(8 * g, 8 * g + 8), slice(None)),
+            g_first[rows : rows + 8, g * across : (g + 1) * across],
+        )
+    start = (height // 8) * across
+    room = wide - start
+    entries = ins[15].shape[0]
+    vector[:, :room] = g_first[rows : rows + 1, start:]
+    vector[:, room:] = g_first[rows + 1 : rows + 2, start : start + entries - room]
+    state = (ins[15 + i][...].reshape(1, entries) for i in range(3))
+    new = adam(*state, vector[...], clip, *rates[5])
+    for i in range(4):
+        outs[20 + i][...] = new[i].reshape(entries)
+
+
+def update(place, squares, g_first, g_up, g_down, states, rates):
+    outs = [sds((1, 1), F32)]
+    for n in range(6):
+        shape = states[3 * n].shape
+        outs += [sds(shape, F32)] * 3 + [sds(shape, BF)]
+    return call(
+        functools.partial(update_kernel, rates),
+        "update",
+        outs,
+        (squares, g_first, g_up, g_down, *states),
+        scratch=[
+            pltpu.VMEM((1, *states[15].shape), F32),
+            pltpu.VMEM(states[0].shape, F32),
+            pltpu.VMEM((2, *states[3].shape), F32),
+        ],
+        place=place,
+    )
+
+
+def on_device(
+    tokens,
+    cotangent,
+    positions,
+    counts,
+    qkv_weight,
+    qkv_moment,
+    qkv_second,
+    out_weight,
+    out_moment,
+    out_second,
+    up_weight,
+    up_moment,
+    up_second,
+    down_projection_weight,
+    down_moment,
+    down_second,
+    proj_weight,
+    proj_moment,
+    proj_second,
+    vec_weight,
+    vec_moment,
+    vec_second,
+):
+    fsdp, slots = lax.axis_size("fsdp"), lax.axis_size("dp") // 2
+    place = jnp.stack(
+        [lax.axis_index("fsdp"), lax.axis_index("dp") // 2, lax.axis_index("dp") % 2]
+    ).astype(jnp.int32)
+    seqs = counts.shape[0]
+    rows, width = tokens.shape
+    length = rows // seqs
+    half = length // 2
+    marked = positions.shape[1]
+    hidden = down_projection_weight.shape[0] * slots * 2
+    proj_shape = (proj_weight.shape[0] * fsdp, proj_weight.shape[1] * 2 * slots)
+    entries = vec_weight.shape[0] * fsdp * 2 * slots
+    rates = (
+        (RATE_QKV, DECAY_RATE),
+        (RATE_OUT, DECAY_RATE),
+        (RATE_UP, DECAY_RATE),
+        (RATE_DOWN, DECAY_RATE),
+        (RATE_PROJ, DECAY_RATE),
+        (RATE_VEC, 0.0),
+    )
+
+    own, own_first, own_rest = pack(
+        place,
+        qkv_weight,
+        out_weight,
+        up_weight,
+        down_projection_weight.T,
+        proj_weight,
+        vec_weight,
+    )
+    rows_first, rows_up = own_first.shape[0], own_rest.shape[0] // 2
+
+    def across(value, name):
+        return swap_fsdp(value, 1, name), swap_fsdp(value, 2, name)
+
+    def cores(arrays, name):
+        return [swap_core(a, name) for a in arrays]
+
+    back_first = [shift_slot(own_first, k, "first") for k in (1, 2, 3)]
+    own_x, own_y = across(own, "own")
+    x = tokens.reshape(seqs, length, width)
+    front, rest, frontt, frontt_give, xt, xt_give, back = order_rows(place, x, positions, slots)
+    live = jnp.arange(marked, dtype=jnp.int32)[None, :] < counts[:, None]
+    dy = jnp.pad(
+        jnp.where(live[:, :, None], cotangent, jnp.zeros_like(cotangent)),
+        ((0, 0), (0, half - marked), (0, 0)),
+    ).reshape(seqs * half, width)
+    back_first, own_x, own_y, own_rest, own, frontt_give, xt_give, dy, front = tie(
+        back_first, own_x, own_y, own_rest, own, frontt_give, xt_give, dy, front
+    )
+
+    def all_of(*arrays):
+        return stack(*((a, 0, a.shape[0]) for a in arrays))
+
+    far_first = all_of(*back_first)
+    first_x, first_y = across(far_first, "first")
+    back_rest = [None, shift_slot(own_rest, 1, "rest"), None, shift_slot(own_rest, 3, "rest")]
+    near = all_of(own, own_x, own_y)
+    near_other = swap_core(near, "near_core")
+    own_x, own_y, own, far_first, first_x, first_y, own_rest, near, near_other, back_rest = tie(
+        own_x, own_y, own, far_first, first_x, first_y, own_rest, near, near_other, back_rest
+    )
+
+    tall, far = own.shape[0], far_first.shape[0]
+    half_own = tall // 32 * 16
+    half_first = (tall + far) // 32 * 16 - half_own
+    low = stack((own_x, 0, half_own), (first_x, 0, half_first))
+    high = stack((own_y, half_own, tall), (first_y, half_first, far))
+    diagonal = [swap_fsdp(low, 2, "diag"), swap_fsdp(high, 1, "diag")]
+    back_rest[2] = shift_slot(own_rest, 2, "rest")
+    first = all_of(far_first, first_x, first_y)
+    first_other = swap_core(first, "first_core")
+    diagonal, first_other, back_rest = tie(diagonal, first_other, back_rest)
+    diagonal = all_of(*diagonal)
+    diagonal_other = swap_core(diagonal, "diag_core")
+    diagonal, diagonal_other = tie(diagonal, diagonal_other)
+    high_at = half_own + half_first
+
+    def near_segments(first, rows):
+        return segments_of(0, tall, [(first, 0, rows)], half_own, 1, 0, high_at)
+
+    far_up = stack(*((a, 0, rows_up) for a in back_rest[1:]))
+    far_down = stack(*((a, rows_up, 2 * rows_up) for a in back_rest[1:]))
+    up_x, up_y = across(far_up, "up")
+    blocks = [(k * rows_first, k + 1, rows_first) for k in range(3)]
+    qkv_full, out_full, vec, proj, projt = first_whole(
+        place,
+        [near, diagonal, first, near_other, diagonal_other, first_other],
+        near_segments(0, rows_first)
+        + segments_of(2, far, blocks, half_first, 1, half_own, high_at + tall - half_own),
+        fsdp,
+        slots,
+        width,
+        proj_shape,
+        entries,
+    )
+    q_front, q_rest, kv, kvp = make_qkv(front, rest, x, qkv_full, vec, proj)
+    up_x, up_y, q_front, far_down = tie(up_x, up_y, q_front, far_down)
+
+    far = far_up.shape[0]
+    half_up = far // 32 * 16
+    blocks = [(k * rows_up, k + 1, rows_up) for k in range(3)]
+
+    def far_diagonal(from_x, from_y, name):
+        return [swap_fsdp(from_x[:half_up], 2, name), swap_fsdp(from_y[half_up:], 1, name)]
+
+    def rest_segments(first):
+        return near_segments(first, rows_up) + segments_of(2, far, blocks, half_up, 3, 0, half_up)
+
+    up_diagonal = far_diagonal(up_x, up_y, "updiag")
+    down_x, down_y = across(far_down, "down")
+    up = all_of(far_up, up_x, up_y)
+    up_other = swap_core(up, "up_core")
+    a_front, a_rest = attend(q_front, q_rest, kvp)
+
+    m1 = 3 * width
+    m2 = m1 + width
+    m3 = m2 + hidden
+    m4 = m3 + width
+    ends = [m4 + i * width for i in range(5)]
+    marks_one = ((m1, m2), (ends[0], ends[1]), (ends[1], ends[2]))
+    marks_two = ((m3, m4), (ends[2], ends[3]), (ends[3], ends[4]))
+
+    def flat(v):
+        return v.reshape(seqs * half, width)
+
+    h_front, low_front, kept, lowt, lowt_give, attendedt, attendedt_give = join(
+        place, flat(a_front), flat(front), out_full, vec, marks_one, True, slots
+    )
+    up_diagonal, up_other, low_front, lowt_give, attendedt_give, a_rest = tie(
+        up_diagonal, up_other, low_front, lowt_give, attendedt_give, a_rest
+    )
+    up_diagonal = all_of(*up_diagonal)
+    up_diagonal_other = swap_core(up_diagonal, "updiag_core")
+    h_rest, low_rest = join(
+        place, flat(a_rest), flat(rest), out_full, vec, marks_one, False, slots
+    )
+    up_diagonal_other, low_rest, down_x, down_y = tie(
+        up_diagonal_other, low_rest, down_x, down_y
+    )
+    down_diagonal = far_diagonal(down_x, down_y, "downdiag")
+    down = all_of(far_down, down_x, down_y)
+    down_other = swap_core(down, "down_core")
+    lowt_came, attendedt_came = cores((lowt_give, attendedt_give), "given_core")
+    up_full = up_whole(
+        place,
+        [near, diagonal, up, up_diagonal]
+        + [near_other, diagonal_other, up_other, up_diagonal_other],
+        rest_segments(rows_first),
+        rows_up,
+        fsdp,
+        slots,
+    )
+    act_front, slope, act_give = lift(place, low_front, up_full, vec, m2, True)
+    down_diagonal, down_other, act_front, act_give, lowt_came, attendedt_came = tie(
+        down_diagonal, down_other, act_front, act_give, lowt_came, attendedt_came
+    )
+    down_diagonal = all_of(*down_diagonal)
+    down_diagonal_other = swap_core(down_diagonal, "downdiag_core")
+    act_came = swap_core(act_give, "given_core")
+    down_full = down_whole(
+        place,
+        [near, diagonal, down, down_diagonal]
+        + [near_other, diagonal_other, down_other, down_diagonal_other],
+        rest_segments(rows_first + rows_up),
+        rows_up,
+        slots,
+        hidden,
+        width,
+    )
+    out_front, d_sum, d_low, d_lowt, two_sums = lower(
+        act_front, h_front, down_full, vec, marks_two, dy
+    )
+
+    def send(parts, name):
+        send_x, stay_x, send_y, stay_y = parts
+        return swap_fsdp(send_x, 1, name), swap_fsdp(send_y, 2, name), stay_x, stay_y
+
+    def forward(from_x, from_y, stay_x, stay_y, name):
+        over_y, over_x, kept = second_stage(stay_x, from_x, stay_y, from_y)
+        return kept, swap_fsdp(over_y, 2, name), swap_fsdp(over_x, 1, name)
+
+    def along_z(pieces, name):
+        owns, parts = third_stage(*pieces)
+        return owns, [shift_slot(a, k + 1, name) for k, a in enumerate(parts)]
+
+    d_lowt_came = swap_core(d_lowt, "d_low_core")
+    d_hidden, up_sums = hidden_back(d_low, down_full, slope)
+    d_lowt_came, d_hidden, act_came, frontt_give, xt_give = tie(
+        d_lowt_came, d_hidden, act_came, frontt_give, xt_give
+    )
+    d_hidden_came = swap_core(d_hidden, "d_hidden_core")
+    parts_down = grad_down(place, d_lowt, d_lowt_came, act_front, act_came, rows_up, slots)
+    parts_down, d_hidden_came, d_hidden = tie(parts_down, d_hidden_came, d_hidden)
+    sent_down = send(parts_down, "gdown")
+    parts_up = grad_up(place, lowt, lowt_came, d_hidden, d_hidden_came, fsdp, slots)
+    frontt_came, xt_came = cores((frontt_give, xt_give), "given_core")
+    parts_up, d_hidden, frontt_came, xt_came = tie(parts_up, d_hidden, frontt_came, xt_came)
+    d_first, d_first_low, d_attended, one_sums = first_back(
+        d_hidden, up_full, d_sum, kept, vec, out_full, (ends[0], ends[1])
+    )
+    d_attended = d_attended.reshape(seqs, half, width)
+    got = attend_back(0, q_front, kvp, d_attended)
+    got, d_first_low, sent_down, parts_up = tie(got, d_first_low, sent_down, parts_up)
+    over_down = forward(*sent_down, "gdown2")
+    d_first_low_came = swap_core(d_first_low, "d_low_core")
+    for s in range(1, seqs):
+        got = attend_back(s, q_front, kvp, d_attended, got)
+    d_q, d_k, d_v, q_sums = got
+    d_kv, small = spread(d_k, d_v, kv, projt, q_sums, one_sums, up_sums, two_sums, entries)
+    d_kv, small, over_down, d_first_low_came, d_q, parts_up = tie(
+        d_kv, small, over_down, d_first_low_came, d_q, parts_up
+    )
+    sent_up = send(parts_up, "gup")
+    d_kv_came, small_came, d_q_came = cores((d_kv, small, d_q), "d_kv_core")
+    d_kv_came, small_came, d_q_came, over_down = tie(d_kv_came, small_came, d_q_came, over_down)
+    last_down = along_z((over_down,), "gdown3")
+    tall = 2 * width
+    parts_first = grad_rest(
+        place,
+        (
+            xt,
+            xt_came,
+            frontt,
+            frontt_came,
+            attendedt,
+            attendedt_came,
+            flat(d_q),
+            flat(d_q_came),
+            d_kv.reshape(rows, tall),
+            d_kv_came.reshape(rows, tall),
+            d_first_low,
+            d_first_low_came,
+        ),
+        small,
+        small_came,
+        entries,
+        fsdp,
+        slots,
+    )
+    parts_first, low_rest, d_q, sent_up = tie(parts_first, low_rest, d_q, sent_up)
+    over_up = forward(*sent_up, "gup2")
+    parts_first, last_down = tie(parts_first, last_down)
+    sent_first = send(parts_first, "gfirst")
+    act_rest = lift(place, low_rest, up_full, vec, m2, False)[0]
+    act_rest, over_up, last_down = tie(act_rest, over_up, last_down)
+    last_up = along_z((over_up,), "gup3")
+    out_rest = lower(act_rest, h_rest, down_full, vec, marks_two)[0]
+    output = restore(
+        out_front.reshape(seqs, half, width), out_rest.reshape(seqs, half, width), back
+    ).reshape(rows, width)
+    g_down, squares_down = last_stage(*last_down)
+    sent_first, output, last_up, d_q = tie(sent_first, output, last_up, d_q)
+    over_first = forward(*sent_first, "gfirst2")
+    grad_input = input_back(
+        d_kv, d_q, d_first.reshape(seqs, half, width), qkv_full, back
+    ).reshape(rows, width)
+    g_up, squares_up = last_stage(*last_up)
+    over_first, grad_input = tie(over_first, grad_input)
+    last_first = along_z((over_first,), "gfirst3")
+    g_first, squares_first = last_stage(*last_first)
+    squares_rest = squares_up + squares_down
+    squares = sum_everywhere(squares_first + squares_rest)
+    states = (
+        qkv_weight,
+        qkv_moment,
+        qkv_second,
+        out_weight,
+        out_moment,
+        out_second,
+        up_weight,
+        up_moment,
+        up_second,
+        down_projection_weight.T,
+        down_moment.T,
+        down_second.T,
+        proj_weight,
+        proj_moment,
+        proj_second,
+        vec_weight,
+        vec_moment,
+        vec_second,
+    )
+    new = update(place, squares, g_first, g_up, g_down, states, rates)
+    norm, new = new[0].reshape(()), list(new[1:])
+    new[12:16] = [v.T for v in new[12:16]]
+    return (output, grad_input, norm, *new)
 
 
 def split_up(value, dim, peers):
@@ -104,7 +1515,7 @@
     )
 
 
-def on_device(
+def on_any_mesh(
     tokens,
     cotangent,
     positions,
@@ -366,62 +1777,14 @@
 
 
 def solution(mesh):
-    placed = (
-        P(("fsdp", "dp"), None),
-        P(("fsdp", "dp"), None, None),
-        P(("fsdp", "dp"), None),
-        P(("fsdp", "dp")),
-        P("dp", "fsdp"),
-        P("dp", "fsdp"),
-        P("dp", "fsdp"),
-        P("dp", "fsdp"),
-        P("dp", "fsdp"),
-        P("dp", "fsdp"),
-        P("dp", "fsdp"),
-        P("dp", "fsdp"),
-        P("dp", "fsdp"),
-        P("dp", "fsdp"),
-        P("dp", "fsdp"),
-        P("dp", "fsdp"),
-        P("fsdp", "dp"),
-        P("fsdp", "dp"),
-        P("fsdp", "dp"),
-        P(("fsdp", "dp")),
-        P(("fsdp", "dp")),
-        P(("fsdp", "dp")),
-    )
+    matrix = P("dp", "fsdp")
+    tall = P("fsdp", "dp")
+    every = P(("fsdp", "dp"))
+    small = mesh.shape["fsdp"] == 4 and mesh.shape["dp"] == 8
     return jax.shard_map(
-        on_device,
+        on_device if small else on_any_mesh,
         mesh=mesh,
-        in_specs=placed,
-        out_specs=(
-            P(("fsdp", "dp"), None),
-            P(("fsdp", "dp"), None),
-            P(),
-            P("dp", "fsdp"),
-            P("dp", "fsdp"),
-            P("dp", "fsdp"),
-            P("dp", "fsdp"),
-            P("dp", "fsdp"),
-            P("dp", "fsdp"),
-            P("dp", "fsdp"),
-            P("dp", "fsdp"),
-            P("dp", "fsdp"),
-            P("dp", "fsdp"),
-            P("dp", "fsdp"),
-            P("dp", "fsdp"),
-            P("dp", "fsdp"),
-            P("dp", "fsdp"),
-            P("dp", "fsdp"),
-            P("dp", "fsdp"),
-            P("fsdp", "dp"),
-            P("fsdp", "dp"),
-            P("fsdp", "dp"),
-            P("fsdp", "dp"),
-            P(("fsdp", "dp")),
-            P(("fsdp", "dp")),
-            P(("fsdp", "dp")),
-            P(("fsdp", "dp")),
-        ),
+        in_specs=(every,) * 4 + (matrix,) * 12 + (tall,) * 3 + (every,) * 3,
+        out_specs=(every, every, P()) + (matrix,) * 16 + (tall,) * 4 + (every,) * 4,
         check_vma=False,
     )

time: 715 us -> 267 us (0.37)
  matrix products: 197 us -> 0 us
  blocking collectives: 144 us -> 0 us
  waiting for transfers between devices: 226 us -> 88.1 us
  Pallas kernels: 0 us -> 93.8 us
  local copies, waits for them, and re-layouts: 65.2 us -> 11.6 us
  starting transfers between devices: 17.2 us -> 65.9 us
  other arithmetic: 35.1 us -> 1.46 us
  between operations: 22.9 us -> 2 us
    dot_general x22 -> x0, matrix products: 197 us -> none  [the longest x1 37.6 us: on_device(): jnp.dot(normed_low, up_full, preferred_element_type=jnp.float32) + bias_up]
    reduce_scatter x5 -> x0, waiting for transfers between devices: 108 us -> none  [the longest x1 58.8 us: on_device(): lax.psum_scatter(grad_up.astype(jnp.bfloat16), 'fsdp', scatter_dimension=...]
    pallas_call x0 -> x45, Pallas kernels: none -> 93.8 us  [call(): pl.pallas_call(kernel, name=name, out_shape=outs, in_specs=specs, out_spe...]
    ppermute x0 -> x66, waiting for transfers between devices: none -> 88.1 us  [the longest x18 54.1 us: shift_slot(): return lax.ppermute(value, 'dp', [(i, (i + 2 * by) % n) for i in range(n)])]
    all_gather x6 -> x0, waiting for transfers between devices: 72.7 us -> none  [the longest x1 51.4 us: fetch_whole(): lax.all_gather(rows[2], 'fsdp', axis=1, tiled=True)]
    ppermute x0 -> x66, starting transfers between devices: none -> 65.9 us  [the longest x18 31.9 us: shift_slot(): return lax.ppermute(value, 'dp', [(i, (i + 2 * by) % n) for i in range(n)])]
    all_gather x4 -> x0, blocking collectives: 59.3 us -> none  [the longest x1 22.7 us: fetch_whole(): lax.all_gather(low_qkv, 'dp', axis=0, tiled=True)]
    unnamed x3 -> x0, blocking collectives: 48.1 us -> none
  transfers between devices with their start and end apart: 15 -> 66, of which waited for: 7 -> 26; matrix products, arithmetic and copies ran while one was open for 26% -> 1% of each run, Pallas kernels for 0% -> 33%
where the time goes in v2:
time: 267 us; the launch traced here: 263 us
  Pallas kernels  93.8 us (35%)
  waiting for transfers between devices  88.1 us (33%)
  starting transfers between devices  65.9 us (25%)
  local copies, waits for them, and re-layouts  11.6 us (4%)
    pallas_call x45, Pallas kernels, call(): pl.pallas_call(kernel, name=name, out_shape=outs, in_specs=specs, out_spe...  93.8 us
    ppermute x18, waiting for transfers between devices, shift_slot(): return lax.ppermute(value, 'dp', [(i, (i + 2 * by) % n) for i in range(n)])  54.1 us
    ppermute x18, starting transfers between devices, shift_slot(): return lax.ppermute(value, 'dp', [(i, (i + 2 * by) % n) for i in range(n)])  31.9 us
    ppermute x29, starting transfers between devices, swap_fsdp(): return lax.ppermute(value, 'fsdp', [(i, i ^ bits) for i in range(n)])  30.4 us
    ppermute x29, waiting for transfers between devices, swap_fsdp(): return lax.ppermute(value, 'fsdp', [(i, i ^ bits) for i in range(n)])  22 us
    ppermute x19, waiting for transfers between devices, swap_core(): return lax.ppermute(value, 'dp', [(i, i ^ 1) for i in range(n)])  12.1 us
    unnamed x105, local copies, waits for them, and re-layouts  10.6 us
  transfers between devices with their start and end apart: 66, of which 26 were waited for; matrix products, arithmetic and copies ran while one was open for 1% of the time, Pallas kernels for 33%

profile of v2, /device:TPU:0, one launch (start us, length us, event | category | flops | bytes accessed | tf_op | source)
XLA Modules:
  0.0 262.8 jit_solution(3172973337615302109)
XLA Ops:
  6.0 2.1 pack_weights.1
  8.8 5.0 %collective-permute-start.2 = (bf16[112,768]{1,0:T(8,128)(2,1)}, bf16[112,768]{1,0:T(8,128)(2,1)S(1)}, u32[]{:S(2)}, u32[]{:S(2)}) collective-permute-start(bf16[112,768]{1,0:T(8,128)(2,1)} %get-tuple-element.285), channel_id=1, source_target_pairs={{0,6},{1,7},{2,0},{3,1},{4,2},{5,3},{6,4},{7,5},{8,14},{9,15},{10,... | collective-permute-start | bytes 516104 | tf_op jit(solution)/shard_map/first_z3/ppermute | solution.py:805
  14.9 1.5 collective-permute-start.4
  21.5 2.4 order_rows.1
  23.9 4.7 %collective-permute-done.1.refs_1_ = bf16[112,768]{1,0:T(8,128)(2,1)S(1)} collective-permute-done((bf16[112,768]{1,0:T(8,128)(2,1)}, bf16[112,768]{1,0:T(8,128)(2,1)S(1)}, u32[]{:S(2)}, u32[]{:S(2)}) %collective-permute-start.1) | collective-permute-done | bytes 172064 | tf_op jit(solution)/shard_map/first_z2/ppermute | solution.py:805
  29.0 1.6 collective-permute-start.6
  34.3 6.5 %collective-permute-done.9.refs_2_ = bf16[192,768]{1,0:T(8,128)(2,1)S(1)} collective-permute-done((bf16[192,768]{1,0:T(8,128)(2,1)S(1)}, bf16[192,768]{1,0:T(8,128)(2,1)S(1)}, u32[]{:S(2)}, u32[]{:S(2)}) %collective-permute-start.9) | collective-permute-done | bytes 294944 | tf_op jit(solution)/shard_map/rest_z3/ppermute | solution.py:805
  40.9 8.5 %collective-permute-done.8.refs_0_ = bf16[192,768]{1,0:T(8,128)(2,1)S(1)} collective-permute-done((bf16[192,768]{1,0:T(8,128)(2,1)S(1)}, bf16[192,768]{1,0:T(8,128)(2,1)S(1)}, u32[]{:S(2)}, u32[]{:S(2)}) %collective-permute-start.8) | collective-permute-done | bytes 294944 | tf_op jit(solution)/shard_map/rest_z1/ppermute | solution.py:805
  51.6 14.6 %collective-permute-done.13.refs_1_ = bf16[192,768]{1,0:T(8,128)(2,1)S(1)} collective-permute-done((bf16[192,768]{1,0:T(8,128)(2,1)S(1)}, bf16[192,768]{1,0:T(8,128)(2,1)S(1)}, u32[]{:S(2)}, u32[]{:S(2)}) %collective-permute-start.13) | collective-permute-done | bytes 294944 | tf_op jit(solution)/shard_map/rest_z2/ppermute | solution.py:805
  69.0 2.0 whole_first.1
  71.0 6.7 %make_qkv.1 = (bf16[2,256,768]{2,1,0:T(8,128)(2,1)S(1)}, bf16[2,256,768]{2,1,0:T(8,128)(2,1)S(1)}, bf16[2,512,1536]{2,1,0:T(8,128)(2,1)S(1)}, bf16[2,256,1536]{2,1,0:T(8,128)(2,1)S(1)}) custom-call(bf16[2,256,768]{2,1,0:T(8,128)(2,1)S(1)} %get-tuple-element.309.front, bf16[2,256,768]{2,1,0:T(8,128)(2,1)S(1)} %get-tuple-element.310.rest, ...), custom_call_target="tpu_custom_call" | custom-call | flops 4429185 | bytes 13278 | tf_op jit(solution)/shard_map/make_qkv/pallas_call | solution.py:54
  79.5 1.6 collective-permute-start.18
  83.7 7.4 %attend.1 = (bf16[2,256,768]{2,1,0:T(8,128)(2,1)S(1)}, bf16[2,256,768]{2,1,0:T(8,128)(2,1)S(1)}) custom-call(bf16[2,256,768]{2,1,0:T(8,128)(2,1)S(1)} %get-tuple-element.322.q_front.queries, bf16[2,256,768]{2,1,0:T(8,128)(2,1)S(1)} %get-tuple-element.323.q_rest, bf16[2,256,1536]{2,1,0:T(8,128)(2,1)S(1)} %get-tuple-element.324.kvp), custom_call_target="tpu_custom_call" | custom-call | flops 1610612 | bytes 4718 | tf_op jit(solution)/shard_map/attend/pallas_call | solution.py:54
  91.1 1.9 join_front.1
  93.9 1.7 join_rest.1
  95.6 2.5 collective-permute-done.22.refs_2_
  101.9 7.7 %lift_front.1 = (bf16[512,3072]{1,0:T(8,128)(2,1)S(1)}, bf16[512,3072]{1,0:T(8,128)(2,1)S(1)}, bf16[512,1536]{1,0:T(8,128)(2,1)S(1)}) custom-call(s32[3]{0:T(128)S(1)} %pad_add_fusion.place, bf16[512,768]{1,0:T(8,128)(2,1)S(1)} %get-tuple-element.341.low, bf16[4,768,768]{2,1,0:T(8,128)(2,1)S(1)} %whole_up.1.weight.up, f32[1,9984]{1,0:T(1,128)S(1)} %get-tuple-element.319.vec), custom_call_target="tpu_custom_call" | custom-call | flops 2415919 | bytes 13409 | tf_op jit(solution)/shard_map/lift_front/pallas_call | solution.py:54
  111.9 3.4 %collective-permute-done.28.refs_7_ = bf16[288,768]{1,0:T(8,128)(2,1)S(1)} collective-permute-done((bf16[288,768]{1,0:T(8,128)(2,1)S(1)}, bf16[288,768]{1,0:T(8,128)(2,1)S(1)}, u32[]{:S(2)}, u32[]{:S(2)}) %collective-permute-start.28) | collective-permute-done | bytes 442400 | tf_op jit(solution)/shard_map/downdiag_core/ppermute | solution.py:799
  116.4 4.1 %lower_front.1 = (bf16[512,768]{1,0:T(8,128)(2,1)S(1)}, f32[512,768]{1,0:T(8,128)S(1)}, bf16[512,768]{1,0:T(8,128)(2,1)S(1)}, bf16[768,512]{1,0:T(8,128)(2,1)S(1)}, f32[8,768]{1,0:T(8,128)S(1)}) custom-call(bf16[512,3072]{1,0:T(8,128)(2,1)S(1)} %get-tuple-element.349.active, f32[512,768]{1,0:T(8,128)S(1)} %copy-done.2, ...), custom_call_target="tpu_custom_call" | custom-call | flops 2415919 | bytes 14220 | tf_op jit(solution)/shard_map/lower_front/pallas_call | solution.py:54
  120.7 2.8 %hidden_back.1 = (bf16[512,3072]{1,0:T(8,128)(2,1)S(1)}, f32[1,3072]{1,0:T(1,128)S(1)}) custom-call(bf16[512,768]{1,0:T(8,128)(2,1)S(1)} %get-tuple-element.356.d_low, bf16[768,3072]{1,0:T(8,128)(2,1)S(1)} %whole_down.1.weight, bf16[512,3072]{1,0:T(8,128)(2,1)S(1)} %get-tuple-element.357.slope), custom_call_target="tpu_custom_call" | custom-call | flops 2415919 | bytes 11808 | tf_op jit(solution)/shard_map/hidden_back/pallas_call | solution.py:54
  124.2 4.1 %grad_down.1 = (bf16[2,2,96,768]{3,2,1,0:T(8,128)(2,1)S(1)}, bf16[2,2,96,768]{3,2,1,0:T(8,128)(2,1)S(1)}, bf16[2,2,96,768]{3,2,1,0:T(8,128)(2,1)S(1)}, bf16[2,2,96,768]{3,2,1,0:T(8,128)(2,1)S(1)}) custom-call(s32[3]{0:T(128)S(1)} %pad_add_fusion.place, bf16[768,512]{1,0:T(8,128)(2,1)S(1)} %get-tuple-element.355.d_lowt, ...), custom_call_target="tpu_custom_call" | custom-call | flops 4831838 | bytes 8650 | tf_op jit(solution)/shard_map/grad_down/pallas_call | solution.py:54
  131.3 3.3 %grad_up.1 = (bf16[2,2,96,768]{3,2,1,0:T(8,128)(2,1)S(1)}, bf16[2,2,96,768]{3,2,1,0:T(8,128)(2,1)S(1)}, bf16[2,2,96,768]{3,2,1,0:T(8,128)(2,1)S(1)}, bf16[2,2,96,768]{3,2,1,0:T(8,128)(2,1)S(1)}) custom-call(s32[3]{0:T(128)S(1)} %pad_add_fusion.place, bf16[384,512]{1,0:T(8,128)(2,1)S(1)} %copy-done.22, bf16[384,512]{1,0:T(8,128)(2,1)S(1)} %copy-done.24, ...), custom_call_target="tpu_custom_call" | custom-call | flops 2415919 | bytes 9437 | tf_op jit(solution)/shard_map/grad_up/pallas_call | solution.py:54
  135.6 5.7 %first_back.1 = (f32[512,768]{1,0:T(8,128)S(1)}, bf16[512,768]{1,0:T(8,128)(2,1)S(1)}, bf16[512,768]{1,0:T(8,128)(2,1)S(1)}, f32[8,768]{1,0:T(8,128)S(1)}) custom-call(bf16[512,3072]{1,0:T(8,128)(2,1)S(1)} %get-tuple-element.382.d_hidden, bf16[4,768,768]{2,1,0:T(8,128)(2,1)S(1)} %whole_up.1.weight.up, f32[512,768]{1,0:T(8,128)S(1)} %get-tuple-element.383.d_sum, ...), custom_call_target="tpu_custom_call" | custom-call | flops 3019898 | bytes 15399 | tf_op jit(solution)/shard_map/first_back/pallas_call | solution.py:54
  141.3 5.1 %attend_back.2 = (bf16[2,256,768]{2,1,0:T(8,128)(2,1)S(1)}, bf16[2,256,768]{2,1,0:T(8,128)(2,1)S(1)}, bf16[2,256,768]{2,1,0:T(8,128)(2,1)S(1)}, f32[2,1,768]{2,1,0:T(1,128)S(1)}) custom-call(bf16[2,256,768]{2,1,0:T(8,128)(2,1)S(1)} %get-tuple-element.322.q_front.queries, bf16[2,256,1536]{2,1,0:T(8,128)(2,1)S(1)} %get-tuple-element.324.kvp, ...), custom_call_target="tpu_custom_call" | custom-call | flops 1006632 | bytes 5511 | tf_op jit(solution)/shard_map/attend_back/pallas_call | solution.py:54
  147.3 1.6 collective-permute-start.36
  149.4 5.1 %attend_back.3 = (bf16[2,256,768]{2,1,0:T(8,128)(2,1)S(1)}, bf16[2,256,768]{2,1,0:T(8,128)(2,1)S(1)}, bf16[2,256,768]{2,1,0:T(8,128)(2,1)S(1)}, f32[2,1,768]{2,1,0:T(1,128)S(1)}) custom-call(bf16[2,256,768]{2,1,0:T(8,128)(2,1)S(1)} %get-tuple-element.322.q_front.queries, ...), custom_call_target="tpu_custom_call", output_to_operand_aliasing={{0}: (3, {}), {1}: (4, {}), {2}: (5, {}), {3}: (6, {})} | custom-call | flops 1006632 | bytes 7876 | tf_op jit(solution)/shard_map/attend_back/pallas_call | solution.py:54
  154.6 1.8 spread_kv.1
  159.1 6.0 %collective-permute-done.40.refs_13_ = f32[280,512]{1,0:T(8,128)S(1)} collective-permute-done((f32[280,512]{1,0:T(8,128)S(1)}, f32[280,512]{1,0:T(8,128)S(1)}, u32[]{:S(2)}, u32[]{:S(2)}) %collective-permute-start.40) | collective-permute-done | bytes 573472 | tf_op jit(solution)/shard_map/d_kv_core/ppermute | solution.py:799
  165.3 2.9 %collective-permute-start.45 = (bf16[96,768]{1,0:T(8,128)(2,1)S(1)}, bf16[96,768]{1,0:T(8,128)(2,1)S(1)}, u32[]{:S(2)}, u32[]{:S(2)}) collective-permute-start(bf16[96,768]{1,0:T(8,128)(2,1)S(1)} %get-tuple-element.454), channel_id=1, source_target_pairs={{0,4},{1,5},{2,6},{3,7},{4,0},{5,1},{6,2},{7,3},{8,12},{9,13},{10,... | collective-permute-start | bytes 442376 | tf_op jit(solution)/shard_map/gdown3_z2/ppermute | solution.py:805
  169.2 4.8 %grad_rest.1 = (bf16[2,2,112,768]{3,2,1,0:T(8,128)(2,1)S(1)}, bf16[2,2,112,768]{3,2,1,0:T(8,128)(2,1)S(1)}, bf16[2,2,112,768]{3,2,1,0:T(8,128)(2,1)S(1)}, bf16[2,2,112,768]{3,2,1,0:T(8,128)(2,1)S(1)}) custom-call(s32[3]{0:T(128)S(1)} %pad_add_fusion.place, bf16[384,1024]{1,0:T(8,128)(2,1)S(1)} %copy-done.14, bf16[384,1024]{1,0:T(8,128)(2,1)S(1)} %copy-done.16, ...), custom_call_target="tpu_custom_call" | custom-call | flops 3623878 | bytes 16482 | tf_op jit(solution)/shard_map/grad_rest/pallas_call | solution.py:54
  174.1 5.3 %collective-permute-done.45.refs_2_ = bf16[96,768]{1,0:T(8,128)(2,1)S(1)} collective-permute-done((bf16[96,768]{1,0:T(8,128)(2,1)S(1)}, bf16[96,768]{1,0:T(8,128)(2,1)S(1)}, u32[]{:S(2)}, u32[]{:S(2)}) %collective-permute-start.45) | collective-permute-done | bytes 147488 | tf_op jit(solution)/shard_map/gdown3_z2/ppermute | solution.py:805
  180.7 1.6 collective-permute-start.49
  183.7 6.7 %lift_rest.1.active = bf16[512,3072]{1,0:T(8,128)(2,1)S(1)} custom-call(s32[3]{0:T(128)S(1)} %pad_add_fusion.place, bf16[512,768]{1,0:T(8,128)(2,1)S(1)} %copy-done.10, bf16[4,768,768]{2,1,0:T(8,128)(2,1)S(1)} %whole_up.1.weight.up, f32[1,9984]{1,0:T(1,128)S(1)} %get-tuple-element.319.vec), custom_call_target="tpu_custom_call" | custom-call | flops 2415919 | bytes 8690 | tf_op jit(solution)/shard_map/lift_rest/pallas_call | solution.py:54
  190.5 11.3 %collective-permute-done.49.refs_1_ = bf16[2,96,768]{2,1,0:T(8,128)(2,1)S(1)} collective-permute-done((bf16[2,96,768]{2,1,0:T(8,128)(2,1)S(1)}, bf16[2,96,768]{2,1,0:T(8,128)(2,1)S(1)}, u32[]{:S(2)}, u32[]{:S(2)}) %collective-permute-start.49) | collective-permute-done | bytes 294944 | tf_op jit(solution)/shard_map/gup2_y/ppermute | solution.py:811
  202.0 3.8 %collective-permute-start.51 = (bf16[96,768]{1,0:T(8,128)(2,1)S(1)}, bf16[96,768]{1,0:T(8,128)(2,1)S(1)}, u32[]{:S(2)}, u32[]{:S(2)}) collective-permute-start(bf16[96,768]{1,0:T(8,128)(2,1)S(1)} %get-tuple-element.480), channel_id=1, source_target_pairs={{0,2},{1,3},{2,4},{3,5},{4,6},{5,7},{6,0},{7,1},{8,10},{9,11},{10,... | collective-permute-start | bytes 442376 | tf_op jit(solution)/shard_map/gup3_z1/ppermute | solution.py:805
  206.1 2.3 collective-permute-start.53
  208.3 3.1 %lower_rest.1 = bf16[512,768]{1,0:T(8,128)(2,1)S(1)} custom-call(bf16[512,3072]{1,0:T(8,128)(2,1)S(1)} %lift_rest.1.active, f32[512,768]{1,0:T(8,128)S(1)} %get-tuple-element.474.normed, bf16[768,3072]{1,0:T(8,128)(2,1)S(1)} %whole_down.1.weight, f32[1,9984]{1,0:T(1,128)S(1)} %get-tuple-element.319.vec), custom_call_target="tpu_custom_call" | custom-call | flops 2415919 | bytes 10263 | tf_op jit(solution)/shard_map/lower_rest/pallas_call | solution.py:54
  211.5 2.1 restore_order.1
  217.5 5.4 %input_back.1 = bf16[2,512,768]{2,1,0:T(8,128)(2,1)} custom-call(bf16[2,512,1536]{2,1,0:T(8,128)(2,1)S(1)} %get-tuple-element.427.d_kv, bf16[2,256,768]{2,1,0:T(8,128)(2,1)S(1)} %get-tuple-element.492.d_q, f32[2,256,768]{2,1,0:T(8,128)S(1)} %bitcast.40, bf16[768,2304]{1,0:T(8,128)(2,1)S(1)} %get-tuple-element.318.weight, ...), custom_call_target="tpu_custom_call" | custom-call | flops 3825205 | bytes 11665 | tf_op jit(solution)/shard_map/input_back/pallas_call | solution.py:54
  222.9 2.0 collective-permute-done.54.refs_1_
  225.5 3.8 %collective-permute-start.56 = (bf16[112,768]{1,0:T(8,128)(2,1)S(1)}, bf16[112,768]{1,0:T(8,128)(2,1)S(1)}, u32[]{:S(2)}, u32[]{:S(2)}) collective-permute-start(bf16[112,768]{1,0:T(8,128)(2,1)S(1)} %get-tuple-element.499), channel_id=1, source_target_pairs={{0,2},{1,3},{2,4},{3,5},{4,6},{5,7},{6,0},{7,1},{8,10},{9,11},{10,... | collective-permute-start | bytes 516104 | tf_op jit(solution)/shard_map/gfirst3_z1/ppermute | solution.py:805
  229.3 2.4 collective-permute-start.58
  232.2 2.4 collective-permute-done.56.refs_1_
  234.6 5.6 %collective-permute-done.57.refs_2_ = bf16[112,768]{1,0:T(8,128)(2,1)S(1)} collective-permute-done((bf16[112,768]{1,0:T(8,128)(2,1)S(1)}, bf16[112,768]{1,0:T(8,128)(2,1)S(1)}, u32[]{:S(2)}, u32[]{:S(2)}) %collective-permute-start.57) | collective-permute-done | bytes 172064 | tf_op jit(solution)/shard_map/gfirst3_z2/ppermute | solution.py:805
  240.5 2.4 collective-permute-start.61
  247.1 5.7 %collective-permute-start.64 = (f32[8,128]{1,0:T(8,128)S(1)}, f32[8,128]{1,0:T(8,128)S(1)}, u32[]{:S(2)}, u32[]{:S(2)}) collective-permute-start(f32[8,128]{1,0:T(8,128)S(1)} %add_add_fusion.1), channel_id=1, source_target_pairs={{0,6},{1,7},{2,0},{3,1},{4,2},{5,3},{6,4},{7,5},{8,14},{9,15},{10,... | collective-permute-start | bytes 12296 | tf_op jit(solution)/shard_map/norm_z3/ppermute | solution.py:805
  254.1 4.1 %collective-permute-done.63 = f32[8,128]{1,0:T(8,128)S(1)} collective-permute-done((f32[8,128]{1,0:T(8,128)S(1)}, f32[8,128]{1,0:T(8,128)S(1)}, u32[]{:S(2)}, u32[]{:S(2)}) %collective-permute-start.63) | collective-permute-done | bytes 4128 | tf_op jit(solution)/shard_map/norm_z1/ppermute | solution.py:805
  259.6 3.0 %update.1 = (f32[1,1]{1,0:T(1,128)}, f32[96,576]{1,0:T(8,128)}, f32[96,576]{1,0:T(8,128)}, f32[96,576]{1,0:T(8,128)}, bf16[96,576]{1,0:T(8,128)(2,1)}, /*index=5...) custom-call(s32[3]{0:T(128)S(1)} %pad_add_fusion.place, ...), custom_call_target="tpu_custom_call" | custom-call | bytes 6803 | tf_op jit(solution)/shard_map/update/pallas_call | solution.py:54
  (248 shorter events, 58.4 us)
Async XLA Ops:
  8.8 15.1 %collective-permute-start.2 = (bf16[112,768]{1,0:T(8,128)(2,1)}, bf16[112,768]{1,0:T(8,128)(2,1)S(1)}, u32[]{:S(2)}, u32[]{:S(2)}) collective-permute-start(bf16[112,768]{1,0:T(8,128)(2,1)} %get-tuple-element.285), channel_id=1, source_target_pairs={{0,6},{1,7},{2,0},{3,1},{4,2},{5,3},{6,4},{7,5},{8,14},{9,15},{10,... | collective-permute-start | bytes 516104 | tf_op jit(solution)/shard_map/first_z3/ppermute | solution.py:805
  13.9 14.8 %collective-permute-start.1 = (bf16[112,768]{1,0:T(8,128)(2,1)}, bf16[112,768]{1,0:T(8,128)(2,1)S(1)}, u32[]{:S(2)}, u32[]{:S(2)}) collective-permute-start(bf16[112,768]{1,0:T(8,128)(2,1)} %get-tuple-element.285), channel_id=1, source_target_pairs={{0,4},{1,5},{2,6},{3,7},{4,0},{5,1},{6,2},{7,3},{8,12},{9,13},{10,... | collective-permute-start | bytes 516104 | tf_op jit(solution)/shard_map/first_z2/ppermute | solution.py:805
  13.9 14.8 %collective-permute-start = (bf16[112,768]{1,0:T(8,128)(2,1)}, bf16[112,768]{1,0:T(8,128)(2,1)S(1)}, u32[]{:S(2)}, u32[]{:S(2)}) collective-permute-start(bf16[112,768]{1,0:T(8,128)(2,1)} %get-tuple-element.285), channel_id=1, source_target_pairs={{0,2},{1,3},{2,4},{3,5},{4,6},{5,7},{6,0},{7,1},{8,10},{9,11},{10,... | collective-permute-start | bytes 516104 | tf_op jit(solution)/shard_map/first_z1/ppermute | solution.py:805
  14.9 13.8 %collective-permute-start.4 = (bf16[304,768]{1,0:T(8,128)(2,1)S(1)}, bf16[304,768]{1,0:T(8,128)(2,1)S(1)}, u32[]{:S(2)}, u32[]{:S(2)}) collective-permute-start(bf16[304,768]{1,0:T(8,128)(2,1)S(1)} %get-tuple-element.293.refs_0_), channel_id=1, source_target_pairs={{0,16},{8,24},{16,0},{24,8},{1,17},{9,25},{17,1},{25,9},{2,18},{10... | collective-permute-start | bytes 1400840 | tf_op jit(solution)/shard_map/own_y/ppermute | solution.py:811
  16.4 12.3 %collective-permute-start.3 = (bf16[304,768]{1,0:T(8,128)(2,1)S(1)}, bf16[304,768]{1,0:T(8,128)(2,1)S(1)}, u32[]{:S(2)}, u32[]{:S(2)}) collective-permute-start(bf16[304,768]{1,0:T(8,128)(2,1)S(1)} %get-tuple-element.293.refs_0_), channel_id=1, source_target_pairs={{0,8},{8,0},{16,24},{24,16},{1,9},{9,1},{17,25},{25,17},{2,10},{10... | collective-permute-start | bytes 1400840 | tf_op jit(solution)/shard_map/own_x/ppermute | solution.py:811
  28.8 20.6 %collective-permute-start.7 = (bf16[912,768]{1,0:T(8,128)(2,1)S(1)}, bf16[912,768]{1,0:T(8,128)(2,1)S(1)}, u32[]{:S(2)}, u32[]{:S(2)}) collective-permute-start(bf16[912,768]{1,0:T(8,128)(2,1)S(1)} %stack.29.refs_0_), channel_id=1, source_target_pairs={{0,1},{1,0},{2,3},{3,2},{4,5},{5,4},{6,7},{7,6},{8,9},{9,8},{10,11... | collective-permute-start | bytes 4202504 | tf_op jit(solution)/shard_map/near_core/ppermute | solution.py:799
  29.0 20.5 %collective-permute-start.6 = (bf16[336,768]{1,0:T(8,128)(2,1)S(1)}, bf16[336,768]{1,0:T(8,128)(2,1)S(1)}, u32[]{:S(2)}, u32[]{:S(2)}) collective-permute-start(bf16[336,768]{1,0:T(8,128)(2,1)S(1)} %stack.28.refs_0_), channel_id=1, source_target_pairs={{0,16},{8,24},{16,0},{24,8},{1,17},{9,25},{17,1},{25,9},{2,18},{10... | collective-permute-start | bytes 1548296 | tf_op jit(solution)/shard_map/first_y/ppermute | solution.py:811
  30.5 18.9 %collective-permute-start.5 = (bf16[336,768]{1,0:T(8,128)(2,1)S(1)}, bf16[336,768]{1,0:T(8,128)(2,1)S(1)}, u32[]{:S(2)}, u32[]{:S(2)}) collective-permute-start(bf16[336,768]{1,0:T(8,128)(2,1)S(1)} %stack.28.refs_0_), channel_id=1, source_target_pairs={{0,8},{8,0},{16,24},{24,16},{1,9},{9,1},{17,25},{25,17},{2,10},{10... | collective-permute-start | bytes 1548296 | tf_op jit(solution)/shard_map/first_x/ppermute | solution.py:811
  32.0 8.8 %collective-permute-start.9 = (bf16[192,768]{1,0:T(8,128)(2,1)S(1)}, bf16[192,768]{1,0:T(8,128)(2,1)S(1)}, u32[]{:S(2)}, u32[]{:S(2)}) collective-permute-start(bf16[192,768]{1,0:T(8,128)(2,1)S(1)} %copy-done.50), channel_id=1, source_target_pairs={{0,6},{1,7},{2,0},{3,1},{4,2},{5,3},{6,4},{7,5},{8,14},{9,15},{10,... | collective-permute-start | bytes 884744 | tf_op jit(solution)/shard_map/rest_z3/ppermute | solution.py:805
  33.1 16.3 %collective-permute-start.8 = (bf16[192,768]{1,0:T(8,128)(2,1)S(1)}, bf16[192,768]{1,0:T(8,128)(2,1)S(1)}, u32[]{:S(2)}, u32[]{:S(2)}) collective-permute-start(bf16[192,768]{1,0:T(8,128)(2,1)S(1)} %copy-done.50), channel_id=1, source_target_pairs={{0,2},{1,3},{2,4},{3,5},{4,6},{5,7},{6,0},{7,1},{8,10},{9,11},{10,... | collective-permute-start | bytes 884744 | tf_op jit(solution)/shard_map/rest_z1/ppermute | solution.py:805
  49.5 16.7 %collective-permute-start.12 = (bf16[1008,768]{1,0:T(8,128)(2,1)S(1)}, bf16[1008,768]{1,0:T(8,128)(2,1)S(1)}, u32[]{:S(2)}, u32[]{:S(2)}) collective-permute-start(bf16[1008,768]{1,0:T(8,128)(2,1)S(1)} %stack.32.refs_2_), channel_id=1, source_target_pairs={{0,1},{1,0},{2,3},{3,2},{4,5},{5,4},{6,7},{7,6},{8,9},{9,8},{10,11... | collective-permute-start | bytes 4644872 | tf_op jit(solution)/shard_map/first_core/ppermute | solution.py:799
  49.7 16.5 %collective-permute-start.11 = (bf16[320,768]{1,0:T(8,128)(2,1)S(1)}, bf16[320,768]{1,0:T(8,128)(2,1)S(1)}, u32[]{:S(2)}, u32[]{:S(2)}) collective-permute-start(bf16[320,768]{1,0:T(8,128)(2,1)S(1)} %stack.31), channel_id=1, source_target_pairs={{0,8},{8,0},{16,24},{24,16},{1,9},{9,1},{17,25},{25,17},{2,10},{10... | collective-permute-start | bytes 1474568 | tf_op jit(solution)/shard_map/diag_x/ppermute | solution.py:811
  50.3 15.9 %collective-permute-start.10 = (bf16[320,768]{1,0:T(8,128)(2,1)S(1)}, bf16[320,768]{1,0:T(8,128)(2,1)S(1)}, u32[]{:S(2)}, u32[]{:S(2)}) collective-permute-start(bf16[320,768]{1,0:T(8,128)(2,1)S(1)} %stack.30), channel_id=1, source_target_pairs={{0,16},{8,24},{16,0},{24,8},{1,17},{9,25},{17,1},{25,9},{2,18},{10... | collective-permute-start | bytes 1474568 | tf_op jit(solution)/shard_map/diag_y/ppermute | solution.py:811
  50.8 15.4 %collective-permute-start.13 = (bf16[192,768]{1,0:T(8,128)(2,1)S(1)}, bf16[192,768]{1,0:T(8,128)(2,1)S(1)}, u32[]{:S(2)}, u32[]{:S(2)}) collective-permute-start(bf16[192,768]{1,0:T(8,128)(2,1)S(1)} %copy-done.50), channel_id=1, source_target_pairs={{0,4},{1,5},{2,6},{3,7},{4,0},{5,1},{6,2},{7,3},{8,12},{9,13},{10,... | collective-permute-start | bytes 884744 | tf_op jit(solution)/shard_map/rest_z2/ppermute | solution.py:805
  66.5 12.6 %collective-permute-start.15 = (bf16[288,768]{1,0:T(8,128)(2,1)S(1)}, bf16[288,768]{1,0:T(8,128)(2,1)S(1)}, u32[]{:S(2)}, u32[]{:S(2)}) collective-permute-start(bf16[288,768]{1,0:T(8,128)(2,1)S(1)} %stack.33.refs_0_), channel_id=1, source_target_pairs={{0,16},{8,24},{16,0},{24,8},{1,17},{9,25},{17,1},{25,9},{2,18},{10... | collective-permute-start | bytes 1327112 | tf_op jit(solution)/shard_map/up_y/ppermute | solution.py:811
  67.0 12.3 %collective-permute-start.14 = (bf16[288,768]{1,0:T(8,128)(2,1)S(1)}, bf16[288,768]{1,0:T(8,128)(2,1)S(1)}, u32[]{:S(2)}, u32[]{:S(2)}) collective-permute-start(bf16[288,768]{1,0:T(8,128)(2,1)S(1)} %stack.33.refs_0_), channel_id=1, source_target_pairs={{0,8},{8,0},{16,24},{24,16},{1,9},{9,1},{17,25},{25,17},{2,10},{10... | collective-permute-start | bytes 1327112 | tf_op jit(solution)/shard_map/up_x/ppermute | solution.py:811
  79.4 14.4 %collective-permute-start.19 = (bf16[864,768]{1,0:T(8,128)(2,1)S(1)}, bf16[864,768]{1,0:T(8,128)(2,1)S(1)}, u32[]{:S(2)}, u32[]{:S(2)}) collective-permute-start(bf16[864,768]{1,0:T(8,128)(2,1)S(1)} %stack.36.refs_2_), channel_id=1, source_target_pairs={{0,1},{1,0},{2,3},{3,2},{4,5},{5,4},{6,7},{7,6},{8,9},{9,8},{10,11... | collective-permute-start | bytes 3981320 | tf_op jit(solution)/shard_map/up_core/ppermute | solution.py:799
  79.5 14.2 %collective-permute-start.18 = (bf16[144,768]{1,0:T(8,128)(2,1)S(1)}, bf16[144,768]{1,0:T(8,128)(2,1)S(1)}, u32[]{:S(2)}, u32[]{:S(2)}) collective-permute-start(bf16[144,768]{1,0:T(8,128)(2,1)S(1)} %slice.13), channel_id=1, source_target_pairs={{0,8},{8,0},{16,24},{24,16},{1,9},{9,1},{17,25},{25,17},{2,10},{10... | collective-permute-start | bytes 663560 | tf_op jit(solution)/shard_map/updiag_x/ppermute | solution.py:811
  81.1 12.7 %collective-permute-start.17 = (bf16[144,768]{1,0:T(8,128)(2,1)S(1)}, bf16[144,768]{1,0:T(8,128)(2,1)S(1)}, u32[]{:S(2)}, u32[]{:S(2)}) collective-permute-start(bf16[144,768]{1,0:T(8,128)(2,1)S(1)} %slice.12), channel_id=1, source_target_pairs={{0,16},{8,24},{16,0},{24,8},{1,17},{9,25},{17,1},{25,9},{2,18},{10... | collective-permute-start | bytes 663560 | tf_op jit(solution)/shard_map/updiag_y/ppermute | solution.py:811
  82.6 15.5 %collective-permute-start.22 = (bf16[288,768]{1,0:T(8,128)(2,1)S(1)}, bf16[288,768]{1,0:T(8,128)(2,1)S(1)}, u32[]{:S(2)}, u32[]{:S(2)}) collective-permute-start(bf16[288,768]{1,0:T(8,128)(2,1)S(1)} %stack.35.refs_0_), channel_id=1, source_target_pairs={{0,16},{8,24},{16,0},{24,8},{1,17},{9,25},{17,1},{25,9},{2,18},{10... | collective-permute-start | bytes 1327112 | tf_op jit(solution)/shard_map/down_y/ppermute | solution.py:811
  83.1 15.0 %collective-permute-start.21 = (bf16[288,768]{1,0:T(8,128)(2,1)S(1)}, bf16[288,768]{1,0:T(8,128)(2,1)S(1)}, u32[]{:S(2)}, u32[]{:S(2)}) collective-permute-start(bf16[288,768]{1,0:T(8,128)(2,1)S(1)} %stack.35.refs_0_), channel_id=1, source_target_pairs={{0,8},{8,0},{16,24},{24,16},{1,9},{9,1},{17,25},{25,17},{2,10},{10... | collective-permute-start | bytes 1327112 | tf_op jit(solution)/shard_map/down_x/ppermute | solution.py:811
  98.2 13.0 %collective-permute-start.25 = (bf16[864,768]{1,0:T(8,128)(2,1)S(1)}, bf16[864,768]{1,0:T(8,128)(2,1)S(1)}, u32[]{:S(2)}, u32[]{:S(2)}) collective-permute-start(bf16[864,768]{1,0:T(8,128)(2,1)S(1)} %stack.38.refs_2_), channel_id=1, source_target_pairs={{0,1},{1,0},{2,3},{3,2},{4,5},{5,4},{6,7},{7,6},{8,9},{9,8},{10,11... | collective-permute-start | bytes 3981320 | tf_op jit(solution)/shard_map/down_core/ppermute | solution.py:799
  98.3 11.4 %collective-permute-start.26 = (bf16[384,512]{1,0:T(8,128)(2,1)S(1)}, bf16[384,512]{1,0:T(8,128)(2,1)S(1)}, u32[]{:S(2)}, u32[]{:S(2)}) collective-permute-start(bf16[384,512]{1,0:T(8,128)(2,1)S(1)} %get-tuple-element.346), channel_id=1, source_target_pairs={{0,1},{1,0},{2,3},{3,2},{4,5},{5,4},{6,7},{7,6},{8,9},{9,8},{10,11... | collective-permute-start | bytes 1179656 | tf_op jit(solution)/shard_map/given_core/ppermute | solution.py:799
  98.8 11.7 %collective-permute-start.27 = (bf16[384,512]{1,0:T(8,128)(2,1)S(1)}, bf16[384,512]{1,0:T(8,128)(2,1)S(1)}, u32[]{:S(2)}, u32[]{:S(2)}) collective-permute-start(bf16[384,512]{1,0:T(8,128)(2,1)S(1)} %get-tuple-element.347), channel_id=1, source_target_pairs={{0,1},{1,0},{2,3},{3,2},{4,5},{5,4},{6,7},{7,6},{8,9},{9,8},{10,11... | collective-permute-start | bytes 1179656 | tf_op jit(solution)/shard_map/given_core/ppermute | solution.py:799
  98.9 12.3 %collective-permute-start.24 = (bf16[144,768]{1,0:T(8,128)(2,1)S(1)}, bf16[144,768]{1,0:T(8,128)(2,1)S(1)}, u32[]{:S(2)}, u32[]{:S(2)}) collective-permute-start(bf16[144,768]{1,0:T(8,128)(2,1)S(1)} %slice.15), channel_id=1, source_target_pairs={{0,8},{8,0},{16,24},{24,16},{1,9},{9,1},{17,25},{25,17},{2,10},{10... | collective-permute-start | bytes 663560 | tf_op jit(solution)/shard_map/downdiag_x/ppermute | solution.py:811
  99.5 11.7 %collective-permute-start.23 = (bf16[144,768]{1,0:T(8,128)(2,1)S(1)}, bf16[144,768]{1,0:T(8,128)(2,1)S(1)}, u32[]{:S(2)}, u32[]{:S(2)}) collective-permute-start(bf16[144,768]{1,0:T(8,128)(2,1)S(1)} %slice.14), channel_id=1, source_target_pairs={{0,16},{8,24},{16,0},{24,8},{1,17},{9,25},{17,1},{25,9},{2,18},{10... | collective-permute-start | bytes 663560 | tf_op jit(solution)/shard_map/downdiag_y/ppermute | solution.py:811
  111.2 12.3 %collective-permute-start.30 = (bf16[512,1536]{1,0:T(8,128)(2,1)S(1)}, bf16[512,1536]{1,0:T(8,128)(2,1)S(1)}, u32[]{:S(2)}, u32[]{:S(2)}) collective-permute-start(bf16[512,1536]{1,0:T(8,128)(2,1)S(1)} %get-tuple-element.359), channel_id=1, source_target_pairs={{0,1},{1,0},{2,3},{3,2},{4,5},{5,4},{6,7},{7,6},{8,9},{9,8},{10,11... | collective-permute-start | bytes 4718600 | tf_op jit(solution)/shard_map/given_core/ppermute | solution.py:799
  124.0 10.6 %collective-permute-start.33 = (bf16[384,1024]{1,0:T(8,128)(2,1)S(1)}, bf16[384,1024]{1,0:T(8,128)(2,1)S(1)}, u32[]{:S(2)}, u32[]{:S(2)}) collective-permute-start(bf16[384,1024]{1,0:T(8,128)(2,1)S(1)} %copy-done.46), channel_id=1, source_target_pairs={{0,1},{1,0},{2,3},{3,2},{4,5},{5,4},{6,7},{7,6},{8,9},{9,8},{10,11... | collective-permute-start | bytes 2359304 | tf_op jit(solution)/shard_map/given_core/ppermute | solution.py:799
  129.3 17.1 %collective-permute-start.34 = (bf16[2,2,96,768]{3,2,1,0:T(8,128)(2,1)S(1)}, bf16[2,2,96,768]{3,2,1,0:T(8,128)(2,1)S(1)}, u32[]{:S(2)}, u32[]{:S(2)}) collective-permute-start(bf16[2,2,96,768]{3,2,1,0:T(8,128)(2,1)S(1)} %get-tuple-element.391), channel_id=1, source_target_pairs={{0,8},{8,0},{16,24},{24,16},{1,9},{9,1},{17,25},{25,17},{2,10},{10... | collective-permute-start | bytes 1769480 | tf_op jit(solution)/shard_map/gdown_x/ppermute | solution.py:811
  130.8 15.6 %collective-permute-start.35 = (bf16[2,2,96,768]{3,2,1,0:T(8,128)(2,1)S(1)}, bf16[2,2,96,768]{3,2,1,0:T(8,128)(2,1)S(1)}, u32[]{:S(2)}, u32[]{:S(2)}) collective-permute-start(bf16[2,2,96,768]{3,2,1,0:T(8,128)(2,1)S(1)} %get-tuple-element.392), channel_id=1, source_target_pairs={{0,16},{8,24},{16,0},{24,8},{1,17},{9,25},{17,1},{25,9},{2,18},{10... | collective-permute-start | bytes 1769480 | tf_op jit(solution)/shard_map/gdown_y/ppermute | solution.py:811
  146.4 11.1 %collective-permute-start.38 = (bf16[512,768]{1,0:T(8,128)(2,1)S(1)}, bf16[512,768]{1,0:T(8,128)(2,1)S(1)}, u32[]{:S(2)}, u32[]{:S(2)}) collective-permute-start(bf16[512,768]{1,0:T(8,128)(2,1)S(1)} %get-tuple-element.420.refs_10_), channel_id=1, source_target_pairs={{0,1},{1,0},{2,3},{3,2},{4,5},{5,4},{6,7},{7,6},{8,9},{9,8},{10,11... | collective-permute-start | bytes 2359304 | tf_op jit(solution)/shard_map/d_low_core/ppermute | solution.py:799
  147.3 9.1 %collective-permute-start.36 = (bf16[2,96,768]{2,1,0:T(8,128)(2,1)S(1)}, bf16[2,96,768]{2,1,0:T(8,128)(2,1)S(1)}, u32[]{:S(2)}, u32[]{:S(2)}) collective-permute-start(bf16[2,96,768]{2,1,0:T(8,128)(2,1)S(1)} %get-tuple-element.418), channel_id=1, source_target_pairs={{0,16},{8,24},{16,0},{24,8},{1,17},{9,25},{17,1},{25,9},{2,18},{10... | collective-permute-start | bytes 884744 | tf_op jit(solution)/shard_map/gdown2_y/ppermute | solution.py:811
  158.0 15.9 %collective-permute-start.42 = (bf16[2,2,96,768]{3,2,1,0:T(8,128)(2,1)S(1)}, bf16[2,2,96,768]{3,2,1,0:T(8,128)(2,1)S(1)}, u32[]{:S(2)}, u32[]{:S(2)}) collective-permute-start(bf16[2,2,96,768]{3,2,1,0:T(8,128)(2,1)S(1)} %get-tuple-element.441), channel_id=1, source_target_pairs={{0,8},{8,0},{16,24},{24,16},{1,9},{9,1},{17,25},{25,17},{2,10},{10... | collective-permute-start | bytes 1769480 | tf_op jit(solution)/shard_map/gup_x/ppermute | solution.py:811
  158.6 15.5 %collective-permute-start.43 = (bf16[2,2,96,768]{3,2,1,0:T(8,128)(2,1)S(1)}, bf16[2,2,96,768]{3,2,1,0:T(8,128)(2,1)S(1)}, u32[]{:S(2)}, u32[]{:S(2)}) collective-permute-start(bf16[2,2,96,768]{3,2,1,0:T(8,128)(2,1)S(1)} %get-tuple-element.442), channel_id=1, source_target_pairs={{0,16},{8,24},{16,0},{24,8},{1,17},{9,25},{17,1},{25,9},{2,18},{10... | collective-permute-start | bytes 1769480 | tf_op jit(solution)/shard_map/gup_y/ppermute | solution.py:811
  165.3 14.0 %collective-permute-start.45 = (bf16[96,768]{1,0:T(8,128)(2,1)S(1)}, bf16[96,768]{1,0:T(8,128)(2,1)S(1)}, u32[]{:S(2)}, u32[]{:S(2)}) collective-permute-start(bf16[96,768]{1,0:T(8,128)(2,1)S(1)} %get-tuple-element.454), channel_id=1, source_target_pairs={{0,4},{1,5},{2,6},{3,7},{4,0},{5,1},{6,2},{7,3},{8,12},{9,13},{10,... | collective-permute-start | bytes 442376 | tf_op jit(solution)/shard_map/gdown3_z2/ppermute | solution.py:805
  168.2 11.1 %collective-permute-start.46 = (bf16[96,768]{1,0:T(8,128)(2,1)S(1)}, bf16[96,768]{1,0:T(8,128)(2,1)S(1)}, u32[]{:S(2)}, u32[]{:S(2)}) collective-permute-start(bf16[96,768]{1,0:T(8,128)(2,1)S(1)} %get-tuple-element.455), channel_id=1, source_target_pairs={{0,6},{1,7},{2,0},{3,1},{4,2},{5,3},{6,4},{7,5},{8,14},{9,15},{10,... | collective-permute-start | bytes 442376 | tf_op jit(solution)/shard_map/gdown3_z3/ppermute | solution.py:805
  179.4 35.7 %collective-permute-start.47 = (bf16[2,2,112,768]{3,2,1,0:T(8,128)(2,1)S(1)}, bf16[2,2,112,768]{3,2,1,0:T(8,128)(2,1)S(1)}, u32[]{:S(2)}, u32[]{:S(2)}) collective-permute-start(bf16[2,2,112,768]{3,2,1,0:T(8,128)(2,1)S(1)} %get-tuple-element.456), channel_id=1, source_target_pairs={{0,8},{8,0},{16,24},{24,16},{1,9},{9,1},{17,25},{25,17},{2,10},{10... | collective-permute-start | bytes 2064392 | tf_op jit(solution)/shard_map/gfirst_x/ppermute | solution.py:811
  179.9 35.2 %collective-permute-start.48 = (bf16[2,2,112,768]{3,2,1,0:T(8,128)(2,1)S(1)}, bf16[2,2,112,768]{3,2,1,0:T(8,128)(2,1)S(1)}, u32[]{:S(2)}, u32[]{:S(2)}) collective-permute-start(bf16[2,2,112,768]{3,2,1,0:T(8,128)(2,1)S(1)} %get-tuple-element.457), channel_id=1, source_target_pairs={{0,16},{8,24},{16,0},{24,8},{1,17},{9,25},{17,1},{25,9},{2,18},{10... | collective-permute-start | bytes 2064392 | tf_op jit(solution)/shard_map/gfirst_y/ppermute | solution.py:811
  180.7 21.1 %collective-permute-start.49 = (bf16[2,96,768]{2,1,0:T(8,128)(2,1)S(1)}, bf16[2,96,768]{2,1,0:T(8,128)(2,1)S(1)}, u32[]{:S(2)}, u32[]{:S(2)}) collective-permute-start(bf16[2,96,768]{2,1,0:T(8,128)(2,1)S(1)} %get-tuple-element.467), channel_id=1, source_target_pairs={{0,16},{8,24},{16,0},{24,8},{1,17},{9,25},{17,1},{25,9},{2,18},{10... | collective-permute-start | bytes 884744 | tf_op jit(solution)/shard_map/gup2_y/ppermute | solution.py:811
  182.3 19.6 %collective-permute-start.50 = (bf16[2,96,768]{2,1,0:T(8,128)(2,1)S(1)}, bf16[2,96,768]{2,1,0:T(8,128)(2,1)S(1)}, u32[]{:S(2)}, u32[]{:S(2)}) collective-permute-start(bf16[2,96,768]{2,1,0:T(8,128)(2,1)S(1)} %get-tuple-element.468), channel_id=1, source_target_pairs={{0,8},{8,0},{16,24},{24,16},{1,9},{9,1},{17,25},{25,17},{2,10},{10... | collective-permute-start | bytes 884744 | tf_op jit(solution)/shard_map/gup2_x/ppermute | solution.py:811
  202.0 11.6 %collective-permute-start.51 = (bf16[96,768]{1,0:T(8,128)(2,1)S(1)}, bf16[96,768]{1,0:T(8,128)(2,1)S(1)}, u32[]{:S(2)}, u32[]{:S(2)}) collective-permute-start(bf16[96,768]{1,0:T(8,128)(2,1)S(1)} %get-tuple-element.480), channel_id=1, source_target_pairs={{0,2},{1,3},{2,4},{3,5},{4,6},{5,7},{6,0},{7,1},{8,10},{9,11},{10,... | collective-permute-start | bytes 442376 | tf_op jit(solution)/shard_map/gup3_z1/ppermute | solution.py:805
  205.7 9.4 %collective-permute-start.52 = (bf16[96,768]{1,0:T(8,128)(2,1)S(1)}, bf16[96,768]{1,0:T(8,128)(2,1)S(1)}, u32[]{:S(2)}, u32[]{:S(2)}) collective-permute-start(bf16[96,768]{1,0:T(8,128)(2,1)S(1)} %get-tuple-element.481), channel_id=1, source_target_pairs={{0,4},{1,5},{2,6},{3,7},{4,0},{5,1},{6,2},{7,3},{8,12},{9,13},{10,... | collective-permute-start | bytes 442376 | tf_op jit(solution)/shard_map/gup3_z2/ppermute | solution.py:805
  206.1 9.0 %collective-permute-start.53 = (bf16[96,768]{1,0:T(8,128)(2,1)S(1)}, bf16[96,768]{1,0:T(8,128)(2,1)S(1)}, u32[]{:S(2)}, u32[]{:S(2)}) collective-permute-start(bf16[96,768]{1,0:T(8,128)(2,1)S(1)} %get-tuple-element.482), channel_id=1, source_target_pairs={{0,6},{1,7},{2,0},{3,1},{4,2},{5,3},{6,4},{7,5},{8,14},{9,15},{10,... | collective-permute-start | bytes 442376 | tf_op jit(solution)/shard_map/gup3_z3/ppermute | solution.py:805
  215.4 9.5 %collective-permute-start.54 = (bf16[2,112,768]{2,1,0:T(8,128)(2,1)S(1)}, bf16[2,112,768]{2,1,0:T(8,128)(2,1)S(1)}, u32[]{:S(2)}, u32[]{:S(2)}) collective-permute-start(bf16[2,112,768]{2,1,0:T(8,128)(2,1)S(1)} %get-tuple-element.490), channel_id=1, source_target_pairs={{0,16},{8,24},{16,0},{24,8},{1,17},{9,25},{17,1},{25,9},{2,18},{10... | collective-permute-start | bytes 1032200 | tf_op jit(solution)/shard_map/gfirst2_y/ppermute | solution.py:811
  216.0 9.2 %collective-permute-start.55 = (bf16[2,112,768]{2,1,0:T(8,128)(2,1)S(1)}, bf16[2,112,768]{2,1,0:T(8,128)(2,1)S(1)}, u32[]{:S(2)}, u32[]{:S(2)}) collective-permute-start(bf16[2,112,768]{2,1,0:T(8,128)(2,1)S(1)} %get-tuple-element.491), channel_id=1, source_target_pairs={{0,8},{8,0},{16,24},{24,16},{1,9},{9,1},{17,25},{25,17},{2,10},{10... | collective-permute-start | bytes 1032200 | tf_op jit(solution)/shard_map/gfirst2_x/ppermute | solution.py:811
  225.5 9.1 %collective-permute-start.56 = (bf16[112,768]{1,0:T(8,128)(2,1)S(1)}, bf16[112,768]{1,0:T(8,128)(2,1)S(1)}, u32[]{:S(2)}, u32[]{:S(2)}) collective-permute-start(bf16[112,768]{1,0:T(8,128)(2,1)S(1)} %get-tuple-element.499), channel_id=1, source_target_pairs={{0,2},{1,3},{2,4},{3,5},{4,6},{5,7},{6,0},{7,1},{8,10},{9,11},{10,... | collective-permute-start | bytes 516104 | tf_op jit(solution)/shard_map/gfirst3_z1/ppermute | solution.py:805
  229.3 11.0 %collective-permute-start.57 = (bf16[112,768]{1,0:T(8,128)(2,1)S(1)}, bf16[112,768]{1,0:T(8,128)(2,1)S(1)}, u32[]{:S(2)}, u32[]{:S(2)}) collective-permute-start(bf16[112,768]{1,0:T(8,128)(2,1)S(1)} %get-tuple-element.500), channel_id=1, source_target_pairs={{0,4},{1,5},{2,6},{3,7},{4,0},{5,1},{6,2},{7,3},{8,12},{9,13},{10,... | collective-permute-start | bytes 516104 | tf_op jit(solution)/shard_map/gfirst3_z2/ppermute | solution.py:805
  229.3 11.0 %collective-permute-start.58 = (bf16[112,768]{1,0:T(8,128)(2,1)S(1)}, bf16[112,768]{1,0:T(8,128)(2,1)S(1)}, u32[]{:S(2)}, u32[]{:S(2)}) collective-permute-start(bf16[112,768]{1,0:T(8,128)(2,1)S(1)} %get-tuple-element.501), channel_id=1, source_target_pairs={{0,6},{1,7},{2,0},{3,1},{4,2},{5,3},{6,4},{7,5},{8,14},{9,15},{10,... | collective-permute-start | bytes 516104 | tf_op jit(solution)/shard_map/gfirst3_z3/ppermute | solution.py:805
  (70 other events, 877.3 us)

commit v3 on v2

--- a/solution.py
+++ b/solution.py
@@ -42,7 +42,7 @@
 
 
 def call(
-    kernel, name, out_shape, args, scratch=(), place=None, flops=0, vmem=16, space=pltpu.VMEM, alias=()
+    kernel, name, out_shape, args, scratch=(), place=None, flops=0, vmem=8, space=pltpu.VMEM
 ):
     many = isinstance(out_shape, (list, tuple))
     outs = list(out_shape) if many else [out_shape]
@@ -58,7 +58,6 @@
         in_specs=specs,
         out_specs=[pl.BlockSpec(memory_space=pltpu.VMEM)] * len(outs),
         scratch_shapes=list(scratch),
-        input_output_aliases=dict(alias),
         cost_estimate=pl.CostEstimate(
             flops=int(flops) // 1000, bytes_accessed=int(moved) // 1000, transcendentals=0
         ),
@@ -90,17 +89,23 @@
     return inverse * (inner - first - shaped * second)
 
 
-def normal_parts(values):
-    size = jnp.abs(values)
-    base = 1.0 + (0.3275911 * math.sqrt(0.5)) * size
-    t = pl.reciprocal(base, approx=True)
-    t = t * (2.0 - base * t)
-    bell = jnp.exp2(values * values * (-0.5 * LOG2E))
-    poly = 0.5 * 1.061405429
-    for c in (-1.453152027, 1.421413741, -0.284496736, 0.254829592):
-        poly = poly * t + 0.5 * c
-    tail = poly * t * bell
-    return bell, jnp.where(values >= 0.0, 1.0 - tail, tail)
+SHARE = (
+    1.8312406690584326e-09,
+    -1.3438994500794415e-07,
+    3.981248882617272e-06,
+    -5.530906739278176e-05,
+    -3.29139111098754e-05,
+    0.03633373340914607,
+    0.7978847692370962,
+)
+
+
+def normal_share(u, square):
+    x = jnp.minimum(square, 36.0)
+    p = x * SHARE[0] + SHARE[1]
+    for c in SHARE[2:]:
+        p = p * x + c
+    return jnp.tanh(p * u) * 0.5 + 0.5
 
 
 def lanes_below(width):
@@ -113,7 +118,12 @@
 
 
 def pack_kernel(place, *refs):
-    given, (own, a_ref, bc_ref), (small, sems), held = refs[:6], refs[6:9], refs[9:11], refs[11:]
+    given, (own, a_ref, b_ref, c_ref), held, (small, sems) = (
+        refs[:6],
+        refs[6:10],
+        refs[10:16],
+        refs[16:],
+    )
     copies = [pltpu.make_async_copy(a, b, sems.at[i]) for i, (a, b) in enumerate(zip(given, held))]
     for copy in copies:
         copy.start()
@@ -146,31 +156,36 @@
     left = vec.shape[1] - room
     small[1:2, start : start + left] = vec[:, room:]
     a_ref[rows:, :] = small[...].astype(BF)
-    bc_ref[:rows, :] = up[...].astype(BF)
+    b_ref[...] = up[...].astype(BF)
     across = down.shape[1]
     for h in range(down.shape[0] // rows):
-        bc_ref[rows:, h * across : (h + 1) * across] = down[rows * h : rows * (h + 1), :].astype(BF)
+        c_ref[:, h * across : (h + 1) * across] = down[rows * h : rows * (h + 1), :].astype(BF)
     tall = a_ref.shape[0]
     own[:tall, :] = a_ref[...]
-    own[tall:, :] = bc_ref[...]
+    own[tall : tall + rows, :] = b_ref[...]
+    own[tall + rows :, :] = c_ref[...]
 
 
 def pack(place, *given):
     rows, wide = given[2].shape
     tall = rows + 16
-    return call(
+    got = call(
         pack_kernel,
         "pack_weights",
-        [sds((tall + 2 * rows, wide), BF), sds((tall, wide), BF), sds((2 * rows, wide), BF)],
+        [
+            sds((tall + 2 * rows, wide), BF),
+            sds((tall, wide), BF),
+            sds((rows, wide), BF),
+            sds((rows, wide), BF),
+            *(sds(a.shape, F32) for a in given),
+        ],
         given,
-        scratch=[
-            pltpu.VMEM((16, wide), F32),
-            pltpu.SemaphoreType.DMA((len(given),)),
-            *(pltpu.VMEM(a.shape, F32) for a in given),
-        ],
+        scratch=[pltpu.VMEM((16, wide), F32), pltpu.SemaphoreType.DMA((len(given),))],
         place=place,
         space=pltpu.HBM,
-    )
+        vmem=60,
+    )
+    return got[:4], got[4:]
 
 
 def split_cores(place, value, rows, mine, theirs, cols):
@@ -231,21 +246,22 @@
 
 
 def qkv_kernel(front, rest, x, weight, vec, proj, q_front, q_rest, kv, kvp):
-    seqs, _, width = front.shape
+    seqs, half, width = front.shape
+    length = x.shape[1]
     piece = width // 2
-    for s in range(seqs):
-        for j in range(2):
-            cols = slice(j * piece, (j + 1) * piece)
-            w = weight[:, cols]
-            bias = vec[:, cols]
-            q_front[s, :, cols] = (nn(front[s], w) + bias).astype(BF)
-            q_rest[s, :, cols] = (nn(rest[s], w) + bias).astype(BF)
-        for j in range(4):
-            cols = slice(j * piece, (j + 1) * piece)
-            at = slice(width + j * piece, width + (j + 1) * piece)
-            part = (nn(x[s], weight[:, at]) + vec[:, at]).astype(BF)
-            kv[s, :, cols] = part
-            kvp[s, :, cols] = nn(proj[...], part).astype(BF)
+    for j in range(4):
+        cols = slice(j * piece, (j + 1) * piece)
+        at = slice(width + j * piece, width + (j + 1) * piece)
+        part = nn(x[...].reshape(seqs * length, width), weight[:, at]) + vec[:, at]
+        part = part.astype(BF).reshape(seqs, length, piece)
+        kv[:, :, cols] = part
+        for s in range(seqs):
+            kvp[s, :, cols] = nn(proj[...], part[s]).astype(BF)
+    for j in range(2):
+        cols = slice(j * piece, (j + 1) * piece)
+        for given, result in ((front, q_front), (rest, q_rest)):
+            part = nn(given[...].reshape(seqs * half, width), weight[:, cols]) + vec[:, cols]
+            result[:, :, cols] = part.astype(BF).reshape(seqs, half, piece)
 
 
 def make_qkv(front, rest, x, weight, vec, proj):
@@ -266,30 +282,33 @@
     )
 
 
+def pair_of_heads(head, value):
+    below = lanes_below(head)
+    zero = jnp.zeros_like(value)
+    return jnp.concatenate([jnp.where(below, value, zero), jnp.where(below, zero, value)], axis=0)
+
+
 def attend_kernel(head, q_front, q_rest, kvp, o_front, o_rest):
-    seqs, _, width = q_front.shape
+    seqs, half, width = q_front.shape
+    count = kvp.shape[1]
     below = lanes_below(head)
     factor = LOG2E / math.sqrt(head)
-
-    def pair(p, carry):
-        at = lanes(p * 2 * head, 2 * head)
+    for first in range(0, width, 2 * head):
+        at = slice(first, first + 2 * head)
         for s in range(seqs):
-            k, v = kvp[s, :, at], kvp[s, :, lanes(width + p * 2 * head, 2 * head)]
-            zero = jnp.zeros_like(k)
-            heads = [(jnp.where(own, k, zero), jnp.where(own, v, zero)) for own in (below, ~below)]
-            for q_ref, o_ref in ((q_front, o_front), (q_rest, o_rest)):
-                q = q_ref[s, :, at]
-                total = None
-                for kh, vh in heads:
-                    scores = nt(q, kh)
-                    e = jnp.exp2((scores - jnp.max(scores, axis=-1, keepdims=True)) * factor)
-                    scale = 1.0 / jnp.sum(e, axis=-1, keepdims=True)
-                    part = nn(e.astype(BF), vh) * scale
-                    total = part if total is None else total + part
-                o_ref[s, :, at] = total.astype(BF)
-        return carry
-
-    lax.fori_loop(0, HEADS // 2, pair, 0)
+            q = jnp.concatenate([q_front[s, :, at], q_rest[s, :, at]], axis=0)
+            scores = nt(q, pair_of_heads(head, kvp[s, :, at]))
+            weights, scales = [], []
+            for h in range(2):
+                part = scores[:, h * count : (h + 1) * count]
+                e = jnp.exp2((part - jnp.max(part, axis=-1, keepdims=True)) * factor)
+                scales.append(1.0 / jnp.sum(e, axis=-1, keepdims=True))
+                weights.append(e.astype(BF))
+            values = pair_of_heads(head, kvp[s, :, width + first : width + first + 2 * head])
+            total = nn(jnp.concatenate(weights, axis=1), values)
+            total = (total * jnp.where(below, scales[0], scales[1])).astype(BF)
+            o_front[s, :, at] = total[:half]
+            o_rest[s, :, at] = total[half:]
 
 
 def attend(q_front, q_rest, kvp):
@@ -338,51 +357,60 @@
     )
 
 
-def lift_kernel(mark, keep, place, low, weight, vec, active, *more):
+def lift_kernel(mark, keep, chosen, place, low, weight, vec, active, *more):
     rows = low.shape[0]
-    parts, _, piece = weight.shape
+    piece = weight.shape[2]
     step = 128
-    for f in range(parts):
-        cols = slice(f * piece, (f + 1) * piece)
+    for n, f in enumerate(chosen):
+        cols = slice(n * piece, (n + 1) * piece)
         bias = vec[:, mark + f * piece : mark + (f + 1) * piece]
         for r in range(0, rows, step):
             at = slice(r, r + step)
             u = nn(low[at, :], weight[f]) + bias
-            bell, share = normal_parts(u)
+            square = u * u
+            share = normal_share(u, square)
             a = (u * share).astype(BF)
             active[at, cols] = a
             if keep:
                 slope, give = more
-                factor = 1.0 / math.sqrt(2.0 * math.pi)
-                slope[at, cols] = (share + u * bell * factor).astype(BF)
+                bell = jnp.exp2(square * (-0.5 * LOG2E) - 0.5 * math.log2(2.0 * math.pi))
+                slope[at, cols] = (share + u * bell).astype(BF)
                 half = piece // 2
-                give[at, f * half : (f + 1) * half] = jnp.where(
+                give[at, n * half : (n + 1) * half] = jnp.where(
                     place[2] == 0, a[:, half:], a[:, :half]
                 )
 
 
-def lift(place, low, weight, vec, mark, keep):
+def lift(place, low, weight, vec, mark, keep, chosen):
     rows, width = low.shape
-    parts, _, piece = weight.shape
-    outs = [sds((rows, parts * piece), BF)]
+    piece = weight.shape[2]
+    wide = len(chosen) * piece
+    outs = [sds((rows, wide), BF)]
     if keep:
-        outs += [sds((rows, parts * piece), BF), sds((rows, parts * piece // 2), BF)]
-    return call(
-        functools.partial(lift_kernel, mark, keep),
+        outs += [sds((rows, wide), BF), sds((rows, wide // 2), BF)]
+    return call(
+        functools.partial(lift_kernel, mark, keep, tuple(chosen)),
         "lift_front" if keep else "lift_rest",
         outs,
         (low, weight, vec),
         place=place,
-        flops=2 * rows * width * parts * piece,
-    )
-
-
-def lower_kernel(marks, active, normed, weight, vec, *refs):
+        flops=2 * rows * width * wide,
+    )
+
+
+def lower_kernel(marks, count, *refs):
+    actives, (normed, weight, vec), refs = refs[:count], refs[count : count + 3], refs[count + 3 :]
     bias, gain, shift = (vec[:, a:b] for a, b in marks)
-    step = 256
+    total = normed[...] + bias
+    first = 0
+    for active in actives:
+        last = first + active.shape[1]
+        total = total + nt(active[...], weight[:, first:last])
+        first = last
+    step = 128
     for r in range(0, normed.shape[0], step):
         at = slice(r, r + step)
-        summed = normed[at, :] + nt(active[at, :], weight[...]) + bias
+        summed = total[at, :]
         shaped, inverse = norm_stats(summed)
         if len(refs) == 1:
             refs[0][at, :] = (shaped * gain + shift).astype(BF)
@@ -399,9 +427,8 @@
             sums[i : i + 1, :] = v if r == 0 else sums[i : i + 1, :] + v
 
 
-def lower(active, normed, weight, vec, marks, dy=None):
+def lower(actives, normed, weight, vec, marks, dy=None):
     rows, width = normed.shape
-    hidden = active.shape[1]
     full = (rows, width)
     if dy is None:
         outs, more = [sds(full, BF)], ()
@@ -415,25 +442,21 @@
         ]
         more = (dy,)
     return call(
-        functools.partial(lower_kernel, marks),
+        functools.partial(lower_kernel, marks, len(actives)),
         "lower_rest" if dy is None else "lower_front",
         outs,
-        (active, normed, weight, vec, *more),
-        flops=2 * rows * width * hidden,
+        (*actives, normed, weight, vec, *more),
+        flops=2 * rows * width * weight.shape[1],
     )
 
 
 def hidden_back_kernel(d_low, weight, slope, d_hidden, sums):
-    rows, piece = d_low.shape
-    step = 256
+    piece = d_low.shape[1]
     for f in range(weight.shape[1] // piece):
         cols = slice(f * piece, (f + 1) * piece)
-        for r in range(0, rows, step):
-            at = slice(r, r + step)
-            du = nn(d_low[at, :], weight[:, cols]) * slope[at, cols].astype(F32)
-            d_hidden[at, cols] = du.astype(BF)
-            part = jnp.sum(du, axis=0, keepdims=True)
-            sums[:, cols] = part if r == 0 else sums[:, cols] + part
+        du = nn(d_low[...], weight[:, cols]) * slope[:, cols].astype(F32)
+        d_hidden[:, cols] = du.astype(BF)
+        sums[:, cols] = jnp.sum(du, axis=0, keepdims=True)
 
 
 def hidden_back(d_low, weight, slope):
@@ -449,167 +472,112 @@
 
 
 def first_back_kernel(
-    marks, d_hidden, up, d_sum, kept, vec, weight, d_first, d_low, d_attended, sums
+    marks, d_hidden, up, d_sum, kept, vec, weight, up_sums, two_sums, *refs
 ):
+    d_first, d_low, d_attended, sums = refs
     gain = vec[:, marks[0] : marks[1]]
     parts, _, piece = up.shape
-    step = 256
+    total = d_sum[...]
+    for f in range(parts):
+        total = total + nt(d_hidden[:, f * piece : (f + 1) * piece], up[f])
+    step = 128
     for r in range(0, d_sum.shape[0], step):
         at = slice(r, r + step)
-        grad = d_sum[at, :]
-        for f in range(parts):
-            grad = grad + nt(d_hidden[at, f * piece : (f + 1) * piece], up[f])
+        grad = total[at, :]
         shaped, inverse = norm_stats(kept[at, :])
         back = norm_grad(shaped, inverse, gain, grad)
-        low = back.astype(BF)
         d_first[at, :] = back
-        d_low[at, :] = low
-        d_attended[at, :] = nt(low, weight[...]).astype(BF)
+        d_low[at, :] = back.astype(BF)
         new = [jnp.sum(v, axis=0, keepdims=True) for v in (grad * shaped, grad, back)]
         for i, v in enumerate(new):
             sums[i : i + 1, :] = v if r == 0 else sums[i : i + 1, :] + v
-
-
-def first_back(d_hidden, up, d_sum, kept, vec, weight, marks):
+    d_attended[...] = nt(d_low[...], weight[...]).astype(BF)
+    sums[3:6, :] = two_sums[0:3, :]
+    for f in range(parts):
+        sums[6 + f : 7 + f, :] = up_sums[:, f * piece : (f + 1) * piece]
+    sums[6 + parts :, :] = jnp.zeros((sums.shape[0] - 6 - parts, sums.shape[1]), F32)
+
+
+def first_back(d_hidden, up, d_sum, kept, vec, weight, up_sums, two_sums, marks):
     rows, width = d_sum.shape
     parts, _, piece = up.shape
     full = (rows, width)
     return call(
         functools.partial(first_back_kernel, marks),
         "first_back",
-        [sds(full, F32), sds(full, BF), sds(full, BF), sds((8, width), F32)],
-        (d_hidden, up, d_sum, kept, vec, weight),
+        [sds(full, F32), sds(full, BF), sds(full, BF), sds((16, width), F32)],
+        (d_hidden, up, d_sum, kept, vec, weight, up_sums, two_sums),
         flops=2 * rows * width * (parts * piece + width),
     )
 
 
-def attend_back_kernel(head, s, queries, kvp, grads, *refs):
-    d_q, d_k, d_v, sums = refs[-4:]
-    width = queries.shape[2]
+def attend_back_kernel(head, s, queries, kvp, grads, result):
+    _, half, width = queries.shape
+    count = kvp.shape[1]
     below = lanes_below(head)
-    line = lax.broadcasted_iota(jnp.int32, (2 * head, 1), 0) < head
     scale = 1.0 / math.sqrt(head)
-
-    def pair(n, carry):
-        at = lanes(n * 2 * head, 2 * head)
+    for first in range(0, width, 2 * head):
+        at = slice(first, first + 2 * head)
         q, k, g = queries[s, :, at], kvp[s, :, at], grads[s, :, at]
-        v = kvp[s, :, lanes(width + n * 2 * head, 2 * head)]
-        zero = jnp.zeros_like(k)
-        none = jnp.zeros_like(q)
+        v = kvp[s, :, width + first : width + first + 2 * head]
+        scores = nt(pair_of_heads(head, k), q)
+        d_probs = nt(pair_of_heads(head, v), g)
+        probs, d_scores = [], []
+        for h in range(2):
+            part = scores[h * count : (h + 1) * count]
+            e = jnp.exp2((part - jnp.max(part, axis=0, keepdims=True)) * (LOG2E * scale))
+            p = e * (1.0 / jnp.sum(e, axis=0, keepdims=True))
+            both = p * d_probs[h * count : (h + 1) * count]
+            ds = (both - p * jnp.sum(both, axis=0, keepdims=True)) * scale
+            probs.append(p.astype(BF))
+            d_scores.append(ds.astype(BF))
+        dv = nn(jnp.concatenate(probs, axis=0), g)
+        dk = nn(jnp.concatenate(d_scores, axis=0), q)
         kt = k.T
-        dq = dk = dv = None
-        for own, ownt in ((below, line), (~below, ~line)):
-            scores = nt(jnp.where(own, k, zero), q)
-            top = jnp.max(scores, axis=0, keepdims=True)
-            e = jnp.exp2((scores - top) * (LOG2E * scale))
-            p = e * (1.0 / jnp.sum(e, axis=0, keepdims=True))
-            dv_part = nn(p.astype(BF), jnp.where(own, g, none))
-            dp = nt(jnp.where(own, v, zero), g)
-            both = p * dp
-            ds = ((both - p * jnp.sum(both, axis=0, keepdims=True)) * scale).astype(BF)
-            dk_part = nn(ds, jnp.where(own, q, none))
-            dq_part = nn(jnp.where(ownt, kt, jnp.zeros_like(kt)), ds)
-            dv = dv_part if dv is None else dv + dv_part
-            dk = dk_part if dk is None else dk + dk_part
-            dq = dq_part if dq is None else dq + dq_part
-        dq = dq.T
-        d_q[s, :, at] = dq.astype(BF)
-        d_k[s, :, at] = dk.astype(BF)
-        d_v[s, :, at] = dv.astype(BF)
-        sums[s, :, at] = jnp.sum(dq, axis=0, keepdims=True)
-        return carry
-
-    lax.fori_loop(0, HEADS // 2, pair, 0)
-
-
-def attend_back(s, queries, kvp, grads, before=()):
-    seqs, half, width = queries.shape
+        dq = jnp.concatenate([nn(kt[:head], d_scores[0]), nn(kt[head:], d_scores[1])], axis=0)
+        result[:half, at] = dq.T.astype(BF)
+        result[half : half + count, at] = jnp.where(below, dk[:count], dk[count:]).astype(BF)
+        result[half + count :, at] = jnp.where(below, dv[:count], dv[count:]).astype(BF)
+
+
+def attend_back(s, queries, kvp, grads):
+    _, half, width = queries.shape
     rows = kvp.shape[1]
     head = width // HEADS
     return call(
         functools.partial(attend_back_kernel, head, s),
         "attend_back",
-        [
-            sds(queries.shape, BF),
-            sds((seqs, rows, width), BF),
-            sds((seqs, rows, width), BF),
-            sds((seqs, 1, width), F32),
-        ],
-        (queries, kvp, grads, *before),
+        sds((half + 2 * rows, width), BF),
+        (queries, kvp, grads),
         flops=2 * HEADS * half * rows * 2 * head * 5,
-        alias=[(3 + i, i) for i in range(len(before))],
-    )
-
-
-def spread_kernel(d_k, d_v, kv, projt, q_sums, one_sums, up_sums, two_sums, d_kv, small, vector):
-    width = d_k.shape[2]
-    grad, k_sums = None, [None, None]
-    for s in range(d_k.shape[0]):
-        for j, ref in enumerate((d_k, d_v)):
-            cols = slice(j * width, (j + 1) * width)
-            part = nn(projt[...], ref[s])
-            d_kv[s, :, cols] = part.astype(BF)
-            new = jnp.sum(part, axis=0, keepdims=True)
-            k_sums[j] = new if s == 0 else k_sums[j] + new
-            more = nt(ref[s], kv[s, :, cols])
-            grad = more if grad is None else grad + more
-    rows, across = grad.shape
-    small[:rows, :] = grad
-    at = 0
-    for value in (
-        jnp.sum(q_sums[...], axis=0),
-        *k_sums,
-        one_sums[2:3, :],
-        up_sums[...],
-        two_sums[2:3, :],
-        one_sums[0:1, :],
-        one_sums[1:2, :],
-        two_sums[0:1, :],
-        two_sums[1:2, :],
-    ):
-        size = value.shape[1]
-        vector[:, at : at + size] = value
-        at += size
-    vector[:, at:] = jnp.zeros((1, vector.shape[1] - at), F32)
-    small[rows:, :] = jnp.zeros((small.shape[0] - rows, across), F32)
-    for r in range(vector.shape[1] // across):
-        small[rows + r : rows + r + 1, :] = vector[:, r * across : (r + 1) * across]
-
-
-def spread(d_k, d_v, kv, projt, q_sums, one_sums, up_sums, two_sums, entries):
-    seqs, rows, width = d_k.shape
-    length = kv.shape[1]
-    extra = -(-entries // length)
-    return call(
-        spread_kernel,
-        "spread_kv",
-        [sds((seqs, length, 2 * width), BF), sds((rows + -(-extra // 8) * 8, length), F32)],
-        (d_k, d_v, kv, projt, q_sums, one_sums, up_sums, two_sums),
-        scratch=[pltpu.VMEM((1, extra * length), F32)],
-        flops=2 * seqs * rows * length * 2 * width * 2,
-    )
-
-
-def input_back_kernel(d_kv, d_q, d_first, weight, back, result):
-    seqs, half, width = d_q.shape
-    for s in range(seqs):
-        front = d_first[s] + nt(d_q[s], weight[:, :width])
+    )
+
+
+def input_back_kernel(projt, d_first, weight, back, *refs):
+    grads, result = refs[:-1], refs[-1]
+    _, half, width = d_first.shape
+    rows = projt.shape[1]
+    for s, grad in enumerate(grads):
+        front = d_first[s] + nt(grad[:half, :], weight[:, :width])
         high = front.astype(BF)
         low = (front - high.astype(F32)).astype(BF)
         place = back[s, :, :half]
-        total = nt(d_kv[s], weight[:, width:]) + nn(place, high) + nn(place, low)
+        total = nn(place, high) + nn(place, low)
+        for j in (1, 2):
+            part = nn(projt[...], grad[half + (j - 1) * rows : half + j * rows, :]).astype(BF)
+            total = total + nt(part, weight[:, j * width : (j + 1) * width])
         result[s] = total.astype(BF)
 
 
-def input_back(d_kv, d_q, d_first, weight, back):
-    seqs, length, wide = d_kv.shape
-    half, width = d_q.shape[1:]
+def input_back(projt, d_first, weight, back, grads):
+    seqs, half, width = d_first.shape
+    length = back.shape[1]
     return call(
         input_back_kernel,
         "input_back",
         sds((seqs, length, width), BF),
-        (d_kv, d_q, d_first, weight, back),
-        flops=2 * seqs * length * width * (wide + width // 2 + length),
+        (projt, d_first, weight, back, *grads),
+        flops=2 * seqs * length * width * (3 * width + length),
     )
 
 
@@ -697,37 +665,64 @@
     )
 
 
-def grad_rest_kernel(place, *refs):
-    pairs, sums, refs = refs[:12], refs[12:14], refs[14:]
-    outs, (work_qkv, work_out, vector, smalls, small, d_proj) = refs[:4], refs[4:]
+def grad_rest_kernel(seqs, place, *refs):
+    (xt, xt_o, frontt, frontt_o, attendedt, attendedt_o), refs = refs[:6], refs[6:]
+    grads, refs = refs[: 2 * seqs], refs[2 * seqs :]
+    (d_low, d_low_o, kv, kv_o, sums, sums_o, projt), refs = refs[:7], refs[7:]
+    outs, (work_qkv, work_out, work_kv, vector, smalls, small, d_proj) = refs[:4], refs[4:]
     slots, rows, _ = work_qkv.shape
     _, _, tall, wide = outs[0].shape
     fsdp = smalls.shape[0]
-    xt, xt_o, frontt, frontt_o, attendedt, attendedt_o = pairs[:6]
-    d_q, d_q_o, d_kv, d_kv_o, d_low, d_low_o = pairs[6:]
-    width = d_q.shape[1]
-
-    def both(a, a_o, b, b_o):
+    length, count = projt.shape
+    width = d_low.shape[1]
+    half = d_low.shape[0] // seqs
+    first_sums = [None] * 3
+    for n, grad in enumerate(grads):
+        values = kv if n < seqs else kv_o
+        s = n % seqs
+        new = [jnp.sum(grad[:half, :].astype(F32), axis=0, keepdims=True)]
+        for j in (0, 1):
+            part = nn(projt[...], grad[half + j * count : half + (j + 1) * count, :])
+            work_kv[n * length : (n + 1) * length, j * width : (j + 1) * width] = part.astype(BF)
+            new.append(jnp.sum(part, axis=0, keepdims=True))
+        first_sums = new if n == 0 else [a + b for a, b in zip(first_sums, new)]
+        both = nt(grad[half : half + count, :], values[s, :, :width]) + nt(
+            grad[half + count :, :], values[s, :, width:]
+        )
+        d_proj[...] = both if n == 0 else d_proj[...] + both
+
+    def both_cores(a, a_o, b, b_o):
         total = nn(a[...], b) + nn(a_o[...], b_o)
         return total.astype(BF).reshape(slots, rows, total.shape[1])
 
-    work_qkv[:, :, :width] = both(frontt, frontt_o, d_q[...], d_q_o[...])
+    q_part = None
+    for n, grad in enumerate(grads):
+        left = frontt if n < seqs else frontt_o
+        s = n % seqs
+        part = nn(left[:, s * half : (s + 1) * half], grad[:half, :])
+        q_part = part if q_part is None else q_part + part
+    work_qkv[:, :, :width] = q_part.astype(BF).reshape(slots, rows, width)
+    tokens = seqs * length
     for j in range(2):
         cols = slice(j * width, (j + 1) * width)
-        work_qkv[:, :, (j + 1) * width : (j + 2) * width] = both(
-            xt, xt_o, d_kv[:, cols], d_kv_o[:, cols]
+        work_qkv[:, :, (j + 1) * width : (j + 2) * width] = both_cores(
+            xt, xt_o, work_kv[:tokens, cols], work_kv[tokens:, cols]
         )
-    work_out[...] = both(attendedt, attendedt_o, d_low[...], d_low_o[...])
-    d_proj[...] = sums[0][...] + sums[1][...]
-    across = d_proj.shape[1]
-    height = sums[0].shape[0] - (-(-vector.shape[1] // (8 * across))) * 8
-    for at in range(0, vector.shape[1], across):
-        size = min(across, vector.shape[1] - at)
-        line = height + at // across
-        vector[:, at : at + size] = d_proj[line : line + 1, :size]
+    work_out[...] = both_cores(attendedt, attendedt_o, d_low[...], d_low_o[...])
+    total = sums[...] + sums_o[...]
+    at = 0
+    for value in (
+        *first_sums,
+        total[2:3, :],
+        *(total[i : i + 1, :] for i in range(6, 6 + vector.shape[1] // width - 9)),
+        total[5:6, :],
+        *(total[i : i + 1, :] for i in (0, 1, 3, 4)),
+    ):
+        vector[:, at : at + width] = value
+        at += width
     entries = vector.shape[1] // (2 * fsdp * slots)
-    height = height // fsdp
-    across = across // (2 * slots)
+    height = count // fsdp
+    across = length // (2 * slots)
     start = (height // 8) * across
     room = wide - start
     first = place[2] == 0
@@ -735,11 +730,10 @@
     for f in range(fsdp):
         for z in range(slots):
             for g in range(height // 8):
-                at = (
-                    slice(f * height + 8 * g, f * height + 8 * g + 8),
-                    slice(2 * z * across, 2 * (z + 1) * across),
-                )
-                part = d_proj[at]
+                part = d_proj[
+                    f * height + 8 * g : f * height + 8 * g + 8,
+                    2 * z * across : 2 * (z + 1) * across,
+                ]
                 small[0:8, g * across : (g + 1) * across] = jnp.where(
                     first, part[:, :across], part[:, across:]
                 )
@@ -770,26 +764,27 @@
             put[rows:, :] = smalls[f, z]
 
 
-def grad_rest(place, pairs, small, small_other, entries, fsdp, slots):
-    width, tokens = 2 * pairs[0].shape[0], pairs[0].shape[1]
-    count = pairs[2].shape[1]
+def grad_rest(place, lefts, grads, rights, projt, entries, fsdp, slots):
+    width, tokens = 2 * lefts[0].shape[0], lefts[0].shape[1]
     rows = width // (2 * slots)
     wide = 4 * width // fsdp
     return call(
-        grad_rest_kernel,
+        functools.partial(grad_rest_kernel, len(grads) // 2),
         "grad_rest",
         [sds((2, 2, rows + 16, wide), BF)] * 4,
-        (*pairs, small, small_other),
+        (*lefts, *grads, *rights, projt),
         scratch=[
             pltpu.VMEM((slots, rows, 3 * width), BF),
             pltpu.VMEM((slots, rows, width), BF),
+            pltpu.VMEM((2 * tokens, 2 * width), BF),
             pltpu.VMEM((1, entries), F32),
             pltpu.VMEM((fsdp, slots, 16, wide), BF),
             pltpu.VMEM((16, wide), F32),
-            pltpu.VMEM(small.shape, F32),
+            pltpu.VMEM(projt.shape[::-1], F32),
         ],
         place=place,
-        flops=width * width * (4 * count + 4 * tokens),
+        flops=width * width * 8 * tokens,
+        vmem=20,
     )
 
 
@@ -1164,7 +1159,7 @@
         (RATE_VEC, 0.0),
     )
 
-    own, own_first, own_rest = pack(
+    (own, own_first, own_up, own_down), held = pack(
         place,
         qkv_weight,
         out_weight,
@@ -1173,7 +1168,7 @@
         proj_weight,
         vec_weight,
     )
-    rows_first, rows_up = own_first.shape[0], own_rest.shape[0] // 2
+    rows_first, rows_up = own_first.shape[0], own_up.shape[0]
 
     def across(value, name):
         return swap_fsdp(value, 1, name), swap_fsdp(value, 2, name)
@@ -1190,8 +1185,8 @@
         jnp.where(live[:, :, None], cotangent, jnp.zeros_like(cotangent)),
         ((0, 0), (0, half - marked), (0, 0)),
     ).reshape(seqs * half, width)
-    back_first, own_x, own_y, own_rest, own, frontt_give, xt_give, dy, front = tie(
-        back_first, own_x, own_y, own_rest, own, frontt_give, xt_give, dy, front
+    back_first, own_x, own_y, own_up, own_down, own, frontt_give, xt_give, dy, front = tie(
+        back_first, own_x, own_y, own_up, own_down, own, frontt_give, xt_give, dy, front
     )
 
     def all_of(*arrays):
@@ -1199,11 +1194,11 @@
 
     far_first = all_of(*back_first)
     first_x, first_y = across(far_first, "first")
-    back_rest = [None, shift_slot(own_rest, 1, "rest"), None, shift_slot(own_rest, 3, "rest")]
+    back_up = [shift_slot(own_up, 1, "up"), None, shift_slot(own_up, 3, "up")]
     near = all_of(own, own_x, own_y)
     near_other = swap_core(near, "near_core")
-    own_x, own_y, own, far_first, first_x, first_y, own_rest, near, near_other, back_rest = tie(
-        own_x, own_y, own, far_first, first_x, first_y, own_rest, near, near_other, back_rest
+    own_x, own_y, far_first, first_x, first_y, own_up, own_down, near, near_other, back_up = tie(
+        own_x, own_y, far_first, first_x, first_y, own_up, own_down, near, near_other, back_up
     )
 
     tall, far = own.shape[0], far_first.shape[0]
@@ -1212,20 +1207,22 @@
     low = stack((own_x, 0, half_own), (first_x, 0, half_first))
     high = stack((own_y, half_own, tall), (first_y, half_first, far))
     diagonal = [swap_fsdp(low, 2, "diag"), swap_fsdp(high, 1, "diag")]
-    back_rest[2] = shift_slot(own_rest, 2, "rest")
+    back_up[1] = shift_slot(own_up, 2, "up")
+    back_down = [shift_slot(own_down, 1, "down"), None, None]
     first = all_of(far_first, first_x, first_y)
     first_other = swap_core(first, "first_core")
-    diagonal, first_other, back_rest = tie(diagonal, first_other, back_rest)
+    diagonal, first_other, back_up, back_down, own_down = tie(
+        diagonal, first_other, back_up, back_down, own_down
+    )
     diagonal = all_of(*diagonal)
     diagonal_other = swap_core(diagonal, "diag_core")
-    diagonal, diagonal_other = tie(diagonal, diagonal_other)
     high_at = half_own + half_first
 
     def near_segments(first, rows):
         return segments_of(0, tall, [(first, 0, rows)], half_own, 1, 0, high_at)
 
-    far_up = stack(*((a, 0, rows_up) for a in back_rest[1:]))
-    far_down = stack(*((a, rows_up, 2 * rows_up) for a in back_rest[1:]))
+    far_up = all_of(*back_up)
+    back_down[1:] = [shift_slot(own_down, k, "down") for k in (2, 3)]
     up_x, up_y = across(far_up, "up")
     blocks = [(k * rows_first, k + 1, rows_first) for k in range(3)]
     qkv_full, out_full, vec, proj, projt = first_whole(
@@ -1240,7 +1237,8 @@
         entries,
     )
     q_front, q_rest, kv, kvp = make_qkv(front, rest, x, qkv_full, vec, proj)
-    up_x, up_y, q_front, far_down = tie(up_x, up_y, q_front, far_down)
+    up_x, up_y, q_front, back_down = tie(up_x, up_y, q_front, back_down)
+    far_down = all_of(*back_down)
 
     far = far_up.shape[0]
     half_up = far // 32 * 16
@@ -1296,12 +1294,15 @@
         fsdp,
         slots,
     )
-    act_front, slope, act_give = lift(place, low_front, up_full, vec, m2, True)
+    act_front, slope, act_give = lift(place, low_front, up_full, vec, m2, True, range(fsdp))
     down_diagonal, down_other, act_front, act_give, lowt_came, attendedt_came = tie(
         down_diagonal, down_other, act_front, act_give, lowt_came, attendedt_came
     )
     down_diagonal = all_of(*down_diagonal)
     down_diagonal_other = swap_core(down_diagonal, "downdiag_core")
+    down_diagonal, down_diagonal_other, act_give = tie(
+        down_diagonal, down_diagonal_other, act_give
+    )
     act_came = swap_core(act_give, "given_core")
     down_full = down_whole(
         place,
@@ -1314,15 +1315,17 @@
         width,
     )
     out_front, d_sum, d_low, d_lowt, two_sums = lower(
-        act_front, h_front, down_full, vec, marks_two, dy
+        [act_front], h_front, down_full, vec, marks_two, dy
     )
 
     def send(parts, name):
         send_x, stay_x, send_y, stay_y = parts
         return swap_fsdp(send_x, 1, name), swap_fsdp(send_y, 2, name), stay_x, stay_y
 
-    def forward(from_x, from_y, stay_x, stay_y, name):
-        over_y, over_x, kept = second_stage(stay_x, from_x, stay_y, from_y)
+    def add_up(from_x, from_y, stay_x, stay_y):
+        return second_stage(stay_x, from_x, stay_y, from_y)
+
+    def forward(over_y, over_x, kept, name):
         return kept, swap_fsdp(over_y, 2, name), swap_fsdp(over_x, 1, name)
 
     def along_z(pieces, name):
@@ -1336,96 +1339,83 @@
     )
     d_hidden_came = swap_core(d_hidden, "d_hidden_core")
     parts_down = grad_down(place, d_lowt, d_lowt_came, act_front, act_came, rows_up, slots)
-    parts_down, d_hidden_came, d_hidden = tie(parts_down, d_hidden_came, d_hidden)
+    parts_down, d_hidden_came, d_hidden, kv = tie(parts_down, d_hidden_came, d_hidden, kv)
     sent_down = send(parts_down, "gdown")
+    kv_came = swap_core(kv, "given_core")
     parts_up = grad_up(place, lowt, lowt_came, d_hidden, d_hidden_came, fsdp, slots)
     frontt_came, xt_came = cores((frontt_give, xt_give), "given_core")
     parts_up, d_hidden, frontt_came, xt_came = tie(parts_up, d_hidden, frontt_came, xt_came)
-    d_first, d_first_low, d_attended, one_sums = first_back(
-        d_hidden, up_full, d_sum, kept, vec, out_full, (ends[0], ends[1])
+    d_first, d_first_low, d_attended, sums = first_back(
+        d_hidden, up_full, d_sum, kept, vec, out_full, up_sums, two_sums, (ends[0], ends[1])
     )
     d_attended = d_attended.reshape(seqs, half, width)
-    got = attend_back(0, q_front, kvp, d_attended)
-    got, d_first_low, sent_down, parts_up = tie(got, d_first_low, sent_down, parts_up)
-    over_down = forward(*sent_down, "gdown2")
-    d_first_low_came = swap_core(d_first_low, "d_low_core")
+    grads = [attend_back(0, q_front, kvp, d_attended)]
+    grads, d_first_low, sums, sent_down, parts_up, kv_came = tie(
+        grads, d_first_low, sums, sent_down, parts_up, kv_came
+    )
+    over_down = forward(*add_up(*sent_down), "gdown2")
+    d_first_low_came, sums_came = cores((d_first_low, sums), "d_low_core")
+    grads_came = cores(grads, "d_qkv_core")
     for s in range(1, seqs):
-        got = attend_back(s, q_front, kvp, d_attended, got)
-    d_q, d_k, d_v, q_sums = got
-    d_kv, small = spread(d_k, d_v, kv, projt, q_sums, one_sums, up_sums, two_sums, entries)
-    d_kv, small, over_down, d_first_low_came, d_q, parts_up = tie(
-        d_kv, small, over_down, d_first_low_came, d_q, parts_up
+        grads.append(attend_back(s, q_front, kvp, d_attended))
+    grads, over_down, d_first_low_came, sums_came, grads_came, parts_up = tie(
+        grads, over_down, d_first_low_came, sums_came, grads_came, parts_up
     )
     sent_up = send(parts_up, "gup")
-    d_kv_came, small_came, d_q_came = cores((d_kv, small, d_q), "d_kv_core")
-    d_kv_came, small_came, d_q_came, over_down = tie(d_kv_came, small_came, d_q_came, over_down)
-    last_down = along_z((over_down,), "gdown3")
-    tall = 2 * width
+    grads_came = grads_came + cores(grads[1:], "d_qkv_core")
+    grads_came, over_down = tie(grads_came, over_down)
+    owns_down, (one, two, three) = third_stage(over_down)
+    one, three = shift_slot(one, 1, "gdown3"), shift_slot(three, 3, "gdown3")
     parts_first = grad_rest(
         place,
-        (
-            xt,
-            xt_came,
-            frontt,
-            frontt_came,
-            attendedt,
-            attendedt_came,
-            flat(d_q),
-            flat(d_q_came),
-            d_kv.reshape(rows, tall),
-            d_kv_came.reshape(rows, tall),
-            d_first_low,
-            d_first_low_came,
-        ),
-        small,
-        small_came,
+        (xt, xt_came, frontt, frontt_came, attendedt, attendedt_came),
+        grads + grads_came,
+        (d_first_low, d_first_low_came, kv, kv_came, sums, sums_came),
+        projt,
         entries,
         fsdp,
         slots,
     )
-    parts_first, low_rest, d_q, sent_up = tie(parts_first, low_rest, d_q, sent_up)
-    over_up = forward(*sent_up, "gup2")
-    parts_first, last_down = tie(parts_first, last_down)
+    parts_first, low_rest, sent_up, one, two, three = tie(
+        parts_first, low_rest, sent_up, one, two, three
+    )
+    last_down = (owns_down, (one, shift_slot(two, 2, "gdown3"), three))
+    over_up = forward(*add_up(*sent_up), "gup2")
+    act_rest = lift(place, low_rest, up_full, vec, m2, False, range(fsdp // 2))
+    parts_first, act_rest, over_up, last_down, grads, low_rest = tie(
+        parts_first, act_rest, over_up, last_down, grads, low_rest
+    )
     sent_first = send(parts_first, "gfirst")
-    act_rest = lift(place, low_rest, up_full, vec, m2, False)[0]
-    act_rest, over_up, last_down = tie(act_rest, over_up, last_down)
     last_up = along_z((over_up,), "gup3")
+    act_rest += lift(place, low_rest, up_full, vec, m2, False, range(fsdp // 2, fsdp))
     out_rest = lower(act_rest, h_rest, down_full, vec, marks_two)[0]
     output = restore(
         out_front.reshape(seqs, half, width), out_rest.reshape(seqs, half, width), back
     ).reshape(rows, width)
+    sent_first, output, grads, last_up, last_down = tie(
+        sent_first, output, grads, last_up, last_down
+    )
+    over_first = forward(*add_up(*sent_first), "gfirst2")
     g_down, squares_down = last_stage(*last_down)
-    sent_first, output, last_up, d_q = tie(sent_first, output, last_up, d_q)
-    over_first = forward(*sent_first, "gfirst2")
+    g_up, squares_up = last_stage(*last_up)
+    over_first, squares_down, squares_up, grads = tie(over_first, squares_down, squares_up, grads)
+    last_first = along_z((over_first,), "gfirst3")
     grad_input = input_back(
-        d_kv, d_q, d_first.reshape(seqs, half, width), qkv_full, back
+        projt, d_first.reshape(seqs, half, width), qkv_full, back, grads
     ).reshape(rows, width)
-    g_up, squares_up = last_stage(*last_up)
-    over_first, grad_input = tie(over_first, grad_input)
-    last_first = along_z((over_first,), "gfirst3")
+    last_first, grad_input = tie(last_first, grad_input)
     g_first, squares_first = last_stage(*last_first)
     squares_rest = squares_up + squares_down
     squares = sum_everywhere(squares_first + squares_rest)
-    states = (
-        qkv_weight,
-        qkv_moment,
-        qkv_second,
-        out_weight,
-        out_moment,
-        out_second,
-        up_weight,
-        up_moment,
-        up_second,
-        down_projection_weight.T,
-        down_moment.T,
-        down_second.T,
-        proj_weight,
-        proj_moment,
-        proj_second,
-        vec_weight,
-        vec_moment,
-        vec_second,
-    )
+    moments = (
+        (qkv_moment, qkv_second),
+        (out_moment, out_second),
+        (up_moment, up_second),
+        (down_moment.T, down_second.T),
+        (proj_moment, proj_second),
+        (vec_moment, vec_second),
+    )
+    states = [a for weight, pair in zip(held, moments) for a in (weight, *pair)]
     new = update(place, squares, g_first, g_up, g_down, states, rates)
     norm, new = new[0].reshape(()), list(new[1:])
     new[12:16] = [v.T for v in new[12:16]]

time: 267 us -> 236 us (0.88)
  waiting for transfers between devices: 88.1 us -> 67.9 us
  local copies, waits for them, and re-layouts: 11.6 us -> 2.44 us
  Pallas kernels: 93.8 us -> 90.4 us
    ppermute x18 -> x21, waiting for transfers between devices: 54.1 us -> 37.3 us  [shift_slot(): return lax.ppermute(value, 'dp', [(i, (i + 2 * by) % n) for i in range(n)])]
    unnamed x105 -> x69, local copies, waits for them, and re-layouts: 10.6 us -> 1.49 us
    ppermute x19 -> x20, waiting for transfers between devices: 12.1 us -> 5.45 us  [swap_core(): return lax.ppermute(value, 'dp', [(i, i ^ 1) for i in range(n)])]
    pallas_call x45, Pallas kernels: 93.8 us -> 90.4 us  [call(): pl.pallas_call(kernel, name=name, out_shape=outs, in_specs=specs, out_spe...]
    ppermute x29, waiting for transfers between devices: 22 us -> 25.2 us  [swap_fsdp(): return lax.ppermute(value, 'fsdp', [(i, i ^ bits) for i in range(n)])]
    ppermute x18 -> x21, starting transfers between devices: 31.9 us -> 30.9 us  [shift_slot(): return lax.ppermute(value, 'dp', [(i, (i + 2 * by) % n) for i in range(n)])]
  transfers between devices with their start and end apart: 66 -> 70, of which waited for: 26 -> 30; matrix products, arithmetic and copies ran while one was open for 1% -> 1% of each run, Pallas kernels for 33% -> 36%
where the time goes in v3:
time: 236 us; the launch traced here: 232 us
  Pallas kernels  90.4 us (38%)
  waiting for transfers between devices  67.9 us (29%)
  starting transfers between devices  66.9 us (28%)
  local copies, waits for them, and re-layouts  2.44 us (1%)
    pallas_call x45, Pallas kernels, call(): pl.pallas_call(kernel, name=name, out_shape=outs, in_specs=specs, out_spe...  90.4 us
    ppermute x21, waiting for transfers between devices, shift_slot(): return lax.ppermute(value, 'dp', [(i, (i + 2 * by) % n) for i in range(n)])  37.3 us
    ppermute x29, starting transfers between devices, swap_fsdp(): return lax.ppermute(value, 'fsdp', [(i, i ^ bits) for i in range(n)])  32.9 us
    ppermute x21, starting transfers between devices, shift_slot(): return lax.ppermute(value, 'dp', [(i, (i + 2 * by) % n) for i in range(n)])  30.9 us
    ppermute x29, waiting for transfers between devices, swap_fsdp(): return lax.ppermute(value, 'fsdp', [(i, i ^ bits) for i in range(n)])  25.2 us
    ppermute x20, waiting for transfers between devices, swap_core(): return lax.ppermute(value, 'dp', [(i, i ^ 1) for i in range(n)])  5.45 us
  transfers between devices with their start and end apart: 70, of which 30 were waited for; matrix products, arithmetic and copies ran while one was open for 1% of the time, Pallas kernels for 36%

profile of v3, /device:TPU:0, one launch (start us, length us, event | category | flops | bytes accessed | tf_op | source)
XLA Modules:
  0.0 231.6 jit_solution(13634932379533066752)
XLA Ops:
  1.3 3.2 %pack_weights.1 = (bf16[304,768]{1,0:T(8,128)(2,1)}, bf16[112,768]{1,0:T(8,128)(2,1)}, bf16[96,768]{1,0:T(8,128)(2,1)}, bf16[96,768]{1,0:T(8,128)(2,1)}, f32[96,...) custom-call(s32[3]{0:T(128)} %pad_add_fusion.place, ...), custom_call_target="tpu_custom_call" | custom-call | bytes 2738 | tf_op jit(solution)/shard_map/pack_weights/pallas_call | solution.py:54
  4.5 5.1 %collective-permute-start.2 = (bf16[112,768]{1,0:T(8,128)(2,1)}, bf16[112,768]{1,0:T(8,128)(2,1)S(1)}, u32[]{:S(2)}, u32[]{:S(2)}) collective-permute-start(bf16[112,768]{1,0:T(8,128)(2,1)} %get-tuple-element.303), channel_id=1, source_target_pairs={{0,6},{1,7},{2,0},{3,1},{4,2},{5,3},{6,4},{7,5},{8,14},{9,15},{10,... | collective-permute-start | bytes 516104 | tf_op jit(solution)/shard_map/first_z3/ppermute | solution.py:800
  10.6 1.5 collective-permute-start.4
  17.3 2.4 %order_rows.1 = (bf16[2,256,768]{2,1,0:T(8,128)(2,1)S(1)}, bf16[2,256,768]{2,1,0:T(8,128)(2,1)S(1)}, bf16[384,512]{1,0:T(8,128)(2,1)S(1)}, bf16[384,512]{1,0:T(8...) custom-call(s32[3]{0:T(128)S(1)} %copy-done.21, ...), custom_call_target="tpu_custom_call" | custom-call | flops 805306 | bytes 6555 | tf_op jit(solution)/shard_map/order_rows/pallas_call | solution.py:54
  19.6 4.8 %collective-permute-done.1.refs_1_ = bf16[112,768]{1,0:T(8,128)(2,1)S(1)} collective-permute-done((bf16[112,768]{1,0:T(8,128)(2,1)}, bf16[112,768]{1,0:T(8,128)(2,1)S(1)}, u32[]{:S(2)}, u32[]{:S(2)}) %collective-permute-start.1) | collective-permute-done | bytes 172064 | tf_op jit(solution)/shard_map/first_z2/ppermute | solution.py:800
  24.7 1.6 collective-permute-start.6
  29.8 3.7 %collective-permute-done.9.refs_2_ = bf16[96,768]{1,0:T(8,128)(2,1)S(1)} collective-permute-done((bf16[96,768]{1,0:T(8,128)(2,1)S(1)}, bf16[96,768]{1,0:T(8,128)(2,1)S(1)}, u32[]{:S(2)}, u32[]{:S(2)}) %collective-permute-start.9) | collective-permute-done | bytes 147488 | tf_op jit(solution)/shard_map/up_z3/ppermute | solution.py:800
  33.4 5.4 %collective-permute-done.8.refs_0_ = bf16[96,768]{1,0:T(8,128)(2,1)S(1)} collective-permute-done((bf16[96,768]{1,0:T(8,128)(2,1)S(1)}, bf16[96,768]{1,0:T(8,128)(2,1)S(1)}, u32[]{:S(2)}, u32[]{:S(2)}) %collective-permute-start.8) | collective-permute-done | bytes 147488 | tf_op jit(solution)/shard_map/up_z1/ppermute | solution.py:800
  40.4 1.6 collective-permute-start.11
  42.5 2.8 %collective-permute-start.13 = (bf16[96,768]{1,0:T(8,128)(2,1)S(1)}, bf16[96,768]{1,0:T(8,128)(2,1)S(1)}, u32[]{:S(2)}, u32[]{:S(2)}) collective-permute-start(bf16[96,768]{1,0:T(8,128)(2,1)S(1)} %copy-done.33), channel_id=1, source_target_pairs={{0,4},{1,5},{2,6},{3,7},{4,0},{5,1},{6,2},{7,3},{8,12},{9,13},{10,... | collective-permute-start | bytes 442376 | tf_op jit(solution)/shard_map/up_z2/ppermute | solution.py:800
  45.3 10.2 %collective-permute-done.13.refs_1_ = bf16[96,768]{1,0:T(8,128)(2,1)S(1)} collective-permute-done((bf16[96,768]{1,0:T(8,128)(2,1)S(1)}, bf16[96,768]{1,0:T(8,128)(2,1)S(1)}, u32[]{:S(2)}, u32[]{:S(2)}) %collective-permute-start.13) | collective-permute-done | bytes 147488 | tf_op jit(solution)/shard_map/up_z2/ppermute | solution.py:800
  55.7 1.6 collective-permute-start.16
  59.9 2.0 whole_first.1
  62.0 6.2 %make_qkv.1 = (bf16[2,256,768]{2,1,0:T(8,128)(2,1)S(1)}, bf16[2,256,768]{2,1,0:T(8,128)(2,1)S(1)}, bf16[2,512,1536]{2,1,0:T(8,128)(2,1)S(1)}, bf16[2,256,1536]{2,1,0:T(8,128)(2,1)S(1)}) custom-call(bf16[2,256,768]{2,1,0:T(8,128)(2,1)S(1)} %get-tuple-element.330.front, bf16[2,256,768]{2,1,0:T(8,128)(2,1)S(1)} %get-tuple-element.331.rest, ...), custom_call_target="tpu_custom_call" | custom-call | flops 4429185 | bytes 13278 | tf_op jit(solution)/shard_map/make_qkv/pallas_call | solution.py:54
  68.1 1.8 collective-permute-done.18.refs_1_
  70.1 1.6 collective-permute-start.21
  74.3 4.1 %attend.1 = (bf16[2,256,768]{2,1,0:T(8,128)(2,1)S(1)}, bf16[2,256,768]{2,1,0:T(8,128)(2,1)S(1)}) custom-call(bf16[2,256,768]{2,1,0:T(8,128)(2,1)S(1)} %get-tuple-element.343.q_front.queries, bf16[2,256,768]{2,1,0:T(8,128)(2,1)S(1)} %get-tuple-element.344.q_rest, bf16[2,256,1536]{2,1,0:T(8,128)(2,1)S(1)} %get-tuple-element.345.kvp), custom_call_target="tpu_custom_call" | custom-call | flops 1610612 | bytes 4718 | tf_op jit(solution)/shard_map/attend/pallas_call | solution.py:54
  78.4 1.9 join_front.1
  80.7 1.7 join_rest.1
  82.4 6.3 %collective-permute-done.25.refs_2_ = bf16[288,768]{1,0:T(8,128)(2,1)S(1)} collective-permute-done((bf16[288,768]{1,0:T(8,128)(2,1)S(1)}, bf16[288,768]{1,0:T(8,128)(2,1)S(1)}, u32[]{:S(2)}, u32[]{:S(2)}) %collective-permute-start.25) | collective-permute-done | bytes 442400 | tf_op jit(solution)/shard_map/down_y/ppermute | solution.py:806
  92.4 7.0 %lift_front.1 = (bf16[512,3072]{1,0:T(8,128)(2,1)S(1)}, bf16[512,3072]{1,0:T(8,128)(2,1)S(1)}, bf16[512,1536]{1,0:T(8,128)(2,1)S(1)}) custom-call(s32[3]{0:T(128)S(1)} %copy-done.21, bf16[512,768]{1,0:T(8,128)(2,1)S(1)} %get-tuple-element.364.low, bf16[4,768,768]{2,1,0:T(8,128)(2,1)S(1)} %whole_up.1.weight.up, ...), custom_call_target="tpu_custom_call" | custom-call | flops 2415919 | bytes 13409 | tf_op jit(solution)/shard_map/lift_front/pallas_call | solution.py:54
  99.6 1.8 collective-permute-done.31.refs_7_
  102.6 4.6 %lower_front.1 = (bf16[512,768]{1,0:T(8,128)(2,1)S(1)}, f32[512,768]{1,0:T(8,128)S(1)}, bf16[512,768]{1,0:T(8,128)(2,1)S(1)}, bf16[768,512]{1,0:T(8,128)(2,1)S(1)}, f32[8,768]{1,0:T(8,128)S(1)}) custom-call(bf16[512,3072]{1,0:T(8,128)(2,1)S(1)} %get-tuple-element.372.refs_0_.active, f32[512,768]{1,0:T(8,128)S(1)} %get-tuple-element.373.refs_1_, ...), custom_call_target="tpu_custom_call" | custom-call | flops 2415919 | bytes 14220 | tf_op jit(solution)/shard_map/lower_front/pallas_call | solution.py:54
  107.6 2.7 %hidden_back.1 = (bf16[512,3072]{1,0:T(8,128)(2,1)S(1)}, f32[1,3072]{1,0:T(1,128)S(1)}) custom-call(bf16[512,768]{1,0:T(8,128)(2,1)S(1)} %get-tuple-element.382.d_low, bf16[768,3072]{1,0:T(8,128)(2,1)S(1)} %whole_down.1.refs_2_.weight.refs_3_, bf16[512,3072]{1,0:T(8,128)(2,1)S(1)} %get-tuple-element.383.slope), custom_call_target="tpu_custom_call" | custom-call | flops 2415919 | bytes 11808 | tf_op jit(solution)/shard_map/hidden_back/pallas_call | solution.py:54
  110.5 4.1 %grad_down.1 = (bf16[2,2,96,768]{3,2,1,0:T(8,128)(2,1)S(1)}, bf16[2,2,96,768]{3,2,1,0:T(8,128)(2,1)S(1)}, bf16[2,2,96,768]{3,2,1,0:T(8,128)(2,1)S(1)}, bf16[2,2,96,768]{3,2,1,0:T(8,128)(2,1)S(1)}) custom-call(s32[3]{0:T(128)S(1)} %copy-done.21, bf16[768,512]{1,0:T(8,128)(2,1)S(1)} %get-tuple-element.381.d_lowt, ...), custom_call_target="tpu_custom_call" | custom-call | flops 4831838 | bytes 8650 | tf_op jit(solution)/shard_map/grad_down/pallas_call | solution.py:54
  118.7 4.3 %grad_up.1 = (bf16[2,2,96,768]{3,2,1,0:T(8,128)(2,1)}, bf16[2,2,96,768]{3,2,1,0:T(8,128)(2,1)S(1)}, bf16[2,2,96,768]{3,2,1,0:T(8,128)(2,1)}, bf16[2,2,96,768]{3,2,1,0:T(8,128)(2,1)S(1)}) custom-call(s32[3]{0:T(128)S(1)} %copy-done.21, bf16[384,512]{1,0:T(8,128)(2,1)S(1)} %get-tuple-element.348.lowt, bf16[384,512]{1,0:T(8,128)(2,1)S(1)} %collective-permute-done.29.lowt_other, ...), custom_call_target="tpu_custom_call" | custom-call | flops 2415919 | bytes 9437 | tf_op jit(solution)/shard_map/grad_up/pallas_call | solution.py:54
  123.4 5.1 %first_back.1 = (f32[512,768]{1,0:T(8,128)S(1)}, bf16[512,768]{1,0:T(8,128)(2,1)S(1)}, bf16[512,768]{1,0:T(8,128)(2,1)S(1)}, f32[16,768]{1,0:T(8,128)S(1)}) custom-call(bf16[512,3072]{1,0:T(8,128)(2,1)S(1)} %get-tuple-element.409.d_hidden, bf16[4,768,768]{2,1,0:T(8,128)(2,1)S(1)} %whole_up.1.weight.up, f32[512,768]{1,0:T(8,128)S(1)} %get-tuple-element.410.d_sum, ...), custom_call_target="tpu_custom_call" | custom-call | flops 3019898 | bytes 15461 | tf_op jit(solution)/shard_map/first_back/pallas_call | solution.py:54
  128.5 3.6 %attend_back.2.refs_6_.refs_0_ = bf16[768,768]{1,0:T(8,128)(2,1)S(1)} custom-call(bf16[2,256,768]{2,1,0:T(8,128)(2,1)S(1)} %get-tuple-element.343.q_front.queries, bf16[2,256,1536]{2,1,0:T(8,128)(2,1)S(1)} %get-tuple-element.345.kvp, bf16[2,256,768]{2,1,0:T(8,128)(2,1)S(1)} %bitcast.29), custom_call_target="tpu_custom_call" | custom-call | flops 1006632 | bytes 4325 | tf_op jit(solution)/shard_map/attend_back/pallas_call | solution.py:54
  135.3 3.4 %attend_back.3.refs_7_.refs_1_ = bf16[768,768]{1,0:T(8,128)(2,1)S(1)} custom-call(bf16[2,256,768]{2,1,0:T(8,128)(2,1)S(1)} %get-tuple-element.343.q_front.queries, bf16[2,256,1536]{2,1,0:T(8,128)(2,1)S(1)} %get-tuple-element.345.kvp, bf16[2,256,768]{2,1,0:T(8,128)(2,1)S(1)} %bitcast.30), custom_call_target="tpu_custom_call" | custom-call | flops 1006632 | bytes 4325 | tf_op jit(solution)/shard_map/attend_back/pallas_call | solution.py:54
  138.7 4.2 %collective-permute-done.40.refs_1_ = bf16[2,96,768]{2,1,0:T(8,128)(2,1)S(1)} collective-permute-done((bf16[2,96,768]{2,1,0:T(8,128)(2,1)S(1)}, bf16[2,96,768]{2,1,0:T(8,128)(2,1)S(1)}, u32[]{:S(2)}, u32[]{:S(2)}) %collective-permute-start.40) | collective-permute-done | bytes 294944 | tf_op jit(solution)/shard_map/gdown2_y/ppermute | solution.py:806
  146.5 3.7 %collective-permute-start.49 = (bf16[96,768]{1,0:T(8,128)(2,1)S(1)}, bf16[96,768]{1,0:T(8,128)(2,1)S(1)}, u32[]{:S(2)}, u32[]{:S(2)}) collective-permute-start(bf16[96,768]{1,0:T(8,128)(2,1)S(1)} %get-tuple-element.466), channel_id=1, source_target_pairs={{0,6},{1,7},{2,0},{3,1},{4,2},{5,3},{6,4},{7,5},{8,14},{9,15},{10,... | collective-permute-start | bytes 442376 | tf_op jit(solution)/shard_map/gdown3_z3/ppermute | solution.py:800
  150.2 8.4 %grad_rest.1 = (bf16[2,2,112,768]{3,2,1,0:T(8,128)(2,1)S(1)}, bf16[2,2,112,768]{3,2,1,0:T(8,128)(2,1)S(1)}, bf16[2,2,112,768]{3,2,1,0:T(8,128)(2,1)S(1)}, bf16[2,2,112,768]{3,2,1,0:T(8,128)(2,1)S(1)}) custom-call(s32[3]{0:T(128)S(1)} %copy-done.21, bf16[384,1024]{1,0:T(8,128)(2,1)S(1)} %get-tuple-element.302.refs_0_, ...), custom_call_target="tpu_custom_call" | custom-call | flops 4831838 | bytes 18841 | tf_op jit(solution)/shard_map/grad_rest/pallas_call | solution.py:54
  163.4 3.2 %lift_rest.2.refs_0_ = bf16[512,1536]{1,0:T(8,128)(2,1)S(1)} custom-call(s32[3]{0:T(128)S(1)} %copy-done.21, bf16[512,768]{1,0:T(8,128)(2,1)S(1)} %get-tuple-element.489.low, bf16[4,768,768]{2,1,0:T(8,128)(2,1)S(1)} %whole_up.1.weight.up, f32[1,9984]{1,0:T(1,128)S(1)} %get-tuple-element.338.vec.refs_3_.refs_4_), custom_call_target="tpu_custom_call" | custom-call | flops 1207959 | bytes 7117 | tf_op jit(solution)/shard_map/lift_rest/pallas_call | solution.py:54
  166.6 4.3 %collective-permute-done.52.refs_2_ = bf16[96,768]{1,0:T(8,128)(2,1)S(1)} collective-permute-done((bf16[96,768]{1,0:T(8,128)(2,1)S(1)}, bf16[96,768]{1,0:T(8,128)(2,1)S(1)}, u32[]{:S(2)}, u32[]{:S(2)}) %collective-permute-start.52) | collective-permute-done | bytes 147488 | tf_op jit(solution)/shard_map/gdown3_z2/ppermute | solution.py:800
  172.9 2.6 %collective-permute-start.56 = (bf16[96,768]{1,0:T(8,128)(2,1)S(1)}, bf16[96,768]{1,0:T(8,128)(2,1)S(1)}, u32[]{:S(2)}, u32[]{:S(2)}) collective-permute-start(bf16[96,768]{1,0:T(8,128)(2,1)S(1)} %get-tuple-element.499), channel_id=1, source_target_pairs={{0,4},{1,5},{2,6},{3,7},{4,0},{5,1},{6,2},{7,3},{8,12},{9,13},{10,... | collective-permute-start | bytes 442376 | tf_op jit(solution)/shard_map/gup3_z2/ppermute | solution.py:800
  176.9 3.2 %lift_rest.3.refs_1_ = bf16[512,1536]{1,0:T(8,128)(2,1)S(1)} custom-call(s32[3]{0:T(128)S(1)} %copy-done.21, bf16[512,768]{1,0:T(8,128)(2,1)S(1)} %get-tuple-element.489.low, bf16[4,768,768]{2,1,0:T(8,128)(2,1)S(1)} %whole_up.1.weight.up, f32[1,9984]{1,0:T(1,128)S(1)} %get-tuple-element.338.vec.refs_3_.refs_4_), custom_call_target="tpu_custom_call" | custom-call | flops 1207959 | bytes 7117 | tf_op jit(solution)/shard_map/lift_rest/pallas_call | solution.py:54
  180.1 3.1 %lower_rest.1 = bf16[512,768]{1,0:T(8,128)(2,1)S(1)} custom-call(bf16[512,1536]{1,0:T(8,128)(2,1)S(1)} %lift_rest.2.refs_0_, bf16[512,1536]{1,0:T(8,128)(2,1)S(1)} %lift_rest.3.refs_1_, f32[512,768]{1,0:T(8,128)S(1)} %get-tuple-element.490.refs_2_, bf16[768,3072]{1,0:T(8,128)(2,1)S(1)} %whole_down.1.refs_2_.weight.refs_3_, ...), custom_call_target="tpu_custom_call" | custom-call | flops 2415919 | bytes 10263 | tf_op jit(solution)/shard_map/lower_rest/pallas_call | solution.py:54
  183.3 2.1 restore_order.1
  185.9 1.8 collective-permute-done.53.from_x
  191.4 5.1 %collective-permute-done.58.refs_1_ = bf16[2,112,768]{2,1,0:T(8,128)(2,1)S(1)} collective-permute-done((bf16[2,112,768]{2,1,0:T(8,128)(2,1)S(1)}, bf16[2,112,768]{2,1,0:T(8,128)(2,1)S(1)}, u32[]{:S(2)}, u32[]{:S(2)}) %collective-permute-start.58) | collective-permute-done | bytes 344096 | tf_op jit(solution)/shard_map/gfirst2_y/ppermute | solution.py:806
  197.6 1.7 collective-permute-start.60
  200.1 1.6 collective-permute-start.62
  201.9 6.5 %input_back.1 = bf16[2,512,768]{2,1,0:T(8,128)(2,1)} custom-call(bf16[512,256]{1,0:T(8,128)(2,1)S(1)} %get-tuple-element.451.refs_16_.projt, f32[2,256,768]{2,1,0:T(8,128)S(1)} %bitcast.33, bf16[768,2304]{1,0:T(8,128)(2,1)S(1)} %get-tuple-element.337.weight, bf16[2,512,512]{2,1,0:T(8,128)(2,1)S(1)} %get-tuple-element.491.back, ...), custom_call_target="tpu_custom_call" | custom-call | flops 4429185 | bytes 10354 | tf_op jit(solution)/shard_map/input_back/pallas_call | solution.py:54
  208.4 2.5 %collective-permute-done.61.refs_2_ = bf16[112,768]{1,0:T(8,128)(2,1)S(1)} collective-permute-done((bf16[112,768]{1,0:T(8,128)(2,1)S(1)}, bf16[112,768]{1,0:T(8,128)(2,1)S(1)}, u32[]{:S(2)}, u32[]{:S(2)}) %collective-permute-start.61) | collective-permute-done | bytes 172064 | tf_op jit(solution)/shard_map/gfirst3_z2/ppermute | solution.py:800
  211.2 1.6 collective-permute-start.65
  217.5 4.1 %collective-permute-start.68 = (f32[8,128]{1,0:T(8,128)S(1)}, f32[8,128]{1,0:T(8,128)S(1)}, u32[]{:S(2)}, u32[]{:S(2)}) collective-permute-start(f32[8,128]{1,0:T(8,128)S(1)} %add_add_fusion.1), channel_id=1, source_target_pairs={{0,6},{1,7},{2,0},{3,1},{4,2},{5,3},{6,4},{7,5},{8,14},{9,15},{10,... | collective-permute-start | bytes 12296 | tf_op jit(solution)/shard_map/norm_z3/ppermute | solution.py:800
  222.9 4.1 %collective-permute-done.67 = f32[8,128]{1,0:T(8,128)S(1)} collective-permute-done((f32[8,128]{1,0:T(8,128)S(1)}, f32[8,128]{1,0:T(8,128)S(1)}, u32[]{:S(2)}, u32[]{:S(2)}) %collective-permute-start.67) | collective-permute-done | bytes 4128 | tf_op jit(solution)/shard_map/norm_z1/ppermute | solution.py:800
  228.4 3.0 %update.1 = (f32[1,1]{1,0:T(1,128)}, f32[96,576]{1,0:T(8,128)}, f32[96,576]{1,0:T(8,128)}, f32[96,576]{1,0:T(8,128)}, bf16[96,576]{1,0:T(8,128)(2,1)}, /*index=5...) custom-call(s32[3]{0:T(128)S(1)} %copy-done.21, ...), custom_call_target="tpu_custom_call" | custom-call | bytes 6803 | tf_op jit(solution)/shard_map/update/pallas_call | solution.py:54
  (220 shorter events, 57.2 us)
Async XLA Ops:
  4.5 15.1 %collective-permute-start.2 = (bf16[112,768]{1,0:T(8,128)(2,1)}, bf16[112,768]{1,0:T(8,128)(2,1)S(1)}, u32[]{:S(2)}, u32[]{:S(2)}) collective-permute-start(bf16[112,768]{1,0:T(8,128)(2,1)} %get-tuple-element.303), channel_id=1, source_target_pairs={{0,6},{1,7},{2,0},{3,1},{4,2},{5,3},{6,4},{7,5},{8,14},{9,15},{10,... | collective-permute-start | bytes 516104 | tf_op jit(solution)/shard_map/first_z3/ppermute | solution.py:800
  9.6 14.8 %collective-permute-start.1 = (bf16[112,768]{1,0:T(8,128)(2,1)}, bf16[112,768]{1,0:T(8,128)(2,1)S(1)}, u32[]{:S(2)}, u32[]{:S(2)}) collective-permute-start(bf16[112,768]{1,0:T(8,128)(2,1)} %get-tuple-element.303), channel_id=1, source_target_pairs={{0,4},{1,5},{2,6},{3,7},{4,0},{5,1},{6,2},{7,3},{8,12},{9,13},{10,... | collective-permute-start | bytes 516104 | tf_op jit(solution)/shard_map/first_z2/ppermute | solution.py:800
  9.6 14.8 %collective-permute-start = (bf16[112,768]{1,0:T(8,128)(2,1)}, bf16[112,768]{1,0:T(8,128)(2,1)S(1)}, u32[]{:S(2)}, u32[]{:S(2)}) collective-permute-start(bf16[112,768]{1,0:T(8,128)(2,1)} %get-tuple-element.303), channel_id=1, source_target_pairs={{0,2},{1,3},{2,4},{3,5},{4,6},{5,7},{6,0},{7,1},{8,10},{9,11},{10,... | collective-permute-start | bytes 516104 | tf_op jit(solution)/shard_map/first_z1/ppermute | solution.py:800
  10.6 13.8 %collective-permute-start.4 = (bf16[304,768]{1,0:T(8,128)(2,1)}, bf16[304,768]{1,0:T(8,128)(2,1)S(1)}, u32[]{:S(2)}, u32[]{:S(2)}) collective-permute-start(bf16[304,768]{1,0:T(8,128)(2,1)} %get-tuple-element.317.refs_0_), channel_id=1, source_target_pairs={{0,16},{8,24},{16,0},{24,8},{1,17},{9,25},{17,1},{25,9},{2,18},{10... | collective-permute-start | bytes 1400840 | tf_op jit(solution)/shard_map/own_y/ppermute | solution.py:806
  12.1 12.3 %collective-permute-start.3 = (bf16[304,768]{1,0:T(8,128)(2,1)}, bf16[304,768]{1,0:T(8,128)(2,1)S(1)}, u32[]{:S(2)}, u32[]{:S(2)}) collective-permute-start(bf16[304,768]{1,0:T(8,128)(2,1)} %get-tuple-element.317.refs_0_), channel_id=1, source_target_pairs={{0,8},{8,0},{16,24},{24,16},{1,9},{9,1},{17,25},{25,17},{2,10},{10... | collective-permute-start | bytes 1400840 | tf_op jit(solution)/shard_map/own_x/ppermute | solution.py:806
  24.5 15.6 %collective-permute-start.7 = (bf16[912,768]{1,0:T(8,128)(2,1)S(1)}, bf16[912,768]{1,0:T(8,128)(2,1)S(1)}, u32[]{:S(2)}, u32[]{:S(2)}) collective-permute-start(bf16[912,768]{1,0:T(8,128)(2,1)S(1)} %stack.29.refs_0_), channel_id=1, source_target_pairs={{0,1},{1,0},{2,3},{3,2},{4,5},{5,4},{6,7},{7,6},{8,9},{9,8},{10,11... | collective-permute-start | bytes 4202504 | tf_op jit(solution)/shard_map/near_core/ppermute | solution.py:794
  24.7 14.2 %collective-permute-start.6 = (bf16[336,768]{1,0:T(8,128)(2,1)S(1)}, bf16[336,768]{1,0:T(8,128)(2,1)S(1)}, u32[]{:S(2)}, u32[]{:S(2)}) collective-permute-start(bf16[336,768]{1,0:T(8,128)(2,1)S(1)} %stack.28.refs_0_), channel_id=1, source_target_pairs={{0,16},{8,24},{16,0},{24,8},{1,17},{9,25},{17,1},{25,9},{2,18},{10... | collective-permute-start | bytes 1548296 | tf_op jit(solution)/shard_map/first_y/ppermute | solution.py:806
  26.2 13.9 %collective-permute-start.5 = (bf16[336,768]{1,0:T(8,128)(2,1)S(1)}, bf16[336,768]{1,0:T(8,128)(2,1)S(1)}, u32[]{:S(2)}, u32[]{:S(2)}) collective-permute-start(bf16[336,768]{1,0:T(8,128)(2,1)S(1)} %stack.28.refs_0_), channel_id=1, source_target_pairs={{0,8},{8,0},{16,24},{24,16},{1,9},{9,1},{17,25},{25,17},{2,10},{10... | collective-permute-start | bytes 1548296 | tf_op jit(solution)/shard_map/first_x/ppermute | solution.py:806
  29.0 9.8 %collective-permute-start.8 = (bf16[96,768]{1,0:T(8,128)(2,1)S(1)}, bf16[96,768]{1,0:T(8,128)(2,1)S(1)}, u32[]{:S(2)}, u32[]{:S(2)}) collective-permute-start(bf16[96,768]{1,0:T(8,128)(2,1)S(1)} %copy-done.33), channel_id=1, source_target_pairs={{0,2},{1,3},{2,4},{3,5},{4,6},{5,7},{6,0},{7,1},{8,10},{9,11},{10,... | collective-permute-start | bytes 442376 | tf_op jit(solution)/shard_map/up_z1/ppermute | solution.py:800
  40.2 15.3 %collective-permute-start.12 = (bf16[1008,768]{1,0:T(8,128)(2,1)S(1)}, bf16[1008,768]{1,0:T(8,128)(2,1)S(1)}, u32[]{:S(2)}, u32[]{:S(2)}) collective-permute-start(bf16[1008,768]{1,0:T(8,128)(2,1)S(1)} %stack.32.refs_2_), channel_id=1, source_target_pairs={{0,1},{1,0},{2,3},{3,2},{4,5},{5,4},{6,7},{7,6},{8,9},{9,8},{10,11... | collective-permute-start | bytes 4644872 | tf_op jit(solution)/shard_map/first_core/ppermute | solution.py:794
  40.4 15.1 %collective-permute-start.11 = (bf16[320,768]{1,0:T(8,128)(2,1)S(1)}, bf16[320,768]{1,0:T(8,128)(2,1)S(1)}, u32[]{:S(2)}, u32[]{:S(2)}) collective-permute-start(bf16[320,768]{1,0:T(8,128)(2,1)S(1)} %stack.31), channel_id=1, source_target_pairs={{0,8},{8,0},{16,24},{24,16},{1,9},{9,1},{17,25},{25,17},{2,10},{10... | collective-permute-start | bytes 1474568 | tf_op jit(solution)/shard_map/diag_x/ppermute | solution.py:806
  42.0 13.6 %collective-permute-start.10 = (bf16[320,768]{1,0:T(8,128)(2,1)S(1)}, bf16[320,768]{1,0:T(8,128)(2,1)S(1)}, u32[]{:S(2)}, u32[]{:S(2)}) collective-permute-start(bf16[320,768]{1,0:T(8,128)(2,1)S(1)} %stack.30), channel_id=1, source_target_pairs={{0,16},{8,24},{16,0},{24,8},{1,17},{9,25},{17,1},{25,9},{2,18},{10... | collective-permute-start | bytes 1474568 | tf_op jit(solution)/shard_map/diag_y/ppermute | solution.py:806
  42.5 13.1 %collective-permute-start.13 = (bf16[96,768]{1,0:T(8,128)(2,1)S(1)}, bf16[96,768]{1,0:T(8,128)(2,1)S(1)}, u32[]{:S(2)}, u32[]{:S(2)}) collective-permute-start(bf16[96,768]{1,0:T(8,128)(2,1)S(1)} %copy-done.33), channel_id=1, source_target_pairs={{0,4},{1,5},{2,6},{3,7},{4,0},{5,1},{6,2},{7,3},{8,12},{9,13},{10,... | collective-permute-start | bytes 442376 | tf_op jit(solution)/shard_map/up_z2/ppermute | solution.py:800
  45.3 10.3 %collective-permute-start.14 = (bf16[96,768]{1,0:T(8,128)(2,1)S(1)}, bf16[96,768]{1,0:T(8,128)(2,1)S(1)}, u32[]{:S(2)}, u32[]{:S(2)}) collective-permute-start(bf16[96,768]{1,0:T(8,128)(2,1)S(1)} %copy-done.32), channel_id=1, source_target_pairs={{0,2},{1,3},{2,4},{3,5},{4,6},{5,7},{6,0},{7,1},{8,10},{9,11},{10,... | collective-permute-start | bytes 442376 | tf_op jit(solution)/shard_map/down_z1/ppermute | solution.py:800
  55.7 14.2 %collective-permute-start.16 = (bf16[288,768]{1,0:T(8,128)(2,1)S(1)}, bf16[288,768]{1,0:T(8,128)(2,1)S(1)}, u32[]{:S(2)}, u32[]{:S(2)}) collective-permute-start(bf16[288,768]{1,0:T(8,128)(2,1)S(1)} %stack.33.refs_0_), channel_id=1, source_target_pairs={{0,16},{8,24},{16,0},{24,8},{1,17},{9,25},{17,1},{25,9},{2,18},{10... | collective-permute-start | bytes 1327112 | tf_op jit(solution)/shard_map/up_y/ppermute | solution.py:806
  57.3 12.6 %collective-permute-start.15 = (bf16[288,768]{1,0:T(8,128)(2,1)S(1)}, bf16[288,768]{1,0:T(8,128)(2,1)S(1)}, u32[]{:S(2)}, u32[]{:S(2)}) collective-permute-start(bf16[288,768]{1,0:T(8,128)(2,1)S(1)} %stack.33.refs_0_), channel_id=1, source_target_pairs={{0,8},{8,0},{16,24},{24,16},{1,9},{9,1},{17,25},{25,17},{2,10},{10... | collective-permute-start | bytes 1327112 | tf_op jit(solution)/shard_map/up_x/ppermute | solution.py:806
  57.8 10.3 %collective-permute-start.19 = (bf16[96,768]{1,0:T(8,128)(2,1)S(1)}, bf16[96,768]{1,0:T(8,128)(2,1)S(1)}, u32[]{:S(2)}, u32[]{:S(2)}) collective-permute-start(bf16[96,768]{1,0:T(8,128)(2,1)S(1)} %copy-done.32), channel_id=1, source_target_pairs={{0,6},{1,7},{2,0},{3,1},{4,2},{5,3},{6,4},{7,5},{8,14},{9,15},{10,... | collective-permute-start | bytes 442376 | tf_op jit(solution)/shard_map/down_z3/ppermute | solution.py:800
  59.1 10.8 %collective-permute-start.18 = (bf16[96,768]{1,0:T(8,128)(2,1)S(1)}, bf16[96,768]{1,0:T(8,128)(2,1)S(1)}, u32[]{:S(2)}, u32[]{:S(2)}) collective-permute-start(bf16[96,768]{1,0:T(8,128)(2,1)S(1)} %copy-done.32), channel_id=1, source_target_pairs={{0,4},{1,5},{2,6},{3,7},{4,0},{5,1},{6,2},{7,3},{8,12},{9,13},{10,... | collective-permute-start | bytes 442376 | tf_op jit(solution)/shard_map/down_z2/ppermute | solution.py:800
  70.0 10.4 %collective-permute-start.22 = (bf16[864,768]{1,0:T(8,128)(2,1)S(1)}, bf16[864,768]{1,0:T(8,128)(2,1)S(1)}, u32[]{:S(2)}, u32[]{:S(2)}) collective-permute-start(bf16[864,768]{1,0:T(8,128)(2,1)S(1)} %stack.35.refs_2_), channel_id=1, source_target_pairs={{0,1},{1,0},{2,3},{3,2},{4,5},{5,4},{6,7},{7,6},{8,9},{9,8},{10,11... | collective-permute-start | bytes 3981320 | tf_op jit(solution)/shard_map/up_core/ppermute | solution.py:794
  70.1 10.2 %collective-permute-start.21 = (bf16[144,768]{1,0:T(8,128)(2,1)S(1)}, bf16[144,768]{1,0:T(8,128)(2,1)S(1)}, u32[]{:S(2)}, u32[]{:S(2)}) collective-permute-start(bf16[144,768]{1,0:T(8,128)(2,1)S(1)} %slice.13), channel_id=1, source_target_pairs={{0,8},{8,0},{16,24},{24,16},{1,9},{9,1},{17,25},{25,17},{2,10},{10... | collective-permute-start | bytes 663560 | tf_op jit(solution)/shard_map/updiag_x/ppermute | solution.py:806
  73.1 15.6 %collective-permute-start.25 = (bf16[288,768]{1,0:T(8,128)(2,1)S(1)}, bf16[288,768]{1,0:T(8,128)(2,1)S(1)}, u32[]{:S(2)}, u32[]{:S(2)}) collective-permute-start(bf16[288,768]{1,0:T(8,128)(2,1)S(1)} %stack.37.refs_0_), channel_id=1, source_target_pairs={{0,16},{8,24},{16,0},{24,8},{1,17},{9,25},{17,1},{25,9},{2,18},{10... | collective-permute-start | bytes 1327112 | tf_op jit(solution)/shard_map/down_y/ppermute | solution.py:806
  73.8 14.9 %collective-permute-start.24 = (bf16[288,768]{1,0:T(8,128)(2,1)S(1)}, bf16[288,768]{1,0:T(8,128)(2,1)S(1)}, u32[]{:S(2)}, u32[]{:S(2)}) collective-permute-start(bf16[288,768]{1,0:T(8,128)(2,1)S(1)} %stack.37.refs_0_), channel_id=1, source_target_pairs={{0,8},{8,0},{16,24},{24,16},{1,9},{9,1},{17,25},{25,17},{2,10},{10... | collective-permute-start | bytes 1327112 | tf_op jit(solution)/shard_map/down_x/ppermute | solution.py:806
  88.8 10.7 %collective-permute-start.28 = (bf16[864,768]{1,0:T(8,128)(2,1)S(1)}, bf16[864,768]{1,0:T(8,128)(2,1)S(1)}, u32[]{:S(2)}, u32[]{:S(2)}) collective-permute-start(bf16[864,768]{1,0:T(8,128)(2,1)S(1)} %stack.38.refs_2_), channel_id=1, source_target_pairs={{0,1},{1,0},{2,3},{3,2},{4,5},{5,4},{6,7},{7,6},{8,9},{9,8},{10,11... | collective-permute-start | bytes 3981320 | tf_op jit(solution)/shard_map/down_core/ppermute | solution.py:794
  88.9 10.6 %collective-permute-start.29 = (bf16[384,512]{1,0:T(8,128)(2,1)S(1)}, bf16[384,512]{1,0:T(8,128)(2,1)S(1)}, u32[]{:S(2)}, u32[]{:S(2)}) collective-permute-start(bf16[384,512]{1,0:T(8,128)(2,1)S(1)} %get-tuple-element.369), channel_id=1, source_target_pairs={{0,1},{1,0},{2,3},{3,2},{4,5},{5,4},{6,7},{7,6},{8,9},{9,8},{10,11... | collective-permute-start | bytes 1179656 | tf_op jit(solution)/shard_map/given_core/ppermute | solution.py:794
  89.4 10.1 %collective-permute-start.30 = (bf16[384,512]{1,0:T(8,128)(2,1)S(1)}, bf16[384,512]{1,0:T(8,128)(2,1)S(1)}, u32[]{:S(2)}, u32[]{:S(2)}) collective-permute-start(bf16[384,512]{1,0:T(8,128)(2,1)S(1)} %get-tuple-element.370), channel_id=1, source_target_pairs={{0,1},{1,0},{2,3},{3,2},{4,5},{5,4},{6,7},{7,6},{8,9},{9,8},{10,11... | collective-permute-start | bytes 1179656 | tf_op jit(solution)/shard_map/given_core/ppermute | solution.py:794
  89.5 10.0 %collective-permute-start.27 = (bf16[144,768]{1,0:T(8,128)(2,1)S(1)}, bf16[144,768]{1,0:T(8,128)(2,1)S(1)}, u32[]{:S(2)}, u32[]{:S(2)}) collective-permute-start(bf16[144,768]{1,0:T(8,128)(2,1)S(1)} %slice.15), channel_id=1, source_target_pairs={{0,8},{8,0},{16,24},{24,16},{1,9},{9,1},{17,25},{25,17},{2,10},{10... | collective-permute-start | bytes 663560 | tf_op jit(solution)/shard_map/downdiag_x/ppermute | solution.py:806
  90.1 9.4 %collective-permute-start.26 = (bf16[144,768]{1,0:T(8,128)(2,1)S(1)}, bf16[144,768]{1,0:T(8,128)(2,1)S(1)}, u32[]{:S(2)}, u32[]{:S(2)}) collective-permute-start(bf16[144,768]{1,0:T(8,128)(2,1)S(1)} %slice.14), channel_id=1, source_target_pairs={{0,16},{8,24},{16,0},{24,8},{1,17},{9,25},{17,1},{25,9},{2,18},{10... | collective-permute-start | bytes 663560 | tf_op jit(solution)/shard_map/downdiag_y/ppermute | solution.py:806
  101.4 8.9 %collective-permute-start.33 = (bf16[512,1536]{1,0:T(8,128)(2,1)S(1)}, bf16[512,1536]{1,0:T(8,128)(2,1)S(1)}, u32[]{:S(2)}, u32[]{:S(2)}) collective-permute-start(bf16[512,1536]{1,0:T(8,128)(2,1)S(1)} %get-tuple-element.385), channel_id=1, source_target_pairs={{0,1},{1,0},{2,3},{3,2},{4,5},{5,4},{6,7},{7,6},{8,9},{9,8},{10,11... | collective-permute-start | bytes 4718600 | tf_op jit(solution)/shard_map/given_core/ppermute | solution.py:794
  116.1 17.1 %collective-permute-start.39 = (bf16[2,512,1536]{2,1,0:T(8,128)(2,1)S(1)}, bf16[2,512,1536]{2,1,0:T(8,128)(2,1)S(1)}, u32[]{:S(2)}, u32[]{:S(2)}) collective-permute-start(bf16[2,512,1536]{2,1,0:T(8,128)(2,1)S(1)} %get-tuple-element.425.refs_12_), channel_id=1, source_target_pairs={{0,1},{1,0},{2,3},{3,2},{4,5},{5,4},{6,7},{7,6},{8,9},{9,8},{10,11... | collective-permute-start | bytes 9437192 | tf_op jit(solution)/shard_map/given_core/ppermute | solution.py:794
  116.6 15.6 %collective-permute-start.37 = (bf16[2,2,96,768]{3,2,1,0:T(8,128)(2,1)S(1)}, bf16[2,2,96,768]{3,2,1,0:T(8,128)(2,1)S(1)}, u32[]{:S(2)}, u32[]{:S(2)}) collective-permute-start(bf16[2,2,96,768]{3,2,1,0:T(8,128)(2,1)S(1)} %get-tuple-element.417), channel_id=1, source_target_pairs={{0,8},{8,0},{16,24},{24,16},{1,9},{9,1},{17,25},{25,17},{2,10},{10... | collective-permute-start | bytes 1769480 | tf_op jit(solution)/shard_map/gdown_x/ppermute | solution.py:806
  118.0 15.1 %collective-permute-start.38 = (bf16[2,2,96,768]{3,2,1,0:T(8,128)(2,1)S(1)}, bf16[2,2,96,768]{3,2,1,0:T(8,128)(2,1)S(1)}, u32[]{:S(2)}, u32[]{:S(2)}) collective-permute-start(bf16[2,2,96,768]{3,2,1,0:T(8,128)(2,1)S(1)} %get-tuple-element.418), channel_id=1, source_target_pairs={{0,16},{8,24},{16,0},{24,8},{1,17},{9,25},{17,1},{25,9},{2,18},{10... | collective-permute-start | bytes 1769480 | tf_op jit(solution)/shard_map/gdown_y/ppermute | solution.py:806
  133.1 10.2 %collective-permute-start.44 = (bf16[768,768]{1,0:T(8,128)(2,1)S(1)}, bf16[768,768]{1,0:T(8,128)(2,1)S(1)}, u32[]{:S(2)}, u32[]{:S(2)}) collective-permute-start(bf16[768,768]{1,0:T(8,128)(2,1)S(1)} %attend_back.2.refs_6_.refs_0_), channel_id=1, source_target_pairs={{0,1},{1,0},{2,3},{3,2},{4,5},{5,4},{6,7},{7,6},{8,9},{9,8},{10,11... | collective-permute-start | bytes 3538952 | tf_op jit(solution)/shard_map/d_qkv_core/ppermute | solution.py:794
  133.1 10.2 %collective-permute-start.42 = (bf16[512,768]{1,0:T(8,128)(2,1)S(1)}, bf16[512,768]{1,0:T(8,128)(2,1)S(1)}, u32[]{:S(2)}, u32[]{:S(2)}) collective-permute-start(bf16[512,768]{1,0:T(8,128)(2,1)S(1)} %get-tuple-element.434.refs_10_), channel_id=1, source_target_pairs={{0,1},{1,0},{2,3},{3,2},{4,5},{5,4},{6,7},{7,6},{8,9},{9,8},{10,11... | collective-permute-start | bytes 2359304 | tf_op jit(solution)/shard_map/d_low_core/ppermute | solution.py:794
  133.9 9.0 %collective-permute-start.40 = (bf16[2,96,768]{2,1,0:T(8,128)(2,1)S(1)}, bf16[2,96,768]{2,1,0:T(8,128)(2,1)S(1)}, u32[]{:S(2)}, u32[]{:S(2)}) collective-permute-start(bf16[2,96,768]{2,1,0:T(8,128)(2,1)S(1)} %get-tuple-element.432), channel_id=1, source_target_pairs={{0,16},{8,24},{16,0},{24,8},{1,17},{9,25},{17,1},{25,9},{2,18},{10... | collective-permute-start | bytes 884744 | tf_op jit(solution)/shard_map/gdown2_y/ppermute | solution.py:806
  143.3 15.9 %collective-permute-start.46 = (bf16[2,2,96,768]{3,2,1,0:T(8,128)(2,1)}, bf16[2,2,96,768]{3,2,1,0:T(8,128)(2,1)S(1)}, u32[]{:S(2)}, u32[]{:S(2)}) collective-permute-start(bf16[2,2,96,768]{3,2,1,0:T(8,128)(2,1)} %get-tuple-element.457), channel_id=1, source_target_pairs={{0,8},{8,0},{16,24},{24,16},{1,9},{9,1},{17,25},{25,17},{2,10},{10... | collective-permute-start | bytes 1769480 | tf_op jit(solution)/shard_map/gup_x/ppermute | solution.py:806
  144.1 15.6 %collective-permute-start.47 = (bf16[2,2,96,768]{3,2,1,0:T(8,128)(2,1)}, bf16[2,2,96,768]{3,2,1,0:T(8,128)(2,1)S(1)}, u32[]{:S(2)}, u32[]{:S(2)}) collective-permute-start(bf16[2,2,96,768]{3,2,1,0:T(8,128)(2,1)} %get-tuple-element.458), channel_id=1, source_target_pairs={{0,16},{8,24},{16,0},{24,8},{1,17},{9,25},{17,1},{25,9},{2,18},{10... | collective-permute-start | bytes 1769480 | tf_op jit(solution)/shard_map/gup_y/ppermute | solution.py:806
  146.3 13.4 %collective-permute-start.48 = (bf16[96,768]{1,0:T(8,128)(2,1)S(1)}, bf16[96,768]{1,0:T(8,128)(2,1)S(1)}, u32[]{:S(2)}, u32[]{:S(2)}) collective-permute-start(bf16[96,768]{1,0:T(8,128)(2,1)S(1)} %get-tuple-element.464), channel_id=1, source_target_pairs={{0,2},{1,3},{2,4},{3,5},{4,6},{5,7},{6,0},{7,1},{8,10},{9,11},{10,... | collective-permute-start | bytes 442376 | tf_op jit(solution)/shard_map/gdown3_z1/ppermute | solution.py:800
  146.5 13.2 %collective-permute-start.49 = (bf16[96,768]{1,0:T(8,128)(2,1)S(1)}, bf16[96,768]{1,0:T(8,128)(2,1)S(1)}, u32[]{:S(2)}, u32[]{:S(2)}) collective-permute-start(bf16[96,768]{1,0:T(8,128)(2,1)S(1)} %get-tuple-element.466), channel_id=1, source_target_pairs={{0,6},{1,7},{2,0},{3,1},{4,2},{5,3},{6,4},{7,5},{8,14},{9,15},{10,... | collective-permute-start | bytes 442376 | tf_op jit(solution)/shard_map/gdown3_z3/ppermute | solution.py:800
  160.0 10.9 %collective-permute-start.50 = (bf16[2,96,768]{2,1,0:T(8,128)(2,1)S(1)}, bf16[2,96,768]{2,1,0:T(8,128)(2,1)S(1)}, u32[]{:S(2)}, u32[]{:S(2)}) collective-permute-start(bf16[2,96,768]{2,1,0:T(8,128)(2,1)S(1)} %get-tuple-element.477), channel_id=1, source_target_pairs={{0,16},{8,24},{16,0},{24,8},{1,17},{9,25},{17,1},{25,9},{2,18},{10... | collective-permute-start | bytes 884744 | tf_op jit(solution)/shard_map/gup2_y/ppermute | solution.py:806
  161.5 9.4 %collective-permute-start.51 = (bf16[2,96,768]{2,1,0:T(8,128)(2,1)S(1)}, bf16[2,96,768]{2,1,0:T(8,128)(2,1)S(1)}, u32[]{:S(2)}, u32[]{:S(2)}) collective-permute-start(bf16[2,96,768]{2,1,0:T(8,128)(2,1)S(1)} %get-tuple-element.478), channel_id=1, source_target_pairs={{0,8},{8,0},{16,24},{24,16},{1,9},{9,1},{17,25},{25,17},{2,10},{10... | collective-permute-start | bytes 884744 | tf_op jit(solution)/shard_map/gup2_x/ppermute | solution.py:806
  170.9 16.7 %collective-permute-start.53 = (bf16[2,2,112,768]{3,2,1,0:T(8,128)(2,1)S(1)}, bf16[2,2,112,768]{3,2,1,0:T(8,128)(2,1)S(1)}, u32[]{:S(2)}, u32[]{:S(2)}) collective-permute-start(bf16[2,2,112,768]{3,2,1,0:T(8,128)(2,1)S(1)} %get-tuple-element.483), channel_id=1, source_target_pairs={{0,8},{8,0},{16,24},{24,16},{1,9},{9,1},{17,25},{25,17},{2,10},{10... | collective-permute-start | bytes 2064392 | tf_op jit(solution)/shard_map/gfirst_x/ppermute | solution.py:806
  171.6 16.4 %collective-permute-start.54 = (bf16[2,2,112,768]{3,2,1,0:T(8,128)(2,1)S(1)}, bf16[2,2,112,768]{3,2,1,0:T(8,128)(2,1)S(1)}, u32[]{:S(2)}, u32[]{:S(2)}) collective-permute-start(bf16[2,2,112,768]{3,2,1,0:T(8,128)(2,1)S(1)} %get-tuple-element.484), channel_id=1, source_target_pairs={{0,16},{8,24},{16,0},{24,8},{1,17},{9,25},{17,1},{25,9},{2,18},{10... | collective-permute-start | bytes 2064392 | tf_op jit(solution)/shard_map/gfirst_y/ppermute | solution.py:806
  172.9 12.5 %collective-permute-start.55 = (bf16[96,768]{1,0:T(8,128)(2,1)S(1)}, bf16[96,768]{1,0:T(8,128)(2,1)S(1)}, u32[]{:S(2)}, u32[]{:S(2)}) collective-permute-start(bf16[96,768]{1,0:T(8,128)(2,1)S(1)} %get-tuple-element.498), channel_id=1, source_target_pairs={{0,2},{1,3},{2,4},{3,5},{4,6},{5,7},{6,0},{7,1},{8,10},{9,11},{10,... | collective-permute-start | bytes 442376 | tf_op jit(solution)/shard_map/gup3_z1/ppermute | solution.py:800
  172.9 12.9 %collective-permute-start.56 = (bf16[96,768]{1,0:T(8,128)(2,1)S(1)}, bf16[96,768]{1,0:T(8,128)(2,1)S(1)}, u32[]{:S(2)}, u32[]{:S(2)}) collective-permute-start(bf16[96,768]{1,0:T(8,128)(2,1)S(1)} %get-tuple-element.499), channel_id=1, source_target_pairs={{0,4},{1,5},{2,6},{3,7},{4,0},{5,1},{6,2},{7,3},{8,12},{9,13},{10,... | collective-permute-start | bytes 442376 | tf_op jit(solution)/shard_map/gup3_z2/ppermute | solution.py:800
  175.5 10.3 %collective-permute-start.57 = (bf16[96,768]{1,0:T(8,128)(2,1)S(1)}, bf16[96,768]{1,0:T(8,128)(2,1)S(1)}, u32[]{:S(2)}, u32[]{:S(2)}) collective-permute-start(bf16[96,768]{1,0:T(8,128)(2,1)S(1)} %get-tuple-element.500), channel_id=1, source_target_pairs={{0,6},{1,7},{2,0},{3,1},{4,2},{5,3},{6,4},{7,5},{8,14},{9,15},{10,... | collective-permute-start | bytes 442376 | tf_op jit(solution)/shard_map/gup3_z3/ppermute | solution.py:800
  197.6 10.8 %collective-permute-start.60 = (bf16[112,768]{1,0:T(8,128)(2,1)S(1)}, bf16[112,768]{1,0:T(8,128)(2,1)S(1)}, u32[]{:S(2)}, u32[]{:S(2)}) collective-permute-start(bf16[112,768]{1,0:T(8,128)(2,1)S(1)} %get-tuple-element.529), channel_id=1, source_target_pairs={{0,2},{1,3},{2,4},{3,5},{4,6},{5,7},{6,0},{7,1},{8,10},{9,11},{10,... | collective-permute-start | bytes 516104 | tf_op jit(solution)/shard_map/gfirst3_z1/ppermute | solution.py:800
  199.3 11.6 %collective-permute-start.61 = (bf16[112,768]{1,0:T(8,128)(2,1)S(1)}, bf16[112,768]{1,0:T(8,128)(2,1)S(1)}, u32[]{:S(2)}, u32[]{:S(2)}) collective-permute-start(bf16[112,768]{1,0:T(8,128)(2,1)S(1)} %get-tuple-element.530), channel_id=1, source_target_pairs={{0,4},{1,5},{2,6},{3,7},{4,0},{5,1},{6,2},{7,3},{8,12},{9,13},{10,... | collective-permute-start | bytes 516104 | tf_op jit(solution)/shard_map/gfirst3_z2/ppermute | solution.py:800
  200.1 10.8 %collective-permute-start.62 = (bf16[112,768]{1,0:T(8,128)(2,1)S(1)}, bf16[112,768]{1,0:T(8,128)(2,1)S(1)}, u32[]{:S(2)}, u32[]{:S(2)}) collective-permute-start(bf16[112,768]{1,0:T(8,128)(2,1)S(1)} %get-tuple-element.531), channel_id=1, source_target_pairs={{0,6},{1,7},{2,0},{3,1},{4,2},{5,3},{6,4},{7,5},{8,14},{9,15},{10,... | collective-permute-start | bytes 516104 | tf_op jit(solution)/shard_map/gfirst3_z3/ppermute | solution.py:800
  (56 other events, 712.2 us)

commit v4 on v3

--- a/solution.py
+++ b/solution.py
@@ -118,11 +118,11 @@
 
 
 def pack_kernel(place, *refs):
-    given, (own, a_ref, b_ref, c_ref), held, (small, sems) = (
+    given, (own, a_ref, b_ref, c_ref), (small, sems), held = (
         refs[:6],
         refs[6:10],
-        refs[10:16],
-        refs[16:],
+        refs[10:12],
+        refs[12:],
     )
     copies = [pltpu.make_async_copy(a, b, sems.at[i]) for i, (a, b) in enumerate(zip(given, held))]
     for copy in copies:
@@ -169,7 +169,7 @@
 def pack(place, *given):
     rows, wide = given[2].shape
     tall = rows + 16
-    got = call(
+    return call(
         pack_kernel,
         "pack_weights",
         [
@@ -177,15 +177,17 @@
             sds((tall, wide), BF),
             sds((rows, wide), BF),
             sds((rows, wide), BF),
-            *(sds(a.shape, F32) for a in given),
         ],
         given,
-        scratch=[pltpu.VMEM((16, wide), F32), pltpu.SemaphoreType.DMA((len(given),))],
+        scratch=[
+            pltpu.VMEM((16, wide), F32),
+            pltpu.SemaphoreType.DMA((len(given),)),
+            *(pltpu.VMEM(a.shape, F32) for a in given),
+        ],
         place=place,
         space=pltpu.HBM,
         vmem=60,
     )
-    return got[:4], got[4:]
 
 
 def split_cores(place, value, rows, mine, theirs, cols):
@@ -1023,11 +1025,11 @@
 
 
 def sum_everywhere(value):
-    a, b, c = (swap_fsdp(value, k, "norm") for k in (1, 2, 3))
-    value = (value + a) + (b + c)
     a, b, c = (shift_slot(value, k, "norm") for k in (1, 2, 3))
     value = (value + b) + (a + c)
-    return value + swap_core(value)
+    value = value + swap_core(value)
+    a, b, c = (swap_fsdp(value, k, "norm") for k in (1, 2, 3))
+    return (value + a) + (b + c)
 
 
 def adam(weight, moment, second, grad, scale_clip, rate, decay):
@@ -1159,7 +1161,7 @@
         (RATE_VEC, 0.0),
     )
 
-    (own, own_first, own_up, own_down), held = pack(
+    own, own_first, own_up, own_down = pack(
         place,
         qkv_weight,
         out_weight,
@@ -1194,11 +1196,10 @@
 
     far_first = all_of(*back_first)
     first_x, first_y = across(far_first, "first")
-    back_up = [shift_slot(own_up, 1, "up"), None, shift_slot(own_up, 3, "up")]
+    back_up = [shift_slot(own_up, k, "up") for k in (1, 2, 3)]
     near = all_of(own, own_x, own_y)
-    near_other = swap_core(near, "near_core")
-    own_x, own_y, far_first, first_x, first_y, own_up, own_down, near, near_other, back_up = tie(
-        own_x, own_y, far_first, first_x, first_y, own_up, own_down, near, near_other, back_up
+    own_x, own_y, far_first, first_x, first_y, own_down, near, back_up = tie(
+        own_x, own_y, far_first, first_x, first_y, own_down, near, back_up
     )
 
     tall, far = own.shape[0], far_first.shape[0]
@@ -1207,12 +1208,12 @@
     low = stack((own_x, 0, half_own), (first_x, 0, half_first))
     high = stack((own_y, half_own, tall), (first_y, half_first, far))
     diagonal = [swap_fsdp(low, 2, "diag"), swap_fsdp(high, 1, "diag")]
-    back_up[1] = shift_slot(own_up, 2, "up")
-    back_down = [shift_slot(own_down, 1, "down"), None, None]
+    back_down = [shift_slot(own_down, 1, "down"), None, shift_slot(own_down, 3, "down")]
+    near_other = swap_core(near, "near_core")
     first = all_of(far_first, first_x, first_y)
     first_other = swap_core(first, "first_core")
-    diagonal, first_other, back_up, back_down, own_down = tie(
-        diagonal, first_other, back_up, back_down, own_down
+    diagonal, first_other, near_other, back_down, own_down = tie(
+        diagonal, first_other, near_other, back_down, own_down
     )
     diagonal = all_of(*diagonal)
     diagonal_other = swap_core(diagonal, "diag_core")
@@ -1222,7 +1223,7 @@
         return segments_of(0, tall, [(first, 0, rows)], half_own, 1, 0, high_at)
 
     far_up = all_of(*back_up)
-    back_down[1:] = [shift_slot(own_down, k, "down") for k in (2, 3)]
+    back_down[1] = shift_slot(own_down, 2, "down")
     up_x, up_y = across(far_up, "up")
     blocks = [(k * rows_first, k + 1, rows_first) for k in range(3)]
     qkv_full, out_full, vec, proj, projt = first_whole(
@@ -1275,12 +1276,7 @@
     )
     up_diagonal = all_of(*up_diagonal)
     up_diagonal_other = swap_core(up_diagonal, "updiag_core")
-    h_rest, low_rest = join(
-        place, flat(a_rest), flat(rest), out_full, vec, marks_one, False, slots
-    )
-    up_diagonal_other, low_rest, down_x, down_y = tie(
-        up_diagonal_other, low_rest, down_x, down_y
-    )
+    up_diagonal_other, down_x, down_y = tie(up_diagonal_other, down_x, down_y)
     down_diagonal = far_diagonal(down_x, down_y, "downdiag")
     down = all_of(far_down, down_x, down_y)
     down_other = swap_core(down, "down_core")
@@ -1333,39 +1329,42 @@
         return owns, [shift_slot(a, k + 1, name) for k, a in enumerate(parts)]
 
     d_lowt_came = swap_core(d_lowt, "d_low_core")
+    h_rest, low_rest = join(
+        place, flat(a_rest), flat(rest), out_full, vec, marks_one, False, slots
+    )
+    d_lowt_came, act_came, low_rest, frontt_give, xt_give = tie(
+        d_lowt_came, act_came, low_rest, frontt_give, xt_give
+    )
+    parts_down = grad_down(place, d_lowt, d_lowt_came, act_front, act_came, rows_up, slots)
+    parts_down, d_low = tie(parts_down, d_low)
+    sent_down = send(parts_down, "gdown")
+    frontt_came, xt_came = cores((frontt_give, xt_give), "given_core")
     d_hidden, up_sums = hidden_back(d_low, down_full, slope)
-    d_lowt_came, d_hidden, act_came, frontt_give, xt_give = tie(
-        d_lowt_came, d_hidden, act_came, frontt_give, xt_give
-    )
     d_hidden_came = swap_core(d_hidden, "d_hidden_core")
-    parts_down = grad_down(place, d_lowt, d_lowt_came, act_front, act_came, rows_up, slots)
-    parts_down, d_hidden_came, d_hidden, kv = tie(parts_down, d_hidden_came, d_hidden, kv)
-    sent_down = send(parts_down, "gdown")
-    kv_came = swap_core(kv, "given_core")
-    parts_up = grad_up(place, lowt, lowt_came, d_hidden, d_hidden_came, fsdp, slots)
-    frontt_came, xt_came = cores((frontt_give, xt_give), "given_core")
-    parts_up, d_hidden, frontt_came, xt_came = tie(parts_up, d_hidden, frontt_came, xt_came)
     d_first, d_first_low, d_attended, sums = first_back(
         d_hidden, up_full, d_sum, kept, vec, out_full, up_sums, two_sums, (ends[0], ends[1])
     )
     d_attended = d_attended.reshape(seqs, half, width)
     grads = [attend_back(0, q_front, kvp, d_attended)]
-    grads, d_first_low, sums, sent_down, parts_up, kv_came = tie(
-        grads, d_first_low, sums, sent_down, parts_up, kv_came
+    grads, d_first_low, sums, sent_down, kv, frontt_came, xt_came = tie(
+        grads, d_first_low, sums, sent_down, kv, frontt_came, xt_came
     )
     over_down = forward(*add_up(*sent_down), "gdown2")
-    d_first_low_came, sums_came = cores((d_first_low, sums), "d_low_core")
+    d_first_low_came = swap_core(d_first_low, "d_low_core")
     grads_came = cores(grads, "d_qkv_core")
+    kv_came = swap_core(kv, "given_core")
     for s in range(1, seqs):
         grads.append(attend_back(s, q_front, kvp, d_attended))
-    grads, over_down, d_first_low_came, sums_came, grads_came, parts_up = tie(
-        grads, over_down, d_first_low_came, sums_came, grads_came, parts_up
+    parts_up = grad_up(place, lowt, lowt_came, d_hidden, d_hidden_came, fsdp, slots)
+    grads, d_first_low_came, sums, grads_came, kv_came, parts_up, over_down = tie(
+        grads, d_first_low_came, sums, grads_came, kv_came, parts_up, over_down
     )
     sent_up = send(parts_up, "gup")
+    sums_came = swap_core(sums, "d_low_core")
     grads_came = grads_came + cores(grads[1:], "d_qkv_core")
-    grads_came, over_down = tie(grads_came, over_down)
+    grads_came, sums_came = tie(grads_came, sums_came)
     owns_down, (one, two, three) = third_stage(over_down)
-    one, three = shift_slot(one, 1, "gdown3"), shift_slot(three, 3, "gdown3")
+    two = shift_slot(two, 2, "gdown3")
     parts_first = grad_rest(
         place,
         (xt, xt_came, frontt, frontt_came, attendedt, attendedt_came),
@@ -1379,43 +1378,57 @@
     parts_first, low_rest, sent_up, one, two, three = tie(
         parts_first, low_rest, sent_up, one, two, three
     )
-    last_down = (owns_down, (one, shift_slot(two, 2, "gdown3"), three))
+    three = shift_slot(three, 3, "gdown3")
     over_up = forward(*add_up(*sent_up), "gup2")
     act_rest = lift(place, low_rest, up_full, vec, m2, False, range(fsdp // 2))
-    parts_first, act_rest, over_up, last_down, grads, low_rest = tie(
-        parts_first, act_rest, over_up, last_down, grads, low_rest
+    parts_first, act_rest, over_up, one, three, grads, low_rest = tie(
+        parts_first, act_rest, over_up, one, three, grads, low_rest
     )
     sent_first = send(parts_first, "gfirst")
-    last_up = along_z((over_up,), "gup3")
+    last_down = (owns_down, (shift_slot(one, 1, "gdown3"), two, three))
+    owns_up, (one, two, three) = third_stage(over_up)
+    two, three = shift_slot(two, 2, "gup3"), shift_slot(three, 3, "gup3")
     act_rest += lift(place, low_rest, up_full, vec, m2, False, range(fsdp // 2, fsdp))
     out_rest = lower(act_rest, h_rest, down_full, vec, marks_two)[0]
     output = restore(
         out_front.reshape(seqs, half, width), out_rest.reshape(seqs, half, width), back
     ).reshape(rows, width)
-    sent_first, output, grads, last_up, last_down = tie(
-        sent_first, output, grads, last_up, last_down
+    sent_first, output, grads, one, two, three, last_down = tie(
+        sent_first, output, grads, one, two, three, last_down
     )
     over_first = forward(*add_up(*sent_first), "gfirst2")
+    last_up = (owns_up, (shift_slot(one, 1, "gup3"), two, three))
     g_down, squares_down = last_stage(*last_down)
+    over_first, squares_down, last_up, grads = tie(over_first, squares_down, last_up, grads)
+    last_first = along_z((over_first,), "gfirst3")
     g_up, squares_up = last_stage(*last_up)
-    over_first, squares_down, squares_up, grads = tie(over_first, squares_down, squares_up, grads)
-    last_first = along_z((over_first,), "gfirst3")
     grad_input = input_back(
         projt, d_first.reshape(seqs, half, width), qkv_full, back, grads
     ).reshape(rows, width)
-    last_first, grad_input = tie(last_first, grad_input)
+    last_first, grad_input, squares_up = tie(last_first, grad_input, squares_up)
     g_first, squares_first = last_stage(*last_first)
     squares_rest = squares_up + squares_down
     squares = sum_everywhere(squares_first + squares_rest)
-    moments = (
-        (qkv_moment, qkv_second),
-        (out_moment, out_second),
-        (up_moment, up_second),
-        (down_moment.T, down_second.T),
-        (proj_moment, proj_second),
-        (vec_moment, vec_second),
-    )
-    states = [a for weight, pair in zip(held, moments) for a in (weight, *pair)]
+    states = (
+        qkv_weight,
+        qkv_moment,
+        qkv_second,
+        out_weight,
+        out_moment,
+        out_second,
+        up_weight,
+        up_moment,
+        up_second,
+        down_projection_weight.T,
+        down_moment.T,
+        down_second.T,
+        proj_weight,
+        proj_moment,
+        proj_second,
+        vec_weight,
+        vec_moment,
+        vec_second,
+    )
     new = update(place, squares, g_first, g_up, g_down, states, rates)
     norm, new = new[0].reshape(()), list(new[1:])
     new[12:16] = [v.T for v in new[12:16]]

time: 236 us -> 230 us (0.975)
  waiting for transfers between devices: 67.9 us -> 52 us
  starting transfers between devices: 66.9 us -> 74.8 us
    ppermute x21, waiting for transfers between devices: 37.3 us -> 27.3 us  [shift_slot(): return lax.ppermute(value, 'dp', [(i, (i + 2 * by) % n) for i in range(n)])]
    ppermute x21, starting transfers between devices: 30.9 us -> 38.7 us  [shift_slot(): return lax.ppermute(value, 'dp', [(i, (i + 2 * by) % n) for i in range(n)])]
    ppermute x29, waiting for transfers between devices: 25.2 us -> 20.5 us  [swap_fsdp(): return lax.ppermute(value, 'fsdp', [(i, i ^ bits) for i in range(n)])]
  transfers between devices with their start and end apart: 70 -> 70, of which waited for: 30 -> 28; matrix products, arithmetic and copies ran while one was open for 1% -> 1% of each run, Pallas kernels for 36% -> 37%
where the time goes in v4:
time: 230 us; the launch traced here: 226 us
  Pallas kernels  90.7 us (39%)
  starting transfers between devices  74.8 us (33%)
  waiting for transfers between devices  52 us (23%)
  local copies, waits for them, and re-layouts  4.44 us (2%)
    pallas_call x45, Pallas kernels, call(): pl.pallas_call(kernel, name=name, out_shape=outs, in_specs=specs, out_spe...  90.7 us
    ppermute x21, starting transfers between devices, shift_slot(): return lax.ppermute(value, 'dp', [(i, (i + 2 * by) % n) for i in range(n)])  38.7 us
    ppermute x29, starting transfers between devices, swap_fsdp(): return lax.ppermute(value, 'fsdp', [(i, i ^ bits) for i in range(n)])  32.3 us
    ppermute x21, waiting for transfers between devices, shift_slot(): return lax.ppermute(value, 'dp', [(i, (i + 2 * by) % n) for i in range(n)])  27.3 us
    ppermute x29, waiting for transfers between devices, swap_fsdp(): return lax.ppermute(value, 'fsdp', [(i, i ^ bits) for i in range(n)])  20.5 us
  transfers between devices with their start and end apart: 70, of which 28 were waited for; matrix products, arithmetic and copies ran while one was open for 1% of the time, Pallas kernels for 37%

profile of v4, /device:TPU:0, one launch (start us, length us, event | category | flops | bytes accessed | tf_op | source)
XLA Modules:
  0.0 225.8 jit_solution(10661529229639064621)
XLA Ops:
  1.3 3.0 %pack_weights.1 = (bf16[304,768]{1,0:T(8,128)(2,1)}, bf16[112,768]{1,0:T(8,128)(2,1)}, bf16[96,768]{1,0:T(8,128)(2,1)}, bf16[96,768]{1,0:T(8,128)(2,1)}) custom-call(s32[3]{0:T(128)} %pad_add_fusion.place, f32[96,576]{1,0:T(8,128)} %refs_0_.3, f32[96,192]{1,0:T(8,128)} %refs_3_.1, f32[96,768]{1,0:T(8,128)} %refs_6_.1, f32[192,384]{1,0:T(8,128)} %bitcast.34, ...), custom_call_target="tpu_custom_call" | custom-call | bytes 1836 | tf_op jit(solution)/shard_map/pack_weights/pallas_call | solution.py:54
  4.3 3.1 %collective-permute-start = (bf16[112,768]{1,0:T(8,128)(2,1)}, bf16[112,768]{1,0:T(8,128)(2,1)S(1)}, u32[]{:S(2)}, u32[]{:S(2)}) collective-permute-start(bf16[112,768]{1,0:T(8,128)(2,1)} %get-tuple-element.283), channel_id=1, source_target_pairs={{0,2},{1,3},{2,4},{3,5},{4,6},{5,7},{6,0},{7,1},{8,10},{9,11},{10,... | collective-permute-start | bytes 516104 | tf_op jit(solution)/shard_map/first_z1/ppermute | solution.py:802
  7.4 2.6 %collective-permute-start.1 = (bf16[112,768]{1,0:T(8,128)(2,1)}, bf16[112,768]{1,0:T(8,128)(2,1)S(1)}, u32[]{:S(2)}, u32[]{:S(2)}) collective-permute-start(bf16[112,768]{1,0:T(8,128)(2,1)} %get-tuple-element.283), channel_id=1, source_target_pairs={{0,4},{1,5},{2,6},{3,7},{4,0},{5,1},{6,2},{7,3},{8,12},{9,13},{10,... | collective-permute-start | bytes 516104 | tf_op jit(solution)/shard_map/first_z2/ppermute | solution.py:802
  18.0 2.4 %order_rows.1 = (bf16[2,256,768]{2,1,0:T(8,128)(2,1)S(1)}, bf16[2,256,768]{2,1,0:T(8,128)(2,1)S(1)}, bf16[384,512]{1,0:T(8,128)(2,1)S(1)}, bf16[384,512]{1,0:T(8...) custom-call(s32[3]{0:T(128)S(1)} %copy-done.25, ...), custom_call_target="tpu_custom_call" | custom-call | flops 805306 | bytes 6555 | tf_op jit(solution)/shard_map/order_rows/pallas_call | solution.py:54
  21.5 1.7 collective-permute-done.3.refs_1_.refs_0_
  26.5 2.2 collective-permute-start.7
  28.8 1.6 collective-permute-start.8
  31.3 3.9 %collective-permute-done.7.refs_0_ = bf16[96,768]{1,0:T(8,128)(2,1)S(1)} collective-permute-done((bf16[96,768]{1,0:T(8,128)(2,1)S(1)}, bf16[96,768]{1,0:T(8,128)(2,1)S(1)}, u32[]{:S(2)}, u32[]{:S(2)}) %collective-permute-start.7) | collective-permute-done | bytes 147488 | tf_op jit(solution)/shard_map/up_z1/ppermute | solution.py:802
  35.1 4.0 %collective-permute-done.8.refs_1_ = bf16[96,768]{1,0:T(8,128)(2,1)S(1)} collective-permute-done((bf16[96,768]{1,0:T(8,128)(2,1)S(1)}, bf16[96,768]{1,0:T(8,128)(2,1)S(1)}, u32[]{:S(2)}, u32[]{:S(2)}) %collective-permute-start.8) | collective-permute-done | bytes 147488 | tf_op jit(solution)/shard_map/up_z2/ppermute | solution.py:802
  41.4 3.4 %collective-permute-start.16 = (bf16[96,768]{1,0:T(8,128)(2,1)S(1)}, bf16[96,768]{1,0:T(8,128)(2,1)S(1)}, u32[]{:S(2)}, u32[]{:S(2)}) collective-permute-start(bf16[96,768]{1,0:T(8,128)(2,1)S(1)} %copy-done.36), channel_id=1, source_target_pairs={{0,2},{1,3},{2,4},{3,5},{4,6},{5,7},{6,0},{7,1},{8,10},{9,11},{10,... | collective-permute-start | bytes 442376 | tf_op jit(solution)/shard_map/down_z1/ppermute | solution.py:802
  44.8 4.8 %collective-permute-done.16.refs_0_ = bf16[96,768]{1,0:T(8,128)(2,1)S(1)} collective-permute-done((bf16[96,768]{1,0:T(8,128)(2,1)S(1)}, bf16[96,768]{1,0:T(8,128)(2,1)S(1)}, u32[]{:S(2)}, u32[]{:S(2)}) %collective-permute-start.16) | collective-permute-done | bytes 147488 | tf_op jit(solution)/shard_map/down_z1/ppermute | solution.py:802
  49.6 2.0 collective-permute-start.17
  51.6 3.4 %collective-permute-done.17.refs_2_ = bf16[96,768]{1,0:T(8,128)(2,1)S(1)} collective-permute-done((bf16[96,768]{1,0:T(8,128)(2,1)S(1)}, bf16[96,768]{1,0:T(8,128)(2,1)S(1)}, u32[]{:S(2)}, u32[]{:S(2)}) %collective-permute-start.17) | collective-permute-done | bytes 147488 | tf_op jit(solution)/shard_map/down_z3/ppermute | solution.py:802
  58.6 2.0 whole_first.1
  60.6 6.2 %make_qkv.1 = (bf16[2,256,768]{2,1,0:T(8,128)(2,1)S(1)}, bf16[2,256,768]{2,1,0:T(8,128)(2,1)S(1)}, bf16[2,512,1536]{2,1,0:T(8,128)(2,1)S(1)}, bf16[2,256,1536]{2,1,0:T(8,128)(2,1)S(1)}) custom-call(bf16[2,256,768]{2,1,0:T(8,128)(2,1)S(1)} %get-tuple-element.301.front, bf16[2,256,768]{2,1,0:T(8,128)(2,1)S(1)} %get-tuple-element.302.rest, ...), custom_call_target="tpu_custom_call" | custom-call | flops 4429185 | bytes 13278 | tf_op jit(solution)/shard_map/make_qkv/pallas_call | solution.py:54
  69.3 1.6 collective-permute-start.20
  73.5 4.0 %attend.1 = (bf16[2,256,768]{2,1,0:T(8,128)(2,1)S(1)}, bf16[2,256,768]{2,1,0:T(8,128)(2,1)S(1)}) custom-call(bf16[2,256,768]{2,1,0:T(8,128)(2,1)S(1)} %get-tuple-element.321.q_front.queries, bf16[2,256,768]{2,1,0:T(8,128)(2,1)S(1)} %get-tuple-element.325.q_rest, bf16[2,256,1536]{2,1,0:T(8,128)(2,1)S(1)} %get-tuple-element.322.kvp), custom_call_target="tpu_custom_call" | custom-call | flops 1610612 | bytes 4718 | tf_op jit(solution)/shard_map/attend/pallas_call | solution.py:54
  77.5 2.4 %join_front.1 = (f32[512,768]{1,0:T(8,128)S(1)}, bf16[512,768]{1,0:T(8,128)(2,1)S(1)}, f32[512,768]{1,0:T(8,128)S(1)}, bf16[384,512]{1,0:T(8,128)(2,1)S(1)}, bf1...) custom-call(s32[3]{0:T(128)S(1)} %copy-done.25, ...), custom_call_target="tpu_custom_call" | custom-call | flops 603979 | bytes 8297 | tf_op jit(solution)/shard_map/join_front/pallas_call | solution.py:54
  80.1 7.8 %collective-permute-done.24.refs_1_ = bf16[288,768]{1,0:T(8,128)(2,1)S(1)} collective-permute-done((bf16[288,768]{1,0:T(8,128)(2,1)S(1)}, bf16[288,768]{1,0:T(8,128)(2,1)S(1)}, u32[]{:S(2)}, u32[]{:S(2)}) %collective-permute-start.24) | collective-permute-done | bytes 442400 | tf_op jit(solution)/shard_map/down_x/ppermute | solution.py:808
  90.7 7.0 %lift_front.1 = (bf16[512,3072]{1,0:T(8,128)(2,1)S(1)}, bf16[512,3072]{1,0:T(8,128)(2,1)S(1)}, bf16[512,1536]{1,0:T(8,128)(2,1)S(1)}) custom-call(s32[3]{0:T(128)S(1)} %copy-done.25, bf16[512,768]{1,0:T(8,128)(2,1)S(1)} %get-tuple-element.339.low, bf16[4,768,768]{2,1,0:T(8,128)(2,1)S(1)} %whole_up.1.weight.up, ...), custom_call_target="tpu_custom_call" | custom-call | flops 2415919 | bytes 13409 | tf_op jit(solution)/shard_map/lift_front/pallas_call | solution.py:54
  98.6 1.8 collective-permute-done.31.refs_7_
  101.5 4.1 %lower_front.1 = (bf16[512,768]{1,0:T(8,128)(2,1)S(1)}, f32[512,768]{1,0:T(8,128)S(1)}, bf16[512,768]{1,0:T(8,128)(2,1)S(1)}, bf16[768,512]{1,0:T(8,128)(2,1)S(1)}, f32[8,768]{1,0:T(8,128)S(1)}) custom-call(bf16[512,3072]{1,0:T(8,128)(2,1)S(1)} %get-tuple-element.346.refs_0_.active, f32[512,768]{1,0:T(8,128)S(1)} %get-tuple-element.347.refs_1_, ...), custom_call_target="tpu_custom_call" | custom-call | flops 2415919 | bytes 14220 | tf_op jit(solution)/shard_map/lower_front/pallas_call | solution.py:54
  106.1 1.9 join_rest.1
  108.4 4.1 %grad_down.1 = (bf16[2,2,96,768]{3,2,1,0:T(8,128)(2,1)S(1)}, bf16[2,2,96,768]{3,2,1,0:T(8,128)(2,1)S(1)}, bf16[2,2,96,768]{3,2,1,0:T(8,128)(2,1)S(1)}, bf16[2,2,96,768]{3,2,1,0:T(8,128)(2,1)S(1)}) custom-call(s32[3]{0:T(128)S(1)} %copy-done.25, bf16[768,512]{1,0:T(8,128)(2,1)S(1)} %get-tuple-element.355.d_lowt, ...), custom_call_target="tpu_custom_call" | custom-call | flops 4831838 | bytes 8650 | tf_op jit(solution)/shard_map/grad_down/pallas_call | solution.py:54
  115.6 2.7 %hidden_back.1 = (bf16[512,3072]{1,0:T(8,128)(2,1)S(1)}, f32[1,3072]{1,0:T(1,128)S(1)}) custom-call(bf16[512,768]{1,0:T(8,128)(2,1)S(1)} %get-tuple-element.368.d_low, bf16[768,3072]{1,0:T(8,128)(2,1)S(1)} %whole_down.1.refs_2_.weight.refs_3_, bf16[512,3072]{1,0:T(8,128)(2,1)S(1)} %get-tuple-element.369.slope), custom_call_target="tpu_custom_call" | custom-call | flops 2415919 | bytes 11808 | tf_op jit(solution)/shard_map/hidden_back/pallas_call | solution.py:54
  118.9 5.1 %first_back.1 = (f32[512,768]{1,0:T(8,128)S(1)}, bf16[512,768]{1,0:T(8,128)(2,1)S(1)}, bf16[512,768]{1,0:T(8,128)(2,1)S(1)}, f32[16,768]{1,0:T(8,128)S(1)}) custom-call(bf16[512,3072]{1,0:T(8,128)(2,1)S(1)} %get-tuple-element.370.d_hidden, bf16[4,768,768]{2,1,0:T(8,128)(2,1)S(1)} %whole_up.1.weight.up, f32[512,768]{1,0:T(8,128)S(1)} %get-tuple-element.371.d_sum, ...), custom_call_target="tpu_custom_call" | custom-call | flops 3019898 | bytes 15461 | tf_op jit(solution)/shard_map/first_back/pallas_call | solution.py:54
  124.1 3.5 %attend_back.2.refs_6_.refs_0_ = bf16[768,768]{1,0:T(8,128)(2,1)S(1)} custom-call(bf16[2,256,768]{2,1,0:T(8,128)(2,1)S(1)} %get-tuple-element.321.q_front.queries, bf16[2,256,1536]{2,1,0:T(8,128)(2,1)S(1)} %get-tuple-element.322.kvp, bf16[2,256,768]{2,1,0:T(8,128)(2,1)S(1)} %bitcast.29), custom_call_target="tpu_custom_call" | custom-call | flops 1006632 | bytes 4325 | tf_op jit(solution)/shard_map/attend_back/pallas_call | solution.py:54
  132.4 3.5 %attend_back.3.refs_7_.refs_1_ = bf16[768,768]{1,0:T(8,128)(2,1)S(1)} custom-call(bf16[2,256,768]{2,1,0:T(8,128)(2,1)S(1)} %get-tuple-element.321.q_front.queries, bf16[2,256,1536]{2,1,0:T(8,128)(2,1)S(1)} %get-tuple-element.322.kvp, bf16[2,256,768]{2,1,0:T(8,128)(2,1)S(1)} %bitcast.30), custom_call_target="tpu_custom_call" | custom-call | flops 1006632 | bytes 4325 | tf_op jit(solution)/shard_map/attend_back/pallas_call | solution.py:54
  135.9 4.2 %grad_up.1 = (bf16[2,2,96,768]{3,2,1,0:T(8,128)(2,1)}, bf16[2,2,96,768]{3,2,1,0:T(8,128)(2,1)S(1)}, bf16[2,2,96,768]{3,2,1,0:T(8,128)(2,1)S(1)}, bf16[2,2,96,768]{3,2,1,0:T(8,128)(2,1)S(1)}) custom-call(s32[3]{0:T(128)S(1)} %copy-done.25, bf16[384,512]{1,0:T(8,128)(2,1)S(1)} %get-tuple-element.394.lowt, ...), custom_call_target="tpu_custom_call" | custom-call | flops 2415919 | bytes 9437 | tf_op jit(solution)/shard_map/grad_up/pallas_call | solution.py:54
  146.1 8.8 %grad_rest.1 = (bf16[2,2,112,768]{3,2,1,0:T(8,128)(2,1)S(1)}, bf16[2,2,112,768]{3,2,1,0:T(8,128)(2,1)S(1)}, bf16[2,2,112,768]{3,2,1,0:T(8,128)(2,1)S(1)}, bf16[2,2,112,768]{3,2,1,0:T(8,128)(2,1)S(1)}) custom-call(s32[3]{0:T(128)S(1)} %copy-done.25, bf16[384,1024]{1,0:T(8,128)(2,1)S(1)} %copy-done.7, bf16[384,1024]{1,0:T(8,128)(2,1)S(1)} %collective-permute-done.37.refs_1_, ...), custom_call_target="tpu_custom_call" | custom-call | flops 4831838 | bytes 18841 | tf_op jit(solution)/shard_map/grad_rest/pallas_call | solution.py:54
  154.9 2.2 collective-permute-done.46.from_x
  159.4 3.5 %collective-permute-start.51 = (bf16[96,768]{1,0:T(8,128)(2,1)S(1)}, bf16[96,768]{1,0:T(8,128)(2,1)S(1)}, u32[]{:S(2)}, u32[]{:S(2)}) collective-permute-start(bf16[96,768]{1,0:T(8,128)(2,1)S(1)} %get-tuple-element.445), channel_id=1, source_target_pairs={{0,6},{1,7},{2,0},{3,1},{4,2},{5,3},{6,4},{7,5},{8,14},{9,15},{10,... | collective-permute-start | bytes 442376 | tf_op jit(solution)/shard_map/gdown3_z3/ppermute | solution.py:802
  163.0 3.2 %lift_rest.2.refs_0_ = bf16[512,1536]{1,0:T(8,128)(2,1)S(1)} custom-call(s32[3]{0:T(128)S(1)} %copy-done.25, bf16[512,768]{1,0:T(8,128)(2,1)S(1)} %get-tuple-element.452.low, bf16[4,768,768]{2,1,0:T(8,128)(2,1)S(1)} %whole_up.1.weight.up, f32[1,9984]{1,0:T(1,128)S(1)} %get-tuple-element.315.vec.refs_3_.refs_4_), custom_call_target="tpu_custom_call" | custom-call | flops 1207959 | bytes 7117 | tf_op jit(solution)/shard_map/lift_rest/pallas_call | solution.py:54
  169.6 3.5 %collective-permute-start.55 = (bf16[96,768]{1,0:T(8,128)(2,1)S(1)}, bf16[96,768]{1,0:T(8,128)(2,1)S(1)}, u32[]{:S(2)}, u32[]{:S(2)}) collective-permute-start(bf16[96,768]{1,0:T(8,128)(2,1)S(1)} %get-tuple-element.462), channel_id=1, source_target_pairs={{0,6},{1,7},{2,0},{3,1},{4,2},{5,3},{6,4},{7,5},{8,14},{9,15},{10,... | collective-permute-start | bytes 442376 | tf_op jit(solution)/shard_map/gup3_z3/ppermute | solution.py:802
  173.3 3.2 %lift_rest.3.refs_1_ = bf16[512,1536]{1,0:T(8,128)(2,1)S(1)} custom-call(s32[3]{0:T(128)S(1)} %copy-done.25, bf16[512,768]{1,0:T(8,128)(2,1)S(1)} %get-tuple-element.452.low, bf16[4,768,768]{2,1,0:T(8,128)(2,1)S(1)} %whole_up.1.weight.up, f32[1,9984]{1,0:T(1,128)S(1)} %get-tuple-element.315.vec.refs_3_.refs_4_), custom_call_target="tpu_custom_call" | custom-call | flops 1207959 | bytes 7117 | tf_op jit(solution)/shard_map/lift_rest/pallas_call | solution.py:54
  176.5 3.1 %lower_rest.1 = bf16[512,768]{1,0:T(8,128)(2,1)S(1)} custom-call(bf16[512,1536]{1,0:T(8,128)(2,1)S(1)} %lift_rest.2.refs_0_, bf16[512,1536]{1,0:T(8,128)(2,1)S(1)} %lift_rest.3.refs_1_, f32[512,768]{1,0:T(8,128)S(1)} %get-tuple-element.453.refs_2_, bf16[768,3072]{1,0:T(8,128)(2,1)S(1)} %whole_down.1.refs_2_.weight.refs_3_, ...), custom_call_target="tpu_custom_call" | custom-call | flops 2415919 | bytes 10263 | tf_op jit(solution)/shard_map/lower_rest/pallas_call | solution.py:54
  179.6 2.1 restore_order.1
  183.0 1.6 collective-permute-start.57
  185.8 1.6 collective-permute-start.59
  187.6 5.1 %collective-permute-done.59.refs_1_ = bf16[96,768]{1,0:T(8,128)(2,1)S(1)} collective-permute-done((bf16[96,768]{1,0:T(8,128)(2,1)S(1)}, bf16[96,768]{1,0:T(8,128)(2,1)S(1)}, u32[]{:S(2)}, u32[]{:S(2)}) %collective-permute-start.59) | collective-permute-done | bytes 147488 | tf_op jit(solution)/shard_map/gup3_z1/ppermute | solution.py:802
  192.9 2.0 collective-permute-start.60
  196.1 1.9 collective-permute-start.62
  198.5 6.5 %input_back.1 = bf16[2,512,768]{2,1,0:T(8,128)(2,1)} custom-call(bf16[512,256]{1,0:T(8,128)(2,1)S(1)} %get-tuple-element.416.refs_16_.projt, f32[2,256,768]{2,1,0:T(8,128)S(1)} %bitcast.33, bf16[768,2304]{1,0:T(8,128)(2,1)S(1)} %get-tuple-element.314.weight, bf16[2,512,512]{2,1,0:T(8,128)(2,1)S(1)} %get-tuple-element.454.back, ...), custom_call_target="tpu_custom_call" | custom-call | flops 4429185 | bytes 10354 | tf_op jit(solution)/shard_map/input_back/pallas_call | solution.py:54
  206.2 2.5 %collective-permute-start.64 = (f32[8,128]{1,0:T(8,128)S(1)}, f32[8,128]{1,0:T(8,128)S(1)}, u32[]{:S(2)}, u32[]{:S(2)}) collective-permute-start(f32[8,128]{1,0:T(8,128)S(1)} %add_add_fusion.2), channel_id=1, source_target_pairs={{0,2},{1,3},{2,4},{3,5},{4,6},{5,7},{6,0},{7,1},{8,10},{9,11},{10,... | collective-permute-start | bytes 12296 | tf_op jit(solution)/shard_map/norm_z1/ppermute | solution.py:802
  208.6 2.8 %collective-permute-start.65 = (f32[8,128]{1,0:T(8,128)S(1)}, f32[8,128]{1,0:T(8,128)S(1)}, u32[]{:S(2)}, u32[]{:S(2)}) collective-permute-start(f32[8,128]{1,0:T(8,128)S(1)} %add_add_fusion.2), channel_id=1, source_target_pairs={{0,6},{1,7},{2,0},{3,1},{4,2},{5,3},{6,4},{7,5},{8,14},{9,15},{10,... | collective-permute-start | bytes 12296 | tf_op jit(solution)/shard_map/norm_z3/ppermute | solution.py:802
  213.0 3.0 %collective-permute-done.63 = f32[8,128]{1,0:T(8,128)S(1)} collective-permute-done((f32[8,128]{1,0:T(8,128)S(1)}, f32[8,128]{1,0:T(8,128)S(1)}, u32[]{:S(2)}, u32[]{:S(2)}) %collective-permute-start.63) | collective-permute-done | bytes 4128 | tf_op jit(solution)/shard_map/norm_z2/ppermute | solution.py:802
  218.8 1.8 collective-permute-start.67
  222.6 3.0 %update.1 = (f32[1,1]{1,0:T(1,128)}, f32[96,576]{1,0:T(8,128)}, f32[96,576]{1,0:T(8,128)}, f32[96,576]{1,0:T(8,128)}, bf16[96,576]{1,0:T(8,128)(2,1)}, /*index=5...) custom-call(s32[3]{0:T(128)S(1)} %copy-done.25, ...), custom_call_target="tpu_custom_call" | custom-call | bytes 6803 | tf_op jit(solution)/shard_map/update/pallas_call | solution.py:54
  (228 shorter events, 62.3 us)
Async XLA Ops:
  4.3 16.0 %collective-permute-start = (bf16[112,768]{1,0:T(8,128)(2,1)}, bf16[112,768]{1,0:T(8,128)(2,1)S(1)}, u32[]{:S(2)}, u32[]{:S(2)}) collective-permute-start(bf16[112,768]{1,0:T(8,128)(2,1)} %get-tuple-element.283), channel_id=1, source_target_pairs={{0,2},{1,3},{2,4},{3,5},{4,6},{5,7},{6,0},{7,1},{8,10},{9,11},{10,... | collective-permute-start | bytes 516104 | tf_op jit(solution)/shard_map/first_z1/ppermute | solution.py:802
  7.4 14.1 %collective-permute-start.1 = (bf16[112,768]{1,0:T(8,128)(2,1)}, bf16[112,768]{1,0:T(8,128)(2,1)S(1)}, u32[]{:S(2)}, u32[]{:S(2)}) collective-permute-start(bf16[112,768]{1,0:T(8,128)(2,1)} %get-tuple-element.283), channel_id=1, source_target_pairs={{0,4},{1,5},{2,6},{3,7},{4,0},{5,1},{6,2},{7,3},{8,12},{9,13},{10,... | collective-permute-start | bytes 516104 | tf_op jit(solution)/shard_map/first_z2/ppermute | solution.py:802
  10.0 11.5 %collective-permute-start.2 = (bf16[112,768]{1,0:T(8,128)(2,1)}, bf16[112,768]{1,0:T(8,128)(2,1)S(1)}, u32[]{:S(2)}, u32[]{:S(2)}) collective-permute-start(bf16[112,768]{1,0:T(8,128)(2,1)} %get-tuple-element.283), channel_id=1, source_target_pairs={{0,6},{1,7},{2,0},{3,1},{4,2},{5,3},{6,4},{7,5},{8,14},{9,15},{10,... | collective-permute-start | bytes 516104 | tf_op jit(solution)/shard_map/first_z3/ppermute | solution.py:802
  11.4 11.8 %collective-permute-start.3 = (bf16[304,768]{1,0:T(8,128)(2,1)}, bf16[304,768]{1,0:T(8,128)(2,1)S(1)}, u32[]{:S(2)}, u32[]{:S(2)}) collective-permute-start(bf16[304,768]{1,0:T(8,128)(2,1)} %get-tuple-element.296.refs_0_), channel_id=1, source_target_pairs={{0,8},{8,0},{16,24},{24,16},{1,9},{9,1},{17,25},{25,17},{2,10},{10... | collective-permute-start | bytes 1400840 | tf_op jit(solution)/shard_map/own_x/ppermute | solution.py:808
  12.8 11.5 %collective-permute-start.4 = (bf16[304,768]{1,0:T(8,128)(2,1)}, bf16[304,768]{1,0:T(8,128)(2,1)S(1)}, u32[]{:S(2)}, u32[]{:S(2)}) collective-permute-start(bf16[304,768]{1,0:T(8,128)(2,1)} %get-tuple-element.296.refs_0_), channel_id=1, source_target_pairs={{0,16},{8,24},{16,0},{24,8},{1,17},{9,25},{17,1},{25,9},{2,18},{10... | collective-permute-start | bytes 1400840 | tf_op jit(solution)/shard_map/own_y/ppermute | solution.py:808
  24.4 14.8 %collective-permute-start.5 = (bf16[336,768]{1,0:T(8,128)(2,1)S(1)}, bf16[336,768]{1,0:T(8,128)(2,1)S(1)}, u32[]{:S(2)}, u32[]{:S(2)}) collective-permute-start(bf16[336,768]{1,0:T(8,128)(2,1)S(1)} %stack.28.refs_0_), channel_id=1, source_target_pairs={{0,8},{8,0},{16,24},{24,16},{1,9},{9,1},{17,25},{25,17},{2,10},{10... | collective-permute-start | bytes 1548296 | tf_op jit(solution)/shard_map/first_x/ppermute | solution.py:808
  25.0 14.2 %collective-permute-start.6 = (bf16[336,768]{1,0:T(8,128)(2,1)S(1)}, bf16[336,768]{1,0:T(8,128)(2,1)S(1)}, u32[]{:S(2)}, u32[]{:S(2)}) collective-permute-start(bf16[336,768]{1,0:T(8,128)(2,1)S(1)} %stack.28.refs_0_), channel_id=1, source_target_pairs={{0,16},{8,24},{16,0},{24,8},{1,17},{9,25},{17,1},{25,9},{2,18},{10... | collective-permute-start | bytes 1548296 | tf_op jit(solution)/shard_map/first_y/ppermute | solution.py:808
  28.8 10.4 %collective-permute-start.8 = (bf16[96,768]{1,0:T(8,128)(2,1)S(1)}, bf16[96,768]{1,0:T(8,128)(2,1)S(1)}, u32[]{:S(2)}, u32[]{:S(2)}) collective-permute-start(bf16[96,768]{1,0:T(8,128)(2,1)S(1)} %copy-done.37), channel_id=1, source_target_pairs={{0,4},{1,5},{2,6},{3,7},{4,0},{5,1},{6,2},{7,3},{8,12},{9,13},{10,... | collective-permute-start | bytes 442376 | tf_op jit(solution)/shard_map/up_z2/ppermute | solution.py:802
  30.4 8.7 %collective-permute-start.9 = (bf16[96,768]{1,0:T(8,128)(2,1)S(1)}, bf16[96,768]{1,0:T(8,128)(2,1)S(1)}, u32[]{:S(2)}, u32[]{:S(2)}) collective-permute-start(bf16[96,768]{1,0:T(8,128)(2,1)S(1)} %copy-done.37), channel_id=1, source_target_pairs={{0,6},{1,7},{2,0},{3,1},{4,2},{5,3},{6,4},{7,5},{8,14},{9,15},{10,... | collective-permute-start | bytes 442376 | tf_op jit(solution)/shard_map/up_z3/ppermute | solution.py:802
  39.3 15.7 %collective-permute-start.14 = (bf16[1008,768]{1,0:T(8,128)(2,1)S(1)}, bf16[1008,768]{1,0:T(8,128)(2,1)S(1)}, u32[]{:S(2)}, u32[]{:S(2)}) collective-permute-start(bf16[1008,768]{1,0:T(8,128)(2,1)S(1)} %stack.33.refs_2_), channel_id=1, source_target_pairs={{0,1},{1,0},{2,3},{3,2},{4,5},{5,4},{6,7},{7,6},{8,9},{9,8},{10,11... | collective-permute-start | bytes 4644872 | tf_op jit(solution)/shard_map/first_core/ppermute | solution.py:796
  39.4 15.6 %collective-permute-start.15 = (bf16[912,768]{1,0:T(8,128)(2,1)S(1)}, bf16[912,768]{1,0:T(8,128)(2,1)S(1)}, u32[]{:S(2)}, u32[]{:S(2)}) collective-permute-start(bf16[912,768]{1,0:T(8,128)(2,1)S(1)} %stack.29.refs_0_), channel_id=1, source_target_pairs={{0,1},{1,0},{2,3},{3,2},{4,5},{5,4},{6,7},{7,6},{8,9},{9,8},{10,11... | collective-permute-start | bytes 4202504 | tf_op jit(solution)/shard_map/near_core/ppermute | solution.py:796
  39.9 15.1 %collective-permute-start.12 = (bf16[320,768]{1,0:T(8,128)(2,1)S(1)}, bf16[320,768]{1,0:T(8,128)(2,1)S(1)}, u32[]{:S(2)}, u32[]{:S(2)}) collective-permute-start(bf16[320,768]{1,0:T(8,128)(2,1)S(1)} %stack.31), channel_id=1, source_target_pairs={{0,16},{8,24},{16,0},{24,8},{1,17},{9,25},{17,1},{25,9},{2,18},{10... | collective-permute-start | bytes 1474568 | tf_op jit(solution)/shard_map/diag_y/ppermute | solution.py:808
  40.5 14.5 %collective-permute-start.13 = (bf16[320,768]{1,0:T(8,128)(2,1)S(1)}, bf16[320,768]{1,0:T(8,128)(2,1)S(1)}, u32[]{:S(2)}, u32[]{:S(2)}) collective-permute-start(bf16[320,768]{1,0:T(8,128)(2,1)S(1)} %stack.32), channel_id=1, source_target_pairs={{0,8},{8,0},{16,24},{24,16},{1,9},{9,1},{17,25},{25,17},{2,10},{10... | collective-permute-start | bytes 1474568 | tf_op jit(solution)/shard_map/diag_x/ppermute | solution.py:808
  55.2 12.6 %collective-permute-start.10 = (bf16[288,768]{1,0:T(8,128)(2,1)S(1)}, bf16[288,768]{1,0:T(8,128)(2,1)S(1)}, u32[]{:S(2)}, u32[]{:S(2)}) collective-permute-start(bf16[288,768]{1,0:T(8,128)(2,1)S(1)} %stack.30.refs_0_), channel_id=1, source_target_pairs={{0,8},{8,0},{16,24},{24,16},{1,9},{9,1},{17,25},{25,17},{2,10},{10... | collective-permute-start | bytes 1327112 | tf_op jit(solution)/shard_map/up_x/ppermute | solution.py:808
  56.8 12.3 %collective-permute-start.11 = (bf16[288,768]{1,0:T(8,128)(2,1)S(1)}, bf16[288,768]{1,0:T(8,128)(2,1)S(1)}, u32[]{:S(2)}, u32[]{:S(2)}) collective-permute-start(bf16[288,768]{1,0:T(8,128)(2,1)S(1)} %stack.30.refs_0_), channel_id=1, source_target_pairs={{0,16},{8,24},{16,0},{24,8},{1,17},{9,25},{17,1},{25,9},{2,18},{10... | collective-permute-start | bytes 1327112 | tf_op jit(solution)/shard_map/up_y/ppermute | solution.py:808
  58.3 10.8 %collective-permute-start.19 = (bf16[96,768]{1,0:T(8,128)(2,1)S(1)}, bf16[96,768]{1,0:T(8,128)(2,1)S(1)}, u32[]{:S(2)}, u32[]{:S(2)}) collective-permute-start(bf16[96,768]{1,0:T(8,128)(2,1)S(1)} %copy-done.36), channel_id=1, source_target_pairs={{0,4},{1,5},{2,6},{3,7},{4,0},{5,1},{6,2},{7,3},{8,12},{9,13},{10,... | collective-permute-start | bytes 442376 | tf_op jit(solution)/shard_map/down_z2/ppermute | solution.py:802
  69.1 10.8 %collective-permute-start.22 = (bf16[864,768]{1,0:T(8,128)(2,1)S(1)}, bf16[864,768]{1,0:T(8,128)(2,1)S(1)}, u32[]{:S(2)}, u32[]{:S(2)}) collective-permute-start(bf16[864,768]{1,0:T(8,128)(2,1)S(1)} %stack.35.refs_2_), channel_id=1, source_target_pairs={{0,1},{1,0},{2,3},{3,2},{4,5},{5,4},{6,7},{7,6},{8,9},{9,8},{10,11... | collective-permute-start | bytes 3981320 | tf_op jit(solution)/shard_map/up_core/ppermute | solution.py:796
  69.3 10.7 %collective-permute-start.20 = (bf16[144,768]{1,0:T(8,128)(2,1)S(1)}, bf16[144,768]{1,0:T(8,128)(2,1)S(1)}, u32[]{:S(2)}, u32[]{:S(2)}) collective-permute-start(bf16[144,768]{1,0:T(8,128)(2,1)S(1)} %slice.12), channel_id=1, source_target_pairs={{0,16},{8,24},{16,0},{24,8},{1,17},{9,25},{17,1},{25,9},{2,18},{10... | collective-permute-start | bytes 663560 | tf_op jit(solution)/shard_map/updiag_y/ppermute | solution.py:808
  70.9 9.1 %collective-permute-start.21 = (bf16[144,768]{1,0:T(8,128)(2,1)S(1)}, bf16[144,768]{1,0:T(8,128)(2,1)S(1)}, u32[]{:S(2)}, u32[]{:S(2)}) collective-permute-start(bf16[144,768]{1,0:T(8,128)(2,1)S(1)} %slice.13), channel_id=1, source_target_pairs={{0,8},{8,0},{16,24},{24,16},{1,9},{9,1},{17,25},{25,17},{2,10},{10... | collective-permute-start | bytes 663560 | tf_op jit(solution)/shard_map/updiag_x/ppermute | solution.py:808
  71.4 16.5 %collective-permute-start.24 = (bf16[288,768]{1,0:T(8,128)(2,1)S(1)}, bf16[288,768]{1,0:T(8,128)(2,1)S(1)}, u32[]{:S(2)}, u32[]{:S(2)}) collective-permute-start(bf16[288,768]{1,0:T(8,128)(2,1)S(1)} %stack.37.refs_0_), channel_id=1, source_target_pairs={{0,8},{8,0},{16,24},{24,16},{1,9},{9,1},{17,25},{25,17},{2,10},{10... | collective-permute-start | bytes 1327112 | tf_op jit(solution)/shard_map/down_x/ppermute | solution.py:808
  73.0 14.9 %collective-permute-start.25 = (bf16[288,768]{1,0:T(8,128)(2,1)S(1)}, bf16[288,768]{1,0:T(8,128)(2,1)S(1)}, u32[]{:S(2)}, u32[]{:S(2)}) collective-permute-start(bf16[288,768]{1,0:T(8,128)(2,1)S(1)} %stack.37.refs_0_), channel_id=1, source_target_pairs={{0,16},{8,24},{16,0},{24,8},{1,17},{9,25},{17,1},{25,9},{2,18},{10... | collective-permute-start | bytes 1327112 | tf_op jit(solution)/shard_map/down_y/ppermute | solution.py:808
  88.0 10.5 %collective-permute-start.28 = (bf16[864,768]{1,0:T(8,128)(2,1)S(1)}, bf16[864,768]{1,0:T(8,128)(2,1)S(1)}, u32[]{:S(2)}, u32[]{:S(2)}) collective-permute-start(bf16[864,768]{1,0:T(8,128)(2,1)S(1)} %stack.38.refs_2_), channel_id=1, source_target_pairs={{0,1},{1,0},{2,3},{3,2},{4,5},{5,4},{6,7},{7,6},{8,9},{9,8},{10,11... | collective-permute-start | bytes 3981320 | tf_op jit(solution)/shard_map/down_core/ppermute | solution.py:796
  88.1 9.6 %collective-permute-start.29 = (bf16[384,512]{1,0:T(8,128)(2,1)S(1)}, bf16[384,512]{1,0:T(8,128)(2,1)S(1)}, u32[]{:S(2)}, u32[]{:S(2)}) collective-permute-start(bf16[384,512]{1,0:T(8,128)(2,1)S(1)} %get-tuple-element.344), channel_id=1, source_target_pairs={{0,1},{1,0},{2,3},{3,2},{4,5},{5,4},{6,7},{7,6},{8,9},{9,8},{10,11... | collective-permute-start | bytes 1179656 | tf_op jit(solution)/shard_map/given_core/ppermute | solution.py:796
  88.6 9.2 %collective-permute-start.30 = (bf16[384,512]{1,0:T(8,128)(2,1)S(1)}, bf16[384,512]{1,0:T(8,128)(2,1)S(1)}, u32[]{:S(2)}, u32[]{:S(2)}) collective-permute-start(bf16[384,512]{1,0:T(8,128)(2,1)S(1)} %get-tuple-element.345), channel_id=1, source_target_pairs={{0,1},{1,0},{2,3},{3,2},{4,5},{5,4},{6,7},{7,6},{8,9},{9,8},{10,11... | collective-permute-start | bytes 1179656 | tf_op jit(solution)/shard_map/given_core/ppermute | solution.py:796
  88.7 9.8 %collective-permute-start.26 = (bf16[144,768]{1,0:T(8,128)(2,1)S(1)}, bf16[144,768]{1,0:T(8,128)(2,1)S(1)}, u32[]{:S(2)}, u32[]{:S(2)}) collective-permute-start(bf16[144,768]{1,0:T(8,128)(2,1)S(1)} %slice.14), channel_id=1, source_target_pairs={{0,16},{8,24},{16,0},{24,8},{1,17},{9,25},{17,1},{25,9},{2,18},{10... | collective-permute-start | bytes 663560 | tf_op jit(solution)/shard_map/downdiag_y/ppermute | solution.py:808
  89.3 9.2 %collective-permute-start.27 = (bf16[144,768]{1,0:T(8,128)(2,1)S(1)}, bf16[144,768]{1,0:T(8,128)(2,1)S(1)}, u32[]{:S(2)}, u32[]{:S(2)}) collective-permute-start(bf16[144,768]{1,0:T(8,128)(2,1)S(1)} %slice.15), channel_id=1, source_target_pairs={{0,8},{8,0},{16,24},{24,16},{1,9},{9,1},{17,25},{25,17},{2,10},{10... | collective-permute-start | bytes 663560 | tf_op jit(solution)/shard_map/downdiag_x/ppermute | solution.py:808
  108.1 21.2 %collective-permute-start.37 = (bf16[384,1024]{1,0:T(8,128)(2,1)S(1)}, bf16[384,1024]{1,0:T(8,128)(2,1)S(1)}, u32[]{:S(2)}, u32[]{:S(2)}) collective-permute-start(bf16[384,1024]{1,0:T(8,128)(2,1)S(1)} %get-tuple-element.384), channel_id=1, source_target_pairs={{0,1},{1,0},{2,3},{3,2},{4,5},{5,4},{6,7},{7,6},{8,9},{9,8},{10,11... | collective-permute-start | bytes 2359304 | tf_op jit(solution)/shard_map/given_core/ppermute | solution.py:796
  112.5 15.5 %collective-permute-start.34 = (bf16[2,2,96,768]{3,2,1,0:T(8,128)(2,1)S(1)}, bf16[2,2,96,768]{3,2,1,0:T(8,128)(2,1)S(1)}, u32[]{:S(2)}, u32[]{:S(2)}) collective-permute-start(bf16[2,2,96,768]{3,2,1,0:T(8,128)(2,1)S(1)} %get-tuple-element.378), channel_id=1, source_target_pairs={{0,8},{8,0},{16,24},{24,16},{1,9},{9,1},{17,25},{25,17},{2,10},{10... | collective-permute-start | bytes 1769480 | tf_op jit(solution)/shard_map/gdown_x/ppermute | solution.py:808
  114.1 15.2 %collective-permute-start.35 = (bf16[2,2,96,768]{3,2,1,0:T(8,128)(2,1)S(1)}, bf16[2,2,96,768]{3,2,1,0:T(8,128)(2,1)S(1)}, u32[]{:S(2)}, u32[]{:S(2)}) collective-permute-start(bf16[2,2,96,768]{3,2,1,0:T(8,128)(2,1)S(1)} %get-tuple-element.379), channel_id=1, source_target_pairs={{0,16},{8,24},{16,0},{24,8},{1,17},{9,25},{17,1},{25,9},{2,18},{10... | collective-permute-start | bytes 1769480 | tf_op jit(solution)/shard_map/gdown_y/ppermute | solution.py:808
  115.6 11.9 %collective-permute-start.36 = (bf16[384,512]{1,0:T(8,128)(2,1)S(1)}, bf16[384,512]{1,0:T(8,128)(2,1)S(1)}, u32[]{:S(2)}, u32[]{:S(2)}) collective-permute-start(bf16[384,512]{1,0:T(8,128)(2,1)S(1)} %copy-done.34), channel_id=1, source_target_pairs={{0,1},{1,0},{2,3},{3,2},{4,5},{5,4},{6,7},{7,6},{8,9},{9,8},{10,11... | collective-permute-start | bytes 1179656 | tf_op jit(solution)/shard_map/given_core/ppermute | solution.py:796
  118.4 13.5 %collective-permute-start.41 = (bf16[512,3072]{1,0:T(8,128)(2,1)S(1)}, bf16[512,3072]{1,0:T(8,128)(2,1)S(1)}, u32[]{:S(2)}, u32[]{:S(2)}) collective-permute-start(bf16[512,3072]{1,0:T(8,128)(2,1)S(1)} %get-tuple-element.370.d_hidden), channel_id=1, source_target_pairs={{0,1},{1,0},{2,3},{3,2},{4,5},{5,4},{6,7},{7,6},{8,9},{9,8},{10,11... | collective-permute-start | bytes 9437192 | tf_op jit(solution)/shard_map/d_hidden_core/ppermute | solution.py:796
  129.3 11.7 %collective-permute-start.40 = (bf16[2,512,1536]{2,1,0:T(8,128)(2,1)S(1)}, bf16[2,512,1536]{2,1,0:T(8,128)(2,1)S(1)}, u32[]{:S(2)}, u32[]{:S(2)}) collective-permute-start(bf16[2,512,1536]{2,1,0:T(8,128)(2,1)S(1)} %get-tuple-element.393.refs_12_), channel_id=1, source_target_pairs={{0,1},{1,0},{2,3},{3,2},{4,5},{5,4},{6,7},{7,6},{8,9},{9,8},{10,11... | collective-permute-start | bytes 9437192 | tf_op jit(solution)/shard_map/given_core/ppermute | solution.py:796
  129.3 11.7 %collective-permute-start.39 = (bf16[768,768]{1,0:T(8,128)(2,1)S(1)}, bf16[768,768]{1,0:T(8,128)(2,1)S(1)}, u32[]{:S(2)}, u32[]{:S(2)}) collective-permute-start(bf16[768,768]{1,0:T(8,128)(2,1)S(1)} %attend_back.2.refs_6_.refs_0_), channel_id=1, source_target_pairs={{0,1},{1,0},{2,3},{3,2},{4,5},{5,4},{6,7},{7,6},{8,9},{9,8},{10,11... | collective-permute-start | bytes 3538952 | tf_op jit(solution)/shard_map/d_qkv_core/ppermute | solution.py:796
  129.8 11.2 %collective-permute-start.38 = (bf16[512,768]{1,0:T(8,128)(2,1)S(1)}, bf16[512,768]{1,0:T(8,128)(2,1)S(1)}, u32[]{:S(2)}, u32[]{:S(2)}) collective-permute-start(bf16[512,768]{1,0:T(8,128)(2,1)S(1)} %get-tuple-element.391.refs_10_), channel_id=1, source_target_pairs={{0,1},{1,0},{2,3},{3,2},{4,5},{5,4},{6,7},{7,6},{8,9},{9,8},{10,11... | collective-permute-start | bytes 2359304 | tf_op jit(solution)/shard_map/d_low_core/ppermute | solution.py:796
  130.3 9.8 %collective-permute-start.42 = (bf16[2,96,768]{2,1,0:T(8,128)(2,1)S(1)}, bf16[2,96,768]{2,1,0:T(8,128)(2,1)S(1)}, u32[]{:S(2)}, u32[]{:S(2)}) collective-permute-start(bf16[2,96,768]{2,1,0:T(8,128)(2,1)S(1)} %get-tuple-element.405), channel_id=1, source_target_pairs={{0,16},{8,24},{16,0},{24,8},{1,17},{9,25},{17,1},{25,9},{2,18},{10... | collective-permute-start | bytes 884744 | tf_op jit(solution)/shard_map/gdown2_y/ppermute | solution.py:808
  131.9 9.1 %collective-permute-start.43 = (bf16[2,96,768]{2,1,0:T(8,128)(2,1)S(1)}, bf16[2,96,768]{2,1,0:T(8,128)(2,1)S(1)}, u32[]{:S(2)}, u32[]{:S(2)}) collective-permute-start(bf16[2,96,768]{2,1,0:T(8,128)(2,1)S(1)} %get-tuple-element.406), channel_id=1, source_target_pairs={{0,8},{8,0},{16,24},{24,16},{1,9},{9,1},{17,25},{25,17},{2,10},{10... | collective-permute-start | bytes 884744 | tf_op jit(solution)/shard_map/gdown2_x/ppermute | solution.py:808
  141.1 16.0 %collective-permute-start.46 = (bf16[2,2,96,768]{3,2,1,0:T(8,128)(2,1)}, bf16[2,2,96,768]{3,2,1,0:T(8,128)(2,1)S(1)}, u32[]{:S(2)}, u32[]{:S(2)}) collective-permute-start(bf16[2,2,96,768]{3,2,1,0:T(8,128)(2,1)} %get-tuple-element.422), channel_id=1, source_target_pairs={{0,8},{8,0},{16,24},{24,16},{1,9},{9,1},{17,25},{25,17},{2,10},{10... | collective-permute-start | bytes 1769480 | tf_op jit(solution)/shard_map/gup_x/ppermute | solution.py:808
  141.8 15.4 %collective-permute-start.47 = (bf16[2,2,96,768]{3,2,1,0:T(8,128)(2,1)S(1)}, bf16[2,2,96,768]{3,2,1,0:T(8,128)(2,1)S(1)}, u32[]{:S(2)}, u32[]{:S(2)}) collective-permute-start(bf16[2,2,96,768]{3,2,1,0:T(8,128)(2,1)S(1)} %get-tuple-element.423), channel_id=1, source_target_pairs={{0,16},{8,24},{16,0},{24,8},{1,17},{9,25},{17,1},{25,9},{2,18},{10... | collective-permute-start | bytes 1769480 | tf_op jit(solution)/shard_map/gup_y/ppermute | solution.py:808
  142.4 12.5 %collective-permute-start.48 = (bf16[96,768]{1,0:T(8,128)(2,1)S(1)}, bf16[96,768]{1,0:T(8,128)(2,1)S(1)}, u32[]{:S(2)}, u32[]{:S(2)}) collective-permute-start(bf16[96,768]{1,0:T(8,128)(2,1)S(1)} %get-tuple-element.430), channel_id=1, source_target_pairs={{0,4},{1,5},{2,6},{3,7},{4,0},{5,1},{6,2},{7,3},{8,12},{9,13},{10,... | collective-permute-start | bytes 442376 | tf_op jit(solution)/shard_map/gdown3_z2/ppermute | solution.py:802
  157.4 8.8 %collective-permute-start.49 = (bf16[2,96,768]{2,1,0:T(8,128)(2,1)S(1)}, bf16[2,96,768]{2,1,0:T(8,128)(2,1)S(1)}, u32[]{:S(2)}, u32[]{:S(2)}) collective-permute-start(bf16[2,96,768]{2,1,0:T(8,128)(2,1)S(1)} %get-tuple-element.442), channel_id=1, source_target_pairs={{0,16},{8,24},{16,0},{24,8},{1,17},{9,25},{17,1},{25,9},{2,18},{10... | collective-permute-start | bytes 884744 | tf_op jit(solution)/shard_map/gup2_y/ppermute | solution.py:808
  166.2 15.9 %collective-permute-start.52 = (bf16[2,2,112,768]{3,2,1,0:T(8,128)(2,1)S(1)}, bf16[2,2,112,768]{3,2,1,0:T(8,128)(2,1)S(1)}, u32[]{:S(2)}, u32[]{:S(2)}) collective-permute-start(bf16[2,2,112,768]{3,2,1,0:T(8,128)(2,1)S(1)} %get-tuple-element.446), channel_id=1, source_target_pairs={{0,8},{8,0},{16,24},{24,16},{1,9},{9,1},{17,25},{25,17},{2,10},{10... | collective-permute-start | bytes 2064392 | tf_op jit(solution)/shard_map/gfirst_x/ppermute | solution.py:808
  167.4 15.3 %collective-permute-start.53 = (bf16[2,2,112,768]{3,2,1,0:T(8,128)(2,1)S(1)}, bf16[2,2,112,768]{3,2,1,0:T(8,128)(2,1)S(1)}, u32[]{:S(2)}, u32[]{:S(2)}) collective-permute-start(bf16[2,2,112,768]{3,2,1,0:T(8,128)(2,1)S(1)} %get-tuple-element.447), channel_id=1, source_target_pairs={{0,16},{8,24},{16,0},{24,8},{1,17},{9,25},{17,1},{25,9},{2,18},{10... | collective-permute-start | bytes 2064392 | tf_op jit(solution)/shard_map/gfirst_y/ppermute | solution.py:808
  169.1 12.6 %collective-permute-start.54 = (bf16[96,768]{1,0:T(8,128)(2,1)S(1)}, bf16[96,768]{1,0:T(8,128)(2,1)S(1)}, u32[]{:S(2)}, u32[]{:S(2)}) collective-permute-start(bf16[96,768]{1,0:T(8,128)(2,1)S(1)} %get-tuple-element.461), channel_id=1, source_target_pairs={{0,4},{1,5},{2,6},{3,7},{4,0},{5,1},{6,2},{7,3},{8,12},{9,13},{10,... | collective-permute-start | bytes 442376 | tf_op jit(solution)/shard_map/gup3_z2/ppermute | solution.py:802
  169.6 12.1 %collective-permute-start.55 = (bf16[96,768]{1,0:T(8,128)(2,1)S(1)}, bf16[96,768]{1,0:T(8,128)(2,1)S(1)}, u32[]{:S(2)}, u32[]{:S(2)}) collective-permute-start(bf16[96,768]{1,0:T(8,128)(2,1)S(1)} %get-tuple-element.462), channel_id=1, source_target_pairs={{0,6},{1,7},{2,0},{3,1},{4,2},{5,3},{6,4},{7,5},{8,14},{9,15},{10,... | collective-permute-start | bytes 442376 | tf_op jit(solution)/shard_map/gup3_z3/ppermute | solution.py:802
  183.0 9.7 %collective-permute-start.57 = (bf16[2,112,768]{2,1,0:T(8,128)(2,1)S(1)}, bf16[2,112,768]{2,1,0:T(8,128)(2,1)S(1)}, u32[]{:S(2)}, u32[]{:S(2)}) collective-permute-start(bf16[2,112,768]{2,1,0:T(8,128)(2,1)S(1)} %get-tuple-element.473), channel_id=1, source_target_pairs={{0,16},{8,24},{16,0},{24,8},{1,17},{9,25},{17,1},{25,9},{2,18},{10... | collective-permute-start | bytes 1032200 | tf_op jit(solution)/shard_map/gfirst2_y/ppermute | solution.py:808
  192.9 12.2 %collective-permute-start.60 = (bf16[112,768]{1,0:T(8,128)(2,1)S(1)}, bf16[112,768]{1,0:T(8,128)(2,1)S(1)}, u32[]{:S(2)}, u32[]{:S(2)}) collective-permute-start(bf16[112,768]{1,0:T(8,128)(2,1)S(1)} %get-tuple-element.490), channel_id=1, source_target_pairs={{0,2},{1,3},{2,4},{3,5},{4,6},{5,7},{6,0},{7,1},{8,10},{9,11},{10,... | collective-permute-start | bytes 516104 | tf_op jit(solution)/shard_map/gfirst3_z1/ppermute | solution.py:802
  194.9 11.0 %collective-permute-start.61 = (bf16[112,768]{1,0:T(8,128)(2,1)S(1)}, bf16[112,768]{1,0:T(8,128)(2,1)S(1)}, u32[]{:S(2)}, u32[]{:S(2)}) collective-permute-start(bf16[112,768]{1,0:T(8,128)(2,1)S(1)} %get-tuple-element.491), channel_id=1, source_target_pairs={{0,4},{1,5},{2,6},{3,7},{4,0},{5,1},{6,2},{7,3},{8,12},{9,13},{10,... | collective-permute-start | bytes 516104 | tf_op jit(solution)/shard_map/gfirst3_z2/ppermute | solution.py:802
  196.1 9.8 %collective-permute-start.62 = (bf16[112,768]{1,0:T(8,128)(2,1)S(1)}, bf16[112,768]{1,0:T(8,128)(2,1)S(1)}, u32[]{:S(2)}, u32[]{:S(2)}) collective-permute-start(bf16[112,768]{1,0:T(8,128)(2,1)S(1)} %get-tuple-element.492), channel_id=1, source_target_pairs={{0,6},{1,7},{2,0},{3,1},{4,2},{5,3},{6,4},{7,5},{8,14},{9,15},{10,... | collective-permute-start | bytes 516104 | tf_op jit(solution)/shard_map/gfirst3_z3/ppermute | solution.py:802
  (60 other events, 689.3 us)

commit v5 on v4

--- a/solution.py
+++ b/solution.py
@@ -403,16 +403,20 @@
 def lower_kernel(marks, count, *refs):
     actives, (normed, weight, vec), refs = refs[:count], refs[count : count + 3], refs[count + 3 :]
     bias, gain, shift = (vec[:, a:b] for a, b in marks)
-    total = normed[...] + bias
-    first = 0
-    for active in actives:
-        last = first + active.shape[1]
-        total = total + nt(active[...], weight[:, first:last])
-        first = last
+    half = normed.shape[0] // 2
+    totals = []
+    for r in (0, half):
+        total = normed[r : r + half, :] + bias
+        first = 0
+        for active in actives:
+            last = first + active.shape[1]
+            total = total + nt(active[r : r + half, :], weight[:, first:last])
+            first = last
+        totals.append(total)
     step = 128
     for r in range(0, normed.shape[0], step):
         at = slice(r, r + step)
-        summed = total[at, :]
+        summed = totals[r // half][r % half : r % half + step, :]
         shaped, inverse = norm_stats(summed)
         if len(refs) == 1:
             refs[0][at, :] = (shaped * gain + shift).astype(BF)

time: 230 us -> 229 us (level)
  no operation moved by 1% of the time
where the time goes in v5:
time: 229 us; the launch traced here: 225 us
  Pallas kernels  90.2 us (39%)
  starting transfers between devices  74.7 us (33%)
  waiting for transfers between devices  51.6 us (23%)
  local copies, waits for them, and re-layouts  4.44 us (2%)
    pallas_call x45, Pallas kernels, call(): pl.pallas_call(kernel, name=name, out_shape=outs, in_specs=specs, out_spe...  90.2 us
    ppermute x21, starting transfers between devices, shift_slot(): return lax.ppermute(value, 'dp', [(i, (i + 2 * by) % n) for i in range(n)])  38.7 us
    ppermute x29, starting transfers between devices, swap_fsdp(): return lax.ppermute(value, 'fsdp', [(i, i ^ bits) for i in range(n)])  32.4 us
    ppermute x21, waiting for transfers between devices, shift_slot(): return lax.ppermute(value, 'dp', [(i, (i + 2 * by) % n) for i in range(n)])  27.2 us
    ppermute x29, waiting for transfers between devices, swap_fsdp(): return lax.ppermute(value, 'fsdp', [(i, i ^ bits) for i in range(n)])  20.2 us
  transfers between devices with their start and end apart: 70, of which 28 were waited for; matrix products, arithmetic and copies ran while one was open for 1% of the time, Pallas kernels for 37%

profile of v5, /device:TPU:0, one launch (start us, length us, event | category | flops | bytes accessed | tf_op | source)
XLA Modules:
  0.0 225.1 jit_solution(1377287512908401852)
XLA Ops:
  1.3 3.0 %pack_weights.1 = (bf16[304,768]{1,0:T(8,128)(2,1)}, bf16[112,768]{1,0:T(8,128)(2,1)}, bf16[96,768]{1,0:T(8,128)(2,1)}, bf16[96,768]{1,0:T(8,128)(2,1)}) custom-call(s32[3]{0:T(128)} %pad_add_fusion.place, f32[96,576]{1,0:T(8,128)} %refs_0_.3, f32[96,192]{1,0:T(8,128)} %refs_3_.1, f32[96,768]{1,0:T(8,128)} %refs_6_.1, f32[192,384]{1,0:T(8,128)} %bitcast.34, ...), custom_call_target="tpu_custom_call" | custom-call | bytes 1836 | tf_op jit(solution)/shard_map/pack_weights/pallas_call | solution.py:54
  4.3 3.1 %collective-permute-start = (bf16[112,768]{1,0:T(8,128)(2,1)}, bf16[112,768]{1,0:T(8,128)(2,1)S(1)}, u32[]{:S(2)}, u32[]{:S(2)}) collective-permute-start(bf16[112,768]{1,0:T(8,128)(2,1)} %get-tuple-element.283), channel_id=1, source_target_pairs={{0,2},{1,3},{2,4},{3,5},{4,6},{5,7},{6,0},{7,1},{8,10},{9,11},{10,... | collective-permute-start | bytes 516104 | tf_op jit(solution)/shard_map/first_z1/ppermute | solution.py:806
  7.4 2.6 %collective-permute-start.1 = (bf16[112,768]{1,0:T(8,128)(2,1)}, bf16[112,768]{1,0:T(8,128)(2,1)S(1)}, u32[]{:S(2)}, u32[]{:S(2)}) collective-permute-start(bf16[112,768]{1,0:T(8,128)(2,1)} %get-tuple-element.283), channel_id=1, source_target_pairs={{0,4},{1,5},{2,6},{3,7},{4,0},{5,1},{6,2},{7,3},{8,12},{9,13},{10,... | collective-permute-start | bytes 516104 | tf_op jit(solution)/shard_map/first_z2/ppermute | solution.py:806
  18.0 2.4 %order_rows.1 = (bf16[2,256,768]{2,1,0:T(8,128)(2,1)S(1)}, bf16[2,256,768]{2,1,0:T(8,128)(2,1)S(1)}, bf16[384,512]{1,0:T(8,128)(2,1)S(1)}, bf16[384,512]{1,0:T(8...) custom-call(s32[3]{0:T(128)S(1)} %copy-done.25, ...), custom_call_target="tpu_custom_call" | custom-call | flops 805306 | bytes 6555 | tf_op jit(solution)/shard_map/order_rows/pallas_call | solution.py:54
  21.5 1.7 collective-permute-done.3.refs_1_.refs_0_
  26.5 2.2 collective-permute-start.7
  28.8 1.6 collective-permute-start.8
  31.3 3.9 %collective-permute-done.7.refs_0_ = bf16[96,768]{1,0:T(8,128)(2,1)S(1)} collective-permute-done((bf16[96,768]{1,0:T(8,128)(2,1)S(1)}, bf16[96,768]{1,0:T(8,128)(2,1)S(1)}, u32[]{:S(2)}, u32[]{:S(2)}) %collective-permute-start.7) | collective-permute-done | bytes 147488 | tf_op jit(solution)/shard_map/up_z1/ppermute | solution.py:806
  35.1 4.0 %collective-permute-done.8.refs_1_ = bf16[96,768]{1,0:T(8,128)(2,1)S(1)} collective-permute-done((bf16[96,768]{1,0:T(8,128)(2,1)S(1)}, bf16[96,768]{1,0:T(8,128)(2,1)S(1)}, u32[]{:S(2)}, u32[]{:S(2)}) %collective-permute-start.8) | collective-permute-done | bytes 147488 | tf_op jit(solution)/shard_map/up_z2/ppermute | solution.py:806
  41.4 3.4 %collective-permute-start.16 = (bf16[96,768]{1,0:T(8,128)(2,1)S(1)}, bf16[96,768]{1,0:T(8,128)(2,1)S(1)}, u32[]{:S(2)}, u32[]{:S(2)}) collective-permute-start(bf16[96,768]{1,0:T(8,128)(2,1)S(1)} %copy-done.36), channel_id=1, source_target_pairs={{0,2},{1,3},{2,4},{3,5},{4,6},{5,7},{6,0},{7,1},{8,10},{9,11},{10,... | collective-permute-start | bytes 442376 | tf_op jit(solution)/shard_map/down_z1/ppermute | solution.py:806
  44.8 4.8 %collective-permute-done.16.refs_0_ = bf16[96,768]{1,0:T(8,128)(2,1)S(1)} collective-permute-done((bf16[96,768]{1,0:T(8,128)(2,1)S(1)}, bf16[96,768]{1,0:T(8,128)(2,1)S(1)}, u32[]{:S(2)}, u32[]{:S(2)}) %collective-permute-start.16) | collective-permute-done | bytes 147488 | tf_op jit(solution)/shard_map/down_z1/ppermute | solution.py:806
  49.6 2.0 collective-permute-start.17
  51.6 3.4 %collective-permute-done.17.refs_2_ = bf16[96,768]{1,0:T(8,128)(2,1)S(1)} collective-permute-done((bf16[96,768]{1,0:T(8,128)(2,1)S(1)}, bf16[96,768]{1,0:T(8,128)(2,1)S(1)}, u32[]{:S(2)}, u32[]{:S(2)}) %collective-permute-start.17) | collective-permute-done | bytes 147488 | tf_op jit(solution)/shard_map/down_z3/ppermute | solution.py:806
  58.6 2.0 whole_first.1
  60.6 6.2 %make_qkv.1 = (bf16[2,256,768]{2,1,0:T(8,128)(2,1)S(1)}, bf16[2,256,768]{2,1,0:T(8,128)(2,1)S(1)}, bf16[2,512,1536]{2,1,0:T(8,128)(2,1)S(1)}, bf16[2,256,1536]{2,1,0:T(8,128)(2,1)S(1)}) custom-call(bf16[2,256,768]{2,1,0:T(8,128)(2,1)S(1)} %get-tuple-element.301.front, bf16[2,256,768]{2,1,0:T(8,128)(2,1)S(1)} %get-tuple-element.302.rest, ...), custom_call_target="tpu_custom_call" | custom-call | flops 4429185 | bytes 13278 | tf_op jit(solution)/shard_map/make_qkv/pallas_call | solution.py:54
  69.3 1.6 collective-permute-start.20
  73.5 4.0 %attend.1 = (bf16[2,256,768]{2,1,0:T(8,128)(2,1)S(1)}, bf16[2,256,768]{2,1,0:T(8,128)(2,1)S(1)}) custom-call(bf16[2,256,768]{2,1,0:T(8,128)(2,1)S(1)} %get-tuple-element.321.q_front.queries, bf16[2,256,768]{2,1,0:T(8,128)(2,1)S(1)} %get-tuple-element.325.q_rest, bf16[2,256,1536]{2,1,0:T(8,128)(2,1)S(1)} %get-tuple-element.322.kvp), custom_call_target="tpu_custom_call" | custom-call | flops 1610612 | bytes 4718 | tf_op jit(solution)/shard_map/attend/pallas_call | solution.py:54
  77.5 2.4 %join_front.1 = (f32[512,768]{1,0:T(8,128)S(1)}, bf16[512,768]{1,0:T(8,128)(2,1)S(1)}, f32[512,768]{1,0:T(8,128)S(1)}, bf16[384,512]{1,0:T(8,128)(2,1)S(1)}, bf1...) custom-call(s32[3]{0:T(128)S(1)} %copy-done.25, ...), custom_call_target="tpu_custom_call" | custom-call | flops 603979 | bytes 8297 | tf_op jit(solution)/shard_map/join_front/pallas_call | solution.py:54
  80.1 7.8 %collective-permute-done.24.refs_1_ = bf16[288,768]{1,0:T(8,128)(2,1)S(1)} collective-permute-done((bf16[288,768]{1,0:T(8,128)(2,1)S(1)}, bf16[288,768]{1,0:T(8,128)(2,1)S(1)}, u32[]{:S(2)}, u32[]{:S(2)}) %collective-permute-start.24) | collective-permute-done | bytes 442400 | tf_op jit(solution)/shard_map/down_x/ppermute | solution.py:812
  90.7 7.0 %lift_front.1 = (bf16[512,3072]{1,0:T(8,128)(2,1)S(1)}, bf16[512,3072]{1,0:T(8,128)(2,1)S(1)}, bf16[512,1536]{1,0:T(8,128)(2,1)S(1)}) custom-call(s32[3]{0:T(128)S(1)} %copy-done.25, bf16[512,768]{1,0:T(8,128)(2,1)S(1)} %get-tuple-element.339.low, bf16[4,768,768]{2,1,0:T(8,128)(2,1)S(1)} %whole_up.1.weight.up, ...), custom_call_target="tpu_custom_call" | custom-call | flops 2415919 | bytes 13409 | tf_op jit(solution)/shard_map/lift_front/pallas_call | solution.py:54
  98.6 1.8 collective-permute-done.31.refs_7_
  101.5 3.6 %lower_front.1 = (bf16[512,768]{1,0:T(8,128)(2,1)S(1)}, f32[512,768]{1,0:T(8,128)S(1)}, bf16[512,768]{1,0:T(8,128)(2,1)S(1)}, bf16[768,512]{1,0:T(8,128)(2,1)S(1)}, f32[8,768]{1,0:T(8,128)S(1)}) custom-call(bf16[512,3072]{1,0:T(8,128)(2,1)S(1)} %get-tuple-element.346.refs_0_.active, f32[512,768]{1,0:T(8,128)S(1)} %get-tuple-element.347.refs_1_, ...), custom_call_target="tpu_custom_call" | custom-call | flops 2415919 | bytes 14220 | tf_op jit(solution)/shard_map/lower_front/pallas_call | solution.py:54
  105.6 1.9 join_rest.1
  107.9 4.1 %grad_down.1 = (bf16[2,2,96,768]{3,2,1,0:T(8,128)(2,1)S(1)}, bf16[2,2,96,768]{3,2,1,0:T(8,128)(2,1)S(1)}, bf16[2,2,96,768]{3,2,1,0:T(8,128)(2,1)S(1)}, bf16[2,2,96,768]{3,2,1,0:T(8,128)(2,1)S(1)}) custom-call(s32[3]{0:T(128)S(1)} %copy-done.25, bf16[768,512]{1,0:T(8,128)(2,1)S(1)} %get-tuple-element.355.d_lowt, ...), custom_call_target="tpu_custom_call" | custom-call | flops 4831838 | bytes 8650 | tf_op jit(solution)/shard_map/grad_down/pallas_call | solution.py:54
  115.1 2.7 %hidden_back.1 = (bf16[512,3072]{1,0:T(8,128)(2,1)S(1)}, f32[1,3072]{1,0:T(1,128)S(1)}) custom-call(bf16[512,768]{1,0:T(8,128)(2,1)S(1)} %get-tuple-element.368.d_low, bf16[768,3072]{1,0:T(8,128)(2,1)S(1)} %whole_down.1.refs_2_.weight.refs_3_, bf16[512,3072]{1,0:T(8,128)(2,1)S(1)} %get-tuple-element.369.slope), custom_call_target="tpu_custom_call" | custom-call | flops 2415919 | bytes 11808 | tf_op jit(solution)/shard_map/hidden_back/pallas_call | solution.py:54
  118.5 5.1 %first_back.1 = (f32[512,768]{1,0:T(8,128)S(1)}, bf16[512,768]{1,0:T(8,128)(2,1)S(1)}, bf16[512,768]{1,0:T(8,128)(2,1)S(1)}, f32[16,768]{1,0:T(8,128)S(1)}) custom-call(bf16[512,3072]{1,0:T(8,128)(2,1)S(1)} %get-tuple-element.370.d_hidden, bf16[4,768,768]{2,1,0:T(8,128)(2,1)S(1)} %whole_up.1.weight.up, f32[512,768]{1,0:T(8,128)S(1)} %get-tuple-element.371.d_sum, ...), custom_call_target="tpu_custom_call" | custom-call | flops 3019898 | bytes 15461 | tf_op jit(solution)/shard_map/first_back/pallas_call | solution.py:54
  123.6 3.5 %attend_back.2.refs_6_.refs_0_ = bf16[768,768]{1,0:T(8,128)(2,1)S(1)} custom-call(bf16[2,256,768]{2,1,0:T(8,128)(2,1)S(1)} %get-tuple-element.321.q_front.queries, bf16[2,256,1536]{2,1,0:T(8,128)(2,1)S(1)} %get-tuple-element.322.kvp, bf16[2,256,768]{2,1,0:T(8,128)(2,1)S(1)} %bitcast.29), custom_call_target="tpu_custom_call" | custom-call | flops 1006632 | bytes 4325 | tf_op jit(solution)/shard_map/attend_back/pallas_call | solution.py:54
  129.6 1.6 collective-permute-start.42
  131.8 3.5 %attend_back.3.refs_7_.refs_1_ = bf16[768,768]{1,0:T(8,128)(2,1)S(1)} custom-call(bf16[2,256,768]{2,1,0:T(8,128)(2,1)S(1)} %get-tuple-element.321.q_front.queries, bf16[2,256,1536]{2,1,0:T(8,128)(2,1)S(1)} %get-tuple-element.322.kvp, bf16[2,256,768]{2,1,0:T(8,128)(2,1)S(1)} %bitcast.30), custom_call_target="tpu_custom_call" | custom-call | flops 1006632 | bytes 4325 | tf_op jit(solution)/shard_map/attend_back/pallas_call | solution.py:54
  135.3 4.2 %grad_up.1 = (bf16[2,2,96,768]{3,2,1,0:T(8,128)(2,1)}, bf16[2,2,96,768]{3,2,1,0:T(8,128)(2,1)S(1)}, bf16[2,2,96,768]{3,2,1,0:T(8,128)(2,1)S(1)}, bf16[2,2,96,768]{3,2,1,0:T(8,128)(2,1)S(1)}) custom-call(s32[3]{0:T(128)S(1)} %copy-done.25, bf16[384,512]{1,0:T(8,128)(2,1)S(1)} %get-tuple-element.394.lowt, ...), custom_call_target="tpu_custom_call" | custom-call | flops 2415919 | bytes 9437 | tf_op jit(solution)/shard_map/grad_up/pallas_call | solution.py:54
  145.3 8.8 %grad_rest.1 = (bf16[2,2,112,768]{3,2,1,0:T(8,128)(2,1)S(1)}, bf16[2,2,112,768]{3,2,1,0:T(8,128)(2,1)S(1)}, bf16[2,2,112,768]{3,2,1,0:T(8,128)(2,1)S(1)}, bf16[2,2,112,768]{3,2,1,0:T(8,128)(2,1)S(1)}) custom-call(s32[3]{0:T(128)S(1)} %copy-done.25, bf16[384,1024]{1,0:T(8,128)(2,1)S(1)} %copy-done.7, bf16[384,1024]{1,0:T(8,128)(2,1)S(1)} %collective-permute-done.37.refs_1_, ...), custom_call_target="tpu_custom_call" | custom-call | flops 4831838 | bytes 18841 | tf_op jit(solution)/shard_map/grad_rest/pallas_call | solution.py:54
  154.2 2.2 collective-permute-done.46.from_x
  158.7 3.5 %collective-permute-start.51 = (bf16[96,768]{1,0:T(8,128)(2,1)S(1)}, bf16[96,768]{1,0:T(8,128)(2,1)S(1)}, u32[]{:S(2)}, u32[]{:S(2)}) collective-permute-start(bf16[96,768]{1,0:T(8,128)(2,1)S(1)} %get-tuple-element.445), channel_id=1, source_target_pairs={{0,6},{1,7},{2,0},{3,1},{4,2},{5,3},{6,4},{7,5},{8,14},{9,15},{10,... | collective-permute-start | bytes 442376 | tf_op jit(solution)/shard_map/gdown3_z3/ppermute | solution.py:806
  162.3 3.2 %lift_rest.2.refs_0_ = bf16[512,1536]{1,0:T(8,128)(2,1)S(1)} custom-call(s32[3]{0:T(128)S(1)} %copy-done.25, bf16[512,768]{1,0:T(8,128)(2,1)S(1)} %get-tuple-element.452.low, bf16[4,768,768]{2,1,0:T(8,128)(2,1)S(1)} %whole_up.1.weight.up, f32[1,9984]{1,0:T(1,128)S(1)} %get-tuple-element.315.vec.refs_3_.refs_4_), custom_call_target="tpu_custom_call" | custom-call | flops 1207959 | bytes 7117 | tf_op jit(solution)/shard_map/lift_rest/pallas_call | solution.py:54
  168.9 3.5 %collective-permute-start.55 = (bf16[96,768]{1,0:T(8,128)(2,1)S(1)}, bf16[96,768]{1,0:T(8,128)(2,1)S(1)}, u32[]{:S(2)}, u32[]{:S(2)}) collective-permute-start(bf16[96,768]{1,0:T(8,128)(2,1)S(1)} %get-tuple-element.462), channel_id=1, source_target_pairs={{0,6},{1,7},{2,0},{3,1},{4,2},{5,3},{6,4},{7,5},{8,14},{9,15},{10,... | collective-permute-start | bytes 442376 | tf_op jit(solution)/shard_map/gup3_z3/ppermute | solution.py:806
  172.6 3.2 %lift_rest.3.refs_1_ = bf16[512,1536]{1,0:T(8,128)(2,1)S(1)} custom-call(s32[3]{0:T(128)S(1)} %copy-done.25, bf16[512,768]{1,0:T(8,128)(2,1)S(1)} %get-tuple-element.452.low, bf16[4,768,768]{2,1,0:T(8,128)(2,1)S(1)} %whole_up.1.weight.up, f32[1,9984]{1,0:T(1,128)S(1)} %get-tuple-element.315.vec.refs_3_.refs_4_), custom_call_target="tpu_custom_call" | custom-call | flops 1207959 | bytes 7117 | tf_op jit(solution)/shard_map/lift_rest/pallas_call | solution.py:54
  175.8 3.1 %lower_rest.1 = bf16[512,768]{1,0:T(8,128)(2,1)S(1)} custom-call(bf16[512,1536]{1,0:T(8,128)(2,1)S(1)} %lift_rest.2.refs_0_, bf16[512,1536]{1,0:T(8,128)(2,1)S(1)} %lift_rest.3.refs_1_, f32[512,768]{1,0:T(8,128)S(1)} %get-tuple-element.453.refs_2_, bf16[768,3072]{1,0:T(8,128)(2,1)S(1)} %whole_down.1.refs_2_.weight.refs_3_, ...), custom_call_target="tpu_custom_call" | custom-call | flops 2415919 | bytes 10263 | tf_op jit(solution)/shard_map/lower_rest/pallas_call | solution.py:54
  178.9 2.1 restore_order.1
  185.1 1.6 collective-permute-start.59
  186.9 5.1 %collective-permute-done.59.refs_1_ = bf16[96,768]{1,0:T(8,128)(2,1)S(1)} collective-permute-done((bf16[96,768]{1,0:T(8,128)(2,1)S(1)}, bf16[96,768]{1,0:T(8,128)(2,1)S(1)}, u32[]{:S(2)}, u32[]{:S(2)}) %collective-permute-start.59) | collective-permute-done | bytes 147488 | tf_op jit(solution)/shard_map/gup3_z1/ppermute | solution.py:806
  192.2 2.0 collective-permute-start.60
  195.4 2.0 collective-permute-start.62
  197.8 6.6 %input_back.1 = bf16[2,512,768]{2,1,0:T(8,128)(2,1)} custom-call(bf16[512,256]{1,0:T(8,128)(2,1)S(1)} %get-tuple-element.416.refs_16_.projt, f32[2,256,768]{2,1,0:T(8,128)S(1)} %bitcast.33, bf16[768,2304]{1,0:T(8,128)(2,1)S(1)} %get-tuple-element.314.weight, bf16[2,512,512]{2,1,0:T(8,128)(2,1)S(1)} %get-tuple-element.454.back, ...), custom_call_target="tpu_custom_call" | custom-call | flops 4429185 | bytes 10354 | tf_op jit(solution)/shard_map/input_back/pallas_call | solution.py:54
  205.5 2.5 %collective-permute-start.64 = (f32[8,128]{1,0:T(8,128)S(1)}, f32[8,128]{1,0:T(8,128)S(1)}, u32[]{:S(2)}, u32[]{:S(2)}) collective-permute-start(f32[8,128]{1,0:T(8,128)S(1)} %add_add_fusion.2), channel_id=1, source_target_pairs={{0,2},{1,3},{2,4},{3,5},{4,6},{5,7},{6,0},{7,1},{8,10},{9,11},{10,... | collective-permute-start | bytes 12296 | tf_op jit(solution)/shard_map/norm_z1/ppermute | solution.py:806
  208.0 2.8 %collective-permute-start.65 = (f32[8,128]{1,0:T(8,128)S(1)}, f32[8,128]{1,0:T(8,128)S(1)}, u32[]{:S(2)}, u32[]{:S(2)}) collective-permute-start(f32[8,128]{1,0:T(8,128)S(1)} %add_add_fusion.2), channel_id=1, source_target_pairs={{0,6},{1,7},{2,0},{3,1},{4,2},{5,3},{6,4},{7,5},{8,14},{9,15},{10,... | collective-permute-start | bytes 12296 | tf_op jit(solution)/shard_map/norm_z3/ppermute | solution.py:806
  212.3 3.0 %collective-permute-done.63 = f32[8,128]{1,0:T(8,128)S(1)} collective-permute-done((f32[8,128]{1,0:T(8,128)S(1)}, f32[8,128]{1,0:T(8,128)S(1)}, u32[]{:S(2)}, u32[]{:S(2)}) %collective-permute-start.63) | collective-permute-done | bytes 4128 | tf_op jit(solution)/shard_map/norm_z2/ppermute | solution.py:806
  218.2 1.8 collective-permute-start.67
  221.9 3.0 %update.1 = (f32[1,1]{1,0:T(1,128)}, f32[96,576]{1,0:T(8,128)}, f32[96,576]{1,0:T(8,128)}, f32[96,576]{1,0:T(8,128)}, bf16[96,576]{1,0:T(8,128)(2,1)}, /*index=5...) custom-call(s32[3]{0:T(128)S(1)} %copy-done.25, ...), custom_call_target="tpu_custom_call" | custom-call | bytes 6803 | tf_op jit(solution)/shard_map/update/pallas_call | solution.py:54
  (228 shorter events, 61.8 us)
Async XLA Ops:
  4.3 16.0 %collective-permute-start = (bf16[112,768]{1,0:T(8,128)(2,1)}, bf16[112,768]{1,0:T(8,128)(2,1)S(1)}, u32[]{:S(2)}, u32[]{:S(2)}) collective-permute-start(bf16[112,768]{1,0:T(8,128)(2,1)} %get-tuple-element.283), channel_id=1, source_target_pairs={{0,2},{1,3},{2,4},{3,5},{4,6},{5,7},{6,0},{7,1},{8,10},{9,11},{10,... | collective-permute-start | bytes 516104 | tf_op jit(solution)/shard_map/first_z1/ppermute | solution.py:806
  7.4 14.1 %collective-permute-start.1 = (bf16[112,768]{1,0:T(8,128)(2,1)}, bf16[112,768]{1,0:T(8,128)(2,1)S(1)}, u32[]{:S(2)}, u32[]{:S(2)}) collective-permute-start(bf16[112,768]{1,0:T(8,128)(2,1)} %get-tuple-element.283), channel_id=1, source_target_pairs={{0,4},{1,5},{2,6},{3,7},{4,0},{5,1},{6,2},{7,3},{8,12},{9,13},{10,... | collective-permute-start | bytes 516104 | tf_op jit(solution)/shard_map/first_z2/ppermute | solution.py:806
  10.0 11.5 %collective-permute-start.2 = (bf16[112,768]{1,0:T(8,128)(2,1)}, bf16[112,768]{1,0:T(8,128)(2,1)S(1)}, u32[]{:S(2)}, u32[]{:S(2)}) collective-permute-start(bf16[112,768]{1,0:T(8,128)(2,1)} %get-tuple-element.283), channel_id=1, source_target_pairs={{0,6},{1,7},{2,0},{3,1},{4,2},{5,3},{6,4},{7,5},{8,14},{9,15},{10,... | collective-permute-start | bytes 516104 | tf_op jit(solution)/shard_map/first_z3/ppermute | solution.py:806
  11.4 11.8 %collective-permute-start.3 = (bf16[304,768]{1,0:T(8,128)(2,1)}, bf16[304,768]{1,0:T(8,128)(2,1)S(1)}, u32[]{:S(2)}, u32[]{:S(2)}) collective-permute-start(bf16[304,768]{1,0:T(8,128)(2,1)} %get-tuple-element.296.refs_0_), channel_id=1, source_target_pairs={{0,8},{8,0},{16,24},{24,16},{1,9},{9,1},{17,25},{25,17},{2,10},{10... | collective-permute-start | bytes 1400840 | tf_op jit(solution)/shard_map/own_x/ppermute | solution.py:812
  12.8 11.5 %collective-permute-start.4 = (bf16[304,768]{1,0:T(8,128)(2,1)}, bf16[304,768]{1,0:T(8,128)(2,1)S(1)}, u32[]{:S(2)}, u32[]{:S(2)}) collective-permute-start(bf16[304,768]{1,0:T(8,128)(2,1)} %get-tuple-element.296.refs_0_), channel_id=1, source_target_pairs={{0,16},{8,24},{16,0},{24,8},{1,17},{9,25},{17,1},{25,9},{2,18},{10... | collective-permute-start | bytes 1400840 | tf_op jit(solution)/shard_map/own_y/ppermute | solution.py:812
  24.4 14.8 %collective-permute-start.5 = (bf16[336,768]{1,0:T(8,128)(2,1)S(1)}, bf16[336,768]{1,0:T(8,128)(2,1)S(1)}, u32[]{:S(2)}, u32[]{:S(2)}) collective-permute-start(bf16[336,768]{1,0:T(8,128)(2,1)S(1)} %stack.28.refs_0_), channel_id=1, source_target_pairs={{0,8},{8,0},{16,24},{24,16},{1,9},{9,1},{17,25},{25,17},{2,10},{10... | collective-permute-start | bytes 1548296 | tf_op jit(solution)/shard_map/first_x/ppermute | solution.py:812
  25.0 14.2 %collective-permute-start.6 = (bf16[336,768]{1,0:T(8,128)(2,1)S(1)}, bf16[336,768]{1,0:T(8,128)(2,1)S(1)}, u32[]{:S(2)}, u32[]{:S(2)}) collective-permute-start(bf16[336,768]{1,0:T(8,128)(2,1)S(1)} %stack.28.refs_0_), channel_id=1, source_target_pairs={{0,16},{8,24},{16,0},{24,8},{1,17},{9,25},{17,1},{25,9},{2,18},{10... | collective-permute-start | bytes 1548296 | tf_op jit(solution)/shard_map/first_y/ppermute | solution.py:812
  28.8 10.4 %collective-permute-start.8 = (bf16[96,768]{1,0:T(8,128)(2,1)S(1)}, bf16[96,768]{1,0:T(8,128)(2,1)S(1)}, u32[]{:S(2)}, u32[]{:S(2)}) collective-permute-start(bf16[96,768]{1,0:T(8,128)(2,1)S(1)} %copy-done.37), channel_id=1, source_target_pairs={{0,4},{1,5},{2,6},{3,7},{4,0},{5,1},{6,2},{7,3},{8,12},{9,13},{10,... | collective-permute-start | bytes 442376 | tf_op jit(solution)/shard_map/up_z2/ppermute | solution.py:806
  39.3 15.7 %collective-permute-start.14 = (bf16[1008,768]{1,0:T(8,128)(2,1)S(1)}, bf16[1008,768]{1,0:T(8,128)(2,1)S(1)}, u32[]{:S(2)}, u32[]{:S(2)}) collective-permute-start(bf16[1008,768]{1,0:T(8,128)(2,1)S(1)} %stack.33.refs_2_), channel_id=1, source_target_pairs={{0,1},{1,0},{2,3},{3,2},{4,5},{5,4},{6,7},{7,6},{8,9},{9,8},{10,11... | collective-permute-start | bytes 4644872 | tf_op jit(solution)/shard_map/first_core/ppermute | solution.py:800
  39.4 15.6 %collective-permute-start.15 = (bf16[912,768]{1,0:T(8,128)(2,1)S(1)}, bf16[912,768]{1,0:T(8,128)(2,1)S(1)}, u32[]{:S(2)}, u32[]{:S(2)}) collective-permute-start(bf16[912,768]{1,0:T(8,128)(2,1)S(1)} %stack.29.refs_0_), channel_id=1, source_target_pairs={{0,1},{1,0},{2,3},{3,2},{4,5},{5,4},{6,7},{7,6},{8,9},{9,8},{10,11... | collective-permute-start | bytes 4202504 | tf_op jit(solution)/shard_map/near_core/ppermute | solution.py:800
  39.9 15.1 %collective-permute-start.12 = (bf16[320,768]{1,0:T(8,128)(2,1)S(1)}, bf16[320,768]{1,0:T(8,128)(2,1)S(1)}, u32[]{:S(2)}, u32[]{:S(2)}) collective-permute-start(bf16[320,768]{1,0:T(8,128)(2,1)S(1)} %stack.31), channel_id=1, source_target_pairs={{0,16},{8,24},{16,0},{24,8},{1,17},{9,25},{17,1},{25,9},{2,18},{10... | collective-permute-start | bytes 1474568 | tf_op jit(solution)/shard_map/diag_y/ppermute | solution.py:812
  40.5 14.5 %collective-permute-start.13 = (bf16[320,768]{1,0:T(8,128)(2,1)S(1)}, bf16[320,768]{1,0:T(8,128)(2,1)S(1)}, u32[]{:S(2)}, u32[]{:S(2)}) collective-permute-start(bf16[320,768]{1,0:T(8,128)(2,1)S(1)} %stack.32), channel_id=1, source_target_pairs={{0,8},{8,0},{16,24},{24,16},{1,9},{9,1},{17,25},{25,17},{2,10},{10... | collective-permute-start | bytes 1474568 | tf_op jit(solution)/shard_map/diag_x/ppermute | solution.py:812
  55.2 12.6 %collective-permute-start.10 = (bf16[288,768]{1,0:T(8,128)(2,1)S(1)}, bf16[288,768]{1,0:T(8,128)(2,1)S(1)}, u32[]{:S(2)}, u32[]{:S(2)}) collective-permute-start(bf16[288,768]{1,0:T(8,128)(2,1)S(1)} %stack.30.refs_0_), channel_id=1, source_target_pairs={{0,8},{8,0},{16,24},{24,16},{1,9},{9,1},{17,25},{25,17},{2,10},{10... | collective-permute-start | bytes 1327112 | tf_op jit(solution)/shard_map/up_x/ppermute | solution.py:812
  56.8 12.3 %collective-permute-start.11 = (bf16[288,768]{1,0:T(8,128)(2,1)S(1)}, bf16[288,768]{1,0:T(8,128)(2,1)S(1)}, u32[]{:S(2)}, u32[]{:S(2)}) collective-permute-start(bf16[288,768]{1,0:T(8,128)(2,1)S(1)} %stack.30.refs_0_), channel_id=1, source_target_pairs={{0,16},{8,24},{16,0},{24,8},{1,17},{9,25},{17,1},{25,9},{2,18},{10... | collective-permute-start | bytes 1327112 | tf_op jit(solution)/shard_map/up_y/ppermute | solution.py:812
  58.3 10.8 %collective-permute-start.19 = (bf16[96,768]{1,0:T(8,128)(2,1)S(1)}, bf16[96,768]{1,0:T(8,128)(2,1)S(1)}, u32[]{:S(2)}, u32[]{:S(2)}) collective-permute-start(bf16[96,768]{1,0:T(8,128)(2,1)S(1)} %copy-done.36), channel_id=1, source_target_pairs={{0,4},{1,5},{2,6},{3,7},{4,0},{5,1},{6,2},{7,3},{8,12},{9,13},{10,... | collective-permute-start | bytes 442376 | tf_op jit(solution)/shard_map/down_z2/ppermute | solution.py:806
  69.1 10.8 %collective-permute-start.22 = (bf16[864,768]{1,0:T(8,128)(2,1)S(1)}, bf16[864,768]{1,0:T(8,128)(2,1)S(1)}, u32[]{:S(2)}, u32[]{:S(2)}) collective-permute-start(bf16[864,768]{1,0:T(8,128)(2,1)S(1)} %stack.35.refs_2_), channel_id=1, source_target_pairs={{0,1},{1,0},{2,3},{3,2},{4,5},{5,4},{6,7},{7,6},{8,9},{9,8},{10,11... | collective-permute-start | bytes 3981320 | tf_op jit(solution)/shard_map/up_core/ppermute | solution.py:800
  69.3 10.7 %collective-permute-start.20 = (bf16[144,768]{1,0:T(8,128)(2,1)S(1)}, bf16[144,768]{1,0:T(8,128)(2,1)S(1)}, u32[]{:S(2)}, u32[]{:S(2)}) collective-permute-start(bf16[144,768]{1,0:T(8,128)(2,1)S(1)} %slice.12), channel_id=1, source_target_pairs={{0,16},{8,24},{16,0},{24,8},{1,17},{9,25},{17,1},{25,9},{2,18},{10... | collective-permute-start | bytes 663560 | tf_op jit(solution)/shard_map/updiag_y/ppermute | solution.py:812
  70.9 9.1 %collective-permute-start.21 = (bf16[144,768]{1,0:T(8,128)(2,1)S(1)}, bf16[144,768]{1,0:T(8,128)(2,1)S(1)}, u32[]{:S(2)}, u32[]{:S(2)}) collective-permute-start(bf16[144,768]{1,0:T(8,128)(2,1)S(1)} %slice.13), channel_id=1, source_target_pairs={{0,8},{8,0},{16,24},{24,16},{1,9},{9,1},{17,25},{25,17},{2,10},{10... | collective-permute-start | bytes 663560 | tf_op jit(solution)/shard_map/updiag_x/ppermute | solution.py:812
  71.4 16.5 %collective-permute-start.24 = (bf16[288,768]{1,0:T(8,128)(2,1)S(1)}, bf16[288,768]{1,0:T(8,128)(2,1)S(1)}, u32[]{:S(2)}, u32[]{:S(2)}) collective-permute-start(bf16[288,768]{1,0:T(8,128)(2,1)S(1)} %stack.37.refs_0_), channel_id=1, source_target_pairs={{0,8},{8,0},{16,24},{24,16},{1,9},{9,1},{17,25},{25,17},{2,10},{10... | collective-permute-start | bytes 1327112 | tf_op jit(solution)/shard_map/down_x/ppermute | solution.py:812
  73.0 14.9 %collective-permute-start.25 = (bf16[288,768]{1,0:T(8,128)(2,1)S(1)}, bf16[288,768]{1,0:T(8,128)(2,1)S(1)}, u32[]{:S(2)}, u32[]{:S(2)}) collective-permute-start(bf16[288,768]{1,0:T(8,128)(2,1)S(1)} %stack.37.refs_0_), channel_id=1, source_target_pairs={{0,16},{8,24},{16,0},{24,8},{1,17},{9,25},{17,1},{25,9},{2,18},{10... | collective-permute-start | bytes 1327112 | tf_op jit(solution)/shard_map/down_y/ppermute | solution.py:812
  88.0 10.5 %collective-permute-start.28 = (bf16[864,768]{1,0:T(8,128)(2,1)S(1)}, bf16[864,768]{1,0:T(8,128)(2,1)S(1)}, u32[]{:S(2)}, u32[]{:S(2)}) collective-permute-start(bf16[864,768]{1,0:T(8,128)(2,1)S(1)} %stack.38.refs_2_), channel_id=1, source_target_pairs={{0,1},{1,0},{2,3},{3,2},{4,5},{5,4},{6,7},{7,6},{8,9},{9,8},{10,11... | collective-permute-start | bytes 3981320 | tf_op jit(solution)/shard_map/down_core/ppermute | solution.py:800
  88.1 9.6 %collective-permute-start.29 = (bf16[384,512]{1,0:T(8,128)(2,1)S(1)}, bf16[384,512]{1,0:T(8,128)(2,1)S(1)}, u32[]{:S(2)}, u32[]{:S(2)}) collective-permute-start(bf16[384,512]{1,0:T(8,128)(2,1)S(1)} %get-tuple-element.344), channel_id=1, source_target_pairs={{0,1},{1,0},{2,3},{3,2},{4,5},{5,4},{6,7},{7,6},{8,9},{9,8},{10,11... | collective-permute-start | bytes 1179656 | tf_op jit(solution)/shard_map/given_core/ppermute | solution.py:800
  88.6 9.2 %collective-permute-start.30 = (bf16[384,512]{1,0:T(8,128)(2,1)S(1)}, bf16[384,512]{1,0:T(8,128)(2,1)S(1)}, u32[]{:S(2)}, u32[]{:S(2)}) collective-permute-start(bf16[384,512]{1,0:T(8,128)(2,1)S(1)} %get-tuple-element.345), channel_id=1, source_target_pairs={{0,1},{1,0},{2,3},{3,2},{4,5},{5,4},{6,7},{7,6},{8,9},{9,8},{10,11... | collective-permute-start | bytes 1179656 | tf_op jit(solution)/shard_map/given_core/ppermute | solution.py:800
  88.7 9.8 %collective-permute-start.26 = (bf16[144,768]{1,0:T(8,128)(2,1)S(1)}, bf16[144,768]{1,0:T(8,128)(2,1)S(1)}, u32[]{:S(2)}, u32[]{:S(2)}) collective-permute-start(bf16[144,768]{1,0:T(8,128)(2,1)S(1)} %slice.14), channel_id=1, source_target_pairs={{0,16},{8,24},{16,0},{24,8},{1,17},{9,25},{17,1},{25,9},{2,18},{10... | collective-permute-start | bytes 663560 | tf_op jit(solution)/shard_map/downdiag_y/ppermute | solution.py:812
  89.3 9.2 %collective-permute-start.27 = (bf16[144,768]{1,0:T(8,128)(2,1)S(1)}, bf16[144,768]{1,0:T(8,128)(2,1)S(1)}, u32[]{:S(2)}, u32[]{:S(2)}) collective-permute-start(bf16[144,768]{1,0:T(8,128)(2,1)S(1)} %slice.15), channel_id=1, source_target_pairs={{0,8},{8,0},{16,24},{24,16},{1,9},{9,1},{17,25},{25,17},{2,10},{10... | collective-permute-start | bytes 663560 | tf_op jit(solution)/shard_map/downdiag_x/ppermute | solution.py:812
  107.6 21.2 %collective-permute-start.37 = (bf16[384,1024]{1,0:T(8,128)(2,1)S(1)}, bf16[384,1024]{1,0:T(8,128)(2,1)S(1)}, u32[]{:S(2)}, u32[]{:S(2)}) collective-permute-start(bf16[384,1024]{1,0:T(8,128)(2,1)S(1)} %get-tuple-element.384), channel_id=1, source_target_pairs={{0,1},{1,0},{2,3},{3,2},{4,5},{5,4},{6,7},{7,6},{8,9},{9,8},{10,11... | collective-permute-start | bytes 2359304 | tf_op jit(solution)/shard_map/given_core/ppermute | solution.py:800
  112.1 15.5 %collective-permute-start.34 = (bf16[2,2,96,768]{3,2,1,0:T(8,128)(2,1)S(1)}, bf16[2,2,96,768]{3,2,1,0:T(8,128)(2,1)S(1)}, u32[]{:S(2)}, u32[]{:S(2)}) collective-permute-start(bf16[2,2,96,768]{3,2,1,0:T(8,128)(2,1)S(1)} %get-tuple-element.378), channel_id=1, source_target_pairs={{0,8},{8,0},{16,24},{24,16},{1,9},{9,1},{17,25},{25,17},{2,10},{10... | collective-permute-start | bytes 1769480 | tf_op jit(solution)/shard_map/gdown_x/ppermute | solution.py:812
  113.6 15.2 %collective-permute-start.35 = (bf16[2,2,96,768]{3,2,1,0:T(8,128)(2,1)S(1)}, bf16[2,2,96,768]{3,2,1,0:T(8,128)(2,1)S(1)}, u32[]{:S(2)}, u32[]{:S(2)}) collective-permute-start(bf16[2,2,96,768]{3,2,1,0:T(8,128)(2,1)S(1)} %get-tuple-element.379), channel_id=1, source_target_pairs={{0,16},{8,24},{16,0},{24,8},{1,17},{9,25},{17,1},{25,9},{2,18},{10... | collective-permute-start | bytes 1769480 | tf_op jit(solution)/shard_map/gdown_y/ppermute | solution.py:812
  115.1 11.9 %collective-permute-start.36 = (bf16[384,512]{1,0:T(8,128)(2,1)S(1)}, bf16[384,512]{1,0:T(8,128)(2,1)S(1)}, u32[]{:S(2)}, u32[]{:S(2)}) collective-permute-start(bf16[384,512]{1,0:T(8,128)(2,1)S(1)} %copy-done.34), channel_id=1, source_target_pairs={{0,1},{1,0},{2,3},{3,2},{4,5},{5,4},{6,7},{7,6},{8,9},{9,8},{10,11... | collective-permute-start | bytes 1179656 | tf_op jit(solution)/shard_map/given_core/ppermute | solution.py:800
  117.9 13.3 %collective-permute-start.41 = (bf16[512,3072]{1,0:T(8,128)(2,1)S(1)}, bf16[512,3072]{1,0:T(8,128)(2,1)S(1)}, u32[]{:S(2)}, u32[]{:S(2)}) collective-permute-start(bf16[512,3072]{1,0:T(8,128)(2,1)S(1)} %get-tuple-element.370.d_hidden), channel_id=1, source_target_pairs={{0,1},{1,0},{2,3},{3,2},{4,5},{5,4},{6,7},{7,6},{8,9},{9,8},{10,11... | collective-permute-start | bytes 9437192 | tf_op jit(solution)/shard_map/d_hidden_core/ppermute | solution.py:800
  128.8 11.5 %collective-permute-start.40 = (bf16[2,512,1536]{2,1,0:T(8,128)(2,1)S(1)}, bf16[2,512,1536]{2,1,0:T(8,128)(2,1)S(1)}, u32[]{:S(2)}, u32[]{:S(2)}) collective-permute-start(bf16[2,512,1536]{2,1,0:T(8,128)(2,1)S(1)} %get-tuple-element.393.refs_12_), channel_id=1, source_target_pairs={{0,1},{1,0},{2,3},{3,2},{4,5},{5,4},{6,7},{7,6},{8,9},{9,8},{10,11... | collective-permute-start | bytes 9437192 | tf_op jit(solution)/shard_map/given_core/ppermute | solution.py:800
  128.8 11.5 %collective-permute-start.39 = (bf16[768,768]{1,0:T(8,128)(2,1)S(1)}, bf16[768,768]{1,0:T(8,128)(2,1)S(1)}, u32[]{:S(2)}, u32[]{:S(2)}) collective-permute-start(bf16[768,768]{1,0:T(8,128)(2,1)S(1)} %attend_back.2.refs_6_.refs_0_), channel_id=1, source_target_pairs={{0,1},{1,0},{2,3},{3,2},{4,5},{5,4},{6,7},{7,6},{8,9},{9,8},{10,11... | collective-permute-start | bytes 3538952 | tf_op jit(solution)/shard_map/d_qkv_core/ppermute | solution.py:800
  129.3 11.0 %collective-permute-start.38 = (bf16[512,768]{1,0:T(8,128)(2,1)S(1)}, bf16[512,768]{1,0:T(8,128)(2,1)S(1)}, u32[]{:S(2)}, u32[]{:S(2)}) collective-permute-start(bf16[512,768]{1,0:T(8,128)(2,1)S(1)} %get-tuple-element.391.refs_10_), channel_id=1, source_target_pairs={{0,1},{1,0},{2,3},{3,2},{4,5},{5,4},{6,7},{7,6},{8,9},{9,8},{10,11... | collective-permute-start | bytes 2359304 | tf_op jit(solution)/shard_map/d_low_core/ppermute | solution.py:800
  129.6 9.9 %collective-permute-start.42 = (bf16[2,96,768]{2,1,0:T(8,128)(2,1)S(1)}, bf16[2,96,768]{2,1,0:T(8,128)(2,1)S(1)}, u32[]{:S(2)}, u32[]{:S(2)}) collective-permute-start(bf16[2,96,768]{2,1,0:T(8,128)(2,1)S(1)} %get-tuple-element.405), channel_id=1, source_target_pairs={{0,16},{8,24},{16,0},{24,8},{1,17},{9,25},{17,1},{25,9},{2,18},{10... | collective-permute-start | bytes 884744 | tf_op jit(solution)/shard_map/gdown2_y/ppermute | solution.py:812
  131.2 9.1 %collective-permute-start.43 = (bf16[2,96,768]{2,1,0:T(8,128)(2,1)S(1)}, bf16[2,96,768]{2,1,0:T(8,128)(2,1)S(1)}, u32[]{:S(2)}, u32[]{:S(2)}) collective-permute-start(bf16[2,96,768]{2,1,0:T(8,128)(2,1)S(1)} %get-tuple-element.406), channel_id=1, source_target_pairs={{0,8},{8,0},{16,24},{24,16},{1,9},{9,1},{17,25},{25,17},{2,10},{10... | collective-permute-start | bytes 884744 | tf_op jit(solution)/shard_map/gdown2_x/ppermute | solution.py:812
  140.4 16.0 %collective-permute-start.46 = (bf16[2,2,96,768]{3,2,1,0:T(8,128)(2,1)}, bf16[2,2,96,768]{3,2,1,0:T(8,128)(2,1)S(1)}, u32[]{:S(2)}, u32[]{:S(2)}) collective-permute-start(bf16[2,2,96,768]{3,2,1,0:T(8,128)(2,1)} %get-tuple-element.422), channel_id=1, source_target_pairs={{0,8},{8,0},{16,24},{24,16},{1,9},{9,1},{17,25},{25,17},{2,10},{10... | collective-permute-start | bytes 1769480 | tf_op jit(solution)/shard_map/gup_x/ppermute | solution.py:812
  141.0 15.4 %collective-permute-start.47 = (bf16[2,2,96,768]{3,2,1,0:T(8,128)(2,1)S(1)}, bf16[2,2,96,768]{3,2,1,0:T(8,128)(2,1)S(1)}, u32[]{:S(2)}, u32[]{:S(2)}) collective-permute-start(bf16[2,2,96,768]{3,2,1,0:T(8,128)(2,1)S(1)} %get-tuple-element.423), channel_id=1, source_target_pairs={{0,16},{8,24},{16,0},{24,8},{1,17},{9,25},{17,1},{25,9},{2,18},{10... | collective-permute-start | bytes 1769480 | tf_op jit(solution)/shard_map/gup_y/ppermute | solution.py:812
  141.7 12.5 %collective-permute-start.48 = (bf16[96,768]{1,0:T(8,128)(2,1)S(1)}, bf16[96,768]{1,0:T(8,128)(2,1)S(1)}, u32[]{:S(2)}, u32[]{:S(2)}) collective-permute-start(bf16[96,768]{1,0:T(8,128)(2,1)S(1)} %get-tuple-element.430), channel_id=1, source_target_pairs={{0,4},{1,5},{2,6},{3,7},{4,0},{5,1},{6,2},{7,3},{8,12},{9,13},{10,... | collective-permute-start | bytes 442376 | tf_op jit(solution)/shard_map/gdown3_z2/ppermute | solution.py:806
  156.7 8.8 %collective-permute-start.49 = (bf16[2,96,768]{2,1,0:T(8,128)(2,1)S(1)}, bf16[2,96,768]{2,1,0:T(8,128)(2,1)S(1)}, u32[]{:S(2)}, u32[]{:S(2)}) collective-permute-start(bf16[2,96,768]{2,1,0:T(8,128)(2,1)S(1)} %get-tuple-element.442), channel_id=1, source_target_pairs={{0,16},{8,24},{16,0},{24,8},{1,17},{9,25},{17,1},{25,9},{2,18},{10... | collective-permute-start | bytes 884744 | tf_op jit(solution)/shard_map/gup2_y/ppermute | solution.py:812
  165.5 15.9 %collective-permute-start.52 = (bf16[2,2,112,768]{3,2,1,0:T(8,128)(2,1)S(1)}, bf16[2,2,112,768]{3,2,1,0:T(8,128)(2,1)S(1)}, u32[]{:S(2)}, u32[]{:S(2)}) collective-permute-start(bf16[2,2,112,768]{3,2,1,0:T(8,128)(2,1)S(1)} %get-tuple-element.446), channel_id=1, source_target_pairs={{0,8},{8,0},{16,24},{24,16},{1,9},{9,1},{17,25},{25,17},{2,10},{10... | collective-permute-start | bytes 2064392 | tf_op jit(solution)/shard_map/gfirst_x/ppermute | solution.py:812
  166.7 15.3 %collective-permute-start.53 = (bf16[2,2,112,768]{3,2,1,0:T(8,128)(2,1)S(1)}, bf16[2,2,112,768]{3,2,1,0:T(8,128)(2,1)S(1)}, u32[]{:S(2)}, u32[]{:S(2)}) collective-permute-start(bf16[2,2,112,768]{3,2,1,0:T(8,128)(2,1)S(1)} %get-tuple-element.447), channel_id=1, source_target_pairs={{0,16},{8,24},{16,0},{24,8},{1,17},{9,25},{17,1},{25,9},{2,18},{10... | collective-permute-start | bytes 2064392 | tf_op jit(solution)/shard_map/gfirst_y/ppermute | solution.py:812
  168.4 12.7 %collective-permute-start.54 = (bf16[96,768]{1,0:T(8,128)(2,1)S(1)}, bf16[96,768]{1,0:T(8,128)(2,1)S(1)}, u32[]{:S(2)}, u32[]{:S(2)}) collective-permute-start(bf16[96,768]{1,0:T(8,128)(2,1)S(1)} %get-tuple-element.461), channel_id=1, source_target_pairs={{0,4},{1,5},{2,6},{3,7},{4,0},{5,1},{6,2},{7,3},{8,12},{9,13},{10,... | collective-permute-start | bytes 442376 | tf_op jit(solution)/shard_map/gup3_z2/ppermute | solution.py:806
  168.9 12.2 %collective-permute-start.55 = (bf16[96,768]{1,0:T(8,128)(2,1)S(1)}, bf16[96,768]{1,0:T(8,128)(2,1)S(1)}, u32[]{:S(2)}, u32[]{:S(2)}) collective-permute-start(bf16[96,768]{1,0:T(8,128)(2,1)S(1)} %get-tuple-element.462), channel_id=1, source_target_pairs={{0,6},{1,7},{2,0},{3,1},{4,2},{5,3},{6,4},{7,5},{8,14},{9,15},{10,... | collective-permute-start | bytes 442376 | tf_op jit(solution)/shard_map/gup3_z3/ppermute | solution.py:806
  172.4 8.7 %collective-permute-start.56 = (bf16[96,768]{1,0:T(8,128)(2,1)S(1)}, bf16[96,768]{1,0:T(8,128)(2,1)S(1)}, u32[]{:S(2)}, u32[]{:S(2)}) collective-permute-start(bf16[96,768]{1,0:T(8,128)(2,1)S(1)} %get-tuple-element.464), channel_id=1, source_target_pairs={{0,2},{1,3},{2,4},{3,5},{4,6},{5,7},{6,0},{7,1},{8,10},{9,11},{10,... | collective-permute-start | bytes 442376 | tf_op jit(solution)/shard_map/gdown3_z1/ppermute | solution.py:806
  182.3 9.7 %collective-permute-start.57 = (bf16[2,112,768]{2,1,0:T(8,128)(2,1)S(1)}, bf16[2,112,768]{2,1,0:T(8,128)(2,1)S(1)}, u32[]{:S(2)}, u32[]{:S(2)}) collective-permute-start(bf16[2,112,768]{2,1,0:T(8,128)(2,1)S(1)} %get-tuple-element.473), channel_id=1, source_target_pairs={{0,16},{8,24},{16,0},{24,8},{1,17},{9,25},{17,1},{25,9},{2,18},{10... | collective-permute-start | bytes 1032200 | tf_op jit(solution)/shard_map/gfirst2_y/ppermute | solution.py:812
  192.2 12.2 %collective-permute-start.60 = (bf16[112,768]{1,0:T(8,128)(2,1)S(1)}, bf16[112,768]{1,0:T(8,128)(2,1)S(1)}, u32[]{:S(2)}, u32[]{:S(2)}) collective-permute-start(bf16[112,768]{1,0:T(8,128)(2,1)S(1)} %get-tuple-element.490), channel_id=1, source_target_pairs={{0,2},{1,3},{2,4},{3,5},{4,6},{5,7},{6,0},{7,1},{8,10},{9,11},{10,... | collective-permute-start | bytes 516104 | tf_op jit(solution)/shard_map/gfirst3_z1/ppermute | solution.py:806
  194.2 11.0 %collective-permute-start.61 = (bf16[112,768]{1,0:T(8,128)(2,1)S(1)}, bf16[112,768]{1,0:T(8,128)(2,1)S(1)}, u32[]{:S(2)}, u32[]{:S(2)}) collective-permute-start(bf16[112,768]{1,0:T(8,128)(2,1)S(1)} %get-tuple-element.491), channel_id=1, source_target_pairs={{0,4},{1,5},{2,6},{3,7},{4,0},{5,1},{6,2},{7,3},{8,12},{9,13},{10,... | collective-permute-start | bytes 516104 | tf_op jit(solution)/shard_map/gfirst3_z2/ppermute | solution.py:806
  195.4 9.8 %collective-permute-start.62 = (bf16[112,768]{1,0:T(8,128)(2,1)S(1)}, bf16[112,768]{1,0:T(8,128)(2,1)S(1)}, u32[]{:S(2)}, u32[]{:S(2)}) collective-permute-start(bf16[112,768]{1,0:T(8,128)(2,1)S(1)} %get-tuple-element.492), channel_id=1, source_target_pairs={{0,6},{1,7},{2,0},{3,1},{4,2},{5,3},{6,4},{7,5},{8,14},{9,15},{10,... | collective-permute-start | bytes 516104 | tf_op jit(solution)/shard_map/gfirst3_z3/ppermute | solution.py:806
  (60 other events, 688.5 us)
